TPU v7x, 32 devices: a whole 2x2x4 slice. The times are simulated.
32 devices in a mesh: section: 2 (over core), expert: 4 (over z), shard: 4 (over y, x).
Axes of the slice: x: 2, y: 2, z: 4, core: 2. Of those that a mesh axis runs over, the one named last changes fastest.
Arguments:
- inputs: bfloat16 [2, 4, 1024, 1536], P(None, 'expert', 'shard'), may hold values from -6 to 6
- cotangent: bfloat16 [2, 4, 1024, 1536], P(None, 'expert', 'shard'), may hold values from -6 to 6
- segments: int32 [2, 4, 1024], P(None, 'expert', 'shard'), may hold values from 0 to 2, as said below
- routes: int32 [2, 2, 4, 1024, 8], P('section', None, 'expert', 'shard'), may hold values from 0 to 19, all different within a row; in each aligned block of 256 rows (0 to 255, 256 to 511, ..., all dimensions but the last counted through in order) at most 153 rows name the same one
- attn_gain: bfloat16 [2, 1536], P('section', ('expert', 'shard')), may hold values from 0.5 to 1.5
- w_query: bfloat16 [2, 1536, 1536], P('section', ('expert', 'shard')), may hold values from -0.15625 to 0.15625
- w_key: bfloat16 [2, 1536, 512], P('section', ('expert', 'shard')), may hold values from -0.15625 to 0.15625
- w_value: bfloat16 [2, 1536, 512], P('section', ('expert', 'shard')), may hold values from -0.15625 to 0.15625
- w_output: bfloat16 [2, 1536, 1536], P('section', ('expert', 'shard')), may hold values from -0.625 to 0.625
- ffn_gain: bfloat16 [2, 1536], P('section', ('expert', 'shard')), may hold values from 0.5 to 1.5
- router: bfloat16 [2, 1536, 20], P('section', ('expert', 'shard')), may hold values from -0.078125 to 0.078125
- w_gate: bfloat16 [2, 20, 1536, 512], P('section', 'expert', 'shard'), may hold values from -0.15625 to 0.15625
- w_up: bfloat16 [2, 20, 1536, 512], P('section', 'expert', 'shard'), may hold values from -0.15625 to 0.15625
- w_down: bfloat16 [2, 20, 512, 1536], P('section', 'expert', None, 'shard'), may hold values from -1 to 1
Outputs:
- layer_out: bfloat16 [2, 2, 4, 1024, 1536], P('section', None, 'expert', 'shard')
- input_grad: bfloat16 [2, 2, 4, 1024, 1536], P('section', None, 'expert', 'shard')
- grad_attn_gain: float32 [2, 1536], P('section', ('expert', 'shard'))
- grad_query: float32 [2, 1536, 1536], P('section', ('expert', 'shard'))
- grad_key: float32 [2, 1536, 512], P('section', ('expert', 'shard'))
- grad_value: float32 [2, 1536, 512], P('section', ('expert', 'shard'))
- grad_output: float32 [2, 1536, 1536], P('section', ('expert', 'shard'))
- grad_ffn_gain: float32 [2, 1536], P('section', ('expert', 'shard'))
- grad_router: float32 [2, 1536, 20], P('section', ('expert', 'shard'))
- grad_gate: float32 [2, 20, 1536, 512], P('section', 'expert', 'shard')
- grad_up: float32 [2, 20, 1536, 512], P('section', 'expert', 'shard')
- grad_down: float32 [2, 20, 512, 1536], P('section', 'expert', None, 'shard')
Inputs may be any that keep to these rules, and one draw needn't show every extreme that they name: `segments`: in each sequence the segment numbers never fall: 0 on the first 1 to 128 positions, 2 on the last 1 to 128, 1 on all between. `routes`: each row names 8 different experts. Within one layer and micro-batch, in the 256 rows of one device no expert is named by more than 153 rows.
All inputs are finite; a program needn't handle non-finite values.
Results may differ from a plain program's by a relative error of at most 0.028.
Values may be sent and summed in bfloat16 or wider, within the bound.
No kernel may reach another device: no remote copies, remote signals or barrier semaphores. Data moves between devices by JAX's collectives and lax.ppermute only.
A program may use at most 448 MiB of HBM per device.

v0:
```python
import math

import jax
import jax.numpy as jnp
from jax import lax
from jax.sharding import PartitionSpec as P

HEADS = 24
KV_HEADS = 8
HEAD = 64


EPSILON = 1e-06
ROPE_BASE = 10000.0
NEGATIVE = -1e30
HIGHEST = lax.Precision.HIGHEST


def from_behind(array, axis, by):
    length = lax.axis_size(axis)
    pairs = [(i, i + by) for i in range(length) if 0 <= i + by < length]
    return lax.ppermute(array, axis, pairs)


def rotary(positions, head_size):
    frequency = 1.0 / ROPE_BASE ** (jnp.arange(0, head_size, 2, dtype=jnp.float32) / head_size)
    angles = positions.astype(jnp.float32)[:, None] * frequency[None, :]
    return (jnp.cos(angles)[:, None, :], jnp.sin(angles)[:, None, :])


def rotate(values, cosine_table, sine_table):
    half_size = values.shape[-1] // 2
    first_half = values[..., :half_size]
    second_half = values[..., half_size:]
    return jnp.concatenate(
        [
            first_half * cosine_table - second_half * sine_table,
            second_half * cosine_table + first_half * sine_table,
        ],
        axis=-1,
    )


def norm_back(grad_in, values, scale_rows, scale_gain):
    shaped = grad_in * scale_gain
    grad_values = scale_rows * shaped - values * scale_rows**3 * jnp.mean(
        shaped * values, axis=-1, keepdims=True
    )
    return (grad_values, jnp.sum(grad_in * values * scale_rows, axis=0))


def joined_rows(piece_list, index):
    return jnp.concatenate([piece[index] for piece in piece_list], axis=0)


def weight_grads(piece_list):
    normed = joined_rows(piece_list, 0)
    grad_query_w = jnp.dot(normed.T, joined_rows(piece_list, 1), preferred_element_type=jnp.float32)
    grad_key_w = jnp.dot(normed.T, joined_rows(piece_list, 2), preferred_element_type=jnp.float32)
    grad_value_w = jnp.dot(normed.T, joined_rows(piece_list, 3), preferred_element_type=jnp.float32)
    grad_output_w = jnp.dot(
        joined_rows(piece_list, 4).T, joined_rows(piece_list, 5), preferred_element_type=jnp.float32
    )
    grad_router_w = jnp.dot(
        joined_rows(piece_list, 6).astype(jnp.float32).T,
        joined_rows(piece_list, 7),
        precision=HIGHEST,
    )
    received = joined_rows(piece_list, 8)
    grad_gate_w = jnp.einsum(
        "sxcd,sxcf->xdf", received, joined_rows(piece_list, 9), preferred_element_type=jnp.float32
    )
    grad_up_w = jnp.einsum(
        "sxcd,sxcf->xdf", received, joined_rows(piece_list, 10), preferred_element_type=jnp.float32
    )
    grad_down_w = jnp.einsum(
        "sxcf,sxcd->xfd",
        joined_rows(piece_list, 11),
        joined_rows(piece_list, 12),
        preferred_element_type=jnp.float32,
    )
    grad_gain_one = piece_list[0][13]
    grad_gain_two = piece_list[0][14]
    for piece in piece_list[1:]:
        grad_gain_one = grad_gain_one + piece[13]
        grad_gain_two = grad_gain_two + piece[14]
    attn_part = (
        grad_gain_one,
        grad_query_w,
        grad_key_w,
        grad_value_w,
        grad_output_w,
        grad_gain_two,
        grad_router_w,
    )
    expert_part = (grad_gate_w, grad_up_w, grad_down_w)
    return (attn_part, expert_part)


def on_device(
    inputs,
    cotangent,
    segments,
    routes,
    attn_gain,
    w_query,
    w_key,
    w_value,
    w_output,
    ffn_gain,
    router,
    w_gate,
    w_up,
    w_down,
):
    section_index = lax.axis_index("section")
    shard_index = lax.axis_index("shard")
    shard_count = lax.axis_size("shard")
    expert_count = lax.axis_size("expert")
    micro_count = inputs.shape[0]
    span_rows = inputs.shape[2]
    model_width = inputs.shape[3]
    seq_rows = span_rows * shard_count
    local_experts = w_gate.shape[1]
    all_experts = local_experts * expert_count
    top_count = routes.shape[-1]
    capacity = 3 * span_rows * top_count // (2 * all_experts)
    group_size = HEADS // KV_HEADS
    query_width = HEADS * HEAD
    kv_width = KV_HEADS * HEAD
    score_scale = 1.0 / math.sqrt(HEAD)
    gain_one, query_full, key_full, value_full, output_full, gain_two, router_full = (
        lax.all_gather(attn_gain[0], ("expert", "shard"), axis=0, tiled=True),
        lax.all_gather(w_query[0], ("expert", "shard"), axis=0, tiled=True),
        lax.all_gather(w_key[0], ("expert", "shard"), axis=0, tiled=True),
        lax.all_gather(w_value[0], ("expert", "shard"), axis=0, tiled=True),
        lax.all_gather(w_output[0], ("expert", "shard"), axis=0, tiled=True),
        lax.all_gather(ffn_gain[0], ("expert", "shard"), axis=0, tiled=True),
        lax.all_gather(router[0], ("expert", "shard"), axis=0, tiled=True),
    )
    gate_full, up_full, down_full = (
        lax.all_gather(w_gate[0], "shard", axis=1, tiled=True),
        lax.all_gather(w_up[0], "shard", axis=1, tiled=True),
        lax.all_gather(w_down[0], "shard", axis=2, tiled=True),
    )
    gain_one_wide = gain_one.astype(jnp.float32)
    gain_two_wide = gain_two.astype(jnp.float32)
    router_wide = router_full.astype(jnp.float32)
    positions = shard_index * span_rows + jnp.arange(span_rows, dtype=jnp.int32)
    cosine_table, sine_table = rotary(positions, HEAD)
    all_places = jnp.arange(seq_rows, dtype=jnp.int32)
    expert_ids = jnp.arange(all_experts, dtype=jnp.int32)

    def score_block(query_rot, key_all, segment_local, segment_all):
        allowed = (all_places[None, :] <= positions[:, None]) & (
            segment_all[None, :] == segment_local[:, None]
        )
        grouped = query_rot.reshape(span_rows, KV_HEADS, group_size, HEAD)
        keyed = key_all.reshape(seq_rows, KV_HEADS, HEAD)
        scores = (
            jnp.einsum("cngd,knd->cngk", grouped, keyed, preferred_element_type=jnp.float32)
            * score_scale
        )
        return jnp.where(allowed[:, None, None, :], scores, NEGATIVE)

    tick_count = micro_count + 1
    arrived = jnp.zeros((span_rows, model_width), jnp.bfloat16)
    results = []
    kept_list = []
    for tick_index in range(tick_count):
        own_index = min(tick_index, micro_count - 1)
        prior_index = max(tick_index - 1, 0)
        stream = jnp.where(section_index == 0, inputs[own_index, 0], arrived).astype(jnp.float32)
        segment_local = jnp.where(
            section_index == 0, segments[own_index, 0], segments[prior_index, 0]
        )
        route_rows = jnp.where(
            section_index == 0, routes[0, own_index, 0], routes[0, prior_index, 0]
        )
        forward_scale_one = lax.rsqrt(jnp.mean(stream * stream, axis=-1, keepdims=True) + EPSILON)
        forward_normed = (stream * forward_scale_one * gain_one_wide).astype(jnp.bfloat16)
        query_raw = jnp.dot(forward_normed, query_full, preferred_element_type=jnp.float32)
        key_raw = jnp.dot(forward_normed, key_full, preferred_element_type=jnp.float32)
        value_raw = jnp.dot(forward_normed, value_full, preferred_element_type=jnp.float32)
        forward_query_rot = (
            rotate(query_raw.reshape(span_rows, HEADS, HEAD), cosine_table, sine_table)
            .astype(jnp.bfloat16)
            .reshape(span_rows, query_width)
        )
        key_rot = (
            rotate(key_raw.reshape(span_rows, KV_HEADS, HEAD), cosine_table, sine_table)
            .astype(jnp.bfloat16)
            .reshape(span_rows, kv_width)
        )
        value_low = value_raw.astype(jnp.bfloat16)
        forward_key_all = lax.all_gather(key_rot, "shard", axis=0, tiled=True)
        forward_value_all = lax.all_gather(value_low, "shard", axis=0, tiled=True)
        forward_segment_all = lax.all_gather(segment_local, "shard", axis=0, tiled=True)
        forward_scores = score_block(
            forward_query_rot, forward_key_all, segment_local, forward_segment_all
        )
        forward_row_max = jnp.max(forward_scores, axis=-1, keepdims=True)
        exponent = jnp.exp(forward_scores - forward_row_max)
        forward_row_sum = jnp.sum(exponent, axis=-1, keepdims=True)
        forward_attn_probs = (exponent / forward_row_sum).astype(jnp.bfloat16)
        weighted = jnp.einsum(
            "cngk,knd->cngd",
            forward_attn_probs,
            forward_value_all.reshape(seq_rows, KV_HEADS, HEAD),
            preferred_element_type=jnp.float32,
        )
        forward_attended = weighted.reshape(span_rows, query_width).astype(jnp.bfloat16)
        forward_middle = stream + jnp.dot(
            forward_attended, output_full, preferred_element_type=jnp.float32
        )
        forward_scale_two = lax.rsqrt(
            jnp.mean(forward_middle * forward_middle, axis=-1, keepdims=True) + EPSILON
        )
        forward_hidden_in = (forward_middle * forward_scale_two * gain_two_wide).astype(
            jnp.bfloat16
        )
        logits = jnp.dot(forward_hidden_in, router_full, preferred_element_type=jnp.float32)
        forward_gate_weights = jax.nn.softmax(
            jnp.take_along_axis(logits, route_rows, axis=1), axis=-1
        )
        flat_ids = route_rows.reshape(-1)
        one_hot = (flat_ids[:, None] == expert_ids[None, :]).astype(jnp.int32)
        slot_index = jnp.sum(jnp.cumsum(one_hot, axis=0) * one_hot, axis=1) - 1
        forward_targets = flat_ids * capacity + slot_index
        send_rows = (
            jnp.zeros((all_experts * capacity, model_width), jnp.bfloat16)
            .at[forward_targets]
            .set(jnp.repeat(forward_hidden_in, top_count, axis=0))
        )
        forward_received = lax.all_to_all(
            send_rows.reshape(expert_count, local_experts, capacity, model_width),
            "expert",
            split_axis=0,
            concat_axis=0,
            tiled=True,
        )
        forward_gate_raw = jnp.einsum(
            "sxcd,xdf->sxcf", forward_received, gate_full, preferred_element_type=jnp.float32
        )
        forward_up_raw = jnp.einsum(
            "sxcd,xdf->sxcf", forward_received, up_full, preferred_element_type=jnp.float32
        )
        forward_activated = (jax.nn.silu(forward_gate_raw) * forward_up_raw).astype(jnp.bfloat16)
        expert_out = jnp.einsum(
            "sxcf,xfd->sxcd", forward_activated, down_full, preferred_element_type=jnp.float32
        ).astype(jnp.bfloat16)
        returned = lax.all_to_all(
            expert_out, "expert", split_axis=0, concat_axis=0, tiled=True
        ).reshape(all_experts * capacity, model_width)
        forward_gathered = returned[forward_targets].reshape(span_rows, top_count, model_width)
        combined = jnp.einsum(
            "ck,ckd->cd",
            forward_gate_weights,
            forward_gathered.astype(jnp.float32),
            precision=HIGHEST,
        )
        forward_kept_state = (
            stream,
            forward_scale_one,
            forward_normed,
            forward_query_rot,
            forward_key_all,
            forward_value_all,
            segment_local,
            forward_segment_all,
            forward_row_max,
            forward_row_sum,
            forward_attended,
            forward_middle,
            forward_scale_two,
            forward_hidden_in,
            forward_gate_weights,
            route_rows,
            forward_targets,
            forward_received,
            forward_gate_raw,
            forward_up_raw,
            forward_gathered,
        )
        result = forward_middle + combined
        kept_state = forward_kept_state
        result_low = result.astype(jnp.bfloat16)
        results.append(result_low)
        kept_list.append(kept_state)
        if tick_index + 1 < tick_count:
            arrived = from_behind(result_low, "section", 1)
    layer_local = jnp.stack(
        [
            jnp.where(section_index == 0, results[micro_index], results[micro_index + 1])
            for micro_index in range(micro_count)
        ]
    )
    incoming = jnp.zeros((span_rows, model_width), jnp.bfloat16)
    grad_list = []
    piece_list = []
    attn_total = None
    expert_total = None
    for tick_index in range(tick_count):
        before_index = max(tick_index - 1, 0)
        after_index = min(tick_index + 1, tick_count - 1)
        kept_state = jax.tree.map(
            lambda first_leaf, second_leaf: jnp.where(section_index == 0, first_leaf, second_leaf),
            kept_list[before_index],
            kept_list[after_index],
        )
        micro_now = tick_index + section_index - 1
        valid_flag = ((micro_now >= 0) & (micro_now < micro_count)).astype(jnp.float32)
        own_cotangent = cotangent[min(tick_index, micro_count - 1), 0]
        grad_out = (
            jnp.where(section_index == 1, own_cotangent, incoming).astype(jnp.float32) * valid_flag
        )
        (
            backward_stream,
            scale_one,
            normed,
            backward_query_rot,
            backward_key_all,
            value_all,
            backward_segment_local,
            backward_segment_all,
            row_max,
            row_sum,
            attended,
            middle,
            scale_two,
            hidden_in,
            gate_weights,
            backward_route_rows,
            targets,
            received,
            gate_raw,
            up_raw,
            gathered,
        ) = kept_state
        grad_gates = jnp.einsum(
            "cd,ckd->ck", grad_out, gathered.astype(jnp.float32), precision=HIGHEST
        )
        grad_slots = (
            (gate_weights[:, :, None] * grad_out[:, None, :])
            .astype(jnp.bfloat16)
            .reshape(span_rows * top_count, model_width)
        )
        send_grads = (
            jnp.zeros((all_experts * capacity, model_width), jnp.bfloat16)
            .at[targets]
            .set(grad_slots)
        )
        grad_expert_out = lax.all_to_all(
            send_grads.reshape(expert_count, local_experts, capacity, model_width),
            "expert",
            split_axis=0,
            concat_axis=0,
            tiled=True,
        )
        sigmoid_gate = jax.nn.sigmoid(gate_raw)
        swish_gate = jax.nn.silu(gate_raw)
        activated = (swish_gate * up_raw).astype(jnp.bfloat16)
        grad_act = jnp.einsum(
            "sxcd,xfd->sxcf", grad_expert_out, down_full, preferred_element_type=jnp.float32
        )
        grad_gate_raw = (
            grad_act * up_raw * sigmoid_gate * (1.0 + gate_raw * (1.0 - sigmoid_gate))
        ).astype(jnp.bfloat16)
        grad_up_raw = (grad_act * swish_gate).astype(jnp.bfloat16)
        grad_rows = (
            jnp.einsum(
                "sxcf,xdf->sxcd", grad_gate_raw, gate_full, preferred_element_type=jnp.float32
            )
            + jnp.einsum("sxcf,xdf->sxcd", grad_up_raw, up_full, preferred_element_type=jnp.float32)
        ).astype(jnp.bfloat16)
        grad_returned = lax.all_to_all(
            grad_rows, "expert", split_axis=0, concat_axis=0, tiled=True
        ).reshape(all_experts * capacity, model_width)
        grad_hidden = jnp.sum(
            grad_returned[targets].reshape(span_rows, top_count, model_width).astype(jnp.float32),
            axis=1,
        )
        grad_chosen = gate_weights * (
            grad_gates - jnp.sum(gate_weights * grad_gates, axis=-1, keepdims=True)
        )
        choice_table = (backward_route_rows[:, :, None] == expert_ids[None, None, :]).astype(
            jnp.float32
        )
        grad_logits = jnp.sum(choice_table * grad_chosen[:, :, None], axis=1)
        grad_hidden = grad_hidden + jnp.dot(grad_logits, router_wide.T, precision=HIGHEST)
        grad_middle, grad_gain_two = norm_back(grad_hidden, middle, scale_two, gain_two_wide)
        grad_middle = grad_out + grad_middle
        grad_branch = grad_middle.astype(jnp.bfloat16)
        grad_attended = jnp.dot(
            grad_branch, output_full.T, preferred_element_type=jnp.float32
        ).astype(jnp.bfloat16)
        backward_scores = score_block(
            backward_query_rot, backward_key_all, backward_segment_local, backward_segment_all
        )
        probs_wide = jnp.exp(backward_scores - row_max) / row_sum
        attn_probs = probs_wide.astype(jnp.bfloat16)
        grad_weighted = grad_attended.reshape(span_rows, KV_HEADS, group_size, HEAD)
        value_heads = value_all.reshape(seq_rows, KV_HEADS, HEAD)
        key_heads = backward_key_all.reshape(seq_rows, KV_HEADS, HEAD)
        query_heads = backward_query_rot.reshape(span_rows, KV_HEADS, group_size, HEAD)
        grad_values = jnp.einsum(
            "cngk,cngd->knd", attn_probs, grad_weighted, preferred_element_type=jnp.float32
        )
        grad_probs = jnp.einsum(
            "cngd,knd->cngk", grad_weighted, value_heads, preferred_element_type=jnp.float32
        )
        grad_scores = (
            probs_wide * (grad_probs - jnp.sum(probs_wide * grad_probs, axis=-1, keepdims=True))
        ).astype(jnp.bfloat16)
        grad_queries = (
            jnp.einsum("cngk,knd->cngd", grad_scores, key_heads, preferred_element_type=jnp.float32)
            * score_scale
        )
        grad_keys = (
            jnp.einsum(
                "cngk,cngd->knd", grad_scores, query_heads, preferred_element_type=jnp.float32
            )
            * score_scale
        )
        grad_keys, grad_values = (
            lax.psum_scatter(
                grad_keys.reshape(seq_rows, kv_width).astype(jnp.bfloat16),
                "shard",
                scatter_dimension=0,
                tiled=True,
            ).astype(jnp.float32),
            lax.psum_scatter(
                grad_values.reshape(seq_rows, kv_width).astype(jnp.bfloat16),
                "shard",
                scatter_dimension=0,
                tiled=True,
            ).astype(jnp.float32),
        )
        grad_query_raw = (
            rotate(grad_queries.reshape(span_rows, HEADS, HEAD), cosine_table, -sine_table)
            .astype(jnp.bfloat16)
            .reshape(span_rows, query_width)
        )
        grad_key_raw = (
            rotate(grad_keys.reshape(span_rows, KV_HEADS, HEAD), cosine_table, -sine_table)
            .astype(jnp.bfloat16)
            .reshape(span_rows, kv_width)
        )
        grad_value_raw = grad_values.astype(jnp.bfloat16)
        grad_normed = (
            jnp.dot(grad_query_raw, query_full.T, preferred_element_type=jnp.float32)
            + jnp.dot(grad_key_raw, key_full.T, preferred_element_type=jnp.float32)
            + jnp.dot(grad_value_raw, value_full.T, preferred_element_type=jnp.float32)
        )
        grad_stream, grad_gain_one = norm_back(
            grad_normed, backward_stream, scale_one, gain_one_wide
        )
        grad_stream = grad_middle + grad_stream
        pieces = (
            normed,
            grad_query_raw,
            grad_key_raw,
            grad_value_raw,
            attended,
            grad_branch,
            hidden_in,
            grad_logits,
            received,
            grad_gate_raw,
            grad_up_raw,
            activated,
            grad_expert_out,
            grad_gain_one,
            grad_gain_two,
        )
        grad_stream, pieces = (grad_stream, pieces)
        grad_low = grad_stream.astype(jnp.bfloat16)
        grad_list.append(grad_low)
        piece_list.append(pieces)
        if tick_index + 1 < tick_count:
            incoming = from_behind(grad_low, "section", -1)
    attn_total, expert_total = weight_grads(piece_list)
    attn_total = (
        lax.psum_scatter(attn_total[0], ("expert", "shard"), scatter_dimension=0, tiled=True),
        lax.psum_scatter(attn_total[1], ("expert", "shard"), scatter_dimension=0, tiled=True),
        lax.psum_scatter(attn_total[2], ("expert", "shard"), scatter_dimension=0, tiled=True),
        lax.psum_scatter(attn_total[3], ("expert", "shard"), scatter_dimension=0, tiled=True),
        lax.psum_scatter(attn_total[4], ("expert", "shard"), scatter_dimension=0, tiled=True),
        lax.psum_scatter(attn_total[5], ("expert", "shard"), scatter_dimension=0, tiled=True),
        lax.psum_scatter(attn_total[6], ("expert", "shard"), scatter_dimension=0, tiled=True),
    )
    expert_total = (
        lax.psum_scatter(
            expert_total[0].astype(jnp.bfloat16), "shard", scatter_dimension=1, tiled=True
        ).astype(jnp.float32),
        lax.psum_scatter(
            expert_total[1].astype(jnp.bfloat16), "shard", scatter_dimension=1, tiled=True
        ).astype(jnp.float32),
        lax.psum_scatter(
            expert_total[2].astype(jnp.bfloat16), "shard", scatter_dimension=2, tiled=True
        ).astype(jnp.float32),
    )
    input_local = jnp.stack(
        [
            jnp.where(section_index == 1, grad_list[micro_index], grad_list[micro_index + 1])
            for micro_index in range(micro_count)
        ]
    )
    out_shape = (1, micro_count, 1, span_rows, model_width)
    return (
        layer_local.reshape(out_shape),
        input_local.reshape(out_shape),
        attn_total[0][None],
        attn_total[1][None],
        attn_total[2][None],
        attn_total[3][None],
        attn_total[4][None],
        attn_total[5][None],
        attn_total[6][None],
        expert_total[0][None],
        expert_total[1][None],
        expert_total[2][None],
    )


def solution(mesh):
    placed = (
        P(None, "expert", "shard", None),
        P(None, "expert", "shard", None),
        P(None, "expert", "shard"),
        P("section", None, "expert", "shard", None),
        P("section", ("expert", "shard")),
        P("section", ("expert", "shard"), None),
        P("section", ("expert", "shard"), None),
        P("section", ("expert", "shard"), None),
        P("section", ("expert", "shard"), None),
        P("section", ("expert", "shard")),
        P("section", ("expert", "shard"), None),
        P("section", "expert", "shard", None),
        P("section", "expert", "shard", None),
        P("section", "expert", None, "shard"),
    )
    return jax.shard_map(
        on_device,
        mesh=mesh,
        in_specs=placed,
        out_specs=(
            P("section", None, "expert", "shard", None),
            P("section", None, "expert", "shard", None),
            P("section", ("expert", "shard")),
            P("section", ("expert", "shard"), None),
            P("section", ("expert", "shard"), None),
            P("section", ("expert", "shard"), None),
            P("section", ("expert", "shard"), None),
            P("section", ("expert", "shard")),
            P("section", ("expert", "shard"), None),
            P("section", "expert", "shard", None),
            P("section", "expert", "shard", None),
            P("section", "expert", None, "shard"),
        ),
        check_vma=False,
    )
```

profile of v0, /device:TPU:9, one launch (start us, length us, event | category | flops | bytes accessed | tf_op | source)
XLA Modules:
  0.0 5258.7 jit_solution(676716280396190519)
XLA Ops:
  12.4 29.2 all-reduce.5
  43.1 25.3 all-gather.39.cloned.1.call-done
  72.3 55.5 %all-gather.41.cloned.1.call-done = bf16[1,1536,512]{2,1,0:T(8,128)(2,1)} async-done(((bf16[1,96,512]{2,1,0:T(8,128)(2,1)}), bf16[1,1536,512]{2,1,0:T(8,128)(2,1)}) %all-gather.41.cloned.1.call-update) | async-done | bytes 1572880 | tf_op jit(solution)/shard_map/all_gather | solution.py:135
  187.8 80.3 %all-gather.43.cloned.1.call-done = bf16[1,1536,1536]{2,1,0:T(8,128)(2,1)} async-done(((bf16[1,96,1536]{2,1,0:T(8,128)(2,1)}), bf16[1,1536,1536]{2,1,0:T(8,128)(2,1)}) %all-gather.43.cloned.1.call-update) | async-done | bytes 4718608 | tf_op jit(solution)/shard_map/all_gather | solution.py:134
  312.8 37.2 all-gather.45.cloned.1.call-done
  354.3 15.4 scatter_custom_fusion
  384.9 50.1 all-gather.49.cloned.1.call-done
  435.0 158.6 %all-to-all-done = bf16[4,5,153,1536]{3,2,1,0:T(8,128)(2,1)} async-done(((bf16[4,5,153,1536]{3,2,1,0:T(8,128)(2,1)}), bf16[4,5,153,1536]{3,2,1,0:T(8,128)(2,1)}, u32[]{:S(2)}, u32[]{:S(2)}) %all-to-all-start) | async-done | bytes 9400352 | tf_op jit(solution)/shard_map/all_to_all | solution.py:235
  650.3 237.5 %all-gather.7 = bf16[1,1536,20]{2,0,1:T(2,128)(2,1)} all-gather(bf16[1,96,20]{2,0,1:T(2,128)(2,1)S(1)} %copy.310), channel_id=9, replica_groups=mesh['section'=2,'expert'=4,'shard'=4] {'expert','shard'}, dimensions={1}, use_global_device_ids=true | all-gather | bytes 65280 | tf_op jit(solution)/shard_map/all_gather | solution.py:139
  890.5 16.8 gather_fusion.6
  916.0 18.2 gather_fusion
  963.1 17.5 all-gather.33.cloned.1.call-done
  1027.5 15.6 scatter_custom_fusion.1
  1051.0 216.1 %all_to_all.60 = bf16[4,5,153,1536]{3,2,1,0:T(8,128)(2,1)S(1)} all-to-all(bf16[4,5,153,1536]{3,2,1,0:T(8,128)(2,1)} %reshape.1233), channel_id=1, replica_groups=mesh['section'=2,'expert'=4,'shard'=4] {'expert'}, dimensions={0} | all-to-all | bytes 18800640 | tf_op jit(solution)/shard_map/all_to_all | solution.py:235
  1267.1 14.0 fusion.78
  1320.1 16.8 gather_fusion.7
  1338.0 188.7 %all-to-all-done.3 = bf16[4,5,153,1536]{3,2,1,0:T(8,128)(2,1)} async-done(((bf16[4,5,153,1536]{3,2,1,0:T(8,128)(2,1)}), bf16[4,5,153,1536]{3,2,1,0:T(8,128)(2,1)}, u32[]{:S(2)}, u32[]{:S(2)}) %all-to-all-start.3) | async-done | bytes 9400352 | tf_op jit(solution)/shard_map/all_to_all | solution.py:252
  1534.7 18.3 gather_fusion.1
  1567.3 16.6 scatter_custom_fusion.3
  1591.9 224.2 %all_to_all.61 = bf16[4,5,153,1536]{3,2,1,0:T(8,128)(2,1)} all-to-all(bf16[4,5,153,1536]{3,2,1,0:T(8,128)(2,1)} %reshape.1246), channel_id=1, replica_groups=mesh['section'=2,'expert'=4,'shard'=4] {'expert'}, dimensions={0} | all-to-all | bytes 18800640 | tf_op jit(solution)/shard_map/all_to_all | solution.py:353
  1816.1 21.5 multiply_convert_fusion.2
  1850.2 15.3 fusion.64
  1892.5 198.3 %all-to-all-done.7 = bf16[4,5,153,1536]{3,2,1,0:T(8,128)(2,1)} async-done(((bf16[4,5,153,1536]{3,2,1,0:T(8,128)(2,1)}), bf16[4,5,153,1536]{3,2,1,0:T(8,128)(2,1)}, u32[]{:S(2)}, u32[]{:S(2)}) %all-to-all-start.7) | async-done | bytes 9400352 | tf_op jit(solution)/shard_map/all_to_all | solution.py:376
  2098.9 18.4 gather_fusion.3
  2146.4 17.9 fusion.14
  2164.3 16.3 fusion.16
  2229.3 19.9 reduce-scatter.21.cloned.1.call-done
  2264.7 20.1 all-gather.37.cloned.1.call-done
  2331.6 15.8 scatter_custom_fusion.2
  2355.4 216.1 %all_to_all.62 = bf16[4,5,153,1536]{3,2,1,0:T(8,128)(2,1)S(1)} all-to-all(bf16[4,5,153,1536]{3,2,1,0:T(8,128)(2,1)} %reshape.1242), channel_id=1, replica_groups=mesh['section'=2,'expert'=4,'shard'=4] {'expert'}, dimensions={0} | all-to-all | bytes 18800640 | tf_op jit(solution)/shard_map/all_to_all | solution.py:235
  2571.5 14.1 fusion.76
  2629.7 16.8 gather_fusion.8
  2647.0 184.3 %all-to-all-done.5 = bf16[4,5,153,1536]{3,2,1,0:T(8,128)(2,1)} async-done(((bf16[4,5,153,1536]{3,2,1,0:T(8,128)(2,1)}), bf16[4,5,153,1536]{3,2,1,0:T(8,128)(2,1)}, u32[]{:S(2)}, u32[]{:S(2)}) %all-to-all-start.5) | async-done | bytes 9400352 | tf_op jit(solution)/shard_map/all_to_all | solution.py:252
  2839.3 18.2 gather_fusion.2
  2872.1 16.4 scatter_custom_fusion.4
  2896.5 224.4 %all_to_all.63 = bf16[4,5,153,1536]{3,2,1,0:T(8,128)(2,1)} all-to-all(bf16[4,5,153,1536]{3,2,1,0:T(8,128)(2,1)} %reshape.1254), channel_id=1, replica_groups=mesh['section'=2,'expert'=4,'shard'=4] {'expert'}, dimensions={0} | all-to-all | bytes 18800640 | tf_op jit(solution)/shard_map/all_to_all | solution.py:353
  3120.9 21.6 multiply_convert_fusion.1
  3155.2 15.0 fusion.65
  3200.9 194.5 %all-to-all-done.9 = bf16[4,5,153,1536]{3,2,1,0:T(8,128)(2,1)} async-done(((bf16[4,5,153,1536]{3,2,1,0:T(8,128)(2,1)}), bf16[4,5,153,1536]{3,2,1,0:T(8,128)(2,1)}, u32[]{:S(2)}, u32[]{:S(2)}) %all-to-all-start.9) | async-done | bytes 9400352 | tf_op jit(solution)/shard_map/all_to_all | solution.py:376
  3403.5 18.1 gather_fusion.4
  3445.6 22.0 fusion.8
  3467.6 16.4 fusion.10
  3524.9 25.7 reduce-scatter.25.cloned.1.call-done
  3576.6 16.4 scatter_custom_fusion.5
  3601.0 220.2 %all_to_all.64 = bf16[4,5,153,1536]{3,2,1,0:T(8,128)(2,1)} all-to-all(bf16[4,5,153,1536]{3,2,1,0:T(8,128)(2,1)} %reshape.1262), channel_id=1, replica_groups=mesh['section'=2,'expert'=4,'shard'=4] {'expert'}, dimensions={0} | all-to-all | bytes 18800640 | tf_op jit(solution)/shard_map/all_to_all | solution.py:353
  3821.2 21.6 multiply_convert_fusion
  3855.4 15.1 fusion.66
  3891.2 205.3 %all-to-all-done.11 = bf16[4,5,153,1536]{3,2,1,0:T(8,128)(2,1)} async-done(((bf16[4,5,153,1536]{3,2,1,0:T(8,128)(2,1)}), bf16[4,5,153,1536]{3,2,1,0:T(8,128)(2,1)}, u32[]{:S(2)}, u32[]{:S(2)}) %all-to-all-start.11) | async-done | bytes 9400352 | tf_op jit(solution)/shard_map/all_to_all | solution.py:376
  4104.5 18.2 gather_fusion.5
  4146.7 22.1 fusion.2
  4181.9 16.8 fusion.4
  4211.1 23.1 bitcast_convert_fusion
  4234.2 15.7 copy.446
  4263.1 21.2 broadcast_select_fusion.2
  4284.3 22.8 bitcast_convert_fusion.2
  4309.1 22.8 bitcast_convert_fusion.1
  4385.6 69.8 %reduce-scatter.45.cloned.1.call-done = bf16[384,2560]{1,0:T(8,128)(2,1)} async-done(((bf16[1536,2560]{1,0:T(8,128)(2,1)}), bf16[384,2560]{1,0:T(8,128)(2,1)}) %reduce-scatter.45.cloned.1.call-update) | async-done | bytes 1966096
  4467.1 74.7 %reduce-scatter.39.cloned.1.call-done = bf16[5,384,512]{2,1,0:T(8,128)(2,1)} async-done(((bf16[5,1536,512]{2,1,0:T(8,128)(2,1)}), bf16[5,384,512]{2,1,0:T(8,128)(2,1)}) %reduce-scatter.39.cloned.1.call-update) | async-done | bytes 1966096 | tf_op jit(solution)/shard_map/reduce_scatter | solution.py:493
  4545.8 82.4 %reduce-scatter.41.cloned.1.call-done = bf16[5,384,512]{2,1,0:T(8,128)(2,1)} async-done(((bf16[5,1536,512]{2,1,0:T(8,128)(2,1)}), bf16[5,384,512]{2,1,0:T(8,128)(2,1)}) %reduce-scatter.41.cloned.1.call-update) | async-done | bytes 1966096 | tf_op jit(solution)/shard_map/reduce_scatter | solution.py:496
  4635.2 56.4 %all-reduce.4 = (f32[1536]{0:T(1024)S(1)}, f32[1536]{0:T(1024)S(1)}) all-reduce(f32[1536]{0:T(1024)S(1)} %add_add_fusion.1, f32[1536]{0:T(1024)S(1)} %add_add_fusion), channel_id=20, replica_groups=mesh['section'=2,'expert'=4,'shard'=4] {'expert','shard'}, use_global_device_ids=true, to_apply=%region_60.62.clone | all-reduce | flops 3072 | bytes 24576
  4696.4 66.1 %reduce-scatter.35.cloned.1.call-done = f32[96,512]{1,0:T(8,128)} async-done(((f32[1536,512]{1,0:T(8,128)}), f32[96,512]{1,0:T(8,128)}) %reduce-scatter.35.cloned.1.call-update) | async-done | bytes 196624 | tf_op jit(solution)/shard_map/reduce_scatter | solution.py:487
  4762.6 135.3 %reduce-scatter.33.cloned.1.call-done = f32[96,512]{1,0:T(8,128)} async-done(((f32[1536,512]{1,0:T(8,128)}), f32[96,512]{1,0:T(8,128)}) %reduce-scatter.33.cloned.1.call-update) | async-done | bytes 196624 | tf_op jit(solution)/shard_map/reduce_scatter | solution.py:486
  4897.9 176.7 %reduce-scatter.37.cloned.1.call-done = f32[96,1536]{1,0:T(8,128)} async-done(((f32[1536,1536]{1,0:T(8,128)}), f32[96,1536]{1,0:T(8,128)}) %reduce-scatter.37.cloned.1.call-update) | async-done | bytes 589840 | tf_op jit(solution)/shard_map/reduce_scatter | solution.py:488
  5074.6 177.0 %reduce-scatter.31.cloned.1.call-done = f32[96,1536]{1,0:T(8,128)} async-done(((f32[1536,1536]{1,0:T(8,128)}), f32[96,1536]{1,0:T(8,128)}) %reduce-scatter.31.cloned.1.call-update) | async-done | bytes 589840 | tf_op jit(solution)/shard_map/reduce_scatter | solution.py:485
  (868 shorter events, 960.3 us)
Async XLA Ops:
  7.2 122.3 %copy-start.27 = (bf16[2,1,256,1536]{3,2,1,0:T(8,128)(2,1)S(1)}, bf16[2,1,256,1536]{3,2,1,0:T(8,128)(2,1)}, u32[]{:S(2)}) copy-start(bf16[2,1,256,1536]{3,2,1,0:T(8,128)(2,1)} %param.16) | copy-start | bytes 4718596
  7.2 61.2 %all-gather.39.cloned.1.call-start = ((), (), s32[]{:S(2)}) async-start(), calls=%async_computation.44 | async-start | bytes 1671168 | tf_op jit(solution)/shard_map/all_gather | solution.py:136
  7.9 119.9 %all-gather.41.cloned.1.call-start = ((), (), s32[]{:S(2)}) async-start(), calls=%async_computation.45 | async-start | bytes 1671168 | tf_op jit(solution)/shard_map/all_gather | solution.py:135
  8.7 166.5 %all-gather.27.cloned.1.call-start = ((), (), s32[]{:S(2)}) async-start(), calls=%async_computation.26 | async-start | bytes 1310720 | tf_op jit(solution)/shard_map/all_gather | solution.py:197
  41.6 233.2 %copy-start.168 = (f32[1536]{0:T(1024)}, f32[1536]{0:T(1024)S(1)}, u32[]{:S(2)}) copy-start(f32[1536]{0:T(1024)S(1)} %convert_element_type.568) | copy-start | bytes 18436
  43.1 231.7 %copy-start.217 = (f32[256]{0:T(256)}, f32[256]{0:T(256)S(1)}, u32[]{:S(2)}) copy-start(f32[256]{0:T(256)S(1)} %add_rsqrt_fusion.5) | copy-start | bytes 3076
  71.4 114.9 %all-gather.29.cloned.1.call-start = ((), (), s32[]{:S(2)}) async-start(), calls=%async_computation.27 | async-start | bytes 1310720 | tf_op jit(solution)/shard_map/all_gather | solution.py:196
  72.3 206.4 %copy-start.64 = (f32[256,32]{0,1:T(8,128)}, f32[256,32]{0,1:T(8,128)S(1)}, u32[]{:S(2)}) copy-start(f32[256,32]{0,1:T(8,128)S(1)} %get-tuple-element.215) | copy-start | bytes 98308
  72.3 206.4 %copy-start.104 = (f32[256,32]{0,1:T(8,128)}, f32[256,32]{0,1:T(8,128)S(1)}, u32[]{:S(2)}) copy-start(f32[256,32]{0,1:T(8,128)S(1)} %get-tuple-element.214) | copy-start | bytes 98308
  131.2 136.9 %all-gather.43.cloned.1.call-start = ((), (), s32[]{:S(2)}) async-start(), calls=%async_computation.46 | async-start | bytes 5013504 | tf_op jit(solution)/shard_map/all_gather | solution.py:134
  131.8 218.2 %all-gather.45.cloned.1.call-start = ((), (), s32[]{:S(2)}) async-start(), calls=%async_computation.47 | async-start | bytes 5013504 | tf_op jit(solution)/shard_map/all_gather | solution.py:137
  132.4 302.6 %all-gather.49.cloned.1.call-start = ((), (), s32[]{:S(2)}) async-start(), calls=%async_computation.49 | async-start | bytes 9830400 | tf_op jit(solution)/shard_map/all_gather | solution.py:143
  133.1 472.8 %all-gather.47.cloned.1.call-start = ((), (), s32[]{:S(2)}) async-start(), calls=%async_computation.48 | async-start | bytes 9830400 | tf_op jit(solution)/shard_map/all_gather | solution.py:142
  134.0 515.3 %copy-start.31 = (s32[1,1,1,256,8]{4,3,2,1,0:T(8,128)}, s32[1,1,1,256,8]{4,3,2,1,0:T(8,128)S(1)}, u32[]{:S(2)}) copy-start(s32[1,1,1,256,8]{4,3,2,1,0:T(8,128)S(1)} %copy.449) | copy-start | bytes 24580
  134.4 773.3 %copy-start.34 = (s32[1,1,1,256,8]{4,3,2,1,0:T(8,128)}, s32[1,1,1,256,8]{4,3,2,1,0:T(8,128)S(1)}, u32[]{:S(2)}) copy-start(s32[1,1,1,256,8]{4,3,2,1,0:T(8,128)S(1)} %copy.448) | copy-start | bytes 24580
  152.4 201.7 %copy-start.123 = (f32[1536]{0:T(1024)}, f32[1536]{0:T(1024)S(1)}, u32[]{:S(2)}) copy-start(f32[1536]{0:T(1024)S(1)} %convert_element_type.569) | copy-start | bytes 18436
  312.8 41.3 copy-start.46
  354.1 672.1 %copy-start.3 = (f32[256,1536]{1,0:T(8,128)}, f32[256,1536]{1,0:T(8,128)S(1)}, u32[]{:S(2)}) copy-start(f32[256,1536]{1,0:T(8,128)S(1)} %get-tuple-element.235) | copy-start | bytes 4718596
  377.7 215.9 %all-to-all-start = ((bf16[4,5,153,1536]{3,2,1,0:T(8,128)(2,1)}), bf16[4,5,153,1536]{3,2,1,0:T(8,128)(2,1)}, u32[]{:S(2)}, u32[]{:S(2)}) async-start(bf16[4,5,153,1536]{3,2,1,0:T(8,128)(2,1)} %reshape.1224), calls=%async_computation | async-start | bytes 19660800 | tf_op jit(solution)/shard_map/all_to_all | solution.py:235
  384.2 233.6 %all-gather.51.cloned.1.call-start = ((), (), s32[]{:S(2)}) async-start(), calls=%async_computation.50 | async-start | bytes 9830400 | tf_op jit(solution)/shard_map/all_gather | solution.py:144
  639.1 268.7 %all-to-all-start.1 = ((bf16[4,5,153,1536]{3,2,1,0:T(8,128)(2,1)}), bf16[4,5,153,1536]{3,2,1,0:T(8,128)(2,1)}, u32[]{:S(2)}, u32[]{:S(2)}) async-start(bf16[4,5,153,1536]{3,2,1,0:T(8,128)(2,1)} %copy.316), calls=%async_computation.1 | async-start | bytes 19660800 | tf_op jit(solution)/shard_map/all_to_all | solution.py:252
  649.2 331.4 %all-gather.33.cloned.1.call-start = ((), (), s32[]{:S(2)}) async-start(), calls=%async_computation.29 | async-start | bytes 1310720 | tf_op jit(solution)/shard_map/all_gather | solution.py:196
  941.8 12.2 collective-permute-start
  954.3 69.6 %copy-start.16 = (bf16[256,1536]{1,0:T(8,128)(2,1)}, bf16[256,1536]{1,0:T(8,128)(2,1)S(1)}, u32[]{:S(2)}) copy-start(bf16[256,1536]{1,0:T(8,128)(2,1)S(1)} %get-tuple-element.131) | copy-start | bytes 2359300
  956.9 52.8 %all-gather.31.cloned.1.call-start = ((), (), s32[]{:S(2)}) async-start(), calls=%async_computation.28 | async-start | bytes 1310720 | tf_op jit(solution)/shard_map/all_gather | solution.py:197
  1027.5 292.3 %copy-start.36 = (bf16[256,1536]{1,0:T(8,128)(2,1)}, bf16[256,1536]{1,0:T(8,128)(2,1)S(1)}, u32[]{:S(2)}) copy-start(bf16[256,1536]{1,0:T(8,128)(2,1)S(1)} %get-tuple-element.90) | copy-start | bytes 2359300
  1051.0 230.1 %slice-start.10 = ((s8[7864320]{0:T(1024)(128)(4,1)}), s8[4194304]{0:T(1024)(128)(4,1)S(1)}, s32[]{:S(2)}) async-start(s8[7864320]{0:T(1024)(128)(4,1)} %bitcast.991), calls=%async_computation.63 | async-start | bytes 8388608
  1309.6 217.1 %all-to-all-start.3 = ((bf16[4,5,153,1536]{3,2,1,0:T(8,128)(2,1)}), bf16[4,5,153,1536]{3,2,1,0:T(8,128)(2,1)}, u32[]{:S(2)}, u32[]{:S(2)}) async-start(bf16[4,5,153,1536]{3,2,1,0:T(8,128)(2,1)} %copy.328), calls=%async_computation.3 | async-start | bytes 19660800 | tf_op jit(solution)/shard_map/all_to_all | solution.py:252
  1873.9 217.0 %all-to-all-start.7 = ((bf16[4,5,153,1536]{3,2,1,0:T(8,128)(2,1)}), bf16[4,5,153,1536]{3,2,1,0:T(8,128)(2,1)}, u32[]{:S(2)}, u32[]{:S(2)}) async-start(bf16[4,5,153,1536]{3,2,1,0:T(8,128)(2,1)} %copy.341), calls=%async_computation.7 | async-start | bytes 19660800 | tf_op jit(solution)/shard_map/all_to_all | solution.py:376
  1881.8 343.1 %reduce-scatter.19.cloned.1.call-start = ((), (), s32[]{:S(2)}) async-start(), calls=%async_computation.32 | async-start | bytes 1310720 | tf_op jit(solution)/shard_map/reduce_scatter | solution.py:426
  1892.5 232.1 %copy-start.174 = (f32[256,20]{0,1:T(8,128)}, f32[256,20]{0,1:T(8,128)S(1)}, u32[]{:S(2)}) copy-start(f32[256,20]{0,1:T(8,128)S(1)} %select_reduce_fusion.2) | copy-start | bytes 61444
  2187.3 61.9 %reduce-scatter.21.cloned.1.call-start = ((), (), s32[]{:S(2)}) async-start(), calls=%async_computation.33 | async-start | bytes 1310720 | tf_op jit(solution)/shard_map/reduce_scatter | solution.py:432
  2196.4 56.7 %collective-permute-start.1 = (bf16[256,1536]{1,0:T(8,128)(2,1)}, bf16[256,1536]{1,0:T(8,128)(2,1)}, u32[]{:S(2)}, u32[]{:S(2)}) collective-permute-start(bf16[256,1536]{1,0:T(8,128)(2,1)} %get-tuple-element.125), channel_id=1, source_target_pairs={{0,16},{1,17},{2,18},{3,19},{4,20},{5,21},{6,22},{7,23},{8,24},{9,... | collective-permute-start | bytes 2359304 | tf_op jit(solution)/shard_map/ppermute | solution.py:22
  2211.3 73.4 %all-gather.37.cloned.1.call-start = ((), (), s32[]{:S(2)}) async-start(), calls=%async_computation.31 | async-start | bytes 1310720 | tf_op jit(solution)/shard_map/all_gather | solution.py:196
  2256.0 71.9 %copy-start.24 = (bf16[256,1536]{1,0:T(8,128)(2,1)}, bf16[256,1536]{1,0:T(8,128)(2,1)S(1)}, u32[]{:S(2)}) copy-start(bf16[256,1536]{1,0:T(8,128)(2,1)S(1)} %get-tuple-element.127) | copy-start | bytes 2359300
  2258.5 55.2 %all-gather.35.cloned.1.call-start = ((), (), s32[]{:S(2)}) async-start(), calls=%async_computation.30 | async-start | bytes 1310720 | tf_op jit(solution)/shard_map/all_gather | solution.py:197
  2331.6 297.8 %copy-start.38 = (bf16[256,1536]{1,0:T(8,128)(2,1)}, bf16[256,1536]{1,0:T(8,128)(2,1)S(1)}, u32[]{:S(2)}) copy-start(bf16[256,1536]{1,0:T(8,128)(2,1)S(1)} %get-tuple-element.92) | copy-start | bytes 2359300
  2355.4 230.3 %slice-start.12 = ((s8[7864320]{0:T(1024)(128)(4,1)}), s8[4194304]{0:T(1024)(128)(4,1)S(1)}, s32[]{:S(2)}) async-start(s8[7864320]{0:T(1024)(128)(4,1)} %bitcast.993), calls=%async_computation.65 | async-start | bytes 8388608
  2614.2 217.1 %all-to-all-start.5 = ((bf16[4,5,153,1536]{3,2,1,0:T(8,128)(2,1)}), bf16[4,5,153,1536]{3,2,1,0:T(8,128)(2,1)}, u32[]{:S(2)}, u32[]{:S(2)}) async-start(bf16[4,5,153,1536]{3,2,1,0:T(8,128)(2,1)} %copy.339), calls=%async_computation.5 | async-start | bytes 19660800 | tf_op jit(solution)/shard_map/all_to_all | solution.py:252
  2622.1 5.9 collective-permute-start.2
  3178.5 216.9 %all-to-all-start.9 = ((bf16[4,5,153,1536]{3,2,1,0:T(8,128)(2,1)}), bf16[4,5,153,1536]{3,2,1,0:T(8,128)(2,1)}, u32[]{:S(2)}, u32[]{:S(2)}) async-start(bf16[4,5,153,1536]{3,2,1,0:T(8,128)(2,1)} %copy.351), calls=%async_computation.11 | async-start | bytes 19660800 | tf_op jit(solution)/shard_map/all_to_all | solution.py:376
  3186.4 333.5 %reduce-scatter.23.cloned.1.call-start = ((), (), s32[]{:S(2)}) async-start(), calls=%async_computation.34 | async-start | bytes 1310720 | tf_op jit(solution)/shard_map/reduce_scatter | solution.py:426
  3200.9 228.0 %copy-start.176 = (f32[256,20]{0,1:T(8,128)}, f32[256,20]{0,1:T(8,128)S(1)}, u32[]{:S(2)}) copy-start(f32[256,20]{0,1:T(8,128)S(1)} %select_reduce_fusion.1) | copy-start | bytes 61444
  3488.9 61.7 %reduce-scatter.25.cloned.1.call-start = ((), (), s32[]{:S(2)}) async-start(), calls=%async_computation.35 | async-start | bytes 1310720 | tf_op jit(solution)/shard_map/reduce_scatter | solution.py:432
  3515.9 34.8 copy-start.213
  3557.3 4.5 collective-permute-start.3
  3878.9 217.6 %all-to-all-start.11 = ((bf16[4,5,153,1536]{3,2,1,0:T(8,128)(2,1)}), bf16[4,5,153,1536]{3,2,1,0:T(8,128)(2,1)}, u32[]{:S(2)}, u32[]{:S(2)}) async-start(bf16[4,5,153,1536]{3,2,1,0:T(8,128)(2,1)} %copy.361), calls=%async_computation.15 | async-start | bytes 19660800 | tf_op jit(solution)/shard_map/all_to_all | solution.py:376
  3886.7 445.3 %reduce-scatter.29.cloned.1.call-start = ((), (), s32[]{:S(2)}) async-start(), calls=%async_computation.37 | async-start | bytes 1310720 | tf_op jit(solution)/shard_map/reduce_scatter | solution.py:432
  4181.8 156.0 %reduce-scatter.27.cloned.1.call-start = ((), (), s32[]{:S(2)}) async-start(), calls=%async_computation.36 | async-start | bytes 1310720 | tf_op jit(solution)/shard_map/reduce_scatter | solution.py:426
  4205.5 173.7 %reduce-scatter.43.cloned.1.call-start = ((), (), s32[]{:S(2)}) async-start(), calls=%async_computation.51 | async-start | bytes 835584
  4210.6 244.8 %reduce-scatter.45.cloned.1.call-start = ((), (), s32[]{:S(2)}) async-start(), calls=%async_computation.52 | async-start | bytes 9830400
  4262.9 278.9 %reduce-scatter.39.cloned.1.call-start = ((), (), s32[]{:S(2)}) async-start(), calls=%async_computation.42 | async-start | bytes 9830400 | tf_op jit(solution)/shard_map/reduce_scatter | solution.py:493
  4307.1 321.0 %reduce-scatter.41.cloned.1.call-start = ((), (), s32[]{:S(2)}) async-start(), calls=%async_computation.43 | async-start | bytes 9830400 | tf_op jit(solution)/shard_map/reduce_scatter | solution.py:496
  4332.0 430.6 %reduce-scatter.35.cloned.1.call-start = ((), (), s32[]{:S(2)}) async-start(), calls=%async_computation.40 | async-start | bytes 3342336 | tf_op jit(solution)/shard_map/reduce_scatter | solution.py:487
  4337.8 560.1 %reduce-scatter.33.cloned.1.call-start = ((), (), s32[]{:S(2)}) async-start(), calls=%async_computation.39 | async-start | bytes 3342336 | tf_op jit(solution)/shard_map/reduce_scatter | solution.py:486
  4343.5 731.1 %reduce-scatter.37.cloned.1.call-start = ((), (), s32[]{:S(2)}) async-start(), calls=%async_computation.41 | async-start | bytes 10027008 | tf_op jit(solution)/shard_map/reduce_scatter | solution.py:488
  4353.2 898.4 %reduce-scatter.31.cloned.1.call-start = ((), (), s32[]{:S(2)}) async-start(), calls=%async_computation.38 | async-start | bytes 10027008 | tf_op jit(solution)/shard_map/reduce_scatter | solution.py:485
  4467.1 165.2 %copy-start.23 = (bf16[1,1536,512]{2,1,0:T(8,128)(2,1)S(1)}, bf16[1,1536,512]{2,1,0:T(8,128)(2,1)}, u32[]{:S(2)}) copy-start(bf16[1,1536,512]{2,1,0:T(8,128)(2,1)} %all-gather.41.cloned.1.call-done) | copy-start | bytes 4718596
  4545.8 87.2 %copy-start.19 = (bf16[256,1536]{1,0:T(8,128)(2,1)S(1)}, bf16[256,1536]{1,0:T(8,128)(2,1)}, u32[]{:S(2)}) copy-start(bf16[256,1536]{1,0:T(8,128)(2,1)} %copy-done.16) | copy-start | bytes 2359300
  4545.8 87.2 %copy-start.26 = (bf16[256,1536]{1,0:T(8,128)(2,1)S(1)}, bf16[256,1536]{1,0:T(8,128)(2,1)}, u32[]{:S(2)}) copy-start(bf16[256,1536]{1,0:T(8,128)(2,1)} %copy-done.24) | copy-start | bytes 2359300
  4545.8 87.2 %copy-start.172 = (f32[1536]{0:T(1024)S(1)}, f32[1536]{0:T(1024)}, u32[]{:S(2)}) copy-start(f32[1536]{0:T(1024)} %copy-done.168) | copy-start | bytes 18436
  4545.8 87.2 %copy-start.206 = (f32[256]{0:T(256)S(1)}, f32[256]{0:T(256)}, u32[]{:S(2)}) copy-start(f32[256]{0:T(256)} %get-tuple-element.96) | copy-start | bytes 3076
  4632.4 60.5 %copy-start.223 = (f32[256]{0:T(256)S(1)}, f32[256]{0:T(256)}, u32[]{:S(2)}) copy-start(f32[256]{0:T(256)} %get-tuple-element.95) | copy-start | bytes 3076
  4633.0 59.8 %copy-start.59 = (f32[256,1536]{1,0:T(8,128)S(1)}, f32[256,1536]{1,0:T(8,128)}, u32[]{:S(2)}) copy-start(f32[256,1536]{1,0:T(8,128)} %get-tuple-element.98) | copy-start | bytes 4718596
  (216 other events, 2110.9 us)
Sparse Core Ops, SparseCore 0:
  10.8 57.5 all-gather.38
  71.2 56.5 all-gather.40
  130.2 27.0 all-gather.26
  159.6 26.6 all-gather.28
  189.0 79.1 all-gather.42
  270.8 79.1 all-gather.44
  351.8 83.1 all-gather.48
  436.8 83.2 all-gather.46
  521.9 83.0 all-gather.50
  957.0 23.5 all-gather.32
  983.0 26.6 all-gather.30
  2187.5 30.8 reduce-scatter.18
  2221.5 27.6 reduce-scatter.20
  2258.7 26.0 all-gather.36
  2287.0 26.6 all-gather.34
  3489.0 30.8 reduce-scatter.22
  3522.9 27.7 reduce-scatter.24
  4182.0 30.1 reduce-scatter.28
  4215.3 27.7 reduce-scatter.26
  4247.6 120.6 reduce-scatter.42
  4371.3 84.1 reduce-scatter.44
  4458.4 83.3 reduce-scatter.38
  4544.8 83.3 reduce-scatter.40
  4633.6 128.9 reduce-scatter.34
  4768.1 129.7 reduce-scatter.32
  4904.0 170.5 reduce-scatter.36
  5081.7 169.8 reduce-scatter.30
where the time goes:
time: 5270 us; the launch traced here: 5260 us
  waiting for transfers between devices  2280 us (43%)
  blocking collectives  1440 us (27%)
  matrix products  725 us (14%)
  local copies, waits for them, and re-layouts  455 us (9%)
  other arithmetic  265 us (5%)
  starting transfers between devices  68.3 us (1%)
    all_to_all x3, blocking collectives, on_device(): lax.all_to_all(send_grads.reshape(expert_count, local_experts, capacity,...  669 us
    all_to_all x3, waiting for transfers between devices, on_device(): lax.all_to_all(grad_rows, 'expert', split_axis=0, concat_axis=0, tiled=True)  598 us
    all_to_all x2, blocking collectives, on_device(): lax.all_to_all(send_rows.reshape(expert_count, local_experts, capacity, m...  432 us
    all_to_all x3, waiting for transfers between devices, on_device(): lax.all_to_all(expert_out, 'expert', split_axis=0, concat_axis=0, tiled=T...  373 us
    all_gather x1, blocking collectives, on_device(): lax.all_gather(router[0], ('expert', 'shard'), axis=0, tiled=True)  238 us
    reduce_scatter x1, waiting for transfers between devices, on_device(): lax.psum_scatter(attn_total[1], ('expert', 'shard'), scatter_dimension=0,...  177 us
    reduce_scatter x1, waiting for transfers between devices, on_device(): lax.psum_scatter(attn_total[4], ('expert', 'shard'), scatter_dimension=0,...  177 us
    all_to_all x1, waiting for transfers between devices, on_device(): lax.all_to_all(send_rows.reshape(expert_count, local_experts, capacity, m...  159 us
  transfers between devices with their start and end apart: 38, of which 29 were waited for; matrix products, arithmetic and copies ran while one was open for 11% of the time, Pallas kernels for 0%

commit v1 on v0

v1 whole, which is shorter than its diff:
```python
import functools
import math

import jax
import jax.numpy as jnp
from jax import lax
from jax.experimental import pallas as pl
from jax.experimental.pallas import tpu as pltpu
from jax.sharding import PartitionSpec as P

HEADS = 24
KV_HEADS = 8
HEAD = 64

EPSILON = 1e-06
ROPE_BASE = 10000.0
NEGATIVE = -1e30
LANES = 128
MISC = 256
TILE = 256
VMEM_LIMIT = 60 * 1024 * 1024

F32 = jnp.float32
BF16 = jnp.bfloat16


def swap(array):
    return lax.ppermute(array, "section", [(0, 1), (1, 0)])


def shifted(array, axis, by):
    length = lax.axis_size(axis)
    return lax.ppermute(array, axis, [(i, (i + by) % length) for i in range(length)])


def flipped(array, mask):
    return lax.ppermute(array, "shard", [(i, i ^ mask) for i in range(lax.axis_size("shard"))])


def slots_of(array, axis):
    return [array] + [shifted(array, axis, k) for k in range(1, lax.axis_size(axis))]


def after(array, *others):
    return lax.optimization_barrier((array, *others))[0]


def cut(array, start, stop, axis):
    return lax.slice_in_dim(array, start, stop, axis=axis)


def ring_gather(array, axis):
    count = lax.axis_size("shard")
    me = lax.axis_index("shard")
    if count != 4:
        return [
            (slot, lax.rem(me - k + count, count), 0)
            for k, slot in enumerate(slots_of(array, "shard"))
        ]
    length = array.shape[axis]
    half = length // 2
    one = flipped(array, 1)
    two = flipped(array, 2)
    far_low = flipped(cut(one, 0, half, axis), 2)
    far_high = flipped(cut(two, half, length, axis), 1)
    return [
        (array, me, 0),
        (one, me ^ 1, 0),
        (two, me ^ 2, 0),
        (far_low, me ^ 3, 0),
        (far_high, me ^ 3, half),
    ]


def ring_scatter(pieces, axis):
    count = lax.axis_size("shard")
    if count != 4:
        total = pieces[0].astype(F32)
        for k in range(1, count):
            total = total + shifted(pieces[k], "shard", -k).astype(F32)
        return total
    own, one, two, far_low, far_high = pieces
    half = far_low.shape[axis]
    length = own.shape[axis]
    low = flipped(far_low, 2)
    high = flipped(far_high, 1)
    one_high = flipped(cut(one, half, length, axis), 1)
    two_low = flipped(cut(two, 0, half, axis), 2)
    one_low = flipped((cut(one, 0, half, axis).astype(F32) + low.astype(F32)).astype(BF16), 1)
    two_high = flipped(
        (cut(two, half, length, axis).astype(F32) + high.astype(F32)).astype(BF16), 2
    )
    return own.astype(F32) + jnp.concatenate(
        [
            one_low.astype(F32) + two_low.astype(F32),
            one_high.astype(F32) + two_high.astype(F32),
        ],
        axis=axis,
    )


def rotary(positions, head_size):
    frequency = 1.0 / ROPE_BASE ** (jnp.arange(0, head_size, 2, dtype=F32) / head_size)
    angles = positions.astype(F32)[:, None] * frequency[None, :]
    return (jnp.cos(angles)[:, None, :], jnp.sin(angles)[:, None, :])


def rotate(values, cosine_table, sine_table):
    half_size = values.shape[-1] // 2
    first_half = values[..., :half_size]
    second_half = values[..., half_size:]
    return jnp.concatenate(
        [
            first_half * cosine_table - second_half * sine_table,
            second_half * cosine_table + first_half * sine_table,
        ],
        axis=-1,
    )


def norm_back(grad_in, values, scale_rows, scale_gain):
    shaped = grad_in * scale_gain
    grad_values = scale_rows * shaped - values * scale_rows**3 * jnp.mean(
        shaped * values, axis=-1, keepdims=True
    )
    return (grad_values, jnp.sum(grad_in * values * scale_rows, axis=0))


def dot_nt(left, right):
    return lax.dot_general(left, right, (((1,), (1,)), ((), ())), preferred_element_type=F32)


def dot_nn(left, right):
    return jnp.dot(left, right, preferred_element_type=F32)


def dot_tn(left, right):
    return lax.dot_general(left, right, (((0,), (0,)), ((), ())), preferred_element_type=F32)


def fill_weights(off_ref, piece_refs, count, gate_up, down):
    for index in range(2 * count):
        half, place = divmod(index, count)
        ref = piece_refs[index]
        rows = ref.shape[1]
        width = ref.shape[2] // 3
        span = pl.ds(pl.multiple_of(off_ref[place], 16), rows)
        gate_up[span, 2 * half * width : 2 * (half + 1) * width] = ref[0, :, : 2 * width]
        down[span, half * width : (half + 1) * width] = ref[0, :, 2 * width :]


def column_of(table, index):
    lane = lax.broadcasted_iota(jnp.int32, table.shape, 1)
    return jnp.sum(jnp.where(lane == index, table, 0.0), axis=1, keepdims=True)


def split_gate_up(raw, width):
    gate = jnp.concatenate([raw[:, :width], raw[:, 2 * width : 3 * width]], axis=1)
    up = jnp.concatenate([raw[:, width : 2 * width], raw[:, 3 * width :]], axis=1)
    return gate, up


def join_gate_up(gate, up, width):
    return jnp.concatenate(
        [gate[:, :width], up[:, :width], gate[:, width:], up[:, width:]], axis=1
    )


def moe_forward(rows, gates, mine, other, offsets):
    total, model = rows.shape
    experts = mine[0].shape[0]
    width = mine[0].shape[2] // 3
    count = len(mine)
    tile = min(TILE, total)

    def body(off_ref, rows_ref, gates_ref, *rest):
        pieces = rest[: 2 * count]
        out_ref, raw_ref, gate_up, down, sums = rest[2 * count :]
        expert = pl.program_id(0)
        fill_weights(off_ref, pieces, count, gate_up, down)

        def step(index, carry):
            span = pl.ds(pl.multiple_of(index * tile, tile), tile)
            raw = dot_nn(rows_ref[span, :], gate_up[...])
            raw_ref[0, span, :] = raw.astype(BF16)
            gate, up = split_gate_up(raw, width)
            weight = column_of(gates_ref[span, :], expert)
            act = (gate * jax.nn.sigmoid(gate) * up * weight).astype(BF16)
            part = dot_nt(act, down[...])

            @pl.when(expert == 0)
            def _():
                sums[span, :] = part

            @pl.when(expert > 0)
            def _():
                sums[span, :] += part

            @pl.when(expert == experts - 1)
            def _():
                out_ref[span, :] = sums[span, :].astype(BF16)

            return carry

        lax.fori_loop(0, total // tile, step, 0)

    whole = lambda e, *_: (0, 0)
    per_expert = lambda e, *_: (e, 0, 0)
    once = pl.Buffered(1)
    return pl.pallas_call(
        body,
        grid_spec=pltpu.PrefetchScalarGridSpec(
            num_scalar_prefetch=1,
            grid=(experts,),
            in_specs=[
                pl.BlockSpec((total, model), whole, pipeline_mode=once),
                pl.BlockSpec((total, LANES), whole, pipeline_mode=once),
            ]
            + [pl.BlockSpec((1, *piece.shape[1:]), per_expert) for piece in mine + other],
            out_specs=[
                pl.BlockSpec((total, model), whole),
                pl.BlockSpec((1, total, 4 * width), per_expert),
            ],
            scratch_shapes=[
                pltpu.VMEM((model, 4 * width), BF16),
                pltpu.VMEM((model, 2 * width), BF16),
                pltpu.VMEM((total, model), F32),
            ],
        ),
        out_shape=[
            jax.ShapeDtypeStruct((total, model), BF16),
            jax.ShapeDtypeStruct((experts, total, 4 * width), BF16),
        ],
        compiler_params=pltpu.CompilerParams(vmem_limit_bytes=VMEM_LIMIT),
        cost_estimate=pl.CostEstimate(
            flops=2 * experts * total * model * 6 * width,
            bytes_accessed=experts * model * 12 * width,
            transcendentals=0,
        ),
        name="moe_forward",
    )(offsets, rows, gates, *mine, *other)


def moe_backward_rows(grads, gates, raws, mine, other, offsets):
    total, model = grads.shape
    experts = mine[0].shape[0]
    width = mine[0].shape[2] // 3
    count = len(mine)
    tile = min(TILE, total)

    def body(off_ref, grads_ref, gates_ref, raw_ref, *rest):
        pieces = rest[: 2 * count]
        out_ref, scores_ref, d_raw_ref, act_ref, gate_up, down, sums = rest[2 * count :]
        expert = pl.program_id(0)
        fill_weights(off_ref, pieces, count, gate_up, down)

        def step(index, carry):
            span = pl.ds(pl.multiple_of(index * tile, tile), tile)
            weight = column_of(gates_ref[span, :], expert)
            gate, up = split_gate_up(raw_ref[0, span, :].astype(F32), width)
            back = dot_nn(grads_ref[span, :], down[...])
            sigmoid = jax.nn.sigmoid(gate)
            swish = gate * sigmoid
            act = swish * up
            score = jnp.sum(back * act, axis=1, keepdims=True)
            act_ref[0, span, :] = (act * weight).astype(BF16)
            d_act = back * weight
            d_gate = d_act * up * sigmoid * (1.0 + gate * (1.0 - sigmoid))
            d_raw = join_gate_up(d_gate, d_act * swish, width).astype(BF16)
            d_raw_ref[0, span, :] = d_raw
            part = dot_nt(d_raw, gate_up[...])
            lane = lax.broadcasted_iota(jnp.int32, (tile, LANES), 1)

            @pl.when(expert == 0)
            def _():
                sums[span, :] = part
                scores_ref[span, :] = jnp.where(lane == 0, score, 0.0)

            @pl.when(expert > 0)
            def _():
                sums[span, :] += part
                scores_ref[span, :] = jnp.where(lane == expert, score, scores_ref[span, :])

            @pl.when(expert == experts - 1)
            def _():
                out_ref[span, :] = sums[span, :].astype(BF16)

            return carry

        lax.fori_loop(0, total // tile, step, 0)

    whole = lambda e, *_: (0, 0)
    per_expert = lambda e, *_: (e, 0, 0)
    once = pl.Buffered(1)
    return pl.pallas_call(
        body,
        grid_spec=pltpu.PrefetchScalarGridSpec(
            num_scalar_prefetch=1,
            grid=(experts,),
            in_specs=[
                pl.BlockSpec((total, model), whole, pipeline_mode=once),
                pl.BlockSpec((total, LANES), whole, pipeline_mode=once),
                pl.BlockSpec((1, total, 4 * width), per_expert),
            ]
            + [pl.BlockSpec((1, *piece.shape[1:]), per_expert) for piece in mine + other],
            out_specs=[
                pl.BlockSpec((total, model), whole),
                pl.BlockSpec((total, LANES), whole),
                pl.BlockSpec((1, total, 4 * width), per_expert),
                pl.BlockSpec((1, total, 2 * width), per_expert),
            ],
            scratch_shapes=[
                pltpu.VMEM((model, 4 * width), BF16),
                pltpu.VMEM((model, 2 * width), BF16),
                pltpu.VMEM((total, model), F32),
            ],
        ),
        out_shape=[
            jax.ShapeDtypeStruct((total, model), BF16),
            jax.ShapeDtypeStruct((total, LANES), F32),
            jax.ShapeDtypeStruct((experts, total, 4 * width), BF16),
            jax.ShapeDtypeStruct((experts, total, 2 * width), BF16),
        ],
        compiler_params=pltpu.CompilerParams(vmem_limit_bytes=VMEM_LIMIT),
        cost_estimate=pl.CostEstimate(
            flops=2 * experts * total * model * 6 * width,
            bytes_accessed=experts * model * 12 * width + experts * total * 20 * width,
            transcendentals=0,
        ),
        name="moe_backward_rows",
    )(offsets, grads, gates, raws, *mine, *other)


def moe_backward_weights(rows, grads, d_raws, acts, pieces, offsets):
    total, model = rows.shape
    experts = pieces[0].shape[0]
    width = pieces[0].shape[2] // 3
    count = len(pieces)

    def body(off_ref, rows_ref, grads_ref, d_raw_ref, act_ref, *rest):
        outs = rest[: 2 * count]
        rows_t, grads_t = rest[2 * count :]

        @pl.when(pl.program_id(0) == 0)
        def _():
            for start in range(0, model, TILE):
                rows_t[start : start + TILE, :] = rows_ref[:, start : start + TILE].T
                grads_t[start : start + TILE, :] = grads_ref[:, start : start + TILE].T

        for place in range(count):
            depth = pieces[place].shape[1]
            span = pl.ds(pl.multiple_of(off_ref[place], 16), depth)
            gate_up = dot_nn(rows_t[span, :], d_raw_ref[0]).astype(BF16)
            down = dot_nn(grads_t[span, :], act_ref[0]).astype(BF16)
            for half in range(2):
                ref = outs[half * count + place]
                ref[0, :, : 2 * width] = gate_up[:, 2 * half * width : 2 * (half + 1) * width]
                ref[0, :, 2 * width :] = down[:, half * width : (half + 1) * width]

    whole = lambda e, *_: (0, 0)
    per_expert = lambda e, *_: (e, 0, 0)
    once = pl.Buffered(1)
    return pl.pallas_call(
        body,
        grid_spec=pltpu.PrefetchScalarGridSpec(
            num_scalar_prefetch=1,
            grid=(experts,),
            in_specs=[
                pl.BlockSpec((total, model), whole, pipeline_mode=once),
                pl.BlockSpec((total, model), whole, pipeline_mode=once),
                pl.BlockSpec((1, total, 4 * width), per_expert),
                pl.BlockSpec((1, total, 2 * width), per_expert),
            ],
            out_specs=[
                pl.BlockSpec((1, *piece.shape[1:]), per_expert) for piece in pieces + pieces
            ],
            scratch_shapes=[
                pltpu.VMEM((model, total), BF16),
                pltpu.VMEM((model, total), BF16),
            ],
        ),
        out_shape=[jax.ShapeDtypeStruct(piece.shape, BF16) for piece in pieces + pieces],
        compiler_params=pltpu.CompilerParams(vmem_limit_bytes=VMEM_LIMIT),
        cost_estimate=pl.CostEstimate(
            flops=2 * experts * total * model * 6 * width,
            bytes_accessed=experts * (model * 12 + total * 12) * width,
            transcendentals=0,
        ),
        name="moe_backward_weights",
    )(offsets, rows, grads, d_raws, acts)


def on_device(
    inputs,
    cotangent,
    segments,
    routes,
    attn_gain,
    w_query,
    w_key,
    w_value,
    w_output,
    ffn_gain,
    router,
    w_gate,
    w_up,
    w_down,
):
    core = lax.axis_index("section")
    shard = lax.axis_index("shard")
    plane = lax.axis_index("expert")
    shards = lax.axis_size("shard")
    planes = lax.axis_size("expert")
    span_rows, model = inputs.shape[2:]
    seq_rows = span_rows * shards
    gathered_rows = span_rows * planes
    local_experts = w_gate.shape[1]
    all_experts = local_experts * planes
    hidden = w_gate.shape[3]
    half_hidden = hidden // 2
    part_rows = w_query.shape[1]
    query_width = HEADS * HEAD
    kv_width = KV_HEADS * HEAD
    group_size = HEADS // KV_HEADS
    score_scale = 1.0 / math.sqrt(HEAD)
    first = core == 0

    def mine_of(array):
        return lax.dynamic_index_in_dim(array, core, 0, keepdims=False)

    def by_layer(own, received):
        return [jnp.where(first, own, received), jnp.where(first, received, own)]

    def halved(own_halves):
        kept = jnp.where(first, own_halves[0], own_halves[1])
        sent = jnp.where(first, own_halves[1], own_halves[0])
        return by_layer(kept, swap(sent))

    misc = jnp.concatenate(
        [
            attn_gain[0][:, None],
            ffn_gain[0][:, None],
            router[0],
            jnp.zeros((part_rows, MISC - 2 - all_experts), BF16),
        ],
        axis=1,
    )
    qkv_pack = jnp.concatenate([w_query[0], w_key[0], w_value[0], misc], axis=1)
    qkv_half = qkv_pack.shape[1] // 2
    output_half = model // 2
    qkv_mine = halved([qkv_pack[:, :qkv_half], qkv_pack[:, qkv_half:]])
    output_mine = halved([w_output[0][:, :output_half], w_output[0][:, output_half:]])
    down_turned = jnp.swapaxes(w_down[0], 1, 2)

    def expert_half(start):
        stop = start + half_hidden
        return jnp.concatenate(
            [w_gate[0][:, :, start:stop], w_up[0][:, :, start:stop], down_turned[:, :, start:stop]],
            axis=2,
        )

    expert_mine = halved([expert_half(0), expert_half(half_hidden)])

    def dense_weights(array):
        width = array.shape[1]
        lined = jnp.zeros((planes, part_rows, width), BF16)
        for k, slot in enumerate(slots_of(array, "expert")):
            place = lax.rem(plane - k + planes, planes)
            lined = lax.dynamic_update_slice(lined, slot[None], (place, 0, 0))
        pieces = ring_gather(lined, 0)
        others = [swap(piece) for piece, _, _ in pieces]
        result = jnp.zeros((planes, shards, part_rows, 2 * width), BF16)
        for (piece, owner, start), other in zip(pieces, others):
            result = lax.dynamic_update_slice(
                result, piece[:, None], (start, owner, 0, core * width)
            )
            result = lax.dynamic_update_slice(
                result, other[:, None], (start, owner, 0, (1 - core) * width)
            )
        return result.reshape(model, 2 * width)

    def expert_weights(array):
        pieces = ring_gather(array, 1)
        mine = [piece for piece, _, _ in pieces]
        depth = array.shape[1]
        offsets = jnp.stack([owner * depth + start for _, owner, start in pieces])
        return (mine, [swap(piece) for piece in mine], offsets.astype(jnp.int32))

    qkv_full = [None, None]
    output_full = [None, None]
    experts_full = [None, None]
    qkv_full[0] = dense_weights(qkv_mine[0])
    output_full[0] = dense_weights(after(output_mine[0], qkv_full[0]))
    experts_full[0] = expert_weights(after(expert_mine[0], qkv_full[0]))
    qkv_full[1] = dense_weights(after(qkv_mine[1], experts_full[0][0][-1], experts_full[0][0][-2]))
    output_full[1] = dense_weights(
        after(output_mine[1], experts_full[0][0][-1], experts_full[0][0][-2])
    )
    experts_full[1] = expert_weights(after(expert_mine[1], qkv_full[1], output_full[1]))

    segment_local = mine_of(segments)[0]
    positions = shard * span_rows + jnp.arange(span_rows, dtype=jnp.int32)
    cosine_table, sine_table = rotary(positions, HEAD)
    all_places = jnp.concatenate(
        [
            lax.rem(shard - k + shards, shards) * span_rows
            + jnp.arange(span_rows, dtype=jnp.int32)
            for k in range(shards)
        ]
    )
    segment_all = jnp.concatenate(
        [slot[0] for slot in slots_of(segment_local[None], "shard")]
    )
    allowed = (all_places[None, :] <= positions[:, None]) & (
        segment_all[None, :] == segment_local[:, None]
    )
    own_routes = routes[0, :, 0]
    route_rows = by_layer(
        lax.dynamic_index_in_dim(own_routes, core, 0, keepdims=False),
        swap(lax.dynamic_index_in_dim(own_routes, 1 - core, 0, keepdims=False)),
    )
    expert_ids = jnp.arange(all_experts, dtype=jnp.int32)
    chosen = jnp.stack(
        [
            jnp.any(rows[:, :, None] == expert_ids[None, None, :], axis=1).astype(BF16)
            for rows in route_rows
        ]
    )
    chosen_all = jnp.concatenate(slots_of(jnp.swapaxes(chosen, 1, 2), "expert"), axis=2)
    chosen_all = jnp.swapaxes(chosen_all, 1, 2) > 0.5

    def score_block(query_rot, key_all):
        grouped = query_rot.reshape(span_rows, KV_HEADS, group_size, HEAD)
        keyed = key_all.reshape(seq_rows, KV_HEADS, HEAD)
        scores = (
            jnp.einsum("cngd,knd->cngk", grouped, keyed, preferred_element_type=F32) * score_scale
        )
        return jnp.where(allowed[:, None, None, :], scores, NEGATIVE)

    def forward(layer, stream):
        packed = qkv_full[layer]
        side = packed[:, query_width + 2 * kv_width :]
        gain_one = side[:, 0].astype(F32)
        gain_two = side[:, 1].astype(F32)
        router_full = side[:, 2 : 2 + all_experts]
        scale_one = lax.rsqrt(jnp.mean(stream * stream, axis=-1, keepdims=True) + EPSILON)
        normed = (stream * scale_one * gain_one).astype(BF16)
        raw = dot_nn(normed, packed[:, : query_width + 2 * kv_width])
        query_rot = (
            rotate(raw[:, :query_width].reshape(span_rows, HEADS, HEAD), cosine_table, sine_table)
            .astype(BF16)
            .reshape(span_rows, query_width)
        )
        key_rot = (
            rotate(
                raw[:, query_width : query_width + kv_width].reshape(span_rows, KV_HEADS, HEAD),
                cosine_table,
                sine_table,
            )
            .astype(BF16)
            .reshape(span_rows, kv_width)
        )
        value_low = raw[:, query_width + kv_width :].astype(BF16)
        pair_all = jnp.concatenate(
            slots_of(jnp.concatenate([key_rot, value_low], axis=1), "shard"), axis=0
        )
        key_all = pair_all[:, :kv_width]
        value_all = pair_all[:, kv_width:]
        scores = score_block(query_rot, key_all)
        row_max = jnp.max(scores, axis=-1, keepdims=True)
        exponent = jnp.exp(scores - row_max)
        row_sum = jnp.sum(exponent, axis=-1, keepdims=True)
        attn_probs = (exponent / row_sum).astype(BF16)
        weighted = jnp.einsum(
            "cngk,knd->cngd",
            attn_probs,
            value_all.reshape(seq_rows, KV_HEADS, HEAD),
            preferred_element_type=F32,
        )
        attended = weighted.reshape(span_rows, query_width).astype(BF16)
        middle = stream + dot_nn(attended, output_full[layer])
        scale_two = lax.rsqrt(jnp.mean(middle * middle, axis=-1, keepdims=True) + EPSILON)
        hidden_in = (middle * scale_two * gain_two).astype(BF16)
        rows = jnp.concatenate(slots_of(hidden_in, "expert"), axis=0)
        logits = jnp.where(chosen_all[layer], dot_nn(rows, router_full), NEGATIVE)
        gates = jax.nn.softmax(logits, axis=-1)
        gates = jnp.where(chosen_all[layer], gates, 0.0)
        own_gates = lax.dynamic_slice_in_dim(gates, plane * local_experts, local_experts, axis=1)
        own_gates = jnp.pad(own_gates, ((0, 0), (0, LANES - local_experts)))
        mine, other, offsets = experts_full[layer]
        partial, raws = moe_forward(rows, own_gates, mine, other, offsets)
        combined = partial[:span_rows].astype(F32)
        for k in range(1, planes):
            back = shifted(partial[k * span_rows : (k + 1) * span_rows], "expert", -k)
            combined = combined + back.astype(F32)
        kept = dict(
            stream=stream,
            scale_one=scale_one,
            normed=normed,
            query_rot=query_rot,
            key_all=key_all,
            value_all=value_all,
            row_max=row_max,
            row_sum=row_sum,
            attended=attended,
            middle=middle,
            scale_two=scale_two,
            hidden_in=hidden_in,
            rows=rows,
            gates=gates[:span_rows],
            own_gates=own_gates,
            raws=raws,
            combined=combined,
            gain_one=gain_one,
            gain_two=gain_two,
            router_full=router_full,
        )
        return ((middle + combined).astype(BF16), kept)

    def backward(layer, kept, grad_rows):
        grad_low = grad_rows[:span_rows]
        grad_out = grad_low.astype(F32)
        mine, other, offsets = experts_full[layer]
        d_rows, scores, d_raws, acts = moe_backward_rows(
            grad_rows, kept["own_gates"], kept["raws"], mine, other, offsets
        )
        scores_turned = scores.T[: max(8, local_experts)]
        d_hidden = d_rows[:span_rows].astype(F32)
        d_gates = jnp.zeros((all_experts, span_rows), F32)
        d_gates = lax.dynamic_update_slice(
            d_gates, scores_turned[:local_experts, :span_rows], (plane * local_experts, 0)
        )
        for k in range(1, planes):
            span = slice(k * span_rows, (k + 1) * span_rows)
            d_hidden = d_hidden + shifted(d_rows[span], "expert", -k).astype(F32)
            back = shifted(scores_turned[:, span], "expert", -k)
            place = lax.rem(plane + k, planes) * local_experts
            d_gates = lax.dynamic_update_slice(d_gates, back[:local_experts], (place, 0))
        weight_pieces = moe_backward_weights(kept["rows"], grad_rows, d_raws, acts, mine, offsets)
        gates = kept["gates"]
        share = jnp.sum(grad_out * kept["combined"], axis=-1, keepdims=True)
        d_logits = gates * (d_gates.T - share)
        d_logits_high = d_logits.astype(BF16)
        d_logits_low = (d_logits - d_logits_high.astype(F32)).astype(BF16)
        d_hidden = (
            d_hidden
            + dot_nt(d_logits_high, kept["router_full"])
            + dot_nt(d_logits_low, kept["router_full"])
        )
        grad_router = dot_tn(kept["hidden_in"], d_logits_high) + dot_tn(
            kept["hidden_in"], d_logits_low
        )
        d_middle, grad_gain_two = norm_back(
            d_hidden, kept["middle"], kept["scale_two"], kept["gain_two"]
        )
        d_middle = grad_out + d_middle
        d_branch = d_middle.astype(BF16)
        d_attended = dot_nt(d_branch, output_full[layer]).astype(BF16)
        grad_output = dot_tn(kept["attended"], d_branch)
        probs_wide = (
            jnp.exp(score_block(kept["query_rot"], kept["key_all"]) - kept["row_max"])
            / kept["row_sum"]
        )
        attn_probs = probs_wide.astype(BF16)
        d_weighted = d_attended.reshape(span_rows, KV_HEADS, group_size, HEAD)
        value_heads = kept["value_all"].reshape(seq_rows, KV_HEADS, HEAD)
        key_heads = kept["key_all"].reshape(seq_rows, KV_HEADS, HEAD)
        query_heads = kept["query_rot"].reshape(span_rows, KV_HEADS, group_size, HEAD)
        d_values = jnp.einsum(
            "cngk,cngd->knd", attn_probs, d_weighted, preferred_element_type=F32
        )
        d_probs = jnp.einsum(
            "cngd,knd->cngk", d_weighted, value_heads, preferred_element_type=F32
        )
        d_scores = (
            probs_wide * (d_probs - jnp.sum(probs_wide * d_probs, axis=-1, keepdims=True))
        ).astype(BF16)
        d_queries = (
            jnp.einsum("cngk,knd->cngd", d_scores, key_heads, preferred_element_type=F32)
            * score_scale
        )
        d_keys = (
            jnp.einsum("cngk,cngd->knd", d_scores, query_heads, preferred_element_type=F32)
            * score_scale
        )
        d_pairs = jnp.concatenate(
            [d_keys.reshape(seq_rows, kv_width), d_values.reshape(seq_rows, kv_width)], axis=1
        ).astype(BF16)
        d_pair = d_pairs[:span_rows].astype(F32)
        for k in range(1, shards):
            back = shifted(d_pairs[k * span_rows : (k + 1) * span_rows], "shard", -k)
            d_pair = d_pair + back.astype(F32)
        d_query_raw = (
            rotate(d_queries.reshape(span_rows, HEADS, HEAD), cosine_table, -sine_table)
            .astype(BF16)
            .reshape(span_rows, query_width)
        )
        d_key_raw = (
            rotate(
                d_pair[:, :kv_width].reshape(span_rows, KV_HEADS, HEAD), cosine_table, -sine_table
            )
            .astype(BF16)
            .reshape(span_rows, kv_width)
        )
        d_value_raw = d_pair[:, kv_width:].astype(BF16)
        d_packed = jnp.concatenate([d_query_raw, d_key_raw, d_value_raw], axis=1)
        packed = qkv_full[layer][:, : query_width + 2 * kv_width]
        d_normed = dot_nt(d_packed, packed)
        d_stream, grad_gain_one = norm_back(
            d_normed, kept["stream"], kept["scale_one"], kept["gain_one"]
        )
        d_stream = (d_middle + d_stream).astype(BF16)
        grad_packed = dot_tn(kept["normed"], d_packed).astype(BF16)
        grad_side = jnp.concatenate(
            [
                grad_gain_one[:, None],
                grad_gain_two[:, None],
                grad_router,
                jnp.zeros((model, MISC - 2 - all_experts), F32),
            ],
            axis=1,
        ).astype(BF16)
        grad_qkv = jnp.concatenate([grad_packed, grad_side], axis=1)
        return d_stream, weight_pieces, grad_output.astype(BF16), grad_qkv

    def dense_scatter(grad):
        width = grad.shape[1] // 2
        shaped = grad.reshape(planes, shards, part_rows, 2 * width)
        size = (planes, shards, part_rows, width)
        kept = lax.dynamic_slice(shaped, (0, 0, 0, core * width), size)
        sent = lax.dynamic_slice(shaped, (0, 0, 0, (1 - core) * width), size)
        summed = (kept.astype(F32) + swap(sent).astype(F32)).astype(BF16)

        def chunk(owner, start, stop):
            return lax.dynamic_slice(
                summed, (start, owner, 0, 0), (stop - start, 1, part_rows, width)
            )[:, 0]

        if shards == 4:
            middle = planes // 2
            chunks = [
                chunk(shard, 0, planes),
                chunk(shard ^ 1, 0, planes),
                chunk(shard ^ 2, 0, planes),
                chunk(shard ^ 3, 0, middle),
                chunk(shard ^ 3, middle, planes),
            ]
        else:
            chunks = [
                chunk(lax.rem(shard - k + shards, shards), 0, planes) for k in range(shards)
            ]
        lined = ring_scatter(chunks, 0)
        total = lax.dynamic_index_in_dim(lined, plane, 0, keepdims=False)
        for k in range(1, planes):
            sent = lax.dynamic_index_in_dim(
                lined, lax.rem(plane - k + planes, planes), 0, keepdims=False
            )
            total = total + shifted(sent.astype(BF16), "expert", -k).astype(F32)
        return total

    def expert_scatter(pieces):
        count = len(pieces) // 2
        summed = [
            (mine.astype(F32) + swap(other).astype(F32)).astype(BF16)
            for mine, other in zip(pieces[:count], pieces[count:])
        ]
        return ring_scatter(summed, 1)

    def regrouped(halves):
        kept = jnp.where(first, halves[0], halves[1])
        sent = jnp.where(first, halves[1], halves[0])
        received = swap(sent.astype(BF16)).astype(F32)
        return by_layer(kept, received)

    start = mine_of(inputs)[0]
    result_one, kept_one = forward(0, start.astype(F32))
    result_two, kept_two = forward(1, result_one.astype(F32))
    last = mine_of(cotangent)[0]
    last_rows = jnp.concatenate(slots_of(last, "expert"), axis=0)
    grad_mid, experts_two, output_two, qkv_two = backward(1, kept_two, last_rows)
    mid_rows = jnp.concatenate(slots_of(grad_mid, "expert"), axis=0)
    grad_start, experts_one, output_one, qkv_one = backward(0, kept_one, mid_rows)

    def placed(by_layers):
        own = jnp.where(first, by_layers[0], by_layers[1])
        sent = jnp.where(first, by_layers[1], by_layers[0])
        return jnp.stack(by_layer(own, swap(sent)))

    layer_local = placed([result_one, result_two])
    input_local = placed([grad_start, grad_mid])
    scattered_two = expert_scatter(experts_two)
    scattered_one = expert_scatter(experts_one)
    expert_low, expert_high = regrouped([scattered_one, scattered_two])
    output_halves = regrouped([dense_scatter(output_one), dense_scatter(output_two)])
    grad_output = jnp.concatenate(output_halves, axis=1)
    grad_qkv = jnp.concatenate(
        regrouped([dense_scatter(qkv_one), dense_scatter(qkv_two)]), axis=1
    )
    side = grad_qkv[:, query_width + 2 * kv_width :]

    def third(index):
        start = index * half_hidden
        stop = start + half_hidden
        return jnp.concatenate([expert_low[:, :, start:stop], expert_high[:, :, start:stop]], axis=2)

    out_shape = (1, 2, 1, span_rows, model)
    return (
        layer_local.reshape(out_shape),
        input_local.reshape(out_shape),
        side[:, 0][None],
        grad_qkv[:, :query_width][None],
        grad_qkv[:, query_width : query_width + kv_width][None],
        grad_qkv[:, query_width + kv_width : query_width + 2 * kv_width][None],
        grad_output[None],
        side[:, 1][None],
        side[:, 2 : 2 + all_experts][None],
        third(0)[None],
        third(1)[None],
        jnp.swapaxes(third(2), 1, 2)[None],
    )


def solution(mesh):
    placed = (
        P(None, "expert", "shard", None),
        P(None, "expert", "shard", None),
        P(None, "expert", "shard"),
        P("section", None, "expert", "shard", None),
        P("section", ("expert", "shard")),
        P("section", ("expert", "shard"), None),
        P("section", ("expert", "shard"), None),
        P("section", ("expert", "shard"), None),
        P("section", ("expert", "shard"), None),
        P("section", ("expert", "shard")),
        P("section", ("expert", "shard"), None),
        P("section", "expert", "shard", None),
        P("section", "expert", "shard", None),
        P("section", "expert", None, "shard"),
    )
    return jax.shard_map(
        on_device,
        mesh=mesh,
        in_specs=placed,
        out_specs=(
            P("section", None, "expert", "shard", None),
            P("section", None, "expert", "shard", None),
            P("section", ("expert", "shard")),
            P("section", ("expert", "shard"), None),
            P("section", ("expert", "shard"), None),
            P("section", ("expert", "shard"), None),
            P("section", ("expert", "shard"), None),
            P("section", ("expert", "shard")),
            P("section", ("expert", "shard"), None),
            P("section", "expert", "shard", None),
            P("section", "expert", "shard", None),
            P("section", "expert", None, "shard"),
        ),
        check_vma=False,
    )
```

time: 5270 us -> 1980 us (0.38)
  waiting for transfers between devices: 2280 us -> 819 us
  blocking collectives: 1440 us -> 0 us
  matrix products: 725 us -> 190 us
  Pallas kernels: 0 us -> 249 us
  local copies, waits for them, and re-layouts: 455 us -> 217 us
  starting transfers between devices: 68.3 us -> 277 us
    all_to_all x7 -> x0, waiting for transfers between devices: 1130 us -> none  [the longest x3 598 us: on_device(): lax.all_to_all(grad_rows, 'expert', split_axis=0, concat_axis=0, tiled=True)]
    all_to_all x5 -> x0, blocking collectives: 1100 us -> none  [the longest x3 669 us: on_device(): lax.all_to_all(send_grads.reshape(expert_count, local_experts, capacity,...]
    ppermute x4 -> x185, waiting for transfers between devices: 14.1 us -> 819 us  [the longest x72 452 us: shifted(): lax.ppermute(array, axis, [(i, (i + by) % length) for i in range(length)])]
    reduce_scatter x12 -> x0, waiting for transfers between devices: 762 us -> none  [the longest x1 177 us: on_device(): lax.psum_scatter(attn_total[1], ('expert', 'shard'), scatter_dimension=0,...]
    dot_general x82 -> x32, matrix products: 721 us -> 162 us  [the longest x2 33 us: backward(): jnp.einsum('cngd,knd->cngk', d_weighted, value_heads, preferred_element_t...]
    all_gather x13 -> x0, waiting for transfers between devices: 303 us -> none  [the longest x1 80.3 us: on_device(): lax.all_gather(w_query[0], ('expert', 'shard'), axis=0, tiled=True)]
    ppermute x4 -> x185, starting transfers between devices: 9.65 us -> 277 us  [the longest x53 124 us: swap(): return lax.ppermute(array, 'section', [(0, 1), (1, 0)])]
    all_gather x4 -> x0, blocking collectives: 255 us -> none  [the longest x1 238 us: on_device(): lax.all_gather(router[0], ('expert', 'shard'), axis=0, tiled=True)]
  transfers between devices with their start and end apart: 38 -> 185, of which waited for: 29 -> 66; matrix products, arithmetic and copies ran while one was open for 11% -> 29% of each run, Pallas kernels for 0% -> 8%
where the time goes in v1:
time: 1980 us; the launch traced here: 1970 us
  waiting for transfers between devices  819 us (41%)
  starting transfers between devices  277 us (14%)
  Pallas kernels  249 us (13%)
  local copies, waits for them, and re-layouts  217 us (11%)
  other arithmetic  214 us (11%)
  matrix products  190 us (10%)
    ppermute x72, waiting for transfers between devices, shifted(): lax.ppermute(array, axis, [(i, (i + by) % length) for i in range(length)])  452 us
    ppermute x60, waiting for transfers between devices, flipped(): lax.ppermute(array, 'shard', [(i, i ^ mask) for i in range(lax.axis_size(...  363 us
    ppermute x53, starting transfers between devices, swap(): return lax.ppermute(array, 'section', [(0, 1), (1, 0)])  124 us
    pallas_call x2, Pallas kernels, moe_backward_rows(): pl.pallas_call(body, grid_spec=pltpu.PrefetchScalarGridSpec(num_scalar_pr...  98 us
    ppermute x72, starting transfers between devices, shifted(): lax.ppermute(array, axis, [(i, (i + by) % length) for i in range(length)])  88.6 us
    pallas_call x2, Pallas kernels, moe_forward(): pl.pallas_call(body, grid_spec=pltpu.PrefetchScalarGridSpec(num_scalar_pr...  82.8 us
    pallas_call x2, Pallas kernels, moe_backward_weights(): pl.pallas_call(body, grid_spec=pltpu.PrefetchScalarGridSpec(num_scalar_pr...  68.6 us
    ppermute x60, starting transfers between devices, flipped(): lax.ppermute(array, 'shard', [(i, i ^ mask) for i in range(lax.axis_size(...  63.8 us
  transfers between devices with their start and end apart: 185, of which 66 were waited for; matrix products, arithmetic and copies ran while one was open for 29% of the time, Pallas kernels for 8%

profile of v1, /device:TPU:9, one launch (start us, length us, event | category | flops | bytes accessed | tf_op | source)
XLA Modules:
  0.0 1970.2 jit_solution(13596224860133624508)
XLA Ops:
  39.4 10.5 collective-permute-done.2
  66.2 20.3 %collective-permute-done.5 = bf16[4,96,1408]{2,1,0:T(8,128)(2,1)S(1)} collective-permute-done((bf16[4,96,1408]{2,1,0:T(8,128)(2,1)}, bf16[4,96,1408]{2,1,0:T(8,128)(2,1)S(1)}, u32[]{:S(2)}, u32[]{:S(2)}) %collective-permute-start.5) | collective-permute-done | bytes 1081376 | tf_op jit(solution)/shard_map/ppermute | solution.py:37
  92.1 11.7 collective-permute-done.9
  167.7 14.2 fusion.179
  183.4 9.5 fusion.67
  205.0 41.7 %collective-permute-done.28 = bf16[2,96,768]{2,1,0:T(8,128)(2,1)S(1)} collective-permute-done((bf16[2,96,768]{2,1,0:T(8,128)(2,1)S(1)}, bf16[2,96,768]{2,1,0:T(8,128)(2,1)S(1)}, u32[]{:S(2)}, u32[]{:S(2)}) %collective-permute-start.28) | collective-permute-done | bytes 294944 | tf_op jit(solution)/shard_map/ppermute | solution.py:37
  271.0 60.6 %collective-permute-done.37 = bf16[2,20,256]{2,1,0:T(8,128)(2,1)S(1)} collective-permute-done((bf16[2,20,256]{2,1,0:T(8,128)(2,1)S(1)}, bf16[2,20,256]{2,1,0:T(8,128)(2,1)S(1)}, u32[]{:S(2)}, u32[]{:S(2)}) %collective-permute-start.37) | collective-permute-done | bytes 20512 | tf_op jit(solution)/shard_map/ppermute | solution.py:33
  338.5 26.7 %collective-permute-done.42.rest_3_ = bf16[5,192,768]{2,1,0:T(8,128)(2,1)} collective-permute-done((bf16[5,192,768]{2,1,0:T(8,128)(2,1)}, bf16[5,192,768]{2,1,0:T(8,128)(2,1)}, u32[]{:S(2)}, u32[]{:S(2)}) %collective-permute-start.42) | collective-permute-done | bytes 1474592 | tf_op jit(solution)/shard_map/ppermute | solution.py:37
  370.4 9.3 collective-permute-done.68
  385.4 11.0 collective-permute-done.71
  424.5 11.7 collective-permute-done.56
  448.3 41.3 %moe_forward.2 = (bf16[1024,1536]{1,0:T(8,128)(2,1)}, bf16[5,1024,1024]{2,1,0:T(8,128)(2,1)}) custom-call(s32[5]{0:T(128)} %stack.53.off_ref, bf16[1024,1536]{1,0:T(8,128)(2,1)} %copy-done.46, f32[1024,128]{1,0:T(8,128)} %pad.7.gates_ref, bf16[5,384,768]{2,1,0:T(8,128)(2,1)} %get-tuple-element.50.rest_0_, ...), custom_call_target="tpu_custom_call" | custom-call | flops 24159191040 | bytes 23592960 | tf_op jit(solution)/shard_map/moe_forward/pallas_call | solution.py:210
  501.3 9.3 collective-permute-done.51
  512.0 47.2 %collective-permute-done.50 = bf16[256,1536]{1,0:T(8,128)(2,1)S(1)} collective-permute-done((bf16[256,1536]{1,0:T(8,128)(2,1)S(1)}, bf16[256,1536]{1,0:T(8,128)(2,1)S(1)}, u32[]{:S(2)}, u32[]{:S(2)}) %collective-permute-start.50) | collective-permute-done | bytes 786464 | tf_op jit(solution)/shard_map/ppermute | solution.py:33
  597.8 11.5 collective-permute-done.64
  614.4 14.1 fusion.181
  628.6 9.6 fusion.70
  644.2 27.7 %collective-permute-done.82.rest_1_ = bf16[5,384,768]{2,1,0:T(8,128)(2,1)} collective-permute-done((bf16[5,384,768]{2,1,0:T(8,128)(2,1)}, bf16[5,384,768]{2,1,0:T(8,128)(2,1)}, u32[]{:S(2)}, u32[]{:S(2)}) %collective-permute-start.82) | collective-permute-done | bytes 2949152 | tf_op jit(solution)/shard_map/ppermute | solution.py:37
  677.0 22.0 %collective-permute-start.87 = (bf16[5,384,768]{2,1,0:T(8,128)(2,1)}, bf16[5,384,768]{2,1,0:T(8,128)(2,1)}, u32[]{:S(2)}, u32[]{:S(2)}) collective-permute-start(bf16[5,384,768]{2,1,0:T(8,128)(2,1)} %collective-permute-done.82.rest_1_), channel_id=1, source_target_pairs={{0,16},{16,0},{1,17},{17,1},{2,18},{18,2},{3,19},{19,3},{4,20},{20... | collective-permute-start | bytes 8847368 | tf_op jit(solution)/shard_map/ppermute | solution.py:28
  699.0 11.1 collective-permute-done.79
  712.1 31.3 %collective-permute-done.85.rest_4_ = bf16[5,192,768]{2,1,0:T(8,128)(2,1)S(1)} collective-permute-done((bf16[5,192,768]{2,1,0:T(8,128)(2,1)S(1)}, bf16[5,192,768]{2,1,0:T(8,128)(2,1)S(1)}, u32[]{:S(2)}, u32[]{:S(2)}) %collective-permute-start.85) | collective-permute-done | bytes 1474592 | tf_op jit(solution)/shard_map/ppermute | solution.py:37
  751.3 41.5 %moe_forward.3 = (bf16[1024,1536]{1,0:T(8,128)(2,1)}, bf16[5,1024,1024]{2,1,0:T(8,128)(2,1)}) custom-call(s32[5]{0:T(128)} %stack.53.off_ref, bf16[1024,1536]{1,0:T(8,128)(2,1)} %copy-done.47, f32[1024,128]{1,0:T(8,128)} %pad.8.gates_ref, bf16[5,384,768]{2,1,0:T(8,128)(2,1)} %get-tuple-element.54.rest_0_, ...), custom_call_target="tpu_custom_call" | custom-call | flops 24159191040 | bytes 23592960 | tf_op jit(solution)/shard_map/moe_forward/pallas_call | solution.py:210
  801.1 15.1 collective-permute-done.93
  816.2 47.4 %collective-permute-done.92 = bf16[256,1536]{1,0:T(8,128)(2,1)S(1)} collective-permute-done((bf16[256,1536]{1,0:T(8,128)(2,1)S(1)}, bf16[256,1536]{1,0:T(8,128)(2,1)S(1)}, u32[]{:S(2)}, u32[]{:S(2)}) %collective-permute-start.92) | collective-permute-done | bytes 786464 | tf_op jit(solution)/shard_map/ppermute | solution.py:33
  878.7 11.3 collective-permute-done.97
  890.0 32.2 %collective-permute-done.96 = bf16[256,1536]{1,0:T(8,128)(2,1)} collective-permute-done((bf16[256,1536]{1,0:T(8,128)(2,1)}, bf16[256,1536]{1,0:T(8,128)(2,1)}, u32[]{:S(2)}, u32[]{:S(2)}) %collective-permute-start.96) | collective-permute-done | bytes 786464 | tf_op jit(solution)/shard_map/ppermute | solution.py:33
  922.2 16.9 collective-permute-done.95
  942.2 49.0 %moe_backward_rows.2 = (bf16[1024,1536]{1,0:T(8,128)(2,1)}, f32[1024,128]{1,0:T(8,128)}, bf16[5,1024,1024]{2,1,0:T(8,128)(2,1)}, bf16[5,1024,512]{2,1,0:T(8,128)(2,1)}) custom-call(s32[5]{0:T(128)} %stack.53.off_ref, bf16[1024,1536]{1,0:T(8,128)(2,1)} %pad_maximum_fusion.2.grads_ref, f32[1024,128]{1,0:T(8,128)} %pad.8.gates_ref, ...), custom_call_target="tpu_custom_call" | custom-call | flops 24159191040 | bytes 49807360 | tf_op jit(solution)/shard_map/moe_backward_rows/pallas_call | solution.py:295
  1000.5 34.2 %moe_backward_weights.3 = (bf16[5,384,768]{2,1,0:T(8,128)(2,1)}, bf16[5,384,768]{2,1,0:T(8,128)(2,1)}, bf16[5,384,768]{2,1,0:T(8,128)(2,1)}, bf16[5,192,768]{2,1...) custom-call(s32[5]{0:T(128)} %stack.53.off_ref, ...), custom_call_target="tpu_custom_call" | custom-call | flops 24159191040 | bytes 39321600 | tf_op jit(solution)/shard_map/moe_backward_weights/pallas_call | solution.py:363
  1052.8 35.6 %collective-permute-done.99 = bf16[256,1536]{1,0:T(8,128)(2,1)} collective-permute-done((bf16[256,1536]{1,0:T(8,128)(2,1)}, bf16[256,1536]{1,0:T(8,128)(2,1)}, u32[]{:S(2)}, u32[]{:S(2)}) %collective-permute-start.99) | collective-permute-done | bytes 786464 | tf_op jit(solution)/shard_map/ppermute | solution.py:33
  1099.6 16.4 fusion.5
  1116.0 11.4 bitcast_convert_fusion.1
  1127.5 16.8 fusion.7
  1167.9 12.1 collective-permute-done.105
  1199.2 14.4 concatenate.173
  1220.0 21.2 %collective-permute-done.108 = bf16[256,1536]{1,0:T(8,128)(2,1)} collective-permute-done((bf16[256,1536]{1,0:T(8,128)(2,1)S(1)}, bf16[256,1536]{1,0:T(8,128)(2,1)}, u32[]{:S(2)}, u32[]{:S(2)}) %collective-permute-start.108) | collective-permute-done | bytes 786464 | tf_op jit(solution)/shard_map/ppermute | solution.py:33
  1241.1 16.9 collective-permute-done.107
  1261.0 49.0 %moe_backward_rows.3 = (bf16[1024,1536]{1,0:T(8,128)(2,1)}, f32[1024,128]{1,0:T(8,128)}, bf16[5,1024,1024]{2,1,0:T(8,128)(2,1)}, bf16[5,1024,512]{2,1,0:T(8,128)(2,1)}) custom-call(s32[5]{0:T(128)} %stack.53.off_ref, bf16[1024,1536]{1,0:T(8,128)(2,1)} %pad_maximum_fusion.3.grads_ref, f32[1024,128]{1,0:T(8,128)} %pad.7.gates_ref, ...), custom_call_target="tpu_custom_call" | custom-call | flops 24159191040 | bytes 49807360 | tf_op jit(solution)/shard_map/moe_backward_rows/pallas_call | solution.py:295
  1321.3 34.4 %moe_backward_weights.2 = (bf16[5,384,768]{2,1,0:T(8,128)(2,1)}, bf16[5,384,768]{2,1,0:T(8,128)(2,1)}, bf16[5,384,768]{2,1,0:T(8,128)(2,1)}, bf16[5,192,768]{2,1...) custom-call(s32[5]{0:T(128)} %stack.53.off_ref, ...), custom_call_target="tpu_custom_call" | custom-call | flops 24159191040 | bytes 39321600 | tf_op jit(solution)/shard_map/moe_backward_weights/pallas_call | solution.py:363
  1358.4 36.4 %collective-permute-start.178 = (bf16[5,384,768]{2,1,0:T(8,128)(2,1)}, bf16[5,384,768]{2,1,0:T(8,128)(2,1)}, u32[]{:S(2)}, u32[]{:S(2)}) collective-permute-start(bf16[5,384,768]{2,1,0:T(8,128)(2,1)} %get-tuple-element.83), channel_id=1, source_target_pairs={{0,16},{16,0},{1,17},{17,1},{2,18},{18,2},{3,19},{19,3},{4,20},{20... | collective-permute-start | bytes 8847368 | tf_op jit(solution)/shard_map/ppermute | solution.py:28
  1410.7 16.6 fusion.2
  1427.3 21.2 %fusion.4 = bf16[256,8,3,1024]{0,3,2,1:T(8,128)(2,1)} fusion(f32[8,1024,256,3]{2,1,3,0:T(8,128)} %get-tuple-element.341, f32[256,8,3]{0,2,1:T(4,128)S(1)} %get-tuple-element.340, f32[256,8,3,1024]{0,3,2,1:T(8,128)} %get-tuple-element.324, f32[256,8,3]{0,2,1:T(4,128)S(1)} %copy-done.120), kind=kLoop, calls=%fused_computation.6 | loop fusion | flops 25165824 | bytes 62963712 | tf_op jit(solution)/shard_map/convert_element_type | solution.py:677
  1448.5 12.4 bitcast_convert_fusion
  1460.9 8.8 fusion.39
  1477.6 7.1 constant_dynamic-slice_fusion.1
  1519.8 10.7 collective-permute-done.176
  1531.1 10.5 collective-permute-start.180
  1551.8 14.3 concatenate.175
  1566.7 8.9 constant_dynamic-slice_fusion.5
  1581.5 12.4 collective-permute-done.179
  1605.4 7.2 collective-permute-start.171
  1625.4 20.2 %collective-permute-done.171 = bf16[5,192,768]{2,1,0:T(8,128)(2,1)} collective-permute-done((bf16[5,192,768]{2,1,0:T(8,128)(2,1)}, bf16[5,192,768]{2,1,0:T(8,128)(2,1)}, u32[]{:S(2)}, u32[]{:S(2)}) %collective-permute-start.171) | collective-permute-done | bytes 1474592 | tf_op jit(solution)/shard_map/ppermute | solution.py:37
  1677.5 32.9 %collective-permute-done.147 = bf16[2,96,768]{2,1,0:T(8,128)(2,1)} collective-permute-done((bf16[2,96,768]{2,1,0:T(8,128)(2,1)S(1)}, bf16[2,96,768]{2,1,0:T(8,128)(2,1)}, u32[]{:S(2)}, u32[]{:S(2)}) %collective-permute-start.147) | collective-permute-done | bytes 294944 | tf_op jit(solution)/shard_map/ppermute | solution.py:37
  1723.8 25.0 %collective-permute-done.169 = bf16[5,192,768]{2,1,0:T(8,128)(2,1)S(1)} collective-permute-done((bf16[5,192,768]{2,1,0:T(8,128)(2,1)S(1)}, bf16[5,192,768]{2,1,0:T(8,128)(2,1)S(1)}, u32[]{:S(2)}, u32[]{:S(2)}) %collective-permute-start.169) | collective-permute-done | bytes 1474592 | tf_op jit(solution)/shard_map/ppermute | solution.py:37
  1756.9 23.5 %collective-permute-done.166 = bf16[5,192,768]{2,1,0:T(8,128)(2,1)S(1)} collective-permute-done((bf16[5,192,768]{2,1,0:T(8,128)(2,1)S(1)}, bf16[5,192,768]{2,1,0:T(8,128)(2,1)S(1)}, u32[]{:S(2)}, u32[]{:S(2)}) %collective-permute-start.166) | collective-permute-done | bytes 1474592 | tf_op jit(solution)/shard_map/ppermute | solution.py:37
  1782.6 7.7 add_convert_fusion
  1815.9 12.4 collective-permute-done.125
  1841.2 9.3 collective-permute-done.124
  1850.6 9.0 collective-permute-done.126
  1871.7 19.3 collective-permute-done.160
  1903.1 12.9 collective-permute-start.161
  1916.0 9.7 collective-permute-done.128
  1934.3 11.7 convert_select_fusion.1
  1962.8 7.1 maximum_bitcast_fusion
  (952 shorter events, 670.8 us)
Async XLA Ops:
  1.3 58.4 %collective-permute-start.18 = (s32[1,256]{1,0:T(1,128)S(1)}, s32[1,256]{1,0:T(1,128)S(1)}, u32[]{:S(2)}, u32[]{:S(2)}) collective-permute-start(s32[1,256]{1,0:T(1,128)S(1)} %fusion.225), channel_id=1, source_target_pairs={{0,3},{1,0},{2,1},{3,2},{4,7},{5,4},{6,5},{7,6},{8,11},{9,8},{10,9... | collective-permute-start | bytes 3080 | tf_op jit(solution)/shard_map/ppermute | solution.py:33
  3.5 56.3 %collective-permute-start.17 = (s32[1,256]{1,0:T(1,128)S(1)}, s32[1,256]{1,0:T(1,128)S(1)}, u32[]{:S(2)}, u32[]{:S(2)}) collective-permute-start(s32[1,256]{1,0:T(1,128)S(1)} %fusion.225), channel_id=1, source_target_pairs={{0,2},{1,3},{2,0},{3,1},{4,6},{5,7},{6,4},{7,5},{8,10},{9,11},{10,... | collective-permute-start | bytes 3080 | tf_op jit(solution)/shard_map/ppermute | solution.py:33
  3.5 59.0 %collective-permute-start.16 = (s32[1,256]{1,0:T(1,128)S(1)}, s32[1,256]{1,0:T(1,128)S(1)}, u32[]{:S(2)}, u32[]{:S(2)}) collective-permute-start(s32[1,256]{1,0:T(1,128)S(1)} %fusion.225), channel_id=1, source_target_pairs={{0,1},{1,2},{2,3},{3,0},{4,5},{5,6},{6,7},{7,4},{8,9},{9,10},{10,1... | collective-permute-start | bytes 3080 | tf_op jit(solution)/shard_map/ppermute | solution.py:33
  11.5 53.0 %collective-permute-start.19 = (bf16[96,768]{1,0:T(8,128)(2,1)S(1)}, bf16[96,768]{1,0:T(8,128)(2,1)}, u32[]{:S(2)}, u32[]{:S(2)}) collective-permute-start(bf16[96,768]{1,0:T(8,128)(2,1)S(1)} %broadcast_select_fusion.16), channel_id=1, source_target_pairs={{0,16},{16,0},{1,17},{17,1},{2,18},{18,2},{3,19},{19,3},{4,20},{20... | collective-permute-start | bytes 442376 | tf_op jit(solution)/shard_map/ppermute | solution.py:28
  59.8 96.1 %collective-permute-start.39 = (bf16[5,384,768]{2,1,0:T(8,128)(2,1)}, bf16[5,384,768]{2,1,0:T(8,128)(2,1)}, u32[]{:S(2)}, u32[]{:S(2)}) collective-permute-start(bf16[5,384,768]{2,1,0:T(8,128)(2,1)} %broadcast_select_fusion.2), channel_id=1, source_target_pairs={{0,16},{16,0},{1,17},{17,1},{2,18},{18,2},{3,19},{19,3},{4,20},{20... | collective-permute-start | bytes 8847368 | tf_op jit(solution)/shard_map/ppermute | solution.py:28
  163.0 101.2 %collective-permute-start.40 = (bf16[5,384,768]{2,1,0:T(8,128)(2,1)}, bf16[5,384,768]{2,1,0:T(8,128)(2,1)}, u32[]{:S(2)}, u32[]{:S(2)}) collective-permute-start(bf16[5,384,768]{2,1,0:T(8,128)(2,1)} %get-tuple-element.50.rest_0_), channel_id=1, source_target_pairs={{0,1},{1,0},{2,3},{3,2},{4,5},{5,4},{6,7},{7,6},{8,9},{9,8},{10,11... | collective-permute-start | bytes 8847368 | tf_op jit(solution)/shard_map/ppermute | solution.py:37
  163.1 102.3 %collective-permute-start.41 = (bf16[5,384,768]{2,1,0:T(8,128)(2,1)}, bf16[5,384,768]{2,1,0:T(8,128)(2,1)}, u32[]{:S(2)}, u32[]{:S(2)}) collective-permute-start(bf16[5,384,768]{2,1,0:T(8,128)(2,1)} %get-tuple-element.50.rest_0_), channel_id=1, source_target_pairs={{0,2},{1,3},{2,0},{3,1},{4,6},{5,7},{6,4},{7,5},{8,10},{9,11},{10,... | collective-permute-start | bytes 8847368 | tf_op jit(solution)/shard_map/ppermute | solution.py:37
  194.2 52.5 %collective-permute-start.28 = (bf16[2,96,768]{2,1,0:T(8,128)(2,1)S(1)}, bf16[2,96,768]{2,1,0:T(8,128)(2,1)S(1)}, u32[]{:S(2)}, u32[]{:S(2)}) collective-permute-start(bf16[2,96,768]{2,1,0:T(8,128)(2,1)S(1)} %slice.639), channel_id=1, source_target_pairs={{0,2},{1,3},{2,0},{3,1},{4,6},{5,7},{6,4},{7,5},{8,10},{9,11},{10,... | collective-permute-start | bytes 884744 | tf_op jit(solution)/shard_map/ppermute | solution.py:37
  195.1 55.1 %collective-permute-start.27 = (bf16[4,96,768]{2,1,0:T(8,128)(2,1)}, bf16[4,96,768]{2,1,0:T(8,128)(2,1)S(1)}, u32[]{:S(2)}, u32[]{:S(2)}) collective-permute-start(bf16[4,96,768]{2,1,0:T(8,128)(2,1)} %collective-permute-done.26), channel_id=1, source_target_pairs={{0,16},{16,0},{1,17},{17,1},{2,18},{18,2},{3,19},{19,3},{4,20},{20... | collective-permute-start | bytes 1769480 | tf_op jit(solution)/shard_map/ppermute | solution.py:28
  200.6 48.2 %collective-permute-start.30 = (bf16[2,96,768]{2,1,0:T(8,128)(2,1)S(1)}, bf16[2,96,768]{2,1,0:T(8,128)(2,1)S(1)}, u32[]{:S(2)}, u32[]{:S(2)}) collective-permute-start(bf16[2,96,768]{2,1,0:T(8,128)(2,1)S(1)} %slice.640), channel_id=1, source_target_pairs={{0,1},{1,0},{2,3},{3,2},{4,5},{5,4},{6,7},{7,6},{8,9},{9,8},{10,11... | collective-permute-start | bytes 884744 | tf_op jit(solution)/shard_map/ppermute | solution.py:37
  258.9 74.9 %collective-permute-start.34 = (bf16[256,1536]{1,0:T(8,128)(2,1)S(1)}, bf16[256,1536]{1,0:T(8,128)(2,1)}, u32[]{:S(2)}, u32[]{:S(2)}) collective-permute-start(bf16[256,1536]{1,0:T(8,128)(2,1)S(1)} %multiply_convert_fusion.1), channel_id=1, source_target_pairs={{0,12},{4,0},{8,4},{12,8},{1,13},{5,1},{9,5},{13,9},{2,14},{6,2},{... | collective-permute-start | bytes 2359304 | tf_op jit(solution)/shard_map/ppermute | solution.py:33
  262.9 70.8 %collective-permute-start.33 = (bf16[256,1536]{1,0:T(8,128)(2,1)S(1)}, bf16[256,1536]{1,0:T(8,128)(2,1)}, u32[]{:S(2)}, u32[]{:S(2)}) collective-permute-start(bf16[256,1536]{1,0:T(8,128)(2,1)S(1)} %multiply_convert_fusion.1), channel_id=1, source_target_pairs={{0,8},{4,12},{8,0},{12,4},{1,9},{5,13},{9,1},{13,5},{2,10},{6,14},... | collective-permute-start | bytes 2359304 | tf_op jit(solution)/shard_map/ppermute | solution.py:33
  262.9 70.8 %collective-permute-start.32 = (bf16[256,1536]{1,0:T(8,128)(2,1)S(1)}, bf16[256,1536]{1,0:T(8,128)(2,1)}, u32[]{:S(2)}, u32[]{:S(2)}) collective-permute-start(bf16[256,1536]{1,0:T(8,128)(2,1)S(1)} %multiply_convert_fusion.1), channel_id=1, source_target_pairs={{0,4},{4,8},{8,12},{12,0},{1,5},{5,9},{9,13},{13,1},{2,6},{6,10},{... | collective-permute-start | bytes 2359304 | tf_op jit(solution)/shard_map/ppermute | solution.py:33
  264.2 67.4 %collective-permute-start.37 = (bf16[2,20,256]{2,1,0:T(8,128)(2,1)S(1)}, bf16[2,20,256]{2,1,0:T(8,128)(2,1)S(1)}, u32[]{:S(2)}, u32[]{:S(2)}) collective-permute-start(bf16[2,20,256]{2,1,0:T(8,128)(2,1)S(1)} %fusion.130), channel_id=1, source_target_pairs={{0,8},{4,12},{8,0},{12,4},{1,9},{5,13},{9,1},{13,5},{2,10},{6,14},... | collective-permute-start | bytes 61448 | tf_op jit(solution)/shard_map/ppermute | solution.py:33
  265.4 67.0 %collective-permute-start.36 = (bf16[2,20,256]{2,1,0:T(8,128)(2,1)S(1)}, bf16[2,20,256]{2,1,0:T(8,128)(2,1)S(1)}, u32[]{:S(2)}, u32[]{:S(2)}) collective-permute-start(bf16[2,20,256]{2,1,0:T(8,128)(2,1)S(1)} %fusion.130), channel_id=1, source_target_pairs={{0,4},{4,8},{8,12},{12,0},{1,5},{5,9},{9,13},{13,1},{2,6},{6,10},{... | collective-permute-start | bytes 61448 | tf_op jit(solution)/shard_map/ppermute | solution.py:33
  444.4 51.2 %collective-permute-start.55 = (bf16[4,96,1408]{2,1,0:T(8,128)(2,1)S(1)}, bf16[4,96,1408]{2,1,0:T(8,128)(2,1)}, u32[]{:S(2)}, u32[]{:S(2)}) collective-permute-start(bf16[4,96,1408]{2,1,0:T(8,128)(2,1)S(1)} %bitcast_dynamic-update-slice_fusion.40), channel_id=1, source_target_pairs={{0,16},{16,0},{1,17},{17,1},{2,18},{18,2},{3,19},{19,3},{4,20},{20... | collective-permute-start | bytes 3244040 | tf_op jit(solution)/shard_map/ppermute | solution.py:28
  445.1 54.1 %collective-permute-start.60 = (bf16[2,96,1408]{2,1,0:T(8,128)(2,1)S(1)}, bf16[2,96,1408]{2,1,0:T(8,128)(2,1)}, u32[]{:S(2)}, u32[]{:S(2)}) collective-permute-start(bf16[2,96,1408]{2,1,0:T(8,128)(2,1)S(1)} %slice.652), channel_id=1, source_target_pairs={{0,2},{1,3},{2,0},{3,1},{4,6},{5,7},{6,4},{7,5},{8,10},{9,11},{10,... | collective-permute-start | bytes 1622024 | tf_op jit(solution)/shard_map/ppermute | solution.py:37
  446.9 54.4 %collective-permute-start.62 = (bf16[2,96,1408]{2,1,0:T(8,128)(2,1)}, bf16[2,96,1408]{2,1,0:T(8,128)(2,1)S(1)}, u32[]{:S(2)}, u32[]{:S(2)}) collective-permute-start(bf16[2,96,1408]{2,1,0:T(8,128)(2,1)} %slice.653), channel_id=1, source_target_pairs={{0,1},{1,0},{2,3},{3,2},{4,5},{5,4},{6,7},{7,6},{8,9},{9,8},{10,11... | collective-permute-start | bytes 1622024 | tf_op jit(solution)/shard_map/ppermute | solution.py:37
  491.5 67.6 %collective-permute-start.50 = (bf16[256,1536]{1,0:T(8,128)(2,1)S(1)}, bf16[256,1536]{1,0:T(8,128)(2,1)S(1)}, u32[]{:S(2)}, u32[]{:S(2)}) collective-permute-start(bf16[256,1536]{1,0:T(8,128)(2,1)S(1)} %get-tuple-element.235), channel_id=1, source_target_pairs={{0,8},{4,12},{8,0},{12,4},{1,9},{5,13},{9,1},{13,5},{2,10},{6,14},... | collective-permute-start | bytes 2359304 | tf_op jit(solution)/shard_map/ppermute | solution.py:33
  495.6 68.5 %collective-permute-start.49 = (bf16[256,1536]{1,0:T(8,128)(2,1)S(1)}, bf16[256,1536]{1,0:T(8,128)(2,1)S(1)}, u32[]{:S(2)}, u32[]{:S(2)}) collective-permute-start(bf16[256,1536]{1,0:T(8,128)(2,1)S(1)} %get-tuple-element.233), channel_id=1, source_target_pairs={{0,12},{4,0},{8,4},{12,8},{1,13},{5,1},{9,5},{13,9},{2,14},{6,2},{... | collective-permute-start | bytes 2359304 | tf_op jit(solution)/shard_map/ppermute | solution.py:33
  499.3 67.7 %collective-permute-start.57 = (bf16[4,96,1408]{2,1,0:T(8,128)(2,1)S(1)}, bf16[4,96,1408]{2,1,0:T(8,128)(2,1)S(1)}, u32[]{:S(2)}, u32[]{:S(2)}) collective-permute-start(bf16[4,96,1408]{2,1,0:T(8,128)(2,1)S(1)} %copy-done.74), channel_id=1, source_target_pairs={{0,16},{16,0},{1,17},{17,1},{2,18},{18,2},{3,19},{19,3},{4,20},{20... | collective-permute-start | bytes 3244040 | tf_op jit(solution)/shard_map/ppermute | solution.py:28
  501.3 87.3 %collective-permute-start.78 = (bf16[2,96,768]{2,1,0:T(8,128)(2,1)}, bf16[2,96,768]{2,1,0:T(8,128)(2,1)}, u32[]{:S(2)}, u32[]{:S(2)}) collective-permute-start(bf16[2,96,768]{2,1,0:T(8,128)(2,1)} %collective-permute-done.77), channel_id=1, source_target_pairs={{0,16},{16,0},{1,17},{17,1},{2,18},{18,2},{3,19},{19,3},{4,20},{20... | collective-permute-start | bytes 884744 | tf_op jit(solution)/shard_map/ppermute | solution.py:28
  510.6 58.6 %collective-permute-start.59 = (bf16[4,96,1408]{2,1,0:T(8,128)(2,1)S(1)}, bf16[4,96,1408]{2,1,0:T(8,128)(2,1)S(1)}, u32[]{:S(2)}, u32[]{:S(2)}) collective-permute-start(bf16[4,96,1408]{2,1,0:T(8,128)(2,1)S(1)} %copy-done.72), channel_id=1, source_target_pairs={{0,16},{16,0},{1,17},{17,1},{2,18},{18,2},{3,19},{19,3},{4,20},{20... | collective-permute-start | bytes 3244040 | tf_op jit(solution)/shard_map/ppermute | solution.py:28
  590.4 81.6 %collective-permute-start.82 = (bf16[5,384,768]{2,1,0:T(8,128)(2,1)}, bf16[5,384,768]{2,1,0:T(8,128)(2,1)}, u32[]{:S(2)}, u32[]{:S(2)}) collective-permute-start(bf16[5,384,768]{2,1,0:T(8,128)(2,1)} %get-tuple-element.54.rest_0_), channel_id=1, source_target_pairs={{0,1},{1,0},{2,3},{3,2},{4,5},{5,4},{6,7},{7,6},{8,9},{9,8},{10,11... | collective-permute-start | bytes 8847368 | tf_op jit(solution)/shard_map/ppermute | solution.py:37
  591.2 83.3 %collective-permute-start.83 = (bf16[5,384,768]{2,1,0:T(8,128)(2,1)}, bf16[5,384,768]{2,1,0:T(8,128)(2,1)}, u32[]{:S(2)}, u32[]{:S(2)}) collective-permute-start(bf16[5,384,768]{2,1,0:T(8,128)(2,1)} %get-tuple-element.54.rest_0_), channel_id=1, source_target_pairs={{0,2},{1,3},{2,0},{3,1},{4,6},{5,7},{6,4},{7,5},{8,10},{9,11},{10,... | collective-permute-start | bytes 8847368 | tf_op jit(solution)/shard_map/ppermute | solution.py:37
  642.6 56.4 %collective-permute-start.80 = (bf16[256,1536]{1,0:T(8,128)(2,1)S(1)}, bf16[256,1536]{1,0:T(8,128)(2,1)S(1)}, u32[]{:S(2)}, u32[]{:S(2)}) collective-permute-start(bf16[256,1536]{1,0:T(8,128)(2,1)S(1)} %multiply_convert_fusion), channel_id=1, source_target_pairs={{0,8},{4,12},{8,0},{12,4},{1,9},{5,13},{9,1},{13,5},{2,10},{6,14},... | collective-permute-start | bytes 2359304 | tf_op jit(solution)/shard_map/ppermute | solution.py:33
  643.1 67.0 %collective-permute-start.79 = (bf16[256,1536]{1,0:T(8,128)(2,1)S(1)}, bf16[256,1536]{1,0:T(8,128)(2,1)S(1)}, u32[]{:S(2)}, u32[]{:S(2)}) collective-permute-start(bf16[256,1536]{1,0:T(8,128)(2,1)S(1)} %multiply_convert_fusion), channel_id=1, source_target_pairs={{0,4},{4,8},{8,12},{12,0},{1,5},{5,9},{9,13},{13,1},{2,6},{6,10},{... | collective-permute-start | bytes 2359304 | tf_op jit(solution)/shard_map/ppermute | solution.py:33
  672.0 78.1 %collective-permute-start.86 = (bf16[5,384,768]{2,1,0:T(8,128)(2,1)}, bf16[5,384,768]{2,1,0:T(8,128)(2,1)}, u32[]{:S(2)}, u32[]{:S(2)}) collective-permute-start(bf16[5,384,768]{2,1,0:T(8,128)(2,1)} %get-tuple-element.54.rest_0_), channel_id=1, source_target_pairs={{0,16},{16,0},{1,17},{17,1},{2,18},{18,2},{3,19},{19,3},{4,20},{20... | collective-permute-start | bytes 8847368 | tf_op jit(solution)/shard_map/ppermute | solution.py:28
  677.0 73.1 %collective-permute-start.87 = (bf16[5,384,768]{2,1,0:T(8,128)(2,1)}, bf16[5,384,768]{2,1,0:T(8,128)(2,1)}, u32[]{:S(2)}, u32[]{:S(2)}) collective-permute-start(bf16[5,384,768]{2,1,0:T(8,128)(2,1)} %collective-permute-done.82.rest_1_), channel_id=1, source_target_pairs={{0,16},{16,0},{1,17},{17,1},{2,18},{18,2},{3,19},{19,3},{4,20},{20... | collective-permute-start | bytes 8847368 | tf_op jit(solution)/shard_map/ppermute | solution.py:28
  699.0 51.1 %collective-permute-start.88 = (bf16[5,384,768]{2,1,0:T(8,128)(2,1)}, bf16[5,384,768]{2,1,0:T(8,128)(2,1)}, u32[]{:S(2)}, u32[]{:S(2)}) collective-permute-start(bf16[5,384,768]{2,1,0:T(8,128)(2,1)} %collective-permute-done.83.rest_2_), channel_id=1, source_target_pairs={{0,16},{16,0},{1,17},{17,1},{2,18},{18,2},{3,19},{19,3},{4,20},{20... | collective-permute-start | bytes 8847368 | tf_op jit(solution)/shard_map/ppermute | solution.py:28
  797.1 66.6 %collective-permute-start.92 = (bf16[256,1536]{1,0:T(8,128)(2,1)S(1)}, bf16[256,1536]{1,0:T(8,128)(2,1)S(1)}, u32[]{:S(2)}, u32[]{:S(2)}) collective-permute-start(bf16[256,1536]{1,0:T(8,128)(2,1)S(1)} %get-tuple-element.232), channel_id=1, source_target_pairs={{0,8},{4,12},{8,0},{12,4},{1,9},{5,13},{9,1},{13,5},{2,10},{6,14},... | collective-permute-start | bytes 2359304 | tf_op jit(solution)/shard_map/ppermute | solution.py:33
  801.1 66.9 %collective-permute-start.91 = (bf16[256,1536]{1,0:T(8,128)(2,1)S(1)}, bf16[256,1536]{1,0:T(8,128)(2,1)S(1)}, u32[]{:S(2)}, u32[]{:S(2)}) collective-permute-start(bf16[256,1536]{1,0:T(8,128)(2,1)S(1)} %get-tuple-element.230), channel_id=1, source_target_pairs={{0,12},{4,0},{8,4},{12,8},{1,13},{5,1},{9,5},{13,9},{2,14},{6,2},{... | collective-permute-start | bytes 2359304 | tf_op jit(solution)/shard_map/ppermute | solution.py:33
  870.9 51.2 %collective-permute-start.96 = (bf16[256,1536]{1,0:T(8,128)(2,1)}, bf16[256,1536]{1,0:T(8,128)(2,1)}, u32[]{:S(2)}, u32[]{:S(2)}) collective-permute-start(bf16[256,1536]{1,0:T(8,128)(2,1)} %get-tuple-element.189), channel_id=1, source_target_pairs={{0,8},{4,12},{8,0},{12,4},{1,9},{5,13},{9,1},{13,5},{2,10},{6,14},... | collective-permute-start | bytes 2359304 | tf_op jit(solution)/shard_map/ppermute | solution.py:33
  871.4 67.6 %collective-permute-start.95 = (bf16[256,1536]{1,0:T(8,128)(2,1)}, bf16[256,1536]{1,0:T(8,128)(2,1)}, u32[]{:S(2)}, u32[]{:S(2)}) collective-permute-start(bf16[256,1536]{1,0:T(8,128)(2,1)} %get-tuple-element.189), channel_id=1, source_target_pairs={{0,4},{4,8},{8,12},{12,0},{1,5},{5,9},{9,13},{13,1},{2,6},{6,10},{... | collective-permute-start | bytes 2359304 | tf_op jit(solution)/shard_map/ppermute | solution.py:33
  876.2 158.5 %collective-permute-start.94 = (bf16[256,1536]{1,0:T(8,128)(2,1)}, bf16[256,1536]{1,0:T(8,128)(2,1)}, u32[]{:S(2)}, u32[]{:S(2)}) collective-permute-start(bf16[256,1536]{1,0:T(8,128)(2,1)} %get-tuple-element.190), channel_id=1, source_target_pairs={{0,16},{16,0},{1,17},{17,1},{2,18},{18,2},{3,19},{19,3},{4,20},{20... | collective-permute-start | bytes 2359304 | tf_op jit(solution)/shard_map/ppermute | solution.py:28
  994.6 49.3 %collective-permute-start.102 = (f32[8,256]{0,1:T(8,128)}, f32[8,256]{0,1:T(8,128)}, u32[]{:S(2)}, u32[]{:S(2)}) collective-permute-start(f32[8,256]{0,1:T(8,128)} %get-tuple-element.306), channel_id=1, source_target_pairs={{0,8},{4,12},{8,0},{12,4},{1,9},{5,13},{9,1},{13,5},{2,10},{6,14},... | collective-permute-start | bytes 24584 | tf_op jit(solution)/shard_map/ppermute | solution.py:33
  996.3 51.3 %collective-permute-start.103 = (f32[8,256]{0,1:T(8,128)}, f32[8,256]{0,1:T(8,128)}, u32[]{:S(2)}, u32[]{:S(2)}) collective-permute-start(f32[8,256]{0,1:T(8,128)} %get-tuple-element.305), channel_id=1, source_target_pairs={{0,4},{4,8},{8,12},{12,0},{1,5},{5,9},{9,13},{13,1},{2,6},{6,10},{... | collective-permute-start | bytes 24584 | tf_op jit(solution)/shard_map/ppermute | solution.py:33
  999.4 53.4 %collective-permute-start.100 = (bf16[256,1536]{1,0:T(8,128)(2,1)}, bf16[256,1536]{1,0:T(8,128)(2,1)}, u32[]{:S(2)}, u32[]{:S(2)}) collective-permute-start(bf16[256,1536]{1,0:T(8,128)(2,1)} %get-tuple-element.228), channel_id=1, source_target_pairs={{0,4},{4,8},{8,12},{12,0},{1,5},{5,9},{9,13},{13,1},{2,6},{6,10},{... | collective-permute-start | bytes 2359304 | tf_op jit(solution)/shard_map/ppermute | solution.py:33
  1034.7 53.7 %collective-permute-start.99 = (bf16[256,1536]{1,0:T(8,128)(2,1)}, bf16[256,1536]{1,0:T(8,128)(2,1)}, u32[]{:S(2)}, u32[]{:S(2)}) collective-permute-start(bf16[256,1536]{1,0:T(8,128)(2,1)} %get-tuple-element.229), channel_id=1, source_target_pairs={{0,8},{4,12},{8,0},{12,4},{1,9},{5,13},{9,1},{13,5},{2,10},{6,14},... | collective-permute-start | bytes 2359304 | tf_op jit(solution)/shard_map/ppermute | solution.py:33
  1039.0 49.4 %collective-permute-start.98 = (bf16[256,1536]{1,0:T(8,128)(2,1)}, bf16[256,1536]{1,0:T(8,128)(2,1)S(1)}, u32[]{:S(2)}, u32[]{:S(2)}) collective-permute-start(bf16[256,1536]{1,0:T(8,128)(2,1)} %get-tuple-element.227), channel_id=1, source_target_pairs={{0,12},{4,0},{8,4},{12,8},{1,13},{5,1},{9,5},{13,9},{2,14},{6,2},{... | collective-permute-start | bytes 2359304 | tf_op jit(solution)/shard_map/ppermute | solution.py:33
  1043.9 169.7 %collective-permute-start.181 = (bf16[5,192,768]{2,1,0:T(8,128)(2,1)}, bf16[5,192,768]{2,1,0:T(8,128)(2,1)}, u32[]{:S(2)}, u32[]{:S(2)}) collective-permute-start(bf16[5,192,768]{2,1,0:T(8,128)(2,1)} %get-tuple-element.85), channel_id=1, source_target_pairs={{0,16},{16,0},{1,17},{17,1},{2,18},{18,2},{3,19},{19,3},{4,20},{20... | collective-permute-start | bytes 4423688 | tf_op jit(solution)/shard_map/ppermute | solution.py:28
  1047.6 169.5 %collective-permute-start.175 = (bf16[5,192,768]{2,1,0:T(8,128)(2,1)}, bf16[5,192,768]{2,1,0:T(8,128)(2,1)}, u32[]{:S(2)}, u32[]{:S(2)}) collective-permute-start(bf16[5,192,768]{2,1,0:T(8,128)(2,1)} %get-tuple-element.81), channel_id=1, source_target_pairs={{0,16},{16,0},{1,17},{17,1},{2,18},{18,2},{3,19},{19,3},{4,20},{20... | collective-permute-start | bytes 4423688 | tf_op jit(solution)/shard_map/ppermute | solution.py:28
  1187.8 53.4 %collective-permute-start.108 = (bf16[256,1536]{1,0:T(8,128)(2,1)S(1)}, bf16[256,1536]{1,0:T(8,128)(2,1)}, u32[]{:S(2)}, u32[]{:S(2)}) collective-permute-start(bf16[256,1536]{1,0:T(8,128)(2,1)S(1)} %get-tuple-element.185), channel_id=1, source_target_pairs={{0,8},{4,12},{8,0},{12,4},{1,9},{5,13},{9,1},{13,5},{2,10},{6,14},... | collective-permute-start | bytes 2359304 | tf_op jit(solution)/shard_map/ppermute | solution.py:33
  1190.9 67.1 %collective-permute-start.107 = (bf16[256,1536]{1,0:T(8,128)(2,1)S(1)}, bf16[256,1536]{1,0:T(8,128)(2,1)}, u32[]{:S(2)}, u32[]{:S(2)}) collective-permute-start(bf16[256,1536]{1,0:T(8,128)(2,1)S(1)} %get-tuple-element.185), channel_id=1, source_target_pairs={{0,4},{4,8},{8,12},{12,0},{1,5},{5,9},{9,13},{13,1},{2,6},{6,10},{... | collective-permute-start | bytes 2359304 | tf_op jit(solution)/shard_map/ppermute | solution.py:33
  1314.6 81.0 %collective-permute-start.115 = (f32[8,256]{0,1:T(8,128)S(1)}, f32[8,256]{0,1:T(8,128)S(1)}, u32[]{:S(2)}, u32[]{:S(2)}) collective-permute-start(f32[8,256]{0,1:T(8,128)S(1)} %get-tuple-element.302), channel_id=1, source_target_pairs={{0,4},{4,8},{8,12},{12,0},{1,5},{5,9},{9,13},{13,1},{2,6},{6,10},{... | collective-permute-start | bytes 24584 | tf_op jit(solution)/shard_map/ppermute | solution.py:33
  1317.6 80.5 %collective-permute-start.112 = (bf16[256,1536]{1,0:T(8,128)(2,1)}, bf16[256,1536]{1,0:T(8,128)(2,1)}, u32[]{:S(2)}, u32[]{:S(2)}) collective-permute-start(bf16[256,1536]{1,0:T(8,128)(2,1)} %get-tuple-element.225), channel_id=1, source_target_pairs={{0,4},{4,8},{8,12},{12,0},{1,5},{5,9},{9,13},{13,1},{2,6},{6,10},{... | collective-permute-start | bytes 2359304 | tf_op jit(solution)/shard_map/ppermute | solution.py:33
  1317.9 80.4 %collective-permute-start.111 = (bf16[256,1536]{1,0:T(8,128)(2,1)}, bf16[256,1536]{1,0:T(8,128)(2,1)}, u32[]{:S(2)}, u32[]{:S(2)}) collective-permute-start(bf16[256,1536]{1,0:T(8,128)(2,1)} %get-tuple-element.226), channel_id=1, source_target_pairs={{0,8},{4,12},{8,0},{12,4},{1,9},{5,13},{9,1},{13,5},{2,10},{6,14},... | collective-permute-start | bytes 2359304 | tf_op jit(solution)/shard_map/ppermute | solution.py:33
  1321.2 77.1 %collective-permute-start.110 = (bf16[256,1536]{1,0:T(8,128)(2,1)}, bf16[256,1536]{1,0:T(8,128)(2,1)}, u32[]{:S(2)}, u32[]{:S(2)}) collective-permute-start(bf16[256,1536]{1,0:T(8,128)(2,1)} %get-tuple-element.224), channel_id=1, source_target_pairs={{0,12},{4,0},{8,4},{12,8},{1,13},{5,1},{9,5},{13,9},{2,14},{6,2},{... | collective-permute-start | bytes 2359304 | tf_op jit(solution)/shard_map/ppermute | solution.py:33
  1358.4 134.4 %collective-permute-start.178 = (bf16[5,384,768]{2,1,0:T(8,128)(2,1)}, bf16[5,384,768]{2,1,0:T(8,128)(2,1)}, u32[]{:S(2)}, u32[]{:S(2)}) collective-permute-start(bf16[5,384,768]{2,1,0:T(8,128)(2,1)} %get-tuple-element.83), channel_id=1, source_target_pairs={{0,16},{16,0},{1,17},{17,1},{2,18},{18,2},{3,19},{19,3},{4,20},{20... | collective-permute-start | bytes 8847368 | tf_op jit(solution)/shard_map/ppermute | solution.py:28
  1395.6 102.0 %collective-permute-start.174 = (bf16[5,384,768]{2,1,0:T(8,128)(2,1)}, bf16[5,384,768]{2,1,0:T(8,128)(2,1)}, u32[]{:S(2)}, u32[]{:S(2)}) collective-permute-start(bf16[5,384,768]{2,1,0:T(8,128)(2,1)} %get-tuple-element.79), channel_id=1, source_target_pairs={{0,16},{16,0},{1,17},{17,1},{2,18},{18,2},{3,19},{19,3},{4,20},{20... | collective-permute-start | bytes 8847368 | tf_op jit(solution)/shard_map/ppermute | solution.py:28
  1398.2 116.2 %collective-permute-start.182 = (bf16[5,192,768]{2,1,0:T(8,128)(2,1)}, bf16[5,192,768]{2,1,0:T(8,128)(2,1)}, u32[]{:S(2)}, u32[]{:S(2)}) collective-permute-start(bf16[5,192,768]{2,1,0:T(8,128)(2,1)} %add_convert_fusion.11), channel_id=1, source_target_pairs={{0,1},{1,0},{2,3},{3,2},{4,5},{5,4},{6,7},{7,6},{8,9},{9,8},{10,11... | collective-permute-start | bytes 4423688 | tf_op jit(solution)/shard_map/ppermute | solution.py:37
  1503.0 109.6 %collective-permute-start.167 = (bf16[5,384,768]{2,1,0:T(8,128)(2,1)}, bf16[5,384,768]{2,1,0:T(8,128)(2,1)}, u32[]{:S(2)}, u32[]{:S(2)}) collective-permute-start(bf16[5,384,768]{2,1,0:T(8,128)(2,1)} %get-tuple-element.71), channel_id=1, source_target_pairs={{0,16},{16,0},{1,17},{17,1},{2,18},{18,2},{3,19},{19,3},{4,20},{20... | collective-permute-start | bytes 8847368 | tf_op jit(solution)/shard_map/ppermute | solution.py:28
  1514.4 51.8 %collective-permute-start.119 = (bf16[256,1536]{1,0:T(8,128)(2,1)}, bf16[256,1536]{1,0:T(8,128)(2,1)}, u32[]{:S(2)}, u32[]{:S(2)}) collective-permute-start(bf16[256,1536]{1,0:T(8,128)(2,1)} %get-tuple-element.180), channel_id=1, source_target_pairs={{0,16},{16,0},{1,17},{17,1},{2,18},{18,2},{3,19},{19,3},{4,20},{20... | collective-permute-start | bytes 2359304 | tf_op jit(solution)/shard_map/ppermute | solution.py:28
  1531.1 48.8 %collective-permute-start.180 = (bf16[5,192,768]{2,1,0:T(8,128)(2,1)}, bf16[5,192,768]{2,1,0:T(8,128)(2,1)}, u32[]{:S(2)}, u32[]{:S(2)}) collective-permute-start(bf16[5,192,768]{2,1,0:T(8,128)(2,1)} %slice.723), channel_id=1, source_target_pairs={{0,1},{1,0},{2,3},{3,2},{4,5},{5,4},{6,7},{7,6},{8,9},{9,8},{10,11... | collective-permute-start | bytes 4423688 | tf_op jit(solution)/shard_map/ppermute | solution.py:37
  1545.5 48.4 %collective-permute-start.179 = (bf16[5,192,768]{2,1,0:T(8,128)(2,1)}, bf16[5,192,768]{2,1,0:T(8,128)(2,1)}, u32[]{:S(2)}, u32[]{:S(2)}) collective-permute-start(bf16[5,192,768]{2,1,0:T(8,128)(2,1)} %slice.722), channel_id=1, source_target_pairs={{0,2},{1,3},{2,0},{3,1},{4,6},{5,7},{6,4},{7,5},{8,10},{9,11},{10,... | collective-permute-start | bytes 4423688 | tf_op jit(solution)/shard_map/ppermute | solution.py:37
  1578.6 67.7 %collective-permute-start.163 = (bf16[5,384,768]{2,1,0:T(8,128)(2,1)}, bf16[5,384,768]{2,1,0:T(8,128)(2,1)S(1)}, u32[]{:S(2)}, u32[]{:S(2)}) collective-permute-start(bf16[5,384,768]{2,1,0:T(8,128)(2,1)} %get-tuple-element.67), channel_id=1, source_target_pairs={{0,16},{16,0},{1,17},{17,1},{2,18},{18,2},{3,19},{19,3},{4,20},{20... | collective-permute-start | bytes 8847368 | tf_op jit(solution)/shard_map/ppermute | solution.py:28
  1593.9 53.8 %collective-permute-start.151 = (bf16[4,4,96,768]{3,2,0,1:T(8,128)(2,1)}, bf16[4,4,96,768]{3,2,0,1:T(8,128)(2,1)}, u32[]{:S(2)}, u32[]{:S(2)}) collective-permute-start(bf16[4,4,96,768]{3,2,0,1:T(8,128)(2,1)} %copy.545), channel_id=1, source_target_pairs={{0,16},{16,0},{1,17},{17,1},{2,18},{18,2},{3,19},{19,3},{4,20},{20... | collective-permute-start | bytes 7077896 | tf_op jit(solution)/shard_map/ppermute | solution.py:28
  1621.5 161.1 %collective-permute-start.130 = (bf16[4,4,96,1408]{3,2,0,1:T(8,128)(2,1)S(1)}, bf16[4,4,96,1408]{3,2,0,1:T(8,128)(2,1)}, u32[]{:S(2)}, u32[]{:S(2)}) collective-permute-start(bf16[4,4,96,1408]{3,2,0,1:T(8,128)(2,1)S(1)} %copy.541), channel_id=1, source_target_pairs={{0,16},{16,0},{1,17},{17,1},{2,18},{18,2},{3,19},{19,3},{4,20},{20... | collective-permute-start | bytes 12976136 | tf_op jit(solution)/shard_map/ppermute | solution.py:28
  1666.2 54.0 %collective-permute-start.172 = (bf16[5,192,768]{2,1,0:T(8,128)(2,1)}, bf16[5,192,768]{2,1,0:T(8,128)(2,1)}, u32[]{:S(2)}, u32[]{:S(2)}) collective-permute-start(bf16[5,192,768]{2,1,0:T(8,128)(2,1)} %add_convert_fusion.14), channel_id=1, source_target_pairs={{0,2},{1,3},{2,0},{3,1},{4,6},{5,7},{6,4},{7,5},{8,10},{9,11},{10,... | collective-permute-start | bytes 4423688 | tf_op jit(solution)/shard_map/ppermute | solution.py:37
  1667.1 126.9 %collective-permute-start.120 = (bf16[4,4,96,1408]{3,2,0,1:T(8,128)(2,1)}, bf16[4,4,96,1408]{3,2,0,1:T(8,128)(2,1)}, u32[]{:S(2)}, u32[]{:S(2)}) collective-permute-start(bf16[4,4,96,1408]{3,2,0,1:T(8,128)(2,1)} %copy.539), channel_id=1, source_target_pairs={{0,16},{16,0},{1,17},{17,1},{2,18},{18,2},{3,19},{19,3},{4,20},{20... | collective-permute-start | bytes 12976136 | tf_op jit(solution)/shard_map/ppermute | solution.py:28
  1720.2 60.2 %collective-permute-start.166 = (bf16[5,192,768]{2,1,0:T(8,128)(2,1)S(1)}, bf16[5,192,768]{2,1,0:T(8,128)(2,1)S(1)}, u32[]{:S(2)}, u32[]{:S(2)}) collective-permute-start(bf16[5,192,768]{2,1,0:T(8,128)(2,1)S(1)} %add_convert_fusion.16), channel_id=1, source_target_pairs={{0,1},{1,0},{2,3},{3,2},{4,5},{5,4},{6,7},{7,6},{8,9},{9,8},{10,11... | collective-permute-start | bytes 4423688 | tf_op jit(solution)/shard_map/ppermute | solution.py:37
  1748.8 59.1 %collective-permute-start.173 = (bf16[5,384,768]{2,1,0:T(8,128)(2,1)}, bf16[5,384,768]{2,1,0:T(8,128)(2,1)}, u32[]{:S(2)}, u32[]{:S(2)}) collective-permute-start(bf16[5,384,768]{2,1,0:T(8,128)(2,1)} %get-tuple-element.77), channel_id=1, source_target_pairs={{0,16},{16,0},{1,17},{17,1},{2,18},{18,2},{3,19},{19,3},{4,20},{20... | collective-permute-start | bytes 8847368 | tf_op jit(solution)/shard_map/ppermute | solution.py:28
  1756.8 51.6 %collective-permute-start.162 = (bf16[5,384,768]{2,1,0:T(8,128)(2,1)}, bf16[5,384,768]{2,1,0:T(8,128)(2,1)}, u32[]{:S(2)}, u32[]{:S(2)}) collective-permute-start(bf16[5,384,768]{2,1,0:T(8,128)(2,1)} %get-tuple-element.65), channel_id=1, source_target_pairs={{0,16},{16,0},{1,17},{17,1},{2,18},{18,2},{3,19},{19,3},{4,20},{20... | collective-permute-start | bytes 8847368 | tf_op jit(solution)/shard_map/ppermute | solution.py:28
  1780.4 82.1 %collective-permute-start.150 = (bf16[96,768]{1,0:T(8,128)(2,1)}, bf16[96,768]{1,0:T(8,128)(2,1)}, u32[]{:S(2)}, u32[]{:S(2)}) collective-permute-start(bf16[96,768]{1,0:T(8,128)(2,1)} %get-tuple-element.288), channel_id=1, source_target_pairs={{0,4},{4,8},{8,12},{12,0},{1,5},{5,9},{9,13},{13,1},{2,6},{6,10},{... | collective-permute-start | bytes 442376 | tf_op jit(solution)/shard_map/ppermute | solution.py:33
  (272 other events, 6175.9 us)

commit v2 on v1

v2 whole, which is shorter than its diff:
```python
import functools
import math

import jax
import jax.numpy as jnp
from jax import lax
from jax.experimental import pallas as pl
from jax.experimental.pallas import tpu as pltpu
from jax.sharding import PartitionSpec as P

HEADS = 24
KV_HEADS = 8
HEAD = 64

EPSILON = 1e-06
ROPE_BASE = 10000.0
NEGATIVE = -1e30
LANES = 128
TILE = 256
VMEM_LIMIT = 60 * 1024 * 1024

F32 = jnp.float32
BF16 = jnp.bfloat16


def lasting(micros):
    return pl.CostEstimate(
        flops=int(micros * 1.1e9), bytes_accessed=1000000, transcendentals=0
    )


def swap(array):
    return lax.ppermute(array, "section", [(0, 1), (1, 0)])


def shifted(array, axis, by):
    length = lax.axis_size(axis)
    return lax.ppermute(array, axis, [(i, (i + by) % length) for i in range(length)])


def flipped(array, mask):
    return lax.ppermute(array, "shard", [(i, i ^ mask) for i in range(lax.axis_size("shard"))])


def slots_of(array, axis):
    return [array] + [shifted(array, axis, k) for k in range(1, lax.axis_size(axis))]


def after(array, *others):
    return lax.optimization_barrier((array, *others))[0]


def cut(array, start, stop, axis):
    return lax.slice_in_dim(array, start, stop, axis=axis)


def ring_gather(array, axis, held=()):
    count = lax.axis_size("shard")
    me = lax.axis_index("shard")
    if count != 4:
        pieces = [
            (slot, lax.rem(me - k + count, count), 0)
            for k, slot in enumerate(slots_of(array, "shard"))
        ]
        return pieces, [piece for piece, _, _ in pieces[1:]]
    length = array.shape[axis]
    half = length // 2
    one = flipped(array, 1)
    two = flipped(array, 2)
    if held:
        one, two = lax.optimization_barrier((one, two, *held))[:2]
    far_low = flipped(cut(one, 0, half, axis), 2)
    far_high = flipped(cut(two, half, length, axis), 1)
    return [
        (array, me, 0),
        (one, me ^ 1, 0),
        (two, me ^ 2, 0),
        (far_low, me ^ 3, 0),
        (far_high, me ^ 3, half),
    ], [one, two]


def scatter_first(pieces, axis):
    if lax.axis_size("shard") != 4:
        return [shifted(pieces[k], "shard", -k) for k in range(1, len(pieces))]
    own, one, two, far_low, far_high = pieces
    half = far_low.shape[axis]
    length = own.shape[axis]
    return [
        flipped(far_low, 2),
        flipped(far_high, 1),
        flipped(cut(one, half, length, axis), 1),
        flipped(cut(two, 0, half, axis), 2),
    ]


def scatter_second(pieces, first, axis):
    if lax.axis_size("shard") != 4:
        return []
    own, one, two, far_low, far_high = pieces
    half = far_low.shape[axis]
    length = own.shape[axis]
    low, high = first[:2]
    return [
        flipped((cut(one, 0, half, axis).astype(F32) + low.astype(F32)).astype(BF16), 1),
        flipped((cut(two, half, length, axis).astype(F32) + high.astype(F32)).astype(BF16), 2),
    ]


def scatter_end(pieces, first, second, axis):
    if lax.axis_size("shard") != 4:
        return sum((array.astype(F32) for array in first), pieces[0].astype(F32))
    one_high, two_low = first[2:]
    one_low, two_high = second
    return pieces[0].astype(F32) + jnp.concatenate(
        [
            one_low.astype(F32) + two_low.astype(F32),
            one_high.astype(F32) + two_high.astype(F32),
        ],
        axis=axis,
    )


def rotary_tables(positions):
    frequency = 1.0 / ROPE_BASE ** (jnp.arange(0, HEAD, 2, dtype=F32) / HEAD)
    angles = positions.astype(F32)[:, None] * frequency[None, :]
    cosines, sines = jnp.cos(angles), jnp.sin(angles)
    return (
        jnp.concatenate([cosines] * 4, axis=1),
        jnp.concatenate([-sines, sines] * 2, axis=1),
    )


def norm_back(grad_in, values, scale_rows, scale_gain):
    shaped = grad_in * scale_gain
    grad_values = scale_rows * shaped - values * scale_rows**3 * jnp.mean(
        shaped * values, axis=-1, keepdims=True
    )
    return (grad_values, jnp.sum(grad_in * values * scale_rows, axis=0))


def dot_nt(left, right):
    return lax.dot_general(left, right, (((1,), (1,)), ((), ())), preferred_element_type=F32)


def dot_nn(left, right):
    return jnp.dot(left, right, preferred_element_type=F32)


def dot_tn(left, right):
    return lax.dot_general(left, right, (((0,), (0,)), ((), ())), preferred_element_type=F32)


def fill_weights(ref, gate_up, down):
    parts, _, depth, columns = ref.shape
    width = columns // 3
    for index in range(parts):
        half, place = divmod(index, parts // 2)
        span = slice(place * depth, (place + 1) * depth)
        gate_up[span, 2 * half * width : 2 * (half + 1) * width] = ref[index, 0, :, : 2 * width]
        down[span, half * width : (half + 1) * width] = ref[index, 0, :, 2 * width :]


def column_of(table, index):
    lane = lax.broadcasted_iota(jnp.int32, table.shape, 1)
    return jnp.sum(jnp.where(lane == index, table, 0.0), axis=1, keepdims=True)


def split_gate_up(raw, width):
    gate = jnp.concatenate([raw[:, :width], raw[:, 2 * width : 3 * width]], axis=1)
    up = jnp.concatenate([raw[:, width : 2 * width], raw[:, 3 * width :]], axis=1)
    return gate, up


def join_gate_up(gate, up, width):
    return jnp.concatenate(
        [gate[:, :width], up[:, :width], gate[:, width:], up[:, width:]], axis=1
    )


def moe_forward(rows, gates, weights):
    total, model = rows.shape
    parts, experts, depth, columns = weights.shape
    width = columns // 3
    tile = min(TILE, total)

    def body(rows_ref, gates_ref, weights_ref, out_ref, raw_ref, gate_up, down, sums):
        expert = pl.program_id(0)
        fill_weights(weights_ref, gate_up, down)

        def step(index, carry):
            span = pl.ds(pl.multiple_of(index * tile, tile), tile)
            raw = dot_nn(rows_ref[span, :], gate_up[...])
            raw_ref[0, span, :] = raw.astype(BF16)
            gate, up = split_gate_up(raw, width)
            weight = column_of(gates_ref[span, :], expert)
            act = (gate * jax.nn.sigmoid(gate) * up * weight).astype(BF16)
            part = dot_nt(act, down[...])

            @pl.when(expert == 0)
            def _():
                sums[span, :] = part

            @pl.when(expert > 0)
            def _():
                sums[span, :] += part

            @pl.when(expert == experts - 1)
            def _():
                out_ref[span, :] = sums[span, :].astype(BF16)

            return carry

        lax.fori_loop(0, total // tile, step, 0)

    whole = lambda e: (0, 0)
    per_expert = lambda e: (e, 0, 0)
    once = pl.Buffered(1)
    return pl.pallas_call(
        body,
        grid_spec=pltpu.PrefetchScalarGridSpec(
            num_scalar_prefetch=0,
            grid=(experts,),
            in_specs=[
                pl.BlockSpec((total, model), whole, pipeline_mode=once),
                pl.BlockSpec((total, LANES), whole, pipeline_mode=once),
            ]
            + [pl.BlockSpec((parts, 1, depth, columns), lambda e: (0, e, 0, 0))],
            out_specs=[
                pl.BlockSpec((total, model), whole),
                pl.BlockSpec((1, total, 4 * width), per_expert),
            ],
            scratch_shapes=[
                pltpu.VMEM((model, 4 * width), BF16),
                pltpu.VMEM((model, 2 * width), BF16),
                pltpu.VMEM((total, model), F32),
            ],
        ),
        out_shape=[
            jax.ShapeDtypeStruct((total, model), BF16),
            jax.ShapeDtypeStruct((experts, total, 4 * width), BF16),
        ],
        compiler_params=pltpu.CompilerParams(vmem_limit_bytes=VMEM_LIMIT),
        cost_estimate=lasting(40),
        name="moe_forward",
    )(rows, gates, weights)


def moe_backward_rows(grads, gates, raws, weights):
    total, model = grads.shape
    parts, experts, depth, columns = weights.shape
    width = columns // 3
    tile = min(TILE, total)

    def body(
        grads_ref,
        gates_ref,
        raw_ref,
        weights_ref,
        out_ref,
        scores_ref,
        d_raw_ref,
        act_ref,
        gate_up,
        down,
        sums,
    ):
        expert = pl.program_id(0)
        fill_weights(weights_ref, gate_up, down)

        def step(index, carry):
            span = pl.ds(pl.multiple_of(index * tile, tile), tile)
            weight = column_of(gates_ref[span, :], expert)
            gate, up = split_gate_up(raw_ref[0, span, :].astype(F32), width)
            back = dot_nn(grads_ref[span, :], down[...])
            sigmoid = jax.nn.sigmoid(gate)
            swish = gate * sigmoid
            act = swish * up
            score = jnp.sum(back * act, axis=1, keepdims=True)
            act_ref[0, span, :] = (act * weight).astype(BF16)
            d_act = back * weight
            d_gate = d_act * up * sigmoid * (1.0 + gate * (1.0 - sigmoid))
            d_raw = join_gate_up(d_gate, d_act * swish, width).astype(BF16)
            d_raw_ref[0, span, :] = d_raw
            part = dot_nt(d_raw, gate_up[...])
            lane = lax.broadcasted_iota(jnp.int32, (tile, LANES), 1)

            @pl.when(expert == 0)
            def _():
                sums[span, :] = part
                scores_ref[span, :] = jnp.where(lane == 0, score, 0.0)

            @pl.when(expert > 0)
            def _():
                sums[span, :] += part
                scores_ref[span, :] = jnp.where(lane == expert, score, scores_ref[span, :])

            @pl.when(expert == experts - 1)
            def _():
                out_ref[span, :] = sums[span, :].astype(BF16)

            return carry

        lax.fori_loop(0, total // tile, step, 0)

    whole = lambda e: (0, 0)
    per_expert = lambda e: (e, 0, 0)
    once = pl.Buffered(1)
    return pl.pallas_call(
        body,
        grid_spec=pltpu.PrefetchScalarGridSpec(
            num_scalar_prefetch=0,
            grid=(experts,),
            in_specs=[
                pl.BlockSpec((total, model), whole, pipeline_mode=once),
                pl.BlockSpec((total, LANES), whole, pipeline_mode=once),
                pl.BlockSpec((1, total, 4 * width), per_expert),
            ]
            + [pl.BlockSpec((parts, 1, depth, columns), lambda e: (0, e, 0, 0))],
            out_specs=[
                pl.BlockSpec((total, model), whole),
                pl.BlockSpec((total, LANES), whole),
                pl.BlockSpec((1, total, 4 * width), per_expert),
                pl.BlockSpec((1, total, 2 * width), per_expert),
            ],
            scratch_shapes=[
                pltpu.VMEM((model, 4 * width), BF16),
                pltpu.VMEM((model, 2 * width), BF16),
                pltpu.VMEM((total, model), F32),
            ],
        ),
        out_shape=[
            jax.ShapeDtypeStruct((total, model), BF16),
            jax.ShapeDtypeStruct((total, LANES), F32),
            jax.ShapeDtypeStruct((experts, total, 4 * width), BF16),
            jax.ShapeDtypeStruct((experts, total, 2 * width), BF16),
        ],
        compiler_params=pltpu.CompilerParams(vmem_limit_bytes=VMEM_LIMIT),
        cost_estimate=lasting(48),
        name="moe_backward_rows",
    )(grads, gates, raws, weights)


def moe_backward_weights(rows, grads, d_raws, acts, parts):
    total, model = rows.shape
    experts = d_raws.shape[0]
    width = d_raws.shape[2] // 4
    shards = parts // 2
    depth = model // shards

    def body(rows_ref, grads_ref, d_raw_ref, act_ref, out_ref, rows_t, grads_t):
        @pl.when(pl.program_id(0) == 0)
        def _():
            for start in range(0, model, TILE):
                rows_t[start : start + TILE, :] = rows_ref[:, start : start + TILE].T
                grads_t[start : start + TILE, :] = grads_ref[:, start : start + TILE].T

        for place in range(shards):
            span = slice(place * depth, (place + 1) * depth)
            gate_up = dot_nn(rows_t[span, :], d_raw_ref[0]).astype(BF16)
            down = dot_nn(grads_t[span, :], act_ref[0]).astype(BF16)
            for half in range(2):
                index = half * shards + place
                out_ref[index, 0, :, : 2 * width] = gate_up[
                    :, 2 * half * width : 2 * (half + 1) * width
                ]
                out_ref[index, 0, :, 2 * width :] = down[:, half * width : (half + 1) * width]

    whole = lambda e: (0, 0)
    per_expert = lambda e: (e, 0, 0)
    once = pl.Buffered(1)
    return pl.pallas_call(
        body,
        grid_spec=pltpu.PrefetchScalarGridSpec(
            num_scalar_prefetch=0,
            grid=(experts,),
            in_specs=[
                pl.BlockSpec((total, model), whole, pipeline_mode=once),
                pl.BlockSpec((total, model), whole, pipeline_mode=once),
                pl.BlockSpec((1, total, 4 * width), per_expert),
                pl.BlockSpec((1, total, 2 * width), per_expert),
            ],
            out_specs=pl.BlockSpec((parts, 1, depth, 3 * width), lambda e: (0, e, 0, 0)),
            scratch_shapes=[
                pltpu.VMEM((model, total), BF16),
                pltpu.VMEM((model, total), BF16),
            ],
        ),
        out_shape=jax.ShapeDtypeStruct((parts, experts, depth, 3 * width), BF16),
        compiler_params=pltpu.CompilerParams(vmem_limit_bytes=VMEM_LIMIT),
        cost_estimate=lasting(34),
        name="moe_backward_weights",
    )(rows, grads, d_raws, acts)


def line_up(pieces, owners, planes_of, shards):
    arrays = [piece for piece, _, _ in pieces]
    slots, rows, width = arrays[0].shape
    copies = slots * shards
    if rows % 16:
        result = jnp.zeros((slots, shards, rows, width), BF16)
        for place, (array, _, start) in enumerate(pieces):
            for slot in range(array.shape[0]):
                result = lax.dynamic_update_slice(
                    result,
                    array[slot][None, None],
                    (planes_of[start + slot], owners[place], 0, 0),
                )
        return result.reshape(copies * rows, width)

    def body(owner_ref, plane_ref, *refs):
        out_ref, sems = refs[len(arrays) :]
        started = []
        for place, (array, _, start) in enumerate(pieces):
            for slot in range(array.shape[0]):
                index = plane_ref[start + slot] * shards + owner_ref[place]
                started.append(
                    pltpu.make_async_copy(
                        refs[place].at[slot],
                        out_ref.at[pl.ds(pl.multiple_of(index * rows, 16), rows), :],
                        sems.at[len(started)],
                    )
                )
                started[-1].start()
        for copy in started:
            copy.wait()

    return pl.pallas_call(
        body,
        grid_spec=pltpu.PrefetchScalarGridSpec(
            num_scalar_prefetch=2,
            grid=(1,),
            in_specs=[pl.BlockSpec(memory_space=pl.ANY)] * len(arrays),
            out_specs=pl.BlockSpec((copies * rows, width), lambda i, *_: (0, 0)),
            scratch_shapes=[pltpu.SemaphoreType.DMA((copies * 2,))],
        ),
        out_shape=jax.ShapeDtypeStruct((copies * rows, width), BF16),
        compiler_params=pltpu.CompilerParams(vmem_limit_bytes=VMEM_LIMIT),
        cost_estimate=lasting(4),
        name="line_up",
    )(owners, planes_of, *arrays)


def turned(values, cosines, sines):
    lane = lax.broadcasted_iota(jnp.int32, cosines.shape, 1)
    low = lane % HEAD < HEAD // 2
    parts = []
    for start in range(0, values.shape[1], LANES):
        block = values[:, start : start + LANES]
        partner = jnp.where(
            low,
            pltpu.roll(block, LANES - HEAD // 2, 1),
            pltpu.roll(block, HEAD // 2, 1),
        )
        parts.append(block * cosines + partner * sines)
    return jnp.concatenate(parts, axis=1)


def pair_columns(width):
    return [start for start in range(0, width, 2 * LANES)]


def half_specs(halves, columns):
    return [
        pl.BlockSpec((1, array.shape[1], columns), lambda i, place=place: (place, 0, 0))
        for array, place in halves
    ]


def qkv_forward(stream, gain, halves, cosines, sines, columns):
    rows, model = stream.shape
    queries, kv = columns

    def body(stream_ref, gain_ref, mine_ref, other_ref, cos_ref, sin_ref, q_ref, kv_ref, n_ref):
        values = stream_ref[...]
        scale = lax.rsqrt(jnp.mean(values * values, axis=1, keepdims=True) + EPSILON)
        n_ref[...] = (values * scale * gain_ref[...]).astype(BF16)
        cos, sin = cos_ref[...], sin_ref[...]
        for index, ref in enumerate((mine_ref, other_ref)):
            raw = dot_nn(n_ref[...], ref[0])
            q_ref[:, index * queries : (index + 1) * queries] = turned(
                raw[:, :queries], cos, sin
            ).astype(BF16)
            for start in pair_columns(kv):
                place = index * kv + start
                keys = raw[:, queries + start : queries + start + LANES]
                kv_ref[:, place : place + LANES] = turned(keys, cos, sin).astype(BF16)
                kv_ref[:, place + LANES : place + 2 * LANES] = raw[
                    :, queries + start + LANES : queries + start + 2 * LANES
                ].astype(BF16)

    whole = lambda i: (0, 0)
    return pl.pallas_call(
        body,
        grid=(1,),
        in_specs=[
            pl.BlockSpec((rows, model), whole),
            pl.BlockSpec((1, model), whole),
            *half_specs(halves, queries + kv),
            pl.BlockSpec((rows, LANES), whole),
            pl.BlockSpec((rows, LANES), whole),
        ],
        out_specs=[
            pl.BlockSpec((rows, 2 * queries), whole),
            pl.BlockSpec((rows, 2 * kv), whole),
            pl.BlockSpec((rows, model), whole),
        ],
        out_shape=[
            jax.ShapeDtypeStruct((rows, 2 * queries), BF16),
            jax.ShapeDtypeStruct((rows, 2 * kv), BF16),
            jax.ShapeDtypeStruct((rows, model), BF16),
        ],
        compiler_params=pltpu.CompilerParams(vmem_limit_bytes=VMEM_LIMIT),
        cost_estimate=lasting(7),
        name="qkv_forward",
    )(stream, gain, *[array for array, _ in halves], cosines, sines)


def qkv_backward(
    normed, d_queries, d_kv_slots, halves, cosines, sines, columns, stream, side, owns, extra
):
    rows, model = normed.shape
    queries, kv = columns
    qkv = queries + kv
    count = len(d_kv_slots)
    more = extra[0].shape[1] if extra else 0

    def body(n_ref, dq_ref, *refs):
        slots = refs[:count]
        mine_ref, other_ref, cos_ref, sin_ref, stream_ref, side_ref, owns_ref = refs[
            count : count + 7
        ]
        extra_refs = refs[count + 7 : count + 7 + len(extra)]
        out_ref, grad_ref, n_t = refs[count + 7 + len(extra) :]
        cos, sin = cos_ref[...], -sin_ref[...]
        n_t[...] = n_ref[...].T
        for index, ref in ((0, mine_ref), (1, other_ref)):
            span = slice(index * kv, (index + 1) * kv)
            d_kv = slots[0][:, span].astype(F32)
            for slot in slots[1:]:
                d_kv = d_kv + slot[:, span].astype(F32)
            parts = [dq_ref[:, index * queries : (index + 1) * queries]]
            for start in pair_columns(kv):
                parts.append(turned(d_kv[:, start : start + LANES], cos, sin).astype(BF16))
                parts.append(d_kv[:, start + LANES : start + 2 * LANES].astype(BF16))
            d_raw = jnp.concatenate(parts, axis=1)
            back = dot_nt(d_raw, ref[0])
            if index == 0:
                out_ref[...] = back
            else:
                out_ref[...] += back
            grad_ref[index, :, :qkv] = dot_nn(n_t[...], d_raw).astype(BF16)
        values = stream_ref[...]
        scale = lax.rsqrt(jnp.mean(values * values, axis=1, keepdims=True) + EPSILON)
        gain = jnp.sum(out_ref[...] * values * scale, axis=0, keepdims=True)
        gain = jnp.broadcast_to(gain, (LANES, model)).T
        lane = lax.broadcasted_iota(jnp.int32, (model, LANES), 1)
        whole_side = jnp.where(lane == 0, gain, side_ref[...])
        for index in range(2):
            grad_ref[index, :, qkv : qkv + LANES] = (
                whole_side * owns_ref[index : index + 1, :]
            ).astype(BF16)
            if extra:
                grad_ref[index, :, qkv + LANES :] = extra_refs[index][...]

    whole = lambda i: (0, 0)
    return pl.pallas_call(
        body,
        grid=(1,),
        in_specs=[
            pl.BlockSpec((rows, model), whole),
            pl.BlockSpec((rows, 2 * queries), whole),
        ]
        + [pl.BlockSpec((rows, 2 * kv), whole)] * count
        + half_specs(halves, qkv)
        + [
            pl.BlockSpec((rows, LANES), whole),
            pl.BlockSpec((rows, LANES), whole),
            pl.BlockSpec((rows, model), whole),
            pl.BlockSpec((model, LANES), whole),
            pl.BlockSpec((8, LANES), whole),
        ]
        + [pl.BlockSpec((model, more), whole) for _ in extra],
        out_specs=[
            pl.BlockSpec((rows, model), whole),
            pl.BlockSpec((2, model, qkv + LANES + more), lambda i: (0, 0, 0)),
        ],
        out_shape=[
            jax.ShapeDtypeStruct((rows, model), F32),
            jax.ShapeDtypeStruct((2, model, qkv + LANES + more), BF16),
        ],
        scratch_shapes=[pltpu.VMEM((model, rows), BF16)],
        compiler_params=pltpu.CompilerParams(vmem_limit_bytes=VMEM_LIMIT),
        cost_estimate=lasting(14),
        name="qkv_backward",
    )(
        normed,
        d_queries,
        *d_kv_slots,
        *[array for array, _ in halves],
        cosines,
        sines,
        stream,
        side,
        owns,
        *extra,
    )


def head_sides(block):
    lane = lax.broadcasted_iota(jnp.int32, block.shape, 1)
    low = lane < HEAD
    crossed = jnp.concatenate([block[:, HEAD:], block[:, :HEAD]], axis=1)
    nothing = jnp.zeros_like(block)
    return [
        [jnp.where(low, block, nothing), jnp.where(low, nothing, crossed)],
        [jnp.where(low, crossed, nothing), jnp.where(low, nothing, block)],
    ]


def fill_bias(bias, owner_ref, seg_all_ref, seg_ref, rows, count):
    own = owner_ref[0] * rows + lax.broadcasted_iota(jnp.int32, (rows, rows), 1)
    for slot in range(count):
        span = slice(slot * rows, (slot + 1) * rows)
        place = owner_ref[slot] * rows + lax.broadcasted_iota(jnp.int32, (rows, rows), 0)
        allowed = (place <= own) & (seg_all_ref[span, :1] == seg_ref[:1, :])
        bias[span, :] = jnp.where(allowed, 0.0, NEGATIVE)


def attention_specs(rows, count, group):
    whole = lambda p, *_: (0, 0)
    return (
        [
            pl.BlockSpec((count * rows, LANES), whole),
            pl.BlockSpec((8, rows), whole),
            pl.BlockSpec((rows, 2 * group * HEAD), lambda p, *_: (0, p)),
        ]
        + [pl.BlockSpec((rows, 2 * LANES), lambda p, *_: (0, p))] * count
    )


def attention_forward(queries, kv_slots, owners, seg_all, seg_own):
    rows, width = queries.shape
    count = len(kv_slots)
    group = HEADS // KV_HEADS
    pairs = KV_HEADS // 2
    heads = 2 * group
    total = count * rows
    scale = 1.0 / math.sqrt(HEAD)

    def body(owner_ref, seg_all_ref, seg_ref, q_ref, *refs):
        slots = refs[:count]
        out_ref, stat_ref, bias = refs[count:]

        @pl.when(pl.program_id(0) == 0)
        def _():
            fill_bias(bias, owner_ref, seg_all_ref, seg_ref, rows, count)

        keys = head_sides(jnp.concatenate([ref[:, :LANES] for ref in slots], axis=0))
        values = head_sides(jnp.concatenate([ref[:, LANES:] for ref in slots], axis=0))
        values = [[side.T for side in sides] for sides in values]
        scaled = (q_ref[...].astype(F32) * scale).astype(BF16)
        stats = []
        for block in range(group):
            out = None
            for side in range(2):
                head = 2 * block + side
                kv = head // group
                scores = (
                    dot_nt(keys[kv][side], scaled[:, block * LANES : (block + 1) * LANES])
                    + bias[...]
                )
                top = jnp.max(scores, axis=0, keepdims=True)
                exponent = jnp.exp(scores - top)
                total_of = jnp.sum(exponent, axis=0, keepdims=True)
                probs = (exponent * (1.0 / total_of)).astype(BF16)
                part = dot_nn(values[kv][side], probs)
                out = part if out is None else out + part
                stats.append(top + jnp.log(total_of))
            out_ref[:, block * LANES : (block + 1) * LANES] = out.T.astype(BF16)
        stat_ref[0, :heads, :] = jnp.concatenate(stats, axis=0)

    return pl.pallas_call(
        body,
        grid_spec=pltpu.PrefetchScalarGridSpec(
            num_scalar_prefetch=1,
            grid=(pairs,),
            in_specs=attention_specs(rows, count, group),
            out_specs=[
                pl.BlockSpec((rows, heads * HEAD), lambda p, *_: (0, p)),
                pl.BlockSpec((1, 8, rows), lambda p, *_: (p, 0, 0)),
            ],
            scratch_shapes=[pltpu.VMEM((total, rows), F32)],
        ),
        out_shape=[
            jax.ShapeDtypeStruct((rows, width), BF16),
            jax.ShapeDtypeStruct((pairs, 8, rows), F32),
        ],
        compiler_params=pltpu.CompilerParams(vmem_limit_bytes=VMEM_LIMIT),
        cost_estimate=lasting(17),
        name="attention_forward",
    )(owners, seg_all, seg_own, queries, *kv_slots)


def attention_backward(queries, kv_slots, owners, seg_all, seg_own, d_out, stats, cosines, sines):
    rows, width = queries.shape
    count = len(kv_slots)
    group = HEADS // KV_HEADS
    pairs = KV_HEADS // 2
    heads = 2 * group
    total = count * rows
    scale = 1.0 / math.sqrt(HEAD)

    def body(owner_ref, seg_all_ref, seg_ref, q_ref, *refs):
        slots = refs[:count]
        d_out_ref, stat_ref, cos_ref, sin_ref = refs[count : count + 4]
        d_q_ref = refs[count + 4]
        d_slots = refs[count + 5 : 2 * count + 5]
        bias, d_keys, d_values = refs[2 * count + 5 :]

        @pl.when(pl.program_id(0) == 0)
        def _():
            fill_bias(bias, owner_ref, seg_all_ref, seg_ref, rows, count)

        keys = head_sides(jnp.concatenate([ref[:, :LANES] for ref in slots], axis=0))
        values = head_sides(jnp.concatenate([ref[:, LANES:] for ref in slots], axis=0))
        keys_t = [[side.T for side in sides] for sides in keys]
        cos, sin = cos_ref[...], -sin_ref[...]
        for block in range(group):
            span = slice(block * LANES, (block + 1) * LANES)
            scaled = (q_ref[:, span].astype(F32) * scale).astype(BF16)
            d_block = d_out_ref[:, span]
            q_sides = head_sides(scaled)
            d_sides = head_sides(d_block)
            d_q = None
            for side in range(2):
                head = 2 * block + side
                kv = head // group
                scores = dot_nt(keys[kv][side], scaled) + bias[...]
                probs = jnp.exp(scores - stat_ref[0, head : head + 1, :])
                d_probs = dot_nt(values[kv][side], d_block)
                share = jnp.sum(probs * d_probs, axis=0, keepdims=True)
                d_scores = (probs * (d_probs - share)).astype(BF16)
                part = dot_nn(keys_t[kv][side], d_scores)
                d_q = part if d_q is None else d_q + part
                d_key = dot_nn(d_scores, q_sides[side][kv])
                d_value = dot_nn(probs.astype(BF16), d_sides[side][kv])
                if head == 0:
                    d_keys[...] = d_key
                    d_values[...] = d_value
                else:
                    d_keys[...] += d_key
                    d_values[...] += d_value
            d_q_ref[:, span] = turned(d_q.T * scale, cos, sin).astype(BF16)
        for slot in range(count):
            part = slice(slot * rows, (slot + 1) * rows)
            d_slots[slot][:, :LANES] = d_keys[part, :].astype(BF16)
            d_slots[slot][:, LANES:] = d_values[part, :].astype(BF16)

    whole = lambda p, *_: (0, 0)
    return pl.pallas_call(
        body,
        grid_spec=pltpu.PrefetchScalarGridSpec(
            num_scalar_prefetch=1,
            grid=(pairs,),
            in_specs=attention_specs(rows, count, group)
            + [
                pl.BlockSpec((rows, heads * HEAD), lambda p, *_: (0, p)),
                pl.BlockSpec((1, 8, rows), lambda p, *_: (p, 0, 0)),
                pl.BlockSpec((rows, LANES), whole),
                pl.BlockSpec((rows, LANES), whole),
            ],
            out_specs=[pl.BlockSpec((rows, heads * HEAD), lambda p, *_: (0, p))]
            + [pl.BlockSpec((rows, 2 * LANES), lambda p, *_: (0, p))] * count,
            scratch_shapes=[
                pltpu.VMEM((total, rows), F32),
                pltpu.VMEM((total, LANES), F32),
                pltpu.VMEM((total, LANES), F32),
            ],
        ),
        out_shape=[jax.ShapeDtypeStruct((rows, width), BF16)]
        + [jax.ShapeDtypeStruct((rows, 2 * KV_HEADS * HEAD), BF16)] * count,
        compiler_params=pltpu.CompilerParams(vmem_limit_bytes=VMEM_LIMIT),
        cost_estimate=lasting(27),
        name="attention_backward",
    )(owners, seg_all, seg_own, queries, *kv_slots, d_out, stats, cosines, sines)


def on_device(
    inputs,
    cotangent,
    segments,
    routes,
    attn_gain,
    w_query,
    w_key,
    w_value,
    w_output,
    ffn_gain,
    router,
    w_gate,
    w_up,
    w_down,
):
    core = lax.axis_index("section")
    shard = lax.axis_index("shard")
    plane = lax.axis_index("expert")
    shards = lax.axis_size("shard")
    planes = lax.axis_size("expert")
    span_rows, model = inputs.shape[2:]
    seq_rows = span_rows * shards
    gathered_rows = span_rows * planes
    local_experts = w_gate.shape[1]
    all_experts = local_experts * planes
    hidden = w_gate.shape[3]
    half_hidden = hidden // 2
    part_rows = w_query.shape[1]
    query_width = HEADS * HEAD
    kv_width = KV_HEADS * HEAD
    group_size = HEADS // KV_HEADS
    score_scale = 1.0 / math.sqrt(HEAD)
    first = core == 0

    def mine_of(array):
        return lax.dynamic_index_in_dim(array, core, 0, keepdims=False)

    def by_layer(own, received):
        return [jnp.where(first, own, received), jnp.where(first, received, own)]

    def halved(own_halves):
        kept = jnp.where(first, own_halves[0], own_halves[1])
        sent = jnp.where(first, own_halves[1], own_halves[0])
        return by_layer(kept, swap(sent))

    misc = jnp.concatenate(
        [
            attn_gain[0][:, None],
            ffn_gain[0][:, None],
            router[0],
            jnp.zeros((part_rows, LANES - 2 - all_experts), BF16),
        ],
        axis=1,
    )
    half_query = query_width // 2
    half_kv = kv_width // 2
    half_qkv = half_query + 2 * half_kv

    def head_half(index, side):
        return jnp.concatenate(
            [
                w_query[0][:, index * half_query : (index + 1) * half_query],
            ]
            + [
                array[0][:, start : start + LANES]
                for start in range(index * half_kv, (index + 1) * half_kv, LANES)
                for array in (w_key, w_value)
            ]
            + [side],
            axis=1,
        )

    output_half = model // 2
    qkv_mine = halved([head_half(0, misc), head_half(1, jnp.zeros_like(misc))])
    output_mine = halved([w_output[0][:, :output_half], w_output[0][:, output_half:]])
    down_turned = jnp.swapaxes(w_down[0], 1, 2)

    def expert_half(start):
        stop = start + half_hidden
        return jnp.concatenate(
            [w_gate[0][:, :, start:stop], w_up[0][:, :, start:stop], down_turned[:, :, start:stop]],
            axis=2,
        )

    expert_mine = halved([expert_half(0), expert_half(half_hidden)])

    plane_order = jnp.stack(
        [lax.rem(plane - k + planes, planes) for k in range(planes)]
    ).astype(jnp.int32)

    segment_local = mine_of(segments)[0]
    segment_all = jnp.concatenate(
        [slot[0] for slot in slots_of(segment_local[None], "shard")]
    )
    own_routes = routes[0, :, 0]
    route_rows = by_layer(
        lax.dynamic_index_in_dim(own_routes, core, 0, keepdims=False),
        swap(lax.dynamic_index_in_dim(own_routes, 1 - core, 0, keepdims=False)),
    )
    expert_ids = jnp.arange(all_experts, dtype=jnp.int32)
    chosen = jnp.stack(
        [
            jnp.any(rows[:, :, None] == expert_ids[None, None, :], axis=1).astype(BF16)
            for rows in route_rows
        ]
    )
    chosen_all = jnp.concatenate(slots_of(jnp.swapaxes(chosen, 1, 2), "expert"), axis=2)

    def dense_weights(lined, *held):
        pieces, first_step = ring_gather(lined, 0, held)
        owners = jnp.stack([owner for _, owner, _ in pieces]).astype(jnp.int32)
        mine = line_up(pieces, owners, plane_order, shards)
        return (mine, swap(mine)), [piece for piece, _, _ in pieces[-2:]]

    lined = jnp.stack(slots_of(qkv_mine[0], "expert"))
    lined = after(lined, chosen_all, segment_all)
    lined_output = jnp.stack(slots_of(after(output_mine[0], lined), "expert"))
    first_qkv, ring_end = dense_weights(lined)
    first_experts = lax.all_gather(
        after(expert_mine[0], *ring_end), ("section", "shard"), axis=0
    )
    second_pack = lax.all_gather(
        jnp.concatenate([qkv_mine[1], output_mine[1]], axis=1),
        ("section", "expert", "shard"),
        axis=0,
        tiled=True,
    ).reshape(2, model, half_qkv + LANES + output_half)
    second_experts = lax.all_gather(expert_mine[1], ("section", "shard"), axis=0)

    qkv_columns = half_qkv + LANES

    def natural(halves, relative):
        mine, other = halves
        if not relative:
            return jnp.concatenate([mine, other], axis=1)
        return jnp.concatenate(
            [jnp.where(first, mine, other), jnp.where(first, other, mine)], axis=1
        )

    def parted(array, relative):
        half = array.shape[1] // 2
        low, high = array[:, :half], array[:, half:]
        if not relative:
            return low, high
        return jnp.where(first, low, high), jnp.where(first, high, low)

    positions = shard * span_rows + jnp.arange(span_rows, dtype=jnp.int32)
    cosines, sines = rotary_tables(positions)
    key_owners = jnp.stack(
        [lax.rem(shard - k + shards, shards) for k in range(shards)]
    ).astype(jnp.int32)
    seg_all = jnp.broadcast_to(segment_all[:, None], (seq_rows, LANES))
    seg_own = jnp.broadcast_to(segment_local[None, :], (8, span_rows))
    chosen_all = jnp.swapaxes(chosen_all, 1, 2) > 0.5

    last = mine_of(cotangent)[0]

    def attend(stream, pair, side, relative):
        gain_one = side[:, 0].astype(F32)
        gain_two = side[:, 1].astype(F32)
        query_rot, kv_own, normed = qkv_forward(
            stream, gain_one[None], pair, cosines, sines, (half_query, 2 * half_kv)
        )
        kv_slots = slots_of(kv_own, "shard")
        attended, stats = attention_forward(query_rot, kv_slots, key_owners, seg_all, seg_own)
        kept = dict(
            stream=stream,
            normed=normed,
            query_rot=query_rot,
            kv_slots=kv_slots,
            stats=stats,
            gain_one=gain_one,
            gain_two=gain_two,
            router_full=side[:, 2 : 2 + all_experts],
            qkv=pair,
            relative=relative,
        )
        return attended, kept

    def gathered_rows_of(kept, attended, pair):
        relative = kept["relative"]
        attended = natural(
            (attended[:, : query_width // 2], attended[:, query_width // 2 :]), relative
        )
        middle = kept["stream"] + natural([dot_nn(attended, half) for half in pair], relative)
        scale_two = lax.rsqrt(jnp.mean(middle * middle, axis=-1, keepdims=True) + EPSILON)
        hidden_in = (middle * scale_two * kept["gain_two"]).astype(BF16)
        rows = jnp.concatenate(slots_of(hidden_in, "expert"), axis=0)
        kept.update(
            attended=attended, middle=middle, scale_two=scale_two, hidden_in=hidden_in, output=pair
        )
        return rows

    def mix(layer, kept, rows, experts):
        logits = jnp.where(chosen_all[layer], dot_nn(rows, kept["router_full"]), NEGATIVE)
        gates = jax.nn.softmax(logits, axis=-1)
        gates = jnp.where(chosen_all[layer], gates, 0.0)
        own_gates = lax.dynamic_slice_in_dim(gates, plane * local_experts, local_experts, axis=1)
        own_gates = jnp.pad(own_gates, ((0, 0), (0, LANES - local_experts)))
        partial, raws = moe_forward(rows, own_gates, experts)
        kept.update(
            rows=rows,
            gates=gates[:span_rows],
            own_gates=own_gates,
            raws=raws,
            experts=experts,
            partial=partial,
        )
        return partial

    def combine(kept, partial):
        combined = partial[:span_rows].astype(F32)
        for k in range(1, planes):
            back = shifted(partial[k * span_rows : (k + 1) * span_rows], "expert", -k)
            combined = combined + back.astype(F32)
        return (kept["middle"] + combined).astype(BF16)

    def backward(layer, kept, grad_rows, later):
        grad_low = grad_rows[:span_rows]
        grad_out = grad_low.astype(F32)
        relative = kept["relative"]
        d_rows, scores, d_raws, acts = moe_backward_rows(
            grad_rows, kept["own_gates"], kept["raws"], kept["experts"]
        )
        scores_turned = scores.T[: max(8, local_experts)]
        d_hidden = d_rows[:span_rows].astype(F32)
        d_gates = jnp.zeros((all_experts, span_rows), F32)
        d_gates = lax.dynamic_update_slice(
            d_gates, scores_turned[:local_experts, :span_rows], (plane * local_experts, 0)
        )
        for k in range(1, planes):
            span = slice(k * span_rows, (k + 1) * span_rows)
            d_hidden = d_hidden + shifted(d_rows[span], "expert", -k).astype(F32)
            back = shifted(scores_turned[:, span], "expert", -k)
            place = lax.rem(plane + k, planes) * local_experts
            d_gates = lax.dynamic_update_slice(d_gates, back[:local_experts], (place, 0))
        expert_grads = moe_backward_weights(kept["rows"], grad_rows, d_raws, acts, 2 * shards)
        d_hidden = after(d_hidden, expert_grads)
        scattered = lax.psum_scatter(
            expert_grads, ("section", "shard"), scatter_dimension=0
        )
        gates = kept["gates"]
        d_gates = d_gates.T
        d_logits = gates * (d_gates - jnp.sum(gates * d_gates, axis=-1, keepdims=True))
        d_logits_high = d_logits.astype(BF16)
        d_logits_low = (d_logits - d_logits_high.astype(F32)).astype(BF16)
        d_hidden = (
            d_hidden
            + dot_nt(d_logits_high, kept["router_full"])
            + dot_nt(d_logits_low, kept["router_full"])
        )
        grad_router = dot_tn(kept["hidden_in"], d_logits_high) + dot_tn(
            kept["hidden_in"], d_logits_low
        )
        d_middle, grad_gain_two = norm_back(
            d_hidden, kept["middle"], kept["scale_two"], kept["gain_two"]
        )
        d_middle = grad_out + d_middle
        d_branch = d_middle.astype(BF16)
        branch_parts = parted(d_branch, relative)
        d_attended = (
            dot_nt(branch_parts[0], kept["output"][0])
            + dot_nt(branch_parts[1], kept["output"][1])
        ).astype(BF16)
        d_attended = jnp.concatenate(parted(d_attended, relative), axis=1)
        grad_output = [dot_tn(kept["attended"], part).astype(BF16) for part in branch_parts]
        d_query_raw, *d_slots = attention_backward(
            kept["query_rot"],
            kept["kv_slots"],
            key_owners,
            seg_all,
            seg_own,
            d_attended,
            kept["stats"],
            cosines,
            sines,
        )
        d_kv_slots = [d_slots[0]] + [
            shifted(d_slots[k], "shard", -k) for k in range(1, shards)
        ]
        if layer == 1:
            result = combine(kept, after(kept["partial"], d_hidden))
            d_query_raw = after(d_query_raw, result)
        else:
            result = None
            d_query_raw = after(d_query_raw, later)
        lane = jnp.arange(LANES)[None, :]
        grad_side = jnp.where(
            lane == 1,
            grad_gain_two[:, None],
            jnp.pad(grad_router, ((0, 0), (2, LANES - 2 - all_experts))),
        )
        owner = core if relative else 0
        owns = jnp.broadcast_to(
            (jnp.arange(8, dtype=jnp.int32) == owner).astype(F32)[:, None], (8, LANES)
        )
        stream = kept["stream"]
        d_normed, packed = qkv_backward(
            kept["normed"],
            d_query_raw,
            d_kv_slots,
            kept["qkv"],
            cosines,
            sines,
            (half_query, 2 * half_kv),
            stream,
            grad_side,
            owns,
            grad_output if layer == 1 else [],
        )
        scale_one = lax.rsqrt(jnp.mean(stream * stream, axis=-1, keepdims=True) + EPSILON)
        d_stream, _ = norm_back(d_normed, stream, scale_one, kept["gain_one"])
        d_stream = (d_middle + d_stream).astype(BF16)
        return d_stream, scattered, packed, grad_output, result

    def dense_scatter(halves, swapped, *held):
        width = halves[0].shape[1]
        size = (planes, shards, part_rows, width)
        kept = halves[0].reshape(size)
        received = swapped.reshape(size)
        if held:
            received = after(received, *held)

        def chunk(owner, start, stop):
            place = (start, owner, 0, 0)
            part = (stop - start, 1, part_rows, width)
            summed = lax.dynamic_slice(kept, place, part).astype(F32) + lax.dynamic_slice(
                received, place, part
            ).astype(F32)
            return summed[:, 0].astype(BF16)

        if shards == 4:
            middle = planes // 2
            chunks = [
                chunk(shard, 0, planes),
                chunk(shard ^ 1, 0, planes),
                chunk(shard ^ 2, 0, planes),
                chunk(shard ^ 3, 0, middle),
                chunk(shard ^ 3, middle, planes),
            ]
        else:
            chunks = [
                chunk(lax.rem(shard - k + shards, shards), 0, planes) for k in range(shards)
            ]
        first_step = scatter_first(chunks, 0)
        second_step = scatter_second(chunks, first_step, 0)
        lined = scatter_end(chunks, first_step, second_step, 0)
        return {"first": first_step, "second": second_step, "lined": lined}

    def plane_scatter(lined):
        total = lax.dynamic_index_in_dim(lined, plane, 0, keepdims=False)
        for k in range(1, planes):
            sent = lax.dynamic_index_in_dim(
                lined, lax.rem(plane - k + planes, planes), 0, keepdims=False
            )
            total = total + shifted(sent.astype(BF16), "expert", -k).astype(F32)
        return total

    def regrouped(halves):
        kept = jnp.where(first, halves[0], halves[1])
        sent = jnp.where(first, halves[1], halves[0])
        received = swap(sent.astype(BF16)).astype(F32)
        return by_layer(kept, received)

    start = mine_of(inputs)[0]
    side = jnp.where(
        first, first_qkv[0][:, half_qkv:qkv_columns], first_qkv[1][:, half_qkv:qkv_columns]
    )
    attended, kept_one = attend(
        start.astype(F32), [(half[None], 0) for half in first_qkv], side, True
    )
    first_output, _ = dense_weights(after(lined_output, *ring_end), kept_one["query_rot"])
    rows = gathered_rows_of(kept_one, attended, first_output)
    result_one = combine(kept_one, mix(0, kept_one, rows, first_experts))

    last_rows = jnp.concatenate(slots_of(after(last, result_one), "expert"), axis=0)
    attended, kept_two = attend(
        result_one.astype(F32),
        [(second_pack, 0), (second_pack, 1)],
        second_pack[0, :, half_qkv:qkv_columns],
        False,
    )
    attended = after(attended, last_rows)
    rows = gathered_rows_of(kept_two, attended, [half[:, qkv_columns:] for half in second_pack])
    mix(1, kept_two, rows, second_experts)

    grad_mid, scattered_two, packed_two, _, result_two = backward(1, kept_two, last_rows, None)
    pack_two = lax.psum_scatter(
        packed_two.reshape(2 * model, packed_two.shape[2]),
        ("section", "expert", "shard"),
        scatter_dimension=0,
        tiled=True,
    )
    mid_rows = jnp.concatenate(slots_of(grad_mid, "expert"), axis=0)
    mid_rows = after(mid_rows, scattered_two)
    grad_start, scattered_one, packed_one, output_one, _ = backward(
        0, kept_one, mid_rows, pack_two
    )
    qkv_one = [packed_one[0], packed_one[1]]

    def placed(by_layers):
        own = jnp.where(first, by_layers[0], by_layers[1])
        sent = jnp.where(first, by_layers[1], by_layers[0])
        return jnp.stack(by_layer(own, swap(sent)))

    layer_local = placed([result_one, result_two])
    input_local = placed([grad_start, grad_mid])
    expert_low, expert_high = regrouped([scattered_one, scattered_two])
    output_scatter = dense_scatter(output_one, swap(output_one[1]))
    qkv_scatter = dense_scatter(qkv_one, swap(qkv_one[1]))
    dense_one = jnp.concatenate(
        [plane_scatter(qkv_scatter["lined"]), plane_scatter(output_scatter["lined"])], axis=1
    )
    dense_low, dense_high = regrouped([dense_one, pack_two.astype(F32)])

    def both(start, stop):
        return jnp.concatenate([dense_low[:, start:stop], dense_high[:, start:stop]], axis=1)

    def every_other(start):
        return jnp.concatenate(
            [
                half[:, place : place + LANES]
                for half in (dense_low, dense_high)
                for place in range(start, half_qkv, 2 * LANES)
            ],
            axis=1,
        )

    side = dense_low[:, half_qkv:qkv_columns]

    def third(index):
        start = index * half_hidden
        stop = start + half_hidden
        return jnp.concatenate([expert_low[:, :, start:stop], expert_high[:, :, start:stop]], axis=2)

    out_shape = (1, 2, 1, span_rows, model)
    return (
        layer_local.reshape(out_shape),
        input_local.reshape(out_shape),
        side[:, 0][None],
        both(0, half_query)[None],
        every_other(half_query)[None],
        every_other(half_query + LANES)[None],
        both(qkv_columns, qkv_columns + output_half)[None],
        side[:, 1][None],
        side[:, 2 : 2 + all_experts][None],
        third(0)[None],
        third(1)[None],
        jnp.swapaxes(third(2), 1, 2)[None],
    )


def solution(mesh):
    placed = (
        P(None, "expert", "shard", None),
        P(None, "expert", "shard", None),
        P(None, "expert", "shard"),
        P("section", None, "expert", "shard", None),
        P("section", ("expert", "shard")),
        P("section", ("expert", "shard"), None),
        P("section", ("expert", "shard"), None),
        P("section", ("expert", "shard"), None),
        P("section", ("expert", "shard"), None),
        P("section", ("expert", "shard")),
        P("section", ("expert", "shard"), None),
        P("section", "expert", "shard", None),
        P("section", "expert", "shard", None),
        P("section", "expert", None, "shard"),
    )
    return jax.shard_map(
        on_device,
        mesh=mesh,
        in_specs=placed,
        out_specs=(
            P("section", None, "expert", "shard", None),
            P("section", None, "expert", "shard", None),
            P("section", ("expert", "shard")),
            P("section", ("expert", "shard"), None),
            P("section", ("expert", "shard"), None),
            P("section", ("expert", "shard"), None),
            P("section", ("expert", "shard"), None),
            P("section", ("expert", "shard")),
            P("section", ("expert", "shard"), None),
            P("section", "expert", "shard", None),
            P("section", "expert", "shard", None),
            P("section", "expert", None, "shard"),
        ),
        check_vma=False,
    )
```

time: 1980 us -> 1520 us (0.77)
  starting transfers between devices: 277 us -> 103 us
  matrix products: 190 us -> 33.9 us
  local copies, waits for them, and re-layouts: 217 us -> 83.3 us
  Pallas kernels: 249 us -> 380 us
  other arithmetic: 214 us -> 87 us
    ppermute x60 -> x20, waiting for transfers between devices: 363 us -> 133 us  [flipped(): lax.ppermute(array, 'shard', [(i, i ^ mask) for i in range(lax.axis_size(...]
    ppermute x72 -> x60, waiting for transfers between devices: 452 us -> 620 us  [shifted(): lax.ppermute(array, axis, [(i, (i + by) % length) for i in range(length)])]
    pallas_call x0 -> x10, Pallas kernels: none -> 144 us  [the longest x2 53.3 us: attention_backward(): pl.pallas_call(body, grid_spec=pltpu.PrefetchScalarGridSpec(num_scalar_pr...]
    ppermute x53 -> x12, starting transfers between devices: 124 us -> 21.9 us  [swap(): return lax.ppermute(array, 'section', [(0, 1), (1, 0)])]
    dot_general x10 -> x0, matrix products: 96.6 us -> none  [the longest x2 33 us: backward(): jnp.einsum('cngd,knd->cngk', d_weighted, value_heads, preferred_element_t...]
    convert_element_type x27 -> x20, other arithmetic: 93.9 us -> 20.2 us  [the longest x4 6.83 us: chunk(): return summed[:, 0].astype(BF16)]
    ppermute x60 -> x20, starting transfers between devices: 63.8 us -> 12.5 us  [flipped(): lax.ppermute(array, 'shard', [(i, i ^ mask) for i in range(lax.axis_size(...]
    dynamic_update_slice x55 -> x0, local copies, waits for them, and re-layouts: 43.9 us -> none  [the longest x20 20.5 us: dense_weights(): lax.dynamic_update_slice(result, piece[:, None], (start, owner, 0, core *...]
  transfers between devices with their start and end apart: 185 -> 98, of which waited for: 66 -> 57; matrix products, arithmetic and copies ran while one was open for 29% -> 10% of each run, Pallas kernels for 8% -> 17%
where the time goes in v2:
time: 1520 us; the launch traced here: 1510 us
  waiting for transfers between devices  811 us (53%)
  Pallas kernels  380 us (25%)
  starting transfers between devices  103 us (7%)
  other arithmetic  87 us (6%)
  local copies, waits for them, and re-layouts  83.3 us (5%)
  matrix products  33.9 us (2%)
  between operations  16 us (1%)
    ppermute x60, waiting for transfers between devices, shifted(): lax.ppermute(array, axis, [(i, (i + by) % length) for i in range(length)])  620 us
    ppermute x20, waiting for transfers between devices, flipped(): lax.ppermute(array, 'shard', [(i, i ^ mask) for i in range(lax.axis_size(...  133 us
    pallas_call x2, Pallas kernels, moe_backward_rows(): pl.pallas_call(body, grid_spec=pltpu.PrefetchScalarGridSpec(num_scalar_pr...  92.9 us
    pallas_call x2, Pallas kernels, moe_forward(): pl.pallas_call(body, grid_spec=pltpu.PrefetchScalarGridSpec(num_scalar_pr...  77.3 us
    ppermute x60, starting transfers between devices, shifted(): lax.ppermute(array, axis, [(i, (i + by) % length) for i in range(length)])  68 us
    pallas_call x2, Pallas kernels, moe_backward_weights(): pl.pallas_call(body, grid_spec=pltpu.PrefetchScalarGridSpec(num_scalar_pr...  66.3 us
    pallas_call x2, Pallas kernels, attention_backward(): pl.pallas_call(body, grid_spec=pltpu.PrefetchScalarGridSpec(num_scalar_pr...  53.3 us
    pallas_call x2, Pallas kernels, attention_forward(): pl.pallas_call(body, grid_spec=pltpu.PrefetchScalarGridSpec(num_scalar_pr...  34.5 us
  transfers between devices with their start and end apart: 98, of which 57 were waited for; matrix products, arithmetic and copies ran while one was open for 10% of the time, Pallas kernels for 17%

profile of v2, /device:TPU:9, one launch (start us, length us, event | category | flops | bytes accessed | tf_op | source)
XLA Modules:
  0.0 1513.8 jit_solution(2715910434313262313)
XLA Ops:
  42.3 15.5 %collective-permute-done.5 = bf16[96,1408]{1,0:T(8,128)(2,1)S(1)} collective-permute-done((bf16[96,1408]{1,0:T(8,128)(2,1)S(1)}, bf16[96,1408]{1,0:T(8,128)(2,1)S(1)}, u32[]{:S(2)}, u32[]{:S(2)}) %collective-permute-start.5) | collective-permute-done | bytes 270368 | tf_op jit(solution)/shard_map/ppermute | solution.py:38
  62.4 23.8 %collective-permute-done.11.refs_1_ = bf16[4,96,1408]{2,1,0:T(8,128)(2,1)S(1)} collective-permute-done((bf16[4,96,1408]{2,1,0:T(8,128)(2,1)S(1)}, bf16[4,96,1408]{2,1,0:T(8,128)(2,1)S(1)}, u32[]{:S(2)}, u32[]{:S(2)}) %collective-permute-start.11) | collective-permute-done | bytes 1081376 | tf_op jit(solution)/shard_map/ppermute | solution.py:42
  90.8 7.2 collective-permute-done.13.refs_3_
  105.7 6.3 line_up.2
  119.1 7.4 collective-permute-done.21
  130.4 7.3 qkv_forward.2
  137.7 17.0 %collective-permute-done.23.refs_1_ = bf16[4,96,768]{2,1,0:T(8,128)(2,1)S(1)} collective-permute-done((bf16[4,96,768]{2,1,0:T(8,128)(2,1)S(1)}, bf16[4,96,768]{2,1,0:T(8,128)(2,1)S(1)}, u32[]{:S(2)}, u32[]{:S(2)}) %collective-permute-start.23) | collective-permute-done | bytes 589856 | tf_op jit(solution)/shard_map/ppermute | solution.py:42
  163.7 4.9 line_up.3
  168.5 8.8 collective-permute-start.27
  178.0 5.6 collective-permute-done.16.refs_1_
  183.6 10.8 collective-permute-done.17.refs_2_
  194.4 12.0 collective-permute-done.18.refs_3_
  207.9 17.2 %attention_forward.2 = (bf16[256,1536]{1,0:T(8,128)(2,1)}, f32[4,8,256]{2,1,0:T(8,128)}) custom-call(s32[4]{0:T(128)} %pad_add_fusion.1.owner_ref, s32[1024,128]{1,0:T(8,128)} %broadcast_in_dim.67.seg_all_ref, s32[8,256]{1,0:T(8,128)} %broadcast_in_dim.68.seg_ref, bf16[256,1536]{1,0:T(8,128)(2,1)} %get-tuple-element.63.q_ref, ...), custom_call_target="tpu_custom_call" | custom-call | flops 18699999232 | bytes 1000000 | tf_op jit(solution)/shard_map/attention_forward/pallas_call | solution.py:683
  239.2 5.9 collective-permute-done.28
  245.1 57.6 %collective-permute-done.29 = bf16[256,1536]{1,0:T(8,128)(2,1)} collective-permute-done((bf16[256,1536]{1,0:T(8,128)(2,1)}, bf16[256,1536]{1,0:T(8,128)(2,1)}, u32[]{:S(2)}, u32[]{:S(2)}) %collective-permute-start.29) | collective-permute-done | bytes 786464 | tf_op jit(solution)/shard_map/ppermute | solution.py:38
  302.7 22.6 %collective-permute-done.30 = bf16[256,1536]{1,0:T(8,128)(2,1)} collective-permute-done((bf16[256,1536]{1,0:T(8,128)(2,1)}, bf16[256,1536]{1,0:T(8,128)(2,1)}, u32[]{:S(2)}, u32[]{:S(2)}) %collective-permute-start.30) | collective-permute-done | bytes 786464 | tf_op jit(solution)/shard_map/ppermute | solution.py:38
  331.5 38.6 %moe_forward.2 = (bf16[1024,1536]{1,0:T(8,128)(2,1)}, bf16[5,1024,1024]{2,1,0:T(8,128)(2,1)}) custom-call(bf16[1024,1536]{1,0:T(8,128)(2,1)} %copy-done.30, f32[1024,128]{1,0:T(8,128)} %pad.14.gates_ref, bf16[8,5,384,768]{3,2,1,0:T(8,128)(2,1)} %bitcast.353), custom_call_target="tpu_custom_call" | custom-call | flops 44000002048 | bytes 1000000 | tf_op jit(solution)/shard_map/moe_forward/pallas_call | solution.py:219
  374.8 33.6 %all-gather.6.cloned.1.call-done = bf16[3072,2176]{1,0:T(8,128)(2,1)} async-done(((bf16[96,2176]{1,0:T(8,128)(2,1)}), bf16[3072,2176]{1,0:T(8,128)(2,1)}) %all-gather.6.cloned.1.call-update) | async-done | bytes 13369360 | tf_op jit(solution)/shard_map/all_gather | solution.py:911
  411.0 14.1 collective-permute-done.33
  425.1 16.9 %collective-permute-done.34 = bf16[256,1536]{1,0:T(8,128)(2,1)} collective-permute-done((bf16[256,1536]{1,0:T(8,128)(2,1)}, bf16[256,1536]{1,0:T(8,128)(2,1)}, u32[]{:S(2)}, u32[]{:S(2)}) %collective-permute-start.34) | collective-permute-done | bytes 786464 | tf_op jit(solution)/shard_map/ppermute | solution.py:38
  445.7 7.3 qkv_forward.3
  460.7 4.0 collective-permute-start.39
  465.6 10.6 collective-permute-done.35.refs_1_
  476.2 10.9 collective-permute-done.36.refs_2_
  487.9 17.3 %attention_forward.3 = (bf16[256,1536]{1,0:T(8,128)(2,1)}, f32[4,8,256]{2,1,0:T(8,128)}) custom-call(s32[4]{0:T(128)} %pad_add_fusion.1.owner_ref, s32[1024,128]{1,0:T(8,128)} %broadcast_in_dim.67.seg_all_ref, s32[8,256]{1,0:T(8,128)} %broadcast_in_dim.68.seg_ref, bf16[256,1536]{1,0:T(8,128)(2,1)} %get-tuple-element.72.q_ref, ...), custom_call_target="tpu_custom_call" | custom-call | flops 18699999232 | bytes 1000000 | tf_op jit(solution)/shard_map/attention_forward/pallas_call | solution.py:683
  506.1 20.4 %collective-permute-done.39 = bf16[256,1536]{1,0:T(8,128)(2,1)S(1)} collective-permute-done((bf16[256,1536]{1,0:T(8,128)(2,1)S(1)}, bf16[256,1536]{1,0:T(8,128)(2,1)S(1)}, u32[]{:S(2)}, u32[]{:S(2)}) %collective-permute-start.39) | collective-permute-done | bytes 786464 | tf_op jit(solution)/shard_map/ppermute | solution.py:38
  527.5 4.2 collective-permute-done.40
  542.6 14.9 collective-permute-done.41
  557.5 48.5 %collective-permute-done.42 = bf16[256,1536]{1,0:T(8,128)(2,1)} collective-permute-done((bf16[256,1536]{1,0:T(8,128)(2,1)S(1)}, bf16[256,1536]{1,0:T(8,128)(2,1)}, u32[]{:S(2)}, u32[]{:S(2)}) %collective-permute-start.42) | collective-permute-done | bytes 786464 | tf_op jit(solution)/shard_map/ppermute | solution.py:38
  612.6 38.7 %moe_forward.3 = (bf16[1024,1536]{1,0:T(8,128)(2,1)}, bf16[5,1024,1024]{2,1,0:T(8,128)(2,1)}) custom-call(bf16[1024,1536]{1,0:T(8,128)(2,1)} %copy-done.31, f32[1024,128]{1,0:T(8,128)} %pad.15.gates_ref, bf16[8,5,384,768]{3,2,1,0:T(8,128)(2,1)} %bitcast.355), custom_call_target="tpu_custom_call" | custom-call | flops 44000002048 | bytes 1000000 | tf_op jit(solution)/shard_map/moe_forward/pallas_call | solution.py:219
  651.3 46.2 %moe_backward_rows.2 = (bf16[1024,1536]{1,0:T(8,128)(2,1)}, f32[1024,128]{1,0:T(8,128)}, bf16[5,1024,1024]{2,1,0:T(8,128)(2,1)}, bf16[5,1024,512]{2,1,0:T(8,128)(2,1)}) custom-call(bf16[1024,1536]{1,0:T(8,128)(2,1)} %constant_dynamic-update-slice_fusion.9.grads_ref, f32[1024,128]{1,0:T(8,128)} %pad.15.gates_ref, ...), custom_call_target="tpu_custom_call" | custom-call | flops 52800000000 | bytes 1000000 | tf_op jit(solution)/shard_map/moe_backward_rows/pallas_call | solution.py:309
  706.8 33.1 %moe_backward_weights.2 = bf16[8,5,384,768]{3,2,1,0:T(8,128)(2,1)} custom-call(bf16[1024,1536]{1,0:T(8,128)(2,1)} %copy-done.31, bf16[1024,1536]{1,0:T(8,128)(2,1)} %constant_dynamic-update-slice_fusion.9.grads_ref, bf16[5,1024,1024]{2,1,0:T(8,128)(2,1)} %get-tuple-element.80.d_raw_ref, bf16[5,1024,512]{2,1,0:T(8,128)(2,1)} %get-tuple-element.81.act_ref), custom_call_target="tpu_custom_call" | custom-call | flops 37399998464 | bytes 1000000 | tf_op jit(solution)/shard_map/moe_backward_weights/pallas_call | solution.py:372
  741.8 36.6 %collective-permute-done.47 = f32[8,256]{0,1:T(8,128)} collective-permute-done((f32[8,256]{0,1:T(8,128)}, f32[8,256]{0,1:T(8,128)}, u32[]{:S(2)}, u32[]{:S(2)}) %collective-permute-start.47) | collective-permute-done | bytes 8224 | tf_op jit(solution)/shard_map/ppermute | solution.py:38
  786.0 9.2 collective-permute-done.46
  808.4 26.6 %attention_backward.2 = (bf16[256,1536]{1,0:T(8,128)(2,1)}, bf16[256,1024]{1,0:T(8,128)(2,1)}, bf16[256,1024]{1,0:T(8,128)(2,1)}, bf16[256,1024]{1,0:T(8,128)(2,1)}, bf16[256,1024]{1,0:T(8,128)(2,1)}) custom-call(s32[4]{0:T(128)} %pad_add_fusion.1.owner_ref, s32[1024,128]{1,0:T(8,128)} %broadcast_in_dim.67.seg_all_ref, s32[8,256]{1,0:T(8,128)} %broadcast_in_dim.68.seg_ref, ...), custom_call_target="tpu_custom_call" | custom-call | flops 29699999744 | bytes 1000000 | tf_op jit(solution)/shard_map/attention_backward/pallas_call | solution.py:761
  842.5 9.9 collective-permute-done.50
  853.5 34.8 %collective-permute-done.51 = bf16[256,1536]{1,0:T(8,128)(2,1)S(1)} collective-permute-done((bf16[256,1536]{1,0:T(8,128)(2,1)S(1)}, bf16[256,1536]{1,0:T(8,128)(2,1)S(1)}, u32[]{:S(2)}, u32[]{:S(2)}) %collective-permute-start.51) | collective-permute-done | bytes 786464 | tf_op jit(solution)/shard_map/ppermute | solution.py:38
  888.3 16.9 %collective-permute-done.52 = bf16[256,1536]{1,0:T(8,128)(2,1)S(1)} collective-permute-done((bf16[256,1536]{1,0:T(8,128)(2,1)S(1)}, bf16[256,1536]{1,0:T(8,128)(2,1)S(1)}, u32[]{:S(2)}, u32[]{:S(2)}) %collective-permute-start.52) | collective-permute-done | bytes 786464 | tf_op jit(solution)/shard_map/ppermute | solution.py:38
  909.7 15.9 %qkv_backward.2 = (f32[256,1536]{1,0:T(8,128)}, bf16[2,1536,2176]{2,1,0:T(8,128)(2,1)}) custom-call(bf16[256,1536]{1,0:T(8,128)(2,1)} %get-tuple-element.85.n_ref, bf16[256,1536]{1,0:T(8,128)(2,1)} %get-tuple-element.88.dq_ref, bf16[256,1024]{1,0:T(8,128)(2,1)} %get-tuple-element.89.refs_0_, bf16[256,1024]{1,0:T(8,128)(2,1)} %copy-done.82, ...), custom_call_target="tpu_custom_call" | custom-call | flops 15399999488 | bytes 1000000 | tf_op jit(solution)/shard_map/qkv_backward/pallas_call | solution.py:567
  933.5 17.0 %collective-permute-done.57 = bf16[256,1536]{1,0:T(8,128)(2,1)S(1)} collective-permute-done((bf16[256,1536]{1,0:T(8,128)(2,1)S(1)}, bf16[256,1536]{1,0:T(8,128)(2,1)S(1)}, u32[]{:S(2)}, u32[]{:S(2)}) %collective-permute-start.57) | collective-permute-done | bytes 786464 | tf_op jit(solution)/shard_map/ppermute | solution.py:38
  950.4 82.3 %collective-permute-done.58 = bf16[256,1536]{1,0:T(8,128)(2,1)S(1)} collective-permute-done((bf16[256,1536]{1,0:T(8,128)(2,1)S(1)}, bf16[256,1536]{1,0:T(8,128)(2,1)S(1)}, u32[]{:S(2)}, u32[]{:S(2)}) %collective-permute-start.58) | collective-permute-done | bytes 786464 | tf_op jit(solution)/shard_map/ppermute | solution.py:38
  1034.5 46.7 %moe_backward_rows.3 = (bf16[1024,1536]{1,0:T(8,128)(2,1)}, f32[1024,128]{1,0:T(8,128)}, bf16[5,1024,1024]{2,1,0:T(8,128)(2,1)}, bf16[5,1024,512]{2,1,0:T(8,128)(2,1)}) custom-call(bf16[1024,1536]{1,0:T(8,128)(2,1)} %pad_maximum_fusion.2.grads_ref, f32[1024,128]{1,0:T(8,128)} %pad.14.gates_ref, bf16[5,1024,1024]{2,1,0:T(8,128)(2,1)} %get-tuple-element.95.raw_ref, ...), custom_call_target="tpu_custom_call" | custom-call | flops 52800000000 | bytes 1000000 | tf_op jit(solution)/shard_map/moe_backward_rows/pallas_call | solution.py:309
  1081.2 33.2 %moe_backward_weights.3 = bf16[8,5,384,768]{3,2,1,0:T(8,128)(2,1)} custom-call(bf16[1024,1536]{1,0:T(8,128)(2,1)} %copy-done.30, bf16[1024,1536]{1,0:T(8,128)(2,1)} %pad_maximum_fusion.2.grads_ref, bf16[5,1024,1024]{2,1,0:T(8,128)(2,1)} %get-tuple-element.97.d_raw_ref, bf16[5,1024,512]{2,1,0:T(8,128)(2,1)} %get-tuple-element.98.act_ref), custom_call_target="tpu_custom_call" | custom-call | flops 37399998464 | bytes 1000000 | tf_op jit(solution)/shard_map/moe_backward_weights/pallas_call | solution.py:372
  1130.8 28.9 %collective-permute-done.65 = f32[8,256]{0,1:T(8,128)S(1)} collective-permute-done((f32[8,256]{0,1:T(8,128)S(1)}, f32[8,256]{0,1:T(8,128)S(1)}, u32[]{:S(2)}, u32[]{:S(2)}) %collective-permute-start.65) | collective-permute-done | bytes 8224 | tf_op jit(solution)/shard_map/ppermute | solution.py:38
  1165.1 15.3 %collective-permute-done.60 = bf16[256,1536]{1,0:T(8,128)(2,1)S(1)} collective-permute-done((bf16[256,1536]{1,0:T(8,128)(2,1)}, bf16[256,1536]{1,0:T(8,128)(2,1)S(1)}, u32[]{:S(2)}, u32[]{:S(2)}) %collective-permute-start.60) | collective-permute-done | bytes 786464 | tf_op jit(solution)/shard_map/ppermute | solution.py:38
  1180.4 16.2 %collective-permute-done.62 = bf16[256,1536]{1,0:T(8,128)(2,1)} collective-permute-done((bf16[256,1536]{1,0:T(8,128)(2,1)S(1)}, bf16[256,1536]{1,0:T(8,128)(2,1)}, u32[]{:S(2)}, u32[]{:S(2)}) %collective-permute-start.62) | collective-permute-done | bytes 786464 | tf_op jit(solution)/shard_map/ppermute | solution.py:38
  1206.0 26.7 %attention_backward.3 = (bf16[256,1536]{1,0:T(8,128)(2,1)}, bf16[256,1024]{1,0:T(8,128)(2,1)}, bf16[256,1024]{1,0:T(8,128)(2,1)}, bf16[256,1024]{1,0:T(8,128)(2,1)}, bf16[256,1024]{1,0:T(8,128)(2,1)}) custom-call(s32[4]{0:T(128)} %pad_add_fusion.1.owner_ref, s32[1024,128]{1,0:T(8,128)} %broadcast_in_dim.67.seg_all_ref, s32[8,256]{1,0:T(8,128)} %broadcast_in_dim.68.seg_ref, ...), custom_call_target="tpu_custom_call" | custom-call | flops 29699999744 | bytes 1000000 | tf_op jit(solution)/shard_map/attention_backward/pallas_call | solution.py:761
  1242.5 16.2 %collective-permute-done.66.refs_1_ = bf16[256,1024]{1,0:T(8,128)(2,1)} collective-permute-done((bf16[256,1024]{1,0:T(8,128)(2,1)}, bf16[256,1024]{1,0:T(8,128)(2,1)}, u32[]{:S(2)}, u32[]{:S(2)}) %collective-permute-start.66) | collective-permute-done | bytes 524320 | tf_op jit(solution)/shard_map/ppermute | solution.py:38
  1261.3 15.4 %collective-permute-done.68.refs_3_ = bf16[256,1024]{1,0:T(8,128)(2,1)} collective-permute-done((bf16[256,1024]{1,0:T(8,128)(2,1)}, bf16[256,1024]{1,0:T(8,128)(2,1)}, u32[]{:S(2)}, u32[]{:S(2)}) %collective-permute-start.68) | collective-permute-done | bytes 524320 | tf_op jit(solution)/shard_map/ppermute | solution.py:38
  1277.4 14.2 qkv_backward.3
  1291.6 10.0 fusion.76
  1307.9 4.9 collective-permute-done.81
  1319.1 9.0 collective-permute-done.82
  1334.1 4.7 collective-permute-done.88
  1349.7 19.9 %collective-permute-done.71 = bf16[2,96,1408]{2,1,0:T(8,128)(2,1)S(1)} collective-permute-done((bf16[2,96,1408]{2,1,0:T(8,128)(2,1)S(1)}, bf16[2,96,1408]{2,1,0:T(8,128)(2,1)S(1)}, u32[]{:S(2)}, u32[]{:S(2)}) %collective-permute-start.71) | collective-permute-done | bytes 540704 | tf_op jit(solution)/shard_map/ppermute | solution.py:42
  1379.1 13.7 collective-permute-done.73
  1392.8 26.7 %collective-permute-done.72 = bf16[2,96,1408]{2,1,0:T(8,128)(2,1)S(1)} collective-permute-done((bf16[2,96,1408]{2,1,0:T(8,128)(2,1)S(1)}, bf16[2,96,1408]{2,1,0:T(8,128)(2,1)S(1)}, u32[]{:S(2)}, u32[]{:S(2)}) %collective-permute-start.72) | collective-permute-done | bytes 540704 | tf_op jit(solution)/shard_map/ppermute | solution.py:42
  1428.9 11.3 collective-permute-done.78
  1440.2 5.8 collective-permute-done.79
  1447.5 22.0 %reduce-scatter.8.cloned.1.call-done = bf16[1,5,384,768]{3,2,1,0:T(8,128)(2,1)} async-done(((bf16[8,5,384,768]{3,2,1,0:T(8,128)(2,1)}), bf16[1,5,384,768]{3,2,1,0:T(8,128)(2,1)}) %reduce-scatter.8.cloned.1.call-update) | async-done | bytes 2949136 | tf_op jit(solution)/shard_map/reduce_scatter | solution.py:1028
  1469.5 4.6 bitcast_select_fusion
  1481.9 4.9 convert_select_fusion.1
  1494.5 5.6 copy.251
  1500.1 4.3 maximum_bitcast_fusion.1
  (533 shorter events, 299.2 us)
Async XLA Ops:
  7.2 324.3 %all-gather.8.cloned.1.call-start = ((), (), s32[]{:S(2)}) async-start(), calls=%async_computation.7 | async-start | bytes 26542080 | tf_op jit(solution)/shard_map/all_gather | solution.py:908
  8.6 19.4 %collective-permute-start = (s32[1,256]{1,0:T(1,128)}, s32[1,256]{1,0:T(1,128)}, u32[]{:S(2)}, u32[]{:S(2)}) collective-permute-start(s32[1,256]{1,0:T(1,128)} %fusion.121), channel_id=1, source_target_pairs={{0,1},{1,2},{2,3},{3,0},{4,5},{5,6},{6,7},{7,4},{8,9},{9,10},{10,1... | collective-permute-start | bytes 3080 | tf_op jit(solution)/shard_map/ppermute | solution.py:38
  9.8 18.7 %collective-permute-start.1 = (s32[1,256]{1,0:T(1,128)}, s32[1,256]{1,0:T(1,128)}, u32[]{:S(2)}, u32[]{:S(2)}) collective-permute-start(s32[1,256]{1,0:T(1,128)} %fusion.121), channel_id=1, source_target_pairs={{0,2},{1,3},{2,0},{3,1},{4,6},{5,7},{6,4},{7,5},{8,10},{9,11},{10,... | collective-permute-start | bytes 3080 | tf_op jit(solution)/shard_map/ppermute | solution.py:38
  28.0 59.5 %collective-permute-start.31 = (bf16[5,384,768]{2,1,0:T(8,128)(2,1)S(1)}, bf16[5,384,768]{2,1,0:T(8,128)(2,1)S(1)}, u32[]{:S(2)}, u32[]{:S(2)}) collective-permute-start(bf16[5,384,768]{2,1,0:T(8,128)(2,1)S(1)} %broadcast_select_fusion.2), channel_id=1, source_target_pairs={{0,16},{16,0},{1,17},{17,1},{2,18},{18,2},{3,19},{19,3},{4,20},{20... | collective-permute-start | bytes 8847368 | tf_op jit(solution)/shard_map/ppermute | solution.py:33
  35.3 22.5 %collective-permute-start.5 = (bf16[96,1408]{1,0:T(8,128)(2,1)S(1)}, bf16[96,1408]{1,0:T(8,128)(2,1)S(1)}, u32[]{:S(2)}, u32[]{:S(2)}) collective-permute-start(bf16[96,1408]{1,0:T(8,128)(2,1)S(1)} %get-tuple-element.281), channel_id=1, source_target_pairs={{0,8},{4,12},{8,0},{12,4},{1,9},{5,13},{9,1},{13,5},{2,10},{6,14},... | collective-permute-start | bytes 811016 | tf_op jit(solution)/shard_map/ppermute | solution.py:38
  38.3 23.3 %collective-permute-start.6 = (bf16[96,1408]{1,0:T(8,128)(2,1)S(1)}, bf16[96,1408]{1,0:T(8,128)(2,1)S(1)}, u32[]{:S(2)}, u32[]{:S(2)}) collective-permute-start(bf16[96,1408]{1,0:T(8,128)(2,1)S(1)} %get-tuple-element.281), channel_id=1, source_target_pairs={{0,12},{4,0},{8,4},{12,8},{1,13},{5,1},{9,5},{13,9},{2,14},{6,2},{... | collective-permute-start | bytes 811016 | tf_op jit(solution)/shard_map/ppermute | solution.py:38
  61.8 24.4 %collective-permute-start.11 = (bf16[4,96,1408]{2,1,0:T(8,128)(2,1)S(1)}, bf16[4,96,1408]{2,1,0:T(8,128)(2,1)S(1)}, u32[]{:S(2)}, u32[]{:S(2)}) collective-permute-start(bf16[4,96,1408]{2,1,0:T(8,128)(2,1)S(1)} %pad_maximum_fusion.5.refs_0_), channel_id=1, source_target_pairs={{0,1},{1,0},{2,3},{3,2},{4,5},{5,4},{6,7},{7,6},{8,9},{9,8},{10,11... | collective-permute-start | bytes 3244040 | tf_op jit(solution)/shard_map/ppermute | solution.py:42
  62.1 24.1 %collective-permute-start.12 = (bf16[4,96,1408]{2,1,0:T(8,128)(2,1)S(1)}, bf16[4,96,1408]{2,1,0:T(8,128)(2,1)S(1)}, u32[]{:S(2)}, u32[]{:S(2)}) collective-permute-start(bf16[4,96,1408]{2,1,0:T(8,128)(2,1)S(1)} %pad_maximum_fusion.5.refs_0_), channel_id=1, source_target_pairs={{0,2},{1,3},{2,0},{3,1},{4,6},{5,7},{6,4},{7,5},{8,10},{9,11},{10,... | collective-permute-start | bytes 3244040 | tf_op jit(solution)/shard_map/ppermute | solution.py:42
  98.1 310.3 %all-gather.6.cloned.1.call-start = ((), (), s32[]{:S(2)}) async-start(), calls=%async_computation.3 | async-start | bytes 13787136 | tf_op jit(solution)/shard_map/all_gather | solution.py:911
  103.7 508.9 %all-gather.10.cloned.1.call-start = ((), (), s32[]{:S(2)}) async-start(), calls=%async_computation.8 | async-start | bytes 26542080 | tf_op jit(solution)/shard_map/all_gather | solution.py:917
  104.4 1138.1 %reduce-scatter.6.cloned.1.call-start = ((), (), s32[]{:S(2)}) async-start(), calls=%async_computation.5 | async-start | bytes 13787136 | tf_op jit(solution)/shard_map/reduce_scatter | solution.py:1177
  126.9 27.8 %collective-permute-start.23 = (bf16[4,96,768]{2,1,0:T(8,128)(2,1)S(1)}, bf16[4,96,768]{2,1,0:T(8,128)(2,1)S(1)}, u32[]{:S(2)}, u32[]{:S(2)}) collective-permute-start(bf16[4,96,768]{2,1,0:T(8,128)(2,1)S(1)} %pad_maximum_fusion.9.refs_0_), channel_id=1, source_target_pairs={{0,1},{1,0},{2,3},{3,2},{4,5},{5,4},{6,7},{7,6},{8,9},{9,8},{10,11... | collective-permute-start | bytes 1769480 | tf_op jit(solution)/shard_map/ppermute | solution.py:42
  127.4 27.7 %collective-permute-start.24 = (bf16[4,96,768]{2,1,0:T(8,128)(2,1)S(1)}, bf16[4,96,768]{2,1,0:T(8,128)(2,1)S(1)}, u32[]{:S(2)}, u32[]{:S(2)}) collective-permute-start(bf16[4,96,768]{2,1,0:T(8,128)(2,1)S(1)} %pad_maximum_fusion.9.refs_0_), channel_id=1, source_target_pairs={{0,2},{1,3},{2,0},{3,1},{4,6},{5,7},{6,4},{7,5},{8,10},{9,11},{10,... | collective-permute-start | bytes 1769480 | tf_op jit(solution)/shard_map/ppermute | solution.py:42
  157.2 26.4 %collective-permute-start.16 = (bf16[256,1024]{1,0:T(8,128)(2,1)}, bf16[256,1024]{1,0:T(8,128)(2,1)}, u32[]{:S(2)}, u32[]{:S(2)}) collective-permute-start(bf16[256,1024]{1,0:T(8,128)(2,1)} %get-tuple-element.64.refs_0_), channel_id=1, source_target_pairs={{0,1},{1,2},{2,3},{3,0},{4,5},{5,6},{6,7},{7,4},{8,9},{9,10},{10,1... | collective-permute-start | bytes 1572872 | tf_op jit(solution)/shard_map/ppermute | solution.py:38
  157.5 36.8 %collective-permute-start.17 = (bf16[256,1024]{1,0:T(8,128)(2,1)}, bf16[256,1024]{1,0:T(8,128)(2,1)}, u32[]{:S(2)}, u32[]{:S(2)}) collective-permute-start(bf16[256,1024]{1,0:T(8,128)(2,1)} %get-tuple-element.64.refs_0_), channel_id=1, source_target_pairs={{0,2},{1,3},{2,0},{3,1},{4,6},{5,7},{6,4},{7,5},{8,10},{9,11},{10,... | collective-permute-start | bytes 1572872 | tf_op jit(solution)/shard_map/ppermute | solution.py:38
  158.2 48.1 %collective-permute-start.18 = (bf16[256,1024]{1,0:T(8,128)(2,1)}, bf16[256,1024]{1,0:T(8,128)(2,1)}, u32[]{:S(2)}, u32[]{:S(2)}) collective-permute-start(bf16[256,1024]{1,0:T(8,128)(2,1)} %get-tuple-element.64.refs_0_), channel_id=1, source_target_pairs={{0,3},{1,0},{2,1},{3,2},{4,7},{5,4},{6,5},{7,6},{8,11},{9,8},{10,9... | collective-permute-start | bytes 1572872 | tf_op jit(solution)/shard_map/ppermute | solution.py:38
  168.5 57.8 %collective-permute-start.27 = (bf16[1536,768]{1,0:T(8,128)(2,1)}, bf16[1536,768]{1,0:T(8,128)(2,1)}, u32[]{:S(2)}, u32[]{:S(2)}) collective-permute-start(bf16[1536,768]{1,0:T(8,128)(2,1)} %line_up.3), channel_id=1, source_target_pairs={{0,16},{16,0},{1,17},{17,1},{2,18},{18,2},{3,19},{19,3},{4,20},{20... | collective-permute-start | bytes 7077896 | tf_op jit(solution)/shard_map/ppermute | solution.py:33
  232.7 70.0 %collective-permute-start.29 = (bf16[256,1536]{1,0:T(8,128)(2,1)}, bf16[256,1536]{1,0:T(8,128)(2,1)}, u32[]{:S(2)}, u32[]{:S(2)}) collective-permute-start(bf16[256,1536]{1,0:T(8,128)(2,1)} %multiply_convert_fusion.1), channel_id=1, source_target_pairs={{0,8},{4,12},{8,0},{12,4},{1,9},{5,13},{9,1},{13,5},{2,10},{6,14},... | collective-permute-start | bytes 2359304 | tf_op jit(solution)/shard_map/ppermute | solution.py:38
  236.3 89.0 %collective-permute-start.30 = (bf16[256,1536]{1,0:T(8,128)(2,1)}, bf16[256,1536]{1,0:T(8,128)(2,1)}, u32[]{:S(2)}, u32[]{:S(2)}) collective-permute-start(bf16[256,1536]{1,0:T(8,128)(2,1)} %multiply_convert_fusion.1), channel_id=1, source_target_pairs={{0,12},{4,0},{8,4},{12,8},{1,13},{5,1},{9,5},{13,9},{2,14},{6,2},{... | collective-permute-start | bytes 2359304 | tf_op jit(solution)/shard_map/ppermute | solution.py:38
  373.2 37.8 %collective-permute-start.32 = (bf16[256,1536]{1,0:T(8,128)(2,1)}, bf16[256,1536]{1,0:T(8,128)(2,1)}, u32[]{:S(2)}, u32[]{:S(2)}) collective-permute-start(bf16[256,1536]{1,0:T(8,128)(2,1)} %get-tuple-element.245), channel_id=1, source_target_pairs={{0,12},{4,0},{8,4},{12,8},{1,13},{5,1},{9,5},{13,9},{2,14},{6,2},{... | collective-permute-start | bytes 2359304 | tf_op jit(solution)/shard_map/ppermute | solution.py:38
  373.2 51.9 %collective-permute-start.33 = (bf16[256,1536]{1,0:T(8,128)(2,1)}, bf16[256,1536]{1,0:T(8,128)(2,1)}, u32[]{:S(2)}, u32[]{:S(2)}) collective-permute-start(bf16[256,1536]{1,0:T(8,128)(2,1)} %get-tuple-element.247), channel_id=1, source_target_pairs={{0,8},{4,12},{8,0},{12,4},{1,9},{5,13},{9,1},{13,5},{2,10},{6,14},... | collective-permute-start | bytes 2359304 | tf_op jit(solution)/shard_map/ppermute | solution.py:38
  373.3 68.6 %collective-permute-start.34 = (bf16[256,1536]{1,0:T(8,128)(2,1)}, bf16[256,1536]{1,0:T(8,128)(2,1)}, u32[]{:S(2)}, u32[]{:S(2)}) collective-permute-start(bf16[256,1536]{1,0:T(8,128)(2,1)} %get-tuple-element.246), channel_id=1, source_target_pairs={{0,4},{4,8},{8,12},{12,0},{1,5},{5,9},{9,13},{13,1},{2,6},{6,10},{... | collective-permute-start | bytes 2359304 | tf_op jit(solution)/shard_map/ppermute | solution.py:38
  453.0 23.2 %collective-permute-start.35 = (bf16[256,1024]{1,0:T(8,128)(2,1)}, bf16[256,1024]{1,0:T(8,128)(2,1)S(1)}, u32[]{:S(2)}, u32[]{:S(2)}) collective-permute-start(bf16[256,1024]{1,0:T(8,128)(2,1)} %get-tuple-element.73.refs_0_), channel_id=1, source_target_pairs={{0,1},{1,2},{2,3},{3,0},{4,5},{5,6},{6,7},{7,4},{8,9},{9,10},{10,1... | collective-permute-start | bytes 1572872 | tf_op jit(solution)/shard_map/ppermute | solution.py:38
  454.4 32.8 %collective-permute-start.36 = (bf16[256,1024]{1,0:T(8,128)(2,1)}, bf16[256,1024]{1,0:T(8,128)(2,1)S(1)}, u32[]{:S(2)}, u32[]{:S(2)}) collective-permute-start(bf16[256,1024]{1,0:T(8,128)(2,1)} %get-tuple-element.73.refs_0_), channel_id=1, source_target_pairs={{0,2},{1,3},{2,0},{3,1},{4,6},{5,7},{6,4},{7,5},{8,10},{9,11},{10,... | collective-permute-start | bytes 1572872 | tf_op jit(solution)/shard_map/ppermute | solution.py:38
  455.7 31.5 %collective-permute-start.37 = (bf16[256,1024]{1,0:T(8,128)(2,1)}, bf16[256,1024]{1,0:T(8,128)(2,1)}, u32[]{:S(2)}, u32[]{:S(2)}) collective-permute-start(bf16[256,1024]{1,0:T(8,128)(2,1)} %get-tuple-element.73.refs_0_), channel_id=1, source_target_pairs={{0,3},{1,0},{2,1},{3,2},{4,7},{5,4},{6,5},{7,6},{8,11},{9,8},{10,9... | collective-permute-start | bytes 1572872 | tf_op jit(solution)/shard_map/ppermute | solution.py:38
  456.9 48.4 %collective-permute-start.38 = (bf16[256,1536]{1,0:T(8,128)(2,1)S(1)}, bf16[256,1536]{1,0:T(8,128)(2,1)S(1)}, u32[]{:S(2)}, u32[]{:S(2)}) collective-permute-start(bf16[256,1536]{1,0:T(8,128)(2,1)S(1)} %dynamic-slice_bitcast_fusion), channel_id=1, source_target_pairs={{0,4},{4,8},{8,12},{12,0},{1,5},{5,9},{9,13},{13,1},{2,6},{6,10},{... | collective-permute-start | bytes 2359304 | tf_op jit(solution)/shard_map/ppermute | solution.py:38
  460.7 65.8 %collective-permute-start.39 = (bf16[256,1536]{1,0:T(8,128)(2,1)S(1)}, bf16[256,1536]{1,0:T(8,128)(2,1)S(1)}, u32[]{:S(2)}, u32[]{:S(2)}) collective-permute-start(bf16[256,1536]{1,0:T(8,128)(2,1)S(1)} %dynamic-slice_bitcast_fusion), channel_id=1, source_target_pairs={{0,8},{4,12},{8,0},{12,4},{1,9},{5,13},{9,1},{13,5},{2,10},{6,14},... | collective-permute-start | bytes 2359304 | tf_op jit(solution)/shard_map/ppermute | solution.py:38
  476.2 55.5 %collective-permute-start.40 = (bf16[256,1536]{1,0:T(8,128)(2,1)S(1)}, bf16[256,1536]{1,0:T(8,128)(2,1)}, u32[]{:S(2)}, u32[]{:S(2)}) collective-permute-start(bf16[256,1536]{1,0:T(8,128)(2,1)S(1)} %dynamic-slice_bitcast_fusion), channel_id=1, source_target_pairs={{0,12},{4,0},{8,4},{12,8},{1,13},{5,1},{9,5},{13,9},{2,14},{6,2},{... | collective-permute-start | bytes 2359304 | tf_op jit(solution)/shard_map/ppermute | solution.py:38
  539.9 66.2 %collective-permute-start.42 = (bf16[256,1536]{1,0:T(8,128)(2,1)S(1)}, bf16[256,1536]{1,0:T(8,128)(2,1)}, u32[]{:S(2)}, u32[]{:S(2)}) collective-permute-start(bf16[256,1536]{1,0:T(8,128)(2,1)S(1)} %multiply_convert_fusion), channel_id=1, source_target_pairs={{0,8},{4,12},{8,0},{12,4},{1,9},{5,13},{9,1},{13,5},{2,10},{6,14},... | collective-permute-start | bytes 2359304 | tf_op jit(solution)/shard_map/ppermute | solution.py:38
  540.0 67.5 %collective-permute-start.43 = (bf16[256,1536]{1,0:T(8,128)(2,1)S(1)}, bf16[256,1536]{1,0:T(8,128)(2,1)}, u32[]{:S(2)}, u32[]{:S(2)}) collective-permute-start(bf16[256,1536]{1,0:T(8,128)(2,1)S(1)} %multiply_convert_fusion), channel_id=1, source_target_pairs={{0,12},{4,0},{8,4},{12,8},{1,13},{5,1},{9,5},{13,9},{2,14},{6,2},{... | collective-permute-start | bytes 2359304 | tf_op jit(solution)/shard_map/ppermute | solution.py:38
  700.7 85.3 %collective-permute-start.44 = (bf16[256,1536]{1,0:T(8,128)(2,1)}, bf16[256,1536]{1,0:T(8,128)(2,1)}, u32[]{:S(2)}, u32[]{:S(2)}) collective-permute-start(bf16[256,1536]{1,0:T(8,128)(2,1)} %get-tuple-element.242), channel_id=1, source_target_pairs={{0,12},{4,0},{8,4},{12,8},{1,13},{5,1},{9,5},{13,9},{2,14},{6,2},{... | collective-permute-start | bytes 2359304 | tf_op jit(solution)/shard_map/ppermute | solution.py:38
  700.7 85.3 %collective-permute-start.45 = (bf16[256,1536]{1,0:T(8,128)(2,1)}, bf16[256,1536]{1,0:T(8,128)(2,1)}, u32[]{:S(2)}, u32[]{:S(2)}) collective-permute-start(bf16[256,1536]{1,0:T(8,128)(2,1)} %get-tuple-element.244), channel_id=1, source_target_pairs={{0,8},{4,12},{8,0},{12,4},{1,9},{5,13},{9,1},{13,5},{2,10},{6,14},... | collective-permute-start | bytes 2359304 | tf_op jit(solution)/shard_map/ppermute | solution.py:38
  703.3 75.0 %collective-permute-start.47 = (f32[8,256]{0,1:T(8,128)}, f32[8,256]{0,1:T(8,128)}, u32[]{:S(2)}, u32[]{:S(2)}) collective-permute-start(f32[8,256]{0,1:T(8,128)} %get-tuple-element.291), channel_id=1, source_target_pairs={{0,12},{4,0},{8,4},{12,8},{1,13},{5,1},{9,5},{13,9},{2,14},{6,2},{... | collective-permute-start | bytes 24584 | tf_op jit(solution)/shard_map/ppermute | solution.py:38
  704.5 76.0 %collective-permute-start.48 = (f32[8,256]{0,1:T(8,128)}, f32[8,256]{0,1:T(8,128)}, u32[]{:S(2)}, u32[]{:S(2)}) collective-permute-start(f32[8,256]{0,1:T(8,128)} %get-tuple-element.290), channel_id=1, source_target_pairs={{0,8},{4,12},{8,0},{12,4},{1,9},{5,13},{9,1},{13,5},{2,10},{6,14},... | collective-permute-start | bytes 24584 | tf_op jit(solution)/shard_map/ppermute | solution.py:38
  706.8 75.3 %collective-permute-start.49 = (f32[8,256]{0,1:T(8,128)}, f32[8,256]{0,1:T(8,128)}, u32[]{:S(2)}, u32[]{:S(2)}) collective-permute-start(f32[8,256]{0,1:T(8,128)} %get-tuple-element.289), channel_id=1, source_target_pairs={{0,4},{4,8},{8,12},{12,0},{1,5},{5,9},{9,13},{13,1},{2,6},{6,10},{... | collective-permute-start | bytes 24584 | tf_op jit(solution)/shard_map/ppermute | solution.py:38
  835.0 73.1 %collective-permute-start.54 = (bf16[256,1024]{1,0:T(8,128)(2,1)}, bf16[256,1024]{1,0:T(8,128)(2,1)S(1)}, u32[]{:S(2)}, u32[]{:S(2)}) collective-permute-start(bf16[256,1024]{1,0:T(8,128)(2,1)} %get-tuple-element.90), channel_id=1, source_target_pairs={{0,3},{1,0},{2,1},{3,2},{4,7},{5,4},{6,5},{7,6},{8,11},{9,8},{10,9... | collective-permute-start | bytes 1572872 | tf_op jit(solution)/shard_map/ppermute | solution.py:38
  835.1 73.0 %collective-permute-start.55 = (bf16[256,1024]{1,0:T(8,128)(2,1)}, bf16[256,1024]{1,0:T(8,128)(2,1)S(1)}, u32[]{:S(2)}, u32[]{:S(2)}) collective-permute-start(bf16[256,1024]{1,0:T(8,128)(2,1)} %get-tuple-element.91), channel_id=1, source_target_pairs={{0,2},{1,3},{2,0},{3,1},{4,6},{5,7},{6,4},{7,5},{8,10},{9,11},{10,... | collective-permute-start | bytes 1572872 | tf_op jit(solution)/shard_map/ppermute | solution.py:38
  837.1 51.2 %collective-permute-start.51 = (bf16[256,1536]{1,0:T(8,128)(2,1)S(1)}, bf16[256,1536]{1,0:T(8,128)(2,1)S(1)}, u32[]{:S(2)}, u32[]{:S(2)}) collective-permute-start(bf16[256,1536]{1,0:T(8,128)(2,1)S(1)} %get-tuple-element.241), channel_id=1, source_target_pairs={{0,8},{4,12},{8,0},{12,4},{1,9},{5,13},{9,1},{13,5},{2,10},{6,14},... | collective-permute-start | bytes 2359304 | tf_op jit(solution)/shard_map/ppermute | solution.py:38
  838.6 66.6 %collective-permute-start.52 = (bf16[256,1536]{1,0:T(8,128)(2,1)S(1)}, bf16[256,1536]{1,0:T(8,128)(2,1)S(1)}, u32[]{:S(2)}, u32[]{:S(2)}) collective-permute-start(bf16[256,1536]{1,0:T(8,128)(2,1)S(1)} %get-tuple-element.240), channel_id=1, source_target_pairs={{0,4},{4,8},{8,12},{12,0},{1,5},{5,9},{9,13},{13,1},{2,6},{6,10},{... | collective-permute-start | bytes 2359304 | tf_op jit(solution)/shard_map/ppermute | solution.py:38
  852.4 55.8 %collective-permute-start.56 = (bf16[256,1024]{1,0:T(8,128)(2,1)S(1)}, bf16[256,1024]{1,0:T(8,128)(2,1)S(1)}, u32[]{:S(2)}, u32[]{:S(2)}) collective-permute-start(bf16[256,1024]{1,0:T(8,128)(2,1)S(1)} %copy-done.83), channel_id=1, source_target_pairs={{0,1},{1,2},{2,3},{3,0},{4,5},{5,6},{6,7},{7,4},{8,9},{9,10},{10,1... | collective-permute-start | bytes 1572872 | tf_op jit(solution)/shard_map/ppermute | solution.py:38
  925.7 521.7 %reduce-scatter.4.cloned.1.call-start = ((), (), s32[]{:S(2)}) async-start(), calls=%async_computation.4 | async-start | bytes 26542080 | tf_op jit(solution)/shard_map/reduce_scatter | solution.py:1028
  926.3 543.2 %reduce-scatter.8.cloned.1.call-start = ((), (), s32[]{:S(2)}) async-start(), calls=%async_computation.6 | async-start | bytes 26542080 | tf_op jit(solution)/shard_map/reduce_scatter | solution.py:1028
  929.8 20.7 %collective-permute-start.57 = (bf16[256,1536]{1,0:T(8,128)(2,1)S(1)}, bf16[256,1536]{1,0:T(8,128)(2,1)S(1)}, u32[]{:S(2)}, u32[]{:S(2)}) collective-permute-start(bf16[256,1536]{1,0:T(8,128)(2,1)S(1)} %add_convert_fusion.3), channel_id=1, source_target_pairs={{0,4},{4,8},{8,12},{12,0},{1,5},{5,9},{9,13},{13,1},{2,6},{6,10},{... | collective-permute-start | bytes 2359304 | tf_op jit(solution)/shard_map/ppermute | solution.py:38
  932.0 100.7 %collective-permute-start.58 = (bf16[256,1536]{1,0:T(8,128)(2,1)S(1)}, bf16[256,1536]{1,0:T(8,128)(2,1)S(1)}, u32[]{:S(2)}, u32[]{:S(2)}) collective-permute-start(bf16[256,1536]{1,0:T(8,128)(2,1)S(1)} %add_convert_fusion.3), channel_id=1, source_target_pairs={{0,8},{4,12},{8,0},{12,4},{1,9},{5,13},{9,1},{13,5},{2,10},{6,14},... | collective-permute-start | bytes 2359304 | tf_op jit(solution)/shard_map/ppermute | solution.py:38
  932.0 100.7 %collective-permute-start.59 = (bf16[256,1536]{1,0:T(8,128)(2,1)S(1)}, bf16[256,1536]{1,0:T(8,128)(2,1)S(1)}, u32[]{:S(2)}, u32[]{:S(2)}) collective-permute-start(bf16[256,1536]{1,0:T(8,128)(2,1)S(1)} %add_convert_fusion.3), channel_id=1, source_target_pairs={{0,12},{4,0},{8,4},{12,8},{1,13},{5,1},{9,5},{13,9},{2,14},{6,2},{... | collective-permute-start | bytes 2359304 | tf_op jit(solution)/shard_map/ppermute | solution.py:38
  1118.8 41.0 %collective-permute-start.65 = (f32[8,256]{0,1:T(8,128)S(1)}, f32[8,256]{0,1:T(8,128)S(1)}, u32[]{:S(2)}, u32[]{:S(2)}) collective-permute-start(f32[8,256]{0,1:T(8,128)S(1)} %get-tuple-element.286), channel_id=1, source_target_pairs={{0,4},{4,8},{8,12},{12,0},{1,5},{5,9},{9,13},{13,1},{2,6},{6,10},{... | collective-permute-start | bytes 24584 | tf_op jit(solution)/shard_map/ppermute | solution.py:38
  1124.7 55.8 %collective-permute-start.60 = (bf16[256,1536]{1,0:T(8,128)(2,1)}, bf16[256,1536]{1,0:T(8,128)(2,1)S(1)}, u32[]{:S(2)}, u32[]{:S(2)}) collective-permute-start(bf16[256,1536]{1,0:T(8,128)(2,1)} %get-tuple-element.236), channel_id=1, source_target_pairs={{0,12},{4,0},{8,4},{12,8},{1,13},{5,1},{9,5},{13,9},{2,14},{6,2},{... | collective-permute-start | bytes 2359304 | tf_op jit(solution)/shard_map/ppermute | solution.py:38
  1124.7 55.7 %collective-permute-start.61 = (bf16[256,1536]{1,0:T(8,128)(2,1)}, bf16[256,1536]{1,0:T(8,128)(2,1)}, u32[]{:S(2)}, u32[]{:S(2)}) collective-permute-start(bf16[256,1536]{1,0:T(8,128)(2,1)} %get-tuple-element.238), channel_id=1, source_target_pairs={{0,8},{4,12},{8,0},{12,4},{1,9},{5,13},{9,1},{13,5},{2,10},{6,14},... | collective-permute-start | bytes 2359304 | tf_op jit(solution)/shard_map/ppermute | solution.py:38
  1126.7 69.9 %collective-permute-start.62 = (bf16[256,1536]{1,0:T(8,128)(2,1)S(1)}, bf16[256,1536]{1,0:T(8,128)(2,1)}, u32[]{:S(2)}, u32[]{:S(2)}) collective-permute-start(bf16[256,1536]{1,0:T(8,128)(2,1)S(1)} %get-tuple-element.237), channel_id=1, source_target_pairs={{0,4},{4,8},{8,12},{12,0},{1,5},{5,9},{9,13},{13,1},{2,6},{6,10},{... | collective-permute-start | bytes 2359304 | tf_op jit(solution)/shard_map/ppermute | solution.py:38
  1232.7 26.0 %collective-permute-start.66 = (bf16[256,1024]{1,0:T(8,128)(2,1)}, bf16[256,1024]{1,0:T(8,128)(2,1)}, u32[]{:S(2)}, u32[]{:S(2)}) collective-permute-start(bf16[256,1024]{1,0:T(8,128)(2,1)} %get-tuple-element.107), channel_id=1, source_target_pairs={{0,3},{1,0},{2,1},{3,2},{4,7},{5,4},{6,5},{7,6},{8,11},{9,8},{10,9... | collective-permute-start | bytes 1572872 | tf_op jit(solution)/shard_map/ppermute | solution.py:38
  1236.1 25.2 %collective-permute-start.67 = (bf16[256,1024]{1,0:T(8,128)(2,1)}, bf16[256,1024]{1,0:T(8,128)(2,1)}, u32[]{:S(2)}, u32[]{:S(2)}) collective-permute-start(bf16[256,1024]{1,0:T(8,128)(2,1)} %get-tuple-element.108), channel_id=1, source_target_pairs={{0,2},{1,3},{2,0},{3,1},{4,6},{5,7},{6,4},{7,5},{8,10},{9,11},{10,... | collective-permute-start | bytes 1572872 | tf_op jit(solution)/shard_map/ppermute | solution.py:38
  1236.1 40.6 %collective-permute-start.68 = (bf16[256,1024]{1,0:T(8,128)(2,1)}, bf16[256,1024]{1,0:T(8,128)(2,1)}, u32[]{:S(2)}, u32[]{:S(2)}) collective-permute-start(bf16[256,1024]{1,0:T(8,128)(2,1)} %get-tuple-element.109), channel_id=1, source_target_pairs={{0,1},{1,2},{2,3},{3,0},{4,5},{5,6},{6,7},{7,4},{8,9},{9,10},{10,1... | collective-permute-start | bytes 1572872 | tf_op jit(solution)/shard_map/ppermute | solution.py:38
  1239.1 64.2 %collective-permute-start.80 = (bf16[1536,768]{1,0:T(8,128)(2,1)}, bf16[1536,768]{1,0:T(8,128)(2,1)}, u32[]{:S(2)}, u32[]{:S(2)}) collective-permute-start(bf16[1536,768]{1,0:T(8,128)(2,1)} %convolution_convert_fusion), channel_id=1, source_target_pairs={{0,16},{16,0},{1,17},{17,1},{2,18},{18,2},{3,19},{19,3},{4,20},{20... | collective-permute-start | bytes 7077896 | tf_op jit(solution)/shard_map/ppermute | solution.py:33
  1301.6 41.1 %collective-permute-start.70 = (bf16[1536,1408]{1,0:T(8,128)(2,1)}, bf16[1536,1408]{1,0:T(8,128)(2,1)}, u32[]{:S(2)}, u32[]{:S(2)}) collective-permute-start(bf16[1536,1408]{1,0:T(8,128)(2,1)} %get-tuple-element.225), channel_id=1, source_target_pairs={{0,16},{16,0},{1,17},{17,1},{2,18},{18,2},{3,19},{19,3},{4,20},{20... | collective-permute-start | bytes 12976136 | tf_op jit(solution)/shard_map/ppermute | solution.py:33
  1344.3 25.3 %collective-permute-start.71 = (bf16[2,96,1408]{2,1,0:T(8,128)(2,1)S(1)}, bf16[2,96,1408]{2,1,0:T(8,128)(2,1)S(1)}, u32[]{:S(2)}, u32[]{:S(2)}) collective-permute-start(bf16[2,96,1408]{2,1,0:T(8,128)(2,1)S(1)} %get-tuple-element.220), channel_id=1, source_target_pairs={{0,2},{1,3},{2,0},{3,1},{4,6},{5,7},{6,4},{7,5},{8,10},{9,11},{10,... | collective-permute-start | bytes 1622024 | tf_op jit(solution)/shard_map/ppermute | solution.py:42
  1348.0 44.8 %collective-permute-start.73 = (bf16[2,96,1408]{2,1,0:T(8,128)(2,1)S(1)}, bf16[2,96,1408]{2,1,0:T(8,128)(2,1)S(1)}, u32[]{:S(2)}, u32[]{:S(2)}) collective-permute-start(bf16[2,96,1408]{2,1,0:T(8,128)(2,1)S(1)} %slice_bitcast_fusion.3), channel_id=1, source_target_pairs={{0,2},{1,3},{2,0},{3,1},{4,6},{5,7},{6,4},{7,5},{8,10},{9,11},{10,... | collective-permute-start | bytes 1622024 | tf_op jit(solution)/shard_map/ppermute | solution.py:42
  1348.1 25.0 %collective-permute-start.75 = (bf16[2,96,1408]{2,1,0:T(8,128)(2,1)S(1)}, bf16[2,96,1408]{2,1,0:T(8,128)(2,1)S(1)}, u32[]{:S(2)}, u32[]{:S(2)}) collective-permute-start(bf16[2,96,1408]{2,1,0:T(8,128)(2,1)S(1)} %get-tuple-element.221), channel_id=1, source_target_pairs={{0,1},{1,0},{2,3},{3,2},{4,5},{5,4},{6,7},{7,6},{8,9},{9,8},{10,11... | collective-permute-start | bytes 1622024 | tf_op jit(solution)/shard_map/ppermute | solution.py:42
  1348.8 70.8 %collective-permute-start.74 = (bf16[2,96,1408]{2,1,0:T(8,128)(2,1)S(1)}, bf16[2,96,1408]{2,1,0:T(8,128)(2,1)S(1)}, u32[]{:S(2)}, u32[]{:S(2)}) collective-permute-start(bf16[2,96,1408]{2,1,0:T(8,128)(2,1)S(1)} %slice_bitcast_fusion.2), channel_id=1, source_target_pairs={{0,1},{1,0},{2,3},{3,2},{4,5},{5,4},{6,7},{7,6},{8,9},{9,8},{10,11... | collective-permute-start | bytes 1622024 | tf_op jit(solution)/shard_map/ppermute | solution.py:42
  1369.8 49.7 %collective-permute-start.72 = (bf16[2,96,1408]{2,1,0:T(8,128)(2,1)S(1)}, bf16[2,96,1408]{2,1,0:T(8,128)(2,1)S(1)}, u32[]{:S(2)}, u32[]{:S(2)}) collective-permute-start(bf16[2,96,1408]{2,1,0:T(8,128)(2,1)S(1)} %fusion.17), channel_id=1, source_target_pairs={{0,1},{1,0},{2,3},{3,2},{4,5},{5,4},{6,7},{7,6},{8,9},{9,8},{10,11... | collective-permute-start | bytes 1622024 | tf_op jit(solution)/shard_map/ppermute | solution.py:42
  1373.3 46.3 %collective-permute-start.76 = (bf16[2,96,1408]{2,1,0:T(8,128)(2,1)S(1)}, bf16[2,96,1408]{2,1,0:T(8,128)(2,1)S(1)}, u32[]{:S(2)}, u32[]{:S(2)}) collective-permute-start(bf16[2,96,1408]{2,1,0:T(8,128)(2,1)S(1)} %fusion.16), channel_id=1, source_target_pairs={{0,2},{1,3},{2,0},{3,1},{4,6},{5,7},{6,4},{7,5},{8,10},{9,11},{10,... | collective-permute-start | bytes 1622024 | tf_op jit(solution)/shard_map/ppermute | solution.py:42
  1375.6 49.8 %collective-permute-start.69 = (bf16[256,1536]{1,0:T(8,128)(2,1)S(1)}, bf16[256,1536]{1,0:T(8,128)(2,1)S(1)}, u32[]{:S(2)}, u32[]{:S(2)}) collective-permute-start(bf16[256,1536]{1,0:T(8,128)(2,1)S(1)} %get-tuple-element.198), channel_id=1, source_target_pairs={{0,16},{16,0},{1,17},{17,1},{2,18},{18,2},{3,19},{19,3},{4,20},{20... | collective-permute-start | bytes 2359304 | tf_op jit(solution)/shard_map/ppermute | solution.py:33
  1422.5 17.8 %collective-permute-start.78 = (bf16[96,1408]{1,0:T(8,128)(2,1)S(1)}, bf16[96,1408]{1,0:T(8,128)(2,1)S(1)}, u32[]{:S(2)}, u32[]{:S(2)}) collective-permute-start(bf16[96,1408]{1,0:T(8,128)(2,1)S(1)} %get-tuple-element.254), channel_id=1, source_target_pairs={{0,8},{4,12},{8,0},{12,4},{1,9},{5,13},{9,1},{13,5},{2,10},{6,14},... | collective-permute-start | bytes 811016 | tf_op jit(solution)/shard_map/ppermute | solution.py:38
  1425.5 20.5 %collective-permute-start.79 = (bf16[96,1408]{1,0:T(8,128)(2,1)S(1)}, bf16[96,1408]{1,0:T(8,128)(2,1)S(1)}, u32[]{:S(2)}, u32[]{:S(2)}) collective-permute-start(bf16[96,1408]{1,0:T(8,128)(2,1)S(1)} %get-tuple-element.253), channel_id=1, source_target_pairs={{0,4},{4,8},{8,12},{12,0},{1,5},{5,9},{9,13},{13,1},{2,6},{6,10},{... | collective-permute-start | bytes 811016 | tf_op jit(solution)/shard_map/ppermute | solution.py:38
  1447.0 29.1 %collective-permute-start.90 = (bf16[96,2176]{1,0:T(8,128)(2,1)}, bf16[96,2176]{1,0:T(8,128)(2,1)}, u32[]{:S(2)}, u32[]{:S(2)}) collective-permute-start(bf16[96,2176]{1,0:T(8,128)(2,1)} %fusion.18), channel_id=1, source_target_pairs={{0,16},{16,0},{1,17},{17,1},{2,18},{18,2},{3,19},{19,3},{4,20},{20... | collective-permute-start | bytes 1253384 | tf_op jit(solution)/shard_map/ppermute | solution.py:33
  (124 other events, 2474.7 us)
Sparse Core Ops, SparseCore 0:
  98.2 154.8 all-gather.7
  256.0 152.3 all-gather.5
  410.8 150.5 all-gather.9
  925.8 175.8 reduce-scatter.5
  1105.6 166.6 reduce-scatter.3
  1275.8 193.6 reduce-scatter.7

commit v3 on v2

--- a/solution.py
+++ b/solution.py
@@ -17,6 +17,7 @@
 NEGATIVE = -1e30
 LANES = 128
 TILE = 256
+ROWS = 1024
 VMEM_LIMIT = 60 * 1024 * 1024
 
 F32 = jnp.float32
@@ -42,8 +43,27 @@
     return lax.ppermute(array, "shard", [(i, i ^ mask) for i in range(lax.axis_size("shard"))])
 
 
+def crossed(array, axis, by):
+    length = lax.axis_size(axis)
+    if length & (length - 1):
+        return shifted(array, axis, by)
+    return lax.ppermute(array, axis, [(i, i ^ by) for i in range(length)])
+
+
+def crossed_back(array, axis, by):
+    length = lax.axis_size(axis)
+    return shifted(array, axis, -by) if length & (length - 1) else crossed(array, axis, by)
+
+
+def partner(axis, by, back=False):
+    length, me = lax.axis_size(axis), lax.axis_index(axis)
+    if length & (length - 1):
+        return lax.rem(me + (by if back else length - by), length)
+    return me ^ by
+
+
 def slots_of(array, axis):
-    return [array] + [shifted(array, axis, k) for k in range(1, lax.axis_size(axis))]
+    return [array] + [crossed(array, axis, k) for k in range(1, lax.axis_size(axis))]
 
 
 def after(array, *others):
@@ -59,7 +79,7 @@
     me = lax.axis_index("shard")
     if count != 4:
         pieces = [
-            (slot, lax.rem(me - k + count, count), 0)
+            (slot, partner("shard", k) if k else me, 0)
             for k, slot in enumerate(slots_of(array, "shard"))
         ]
         return pieces, [piece for piece, _, _ in pieces[1:]]
@@ -80,47 +100,6 @@
     ], [one, two]
 
 
-def scatter_first(pieces, axis):
-    if lax.axis_size("shard") != 4:
-        return [shifted(pieces[k], "shard", -k) for k in range(1, len(pieces))]
-    own, one, two, far_low, far_high = pieces
-    half = far_low.shape[axis]
-    length = own.shape[axis]
-    return [
-        flipped(far_low, 2),
-        flipped(far_high, 1),
-        flipped(cut(one, half, length, axis), 1),
-        flipped(cut(two, 0, half, axis), 2),
-    ]
-
-
-def scatter_second(pieces, first, axis):
-    if lax.axis_size("shard") != 4:
-        return []
-    own, one, two, far_low, far_high = pieces
-    half = far_low.shape[axis]
-    length = own.shape[axis]
-    low, high = first[:2]
-    return [
-        flipped((cut(one, 0, half, axis).astype(F32) + low.astype(F32)).astype(BF16), 1),
-        flipped((cut(two, half, length, axis).astype(F32) + high.astype(F32)).astype(BF16), 2),
-    ]
-
-
-def scatter_end(pieces, first, second, axis):
-    if lax.axis_size("shard") != 4:
-        return sum((array.astype(F32) for array in first), pieces[0].astype(F32))
-    one_high, two_low = first[2:]
-    one_low, two_high = second
-    return pieces[0].astype(F32) + jnp.concatenate(
-        [
-            one_low.astype(F32) + two_low.astype(F32),
-            one_high.astype(F32) + two_high.astype(F32),
-        ],
-        axis=axis,
-    )
-
-
 def rotary_tables(positions):
     frequency = 1.0 / ROPE_BASE ** (jnp.arange(0, HEAD, 2, dtype=F32) / HEAD)
     angles = positions.astype(F32)[:, None] * frequency[None, :]
@@ -182,7 +161,7 @@
     total, model = rows.shape
     parts, experts, depth, columns = weights.shape
     width = columns // 3
-    tile = min(TILE, total)
+    tile = math.gcd(ROWS, total)
 
     def body(rows_ref, gates_ref, weights_ref, out_ref, raw_ref, gate_up, down, sums):
         expert = pl.program_id(0)
@@ -250,7 +229,7 @@
     total, model = grads.shape
     parts, experts, depth, columns = weights.shape
     width = columns // 3
-    tile = min(TILE, total)
+    tile = math.gcd(ROWS, total)
 
     def body(
         grads_ref,
@@ -258,12 +237,12 @@
         raw_ref,
         weights_ref,
         out_ref,
-        scores_ref,
         d_raw_ref,
         act_ref,
         gate_up,
         down,
         sums,
+        scores,
     ):
         expert = pl.program_id(0)
         fill_weights(weights_ref, gate_up, down)
@@ -288,16 +267,21 @@
             @pl.when(expert == 0)
             def _():
                 sums[span, :] = part
-                scores_ref[span, :] = jnp.where(lane == 0, score, 0.0)
+                scores[span, :] = jnp.where(lane == 0, score, 0.0)
 
             @pl.when(expert > 0)
             def _():
                 sums[span, :] += part
-                scores_ref[span, :] = jnp.where(lane == expert, score, scores_ref[span, :])
+                scores[span, :] = jnp.where(lane == expert, score, scores[span, :])
 
             @pl.when(expert == experts - 1)
             def _():
-                out_ref[span, :] = sums[span, :].astype(BF16)
+                out_ref[span, :model] = sums[span, :].astype(BF16)
+                whole_scores = scores[span, :]
+                high = whole_scores.astype(BF16).astype(F32)
+                out_ref[span, model:] = jnp.where(
+                    lane < HEAD, high, pltpu.roll(whole_scores - high, HEAD, 1)
+                ).astype(BF16)
 
             return carry
 
@@ -318,8 +302,7 @@
             ]
             + [pl.BlockSpec((parts, 1, depth, columns), lambda e: (0, e, 0, 0))],
             out_specs=[
-                pl.BlockSpec((total, model), whole),
-                pl.BlockSpec((total, LANES), whole),
+                pl.BlockSpec((total, model + LANES), whole),
                 pl.BlockSpec((1, total, 4 * width), per_expert),
                 pl.BlockSpec((1, total, 2 * width), per_expert),
             ],
@@ -327,11 +310,11 @@
                 pltpu.VMEM((model, 4 * width), BF16),
                 pltpu.VMEM((model, 2 * width), BF16),
                 pltpu.VMEM((total, model), F32),
+                pltpu.VMEM((total, LANES), F32),
             ],
         ),
         out_shape=[
-            jax.ShapeDtypeStruct((total, model), BF16),
-            jax.ShapeDtypeStruct((total, LANES), F32),
+            jax.ShapeDtypeStruct((total, model + LANES), BF16),
             jax.ShapeDtypeStruct((experts, total, 4 * width), BF16),
             jax.ShapeDtypeStruct((experts, total, 2 * width), BF16),
         ],
@@ -393,6 +376,45 @@
     )(rows, grads, d_raws, acts)
 
 
+def expert_outputs(mine, other, core):
+    experts, depth, columns = mine.shape
+    width = columns // 3
+
+    def body(core_ref, mine_ref, other_ref, gate_ref, up_ref, down_ref):
+        is_first = core_ref[0] == 0
+        own, received = mine_ref[0].astype(F32), other_ref[0].astype(F32)
+        low = jnp.where(is_first, own, received)
+        high = jnp.where(is_first, received, own)
+        for index, half in enumerate((low, high)):
+            span = slice(index * width, (index + 1) * width)
+            gate_ref[0, :, span] = half[:, :width]
+            up_ref[0, :, span] = half[:, width : 2 * width]
+            down_ref[0, span, :] = half[:, 2 * width :].T
+
+    block = lambda e, *_: (e, 0, 0)
+    return pl.pallas_call(
+        body,
+        grid_spec=pltpu.PrefetchScalarGridSpec(
+            num_scalar_prefetch=1,
+            grid=(experts,),
+            in_specs=[pl.BlockSpec((1, depth, columns), block)] * 2,
+            out_specs=[
+                pl.BlockSpec((1, depth, 2 * width), block),
+                pl.BlockSpec((1, depth, 2 * width), block),
+                pl.BlockSpec((1, 2 * width, depth), block),
+            ],
+        ),
+        out_shape=[
+            jax.ShapeDtypeStruct((experts, depth, 2 * width), F32),
+            jax.ShapeDtypeStruct((experts, depth, 2 * width), F32),
+            jax.ShapeDtypeStruct((experts, 2 * width, depth), F32),
+        ],
+        compiler_params=pltpu.CompilerParams(vmem_limit_bytes=VMEM_LIMIT),
+        cost_estimate=lasting(6),
+        name="expert_outputs",
+    )(jnp.reshape(core, (1,)).astype(jnp.int32), mine, other)
+
+
 def line_up(pieces, owners, planes_of, shards):
     arrays = [piece for piece, _, _ in pieces]
     slots, rows, width = arrays[0].shape
@@ -462,7 +484,7 @@
 
 def half_specs(halves, columns):
     return [
-        pl.BlockSpec((1, array.shape[1], columns), lambda i, place=place: (place, 0, 0))
+        pl.BlockSpec((1, array.shape[1], columns), lambda i, *_, place=place: (place, 0, 0))
         for array, place in halves
     ]
 
@@ -516,23 +538,112 @@
     )(stream, gain, *[array for array, _ in halves], cosines, sines)
 
 
+def branch_backward(backs, places, experts, gates, side, middle, gain, grad_out, halves, flip):
+    rows, model = middle.shape
+    count = len(backs)
+    half_width = halves[0].shape[1]
+
+    def body(places_ref, flip_ref, *refs):
+        slots = refs[:count]
+        gates_ref, side_ref, middle_ref, gain_ref, out_grad_ref, one_ref, two_ref = refs[
+            count : count + 7
+        ]
+        d_middle_ref, branch_ref, attended_ref, high_ref, low_ref, d_gain_ref = refs[count + 7 :]
+        lane = lax.broadcasted_iota(jnp.int32, (LANES, LANES), 0) % HEAD
+        column = lax.broadcasted_iota(jnp.int32, (LANES, LANES), 1)
+        d_hidden = None
+        d_gates = None
+        for index, slot in enumerate(slots):
+            placing = (lane < experts) & (column == lane + 2 + places_ref[index] * experts)
+            part = dot_nn(slot[:, model:], placing.astype(F32).astype(BF16))
+            values = slot[:, :model].astype(F32)
+            d_hidden = values if d_hidden is None else d_hidden + values
+            d_gates = part if d_gates is None else d_gates + part
+        gate_table = gates_ref[...]
+        share = jnp.sum(gate_table * d_gates, axis=1, keepdims=True)
+        d_logits = gate_table * (d_gates - share)
+        high = d_logits.astype(BF16)
+        low = (d_logits - high.astype(F32)).astype(BF16)
+        high_ref[...] = high
+        low_ref[...] = low
+        d_hidden = d_hidden + dot_nt(high, side_ref[...]) + dot_nt(low, side_ref[...])
+        values = middle_ref[...]
+        scale = lax.rsqrt(jnp.mean(values * values, axis=1, keepdims=True) + EPSILON)
+        d_gain = jnp.sum(d_hidden * values * scale, axis=0, keepdims=True)
+        d_gain_ref[...] = jnp.broadcast_to(d_gain, (8, model))
+        shaped = d_hidden * gain_ref[...]
+        mean = jnp.mean(shaped * values, axis=1, keepdims=True)
+        d_middle = (
+            out_grad_ref[...].astype(F32) + scale * shaped - values * (scale * scale * scale * mean)
+        )
+        d_middle_ref[...] = d_middle
+        branch = d_middle.astype(BF16)
+        branch_ref[...] = branch
+        flipped_order = flip_ref[0] == 1
+        first_half, second_half = branch[:, :half_width], branch[:, half_width:]
+        attended = dot_nt(
+            jnp.where(flipped_order, second_half, first_half), one_ref[...]
+        ) + dot_nt(jnp.where(flipped_order, first_half, second_half), two_ref[...])
+        width = attended.shape[1] // 2
+        left, right = attended[:, :width], attended[:, width:]
+        attended_ref[:, :width] = jnp.where(flipped_order, right, left).astype(BF16)
+        attended_ref[:, width:] = jnp.where(flipped_order, left, right).astype(BF16)
+
+    arrays = [*backs, gates, side, middle, gain, grad_out, *halves]
+    whole = lambda i, *_: (0, 0)
+    outs = [
+        ((rows, model), F32),
+        ((rows, model), BF16),
+        ((rows, halves[0].shape[0]), BF16),
+        ((rows, LANES), BF16),
+        ((rows, LANES), BF16),
+        ((8, model), F32),
+    ]
+    return pl.pallas_call(
+        body,
+        grid_spec=pltpu.PrefetchScalarGridSpec(
+            num_scalar_prefetch=2,
+            grid=(1,),
+            in_specs=[pl.BlockSpec(array.shape, whole) for array in arrays],
+            out_specs=[pl.BlockSpec(shape, whole) for shape, _ in outs],
+        ),
+        out_shape=[jax.ShapeDtypeStruct(shape, dtype) for shape, dtype in outs],
+        compiler_params=pltpu.CompilerParams(vmem_limit_bytes=VMEM_LIMIT),
+        cost_estimate=lasting(12),
+        name="branch_backward",
+    )(places, flip, *arrays)
+
+
 def qkv_backward(
-    normed, d_queries, d_kv_slots, halves, cosines, sines, columns, stream, side, owns, extra
+    normed, d_queries, d_kv_slots, halves, cosines, sines, columns, stream, side, flip, extra, grid
 ):
     rows, model = normed.shape
     queries, kv = columns
     qkv = queries + kv
     count = len(d_kv_slots)
-    more = extra[0].shape[1] if extra else 0
-
-    def body(n_ref, dq_ref, *refs):
+    shards, planes = grid
+    depth = model // (shards * planes)
+    more = extra[1].shape[1] if extra else 0
+
+    def body(flip_ref, n_ref, dq_ref, *refs):
         slots = refs[:count]
-        mine_ref, other_ref, cos_ref, sin_ref, stream_ref, side_ref, owns_ref = refs[
-            count : count + 7
-        ]
-        extra_refs = refs[count + 7 : count + 7 + len(extra)]
-        out_ref, grad_ref, n_t = refs[count + 7 + len(extra) :]
+        mine_ref, other_ref, cos_ref, sin_ref, stream_ref = refs[count : count + 5]
+        hidden_ref, high_ref, low_ref, gain_two_ref = refs[count + 5 : count + 9]
+        extra_refs = refs[count + 9 : count + 9 + len(extra)]
+        out_ref, grad_ref, n_t, grads = refs[count + 9 + len(extra) :]
+        flipped_order = flip_ref[0]
         cos, sin = cos_ref[...], -sin_ref[...]
+
+        def write(index, first_column, values):
+            last_column = first_column + values.shape[1]
+            grads[:, : values.shape[1]] = values
+            for plane in range(planes):
+                for shard in range(shards):
+                    start = (plane * shards + shard) * depth
+                    grad_ref[index * shards + shard, plane, :, first_column:last_column] = grads[
+                        start : start + depth, : values.shape[1]
+                    ].astype(BF16)
+
         n_t[...] = n_ref[...].T
         for index, ref in ((0, mine_ref), (1, other_ref)):
             span = slice(index * kv, (index + 1) * kv)
@@ -549,24 +660,30 @@
                 out_ref[...] = back
             else:
                 out_ref[...] += back
-            grad_ref[index, :, :qkv] = dot_nn(n_t[...], d_raw).astype(BF16)
+            place = flipped_order if index == 0 else 1 - flipped_order
+            write(place, 0, dot_nn(n_t[...], d_raw))
         values = stream_ref[...]
         scale = lax.rsqrt(jnp.mean(values * values, axis=1, keepdims=True) + EPSILON)
         gain = jnp.sum(out_ref[...] * values * scale, axis=0, keepdims=True)
         gain = jnp.broadcast_to(gain, (LANES, model)).T
+        gain_two = jnp.broadcast_to(gain_two_ref[:1, :], (LANES, model)).T
+        n_t[...] = hidden_ref[...].T
+        routing = dot_nn(n_t[...], high_ref[...]) + dot_nn(n_t[...], low_ref[...])
         lane = lax.broadcasted_iota(jnp.int32, (model, LANES), 1)
-        whole_side = jnp.where(lane == 0, gain, side_ref[...])
-        for index in range(2):
-            grad_ref[index, :, qkv : qkv + LANES] = (
-                whole_side * owns_ref[index : index + 1, :]
-            ).astype(BF16)
-            if extra:
-                grad_ref[index, :, qkv + LANES :] = extra_refs[index][...]
-
-    whole = lambda i: (0, 0)
+        whole_side = jnp.where(lane == 0, gain, jnp.where(lane == 1, gain_two, routing))
+        write(0, qkv, whole_side)
+        write(1, qkv, jnp.zeros_like(whole_side))
+        if extra:
+            n_t[...] = extra_refs[0][...].T
+            for index in range(2):
+                write(index, qkv + LANES, dot_nn(n_t[...], extra_refs[index + 1][...]))
+
+    whole = lambda i, *_: (0, 0)
     return pl.pallas_call(
         body,
-        grid=(1,),
+        grid_spec=pltpu.PrefetchScalarGridSpec(
+            num_scalar_prefetch=1,
+            grid=(1,),
         in_specs=[
             pl.BlockSpec((rows, model), whole),
             pl.BlockSpec((rows, 2 * queries), whole),
@@ -577,23 +694,25 @@
             pl.BlockSpec((rows, LANES), whole),
             pl.BlockSpec((rows, LANES), whole),
             pl.BlockSpec((rows, model), whole),
-            pl.BlockSpec((model, LANES), whole),
-            pl.BlockSpec((8, LANES), whole),
         ]
-        + [pl.BlockSpec((model, more), whole) for _ in extra],
+        + [pl.BlockSpec(array.shape, whole) for array in (*side, *extra)],
         out_specs=[
             pl.BlockSpec((rows, model), whole),
-            pl.BlockSpec((2, model, qkv + LANES + more), lambda i: (0, 0, 0)),
+            pl.BlockSpec(
+                (2 * shards, planes, depth, qkv + LANES + more), lambda i, *_: (0, 0, 0, 0)
+            ),
         ],
+        scratch_shapes=[pltpu.VMEM((model, rows), BF16), pltpu.VMEM((model, qkv), F32)],
+        ),
         out_shape=[
             jax.ShapeDtypeStruct((rows, model), F32),
-            jax.ShapeDtypeStruct((2, model, qkv + LANES + more), BF16),
+            jax.ShapeDtypeStruct((2 * shards, planes, depth, qkv + LANES + more), BF16),
         ],
-        scratch_shapes=[pltpu.VMEM((model, rows), BF16)],
         compiler_params=pltpu.CompilerParams(vmem_limit_bytes=VMEM_LIMIT),
         cost_estimate=lasting(14),
         name="qkv_backward",
     )(
+        flip,
         normed,
         d_queries,
         *d_kv_slots,
@@ -601,8 +720,7 @@
         cosines,
         sines,
         stream,
-        side,
-        owns,
+        *side,
         *extra,
     )
 
@@ -862,19 +980,9 @@
     output_half = model // 2
     qkv_mine = halved([head_half(0, misc), head_half(1, jnp.zeros_like(misc))])
     output_mine = halved([w_output[0][:, :output_half], w_output[0][:, output_half:]])
-    down_turned = jnp.swapaxes(w_down[0], 1, 2)
-
-    def expert_half(start):
-        stop = start + half_hidden
-        return jnp.concatenate(
-            [w_gate[0][:, :, start:stop], w_up[0][:, :, start:stop], down_turned[:, :, start:stop]],
-            axis=2,
-        )
-
-    expert_mine = halved([expert_half(0), expert_half(half_hidden)])
 
     plane_order = jnp.stack(
-        [lax.rem(plane - k + planes, planes) for k in range(planes)]
+        [plane] + [partner("expert", k) for k in range(1, planes)]
     ).astype(jnp.int32)
 
     segment_local = mine_of(segments)[0]
@@ -895,25 +1003,43 @@
     )
     chosen_all = jnp.concatenate(slots_of(jnp.swapaxes(chosen, 1, 2), "expert"), axis=2)
 
-    def dense_weights(lined, *held):
+    def dense_weights(lined, held=(), before=()):
         pieces, first_step = ring_gather(lined, 0, held)
+        if before:
+            last = lax.optimization_barrier((pieces[-1][0], *before))[0]
+            pieces[-1] = (last, *pieces[-1][1:])
         owners = jnp.stack([owner for _, owner, _ in pieces]).astype(jnp.int32)
         mine = line_up(pieces, owners, plane_order, shards)
-        return (mine, swap(mine)), [piece for piece, _, _ in pieces[-2:]]
+        return (mine, swap(mine)), first_step, [piece for piece, _, _ in pieces[-2:]]
 
     lined = jnp.stack(slots_of(qkv_mine[0], "expert"))
-    lined = after(lined, chosen_all, segment_all)
-    lined_output = jnp.stack(slots_of(after(output_mine[0], lined), "expert"))
-    first_qkv, ring_end = dense_weights(lined)
+    first_qkv, ring_start, ring_end = dense_weights(lined, before=(chosen_all, segment_all))
+    lined_output = jnp.stack(slots_of(after(output_mine[0], *ring_start), "expert"))
+    own_gate, own_up, own_down, *_ = lax.optimization_barrier(
+        (w_gate[0], w_up[0], w_down[0], *ring_start)
+    )
+    down_turned = jnp.swapaxes(own_down, 1, 2)
+
+    def expert_half(start):
+        stop = start + half_hidden
+        return jnp.concatenate(
+            [own_gate[:, :, start:stop], own_up[:, :, start:stop], down_turned[:, :, start:stop]],
+            axis=2,
+        )
+
+    expert_mine = halved([expert_half(0), expert_half(half_hidden)])
     first_experts = lax.all_gather(
         after(expert_mine[0], *ring_end), ("section", "shard"), axis=0
     )
     second_pack = lax.all_gather(
-        jnp.concatenate([qkv_mine[1], output_mine[1]], axis=1),
-        ("section", "expert", "shard"),
-        axis=0,
-        tiled=True,
-    ).reshape(2, model, half_qkv + LANES + output_half)
+        jnp.concatenate([qkv_mine[1], output_mine[1]], axis=1), "expert", axis=0
+    )
+    second_pack = lax.all_gather(second_pack, ("section", "shard"), axis=0)
+    second_pack = (
+        second_pack.reshape(2, shards, planes, part_rows, -1)
+        .swapaxes(1, 2)
+        .reshape(2, model, half_qkv + LANES + output_half)
+    )
     second_experts = lax.all_gather(expert_mine[1], ("section", "shard"), axis=0)
 
     qkv_columns = half_qkv + LANES
@@ -936,7 +1062,7 @@
     positions = shard * span_rows + jnp.arange(span_rows, dtype=jnp.int32)
     cosines, sines = rotary_tables(positions)
     key_owners = jnp.stack(
-        [lax.rem(shard - k + shards, shards) for k in range(shards)]
+        [shard] + [partner("shard", k) for k in range(1, shards)]
     ).astype(jnp.int32)
     seg_all = jnp.broadcast_to(segment_all[:, None], (seq_rows, LANES))
     seg_own = jnp.broadcast_to(segment_local[None, :], (8, span_rows))
@@ -961,6 +1087,7 @@
             gain_one=gain_one,
             gain_two=gain_two,
             router_full=side[:, 2 : 2 + all_experts],
+            side=side,
             qkv=pair,
             relative=relative,
         )
@@ -997,62 +1124,54 @@
         )
         return partial
 
-    def combine(kept, partial):
-        combined = partial[:span_rows].astype(F32)
+    def combine(kept, partial, *held):
+        combined = after(partial[:span_rows], *held).astype(F32)
         for k in range(1, planes):
-            back = shifted(partial[k * span_rows : (k + 1) * span_rows], "expert", -k)
+            back = crossed_back(partial[k * span_rows : (k + 1) * span_rows], "expert", k)
             combined = combined + back.astype(F32)
         return (kept["middle"] + combined).astype(BF16)
 
-    def backward(layer, kept, grad_rows, later):
+    def backward(layer, kept, grad_rows, earlier):
         grad_low = grad_rows[:span_rows]
-        grad_out = grad_low.astype(F32)
         relative = kept["relative"]
-        d_rows, scores, d_raws, acts = moe_backward_rows(
+        d_rows, d_raws, acts = moe_backward_rows(
             grad_rows, kept["own_gates"], kept["raws"], kept["experts"]
         )
-        scores_turned = scores.T[: max(8, local_experts)]
-        d_hidden = d_rows[:span_rows].astype(F32)
-        d_gates = jnp.zeros((all_experts, span_rows), F32)
-        d_gates = lax.dynamic_update_slice(
-            d_gates, scores_turned[:local_experts, :span_rows], (plane * local_experts, 0)
-        )
+        expert_grads = moe_backward_weights(kept["rows"], grad_rows, d_raws, acts, 2 * shards)
+        backs = [after(d_rows[:span_rows], expert_grads)]
         for k in range(1, planes):
-            span = slice(k * span_rows, (k + 1) * span_rows)
-            d_hidden = d_hidden + shifted(d_rows[span], "expert", -k).astype(F32)
-            back = shifted(scores_turned[:, span], "expert", -k)
-            place = lax.rem(plane + k, planes) * local_experts
-            d_gates = lax.dynamic_update_slice(d_gates, back[:local_experts], (place, 0))
-        expert_grads = moe_backward_weights(kept["rows"], grad_rows, d_raws, acts, 2 * shards)
-        d_hidden = after(d_hidden, expert_grads)
-        scattered = lax.psum_scatter(
-            expert_grads, ("section", "shard"), scatter_dimension=0
-        )
-        gates = kept["gates"]
-        d_gates = d_gates.T
-        d_logits = gates * (d_gates - jnp.sum(gates * d_gates, axis=-1, keepdims=True))
-        d_logits_high = d_logits.astype(BF16)
-        d_logits_low = (d_logits - d_logits_high.astype(F32)).astype(BF16)
-        d_hidden = (
-            d_hidden
-            + dot_nt(d_logits_high, kept["router_full"])
-            + dot_nt(d_logits_low, kept["router_full"])
-        )
-        grad_router = dot_tn(kept["hidden_in"], d_logits_high) + dot_tn(
-            kept["hidden_in"], d_logits_low
-        )
-        d_middle, grad_gain_two = norm_back(
-            d_hidden, kept["middle"], kept["scale_two"], kept["gain_two"]
-        )
-        d_middle = grad_out + d_middle
-        d_branch = d_middle.astype(BF16)
-        branch_parts = parted(d_branch, relative)
-        d_attended = (
-            dot_nt(branch_parts[0], kept["output"][0])
-            + dot_nt(branch_parts[1], kept["output"][1])
-        ).astype(BF16)
-        d_attended = jnp.concatenate(parted(d_attended, relative), axis=1)
-        grad_output = [dot_tn(kept["attended"], part).astype(BF16) for part in branch_parts]
+            backs.append(crossed_back(d_rows[k * span_rows : (k + 1) * span_rows], "expert", k))
+        flip = jnp.reshape(core if relative else 0, (1,)).astype(jnp.int32)
+        places = jnp.stack(
+            [plane] + [partner("expert", k, True) for k in range(1, planes)]
+        ).astype(jnp.int32)
+        d_middle, d_branch, d_attended, logits_high, logits_low, d_gain_two = branch_backward(
+            backs,
+            places,
+            local_experts,
+            jnp.pad(kept["gates"], ((0, 0), (2, LANES - 2 - all_experts))),
+            kept["side"],
+            kept["middle"],
+            kept["gain_two"][None],
+            grad_low,
+            kept["output"],
+            flip,
+        )
+        sent_grads = after(expert_grads, d_branch)
+        if earlier is not None:
+            sent_grads, earlier = lax.optimization_barrier((sent_grads, earlier))
+        scattered = lax.psum_scatter(sent_grads, ("section", "shard"), scatter_dimension=0)
+        branch_halves = [d_branch[:, :output_half], d_branch[:, output_half:]]
+        grad_output = None
+        if layer == 0:
+            grad_output = jnp.stack(
+                [dot_tn(kept["attended"], part).astype(BF16) for part in branch_halves]
+            )
+            grad_output = (
+                grad_output.reshape(2, planes, shards, part_rows, output_half)
+                .swapaxes(1, 2)
+                .reshape(2 * shards, planes, part_rows, output_half)
+            )
         d_query_raw, *d_slots = attention_backward(
             kept["query_rot"],
             kept["kv_slots"],
@@ -1064,25 +1183,16 @@
             cosines,
             sines,
         )
+        result = None
+        if layer == 1:
+            partial = after(kept["partial"], d_branch)
+            result = combine(kept, partial, d_slots[0])
+            d_query_raw, result = lax.optimization_barrier((d_query_raw, result))
+        else:
+            grad_output = sum_over("expert", grad_output)
         d_kv_slots = [d_slots[0]] + [
-            shifted(d_slots[k], "shard", -k) for k in range(1, shards)
+            crossed_back(d_slots[k], "shard", k) for k in range(1, shards)
         ]
-        if layer == 1:
-            result = combine(kept, after(kept["partial"], d_hidden))
-            d_query_raw = after(d_query_raw, result)
-        else:
-            result = None
-            d_query_raw = after(d_query_raw, later)
-        lane = jnp.arange(LANES)[None, :]
-        grad_side = jnp.where(
-            lane == 1,
-            grad_gain_two[:, None],
-            jnp.pad(grad_router, ((0, 0), (2, LANES - 2 - all_experts))),
-        )
-        owner = core if relative else 0
-        owns = jnp.broadcast_to(
-            (jnp.arange(8, dtype=jnp.int32) == owner).astype(F32)[:, None], (8, LANES)
-        )
         stream = kept["stream"]
         d_normed, packed = qkv_backward(
             kept["normed"],
@@ -1093,63 +1203,51 @@
             sines,
             (half_query, 2 * half_kv),
             stream,
-            grad_side,
-            owns,
-            grad_output if layer == 1 else [],
+            (kept["hidden_in"], logits_high, logits_low, d_gain_two),
+            flip,
+            [kept["attended"], *branch_halves] if layer == 1 else [],
+            (shards, planes),
         )
         scale_one = lax.rsqrt(jnp.mean(stream * stream, axis=-1, keepdims=True) + EPSILON)
         d_stream, _ = norm_back(d_normed, stream, scale_one, kept["gain_one"])
         d_stream = (d_middle + d_stream).astype(BF16)
-        return d_stream, scattered, packed, grad_output, result
-
-    def dense_scatter(halves, swapped, *held):
-        width = halves[0].shape[1]
-        size = (planes, shards, part_rows, width)
-        kept = halves[0].reshape(size)
-        received = swapped.reshape(size)
+        return d_stream, scattered, packed, grad_output, earlier, result
+
+    homes = {"shard": (shard, shards, 0), "expert": (plane, planes, 1)}
+
+    def place_of(axis, k):
+        return partner(axis, k, True) if k else homes[axis][0]
+
+    def sum_over(axis, array):
+        size = (shards, *array.shape[1:])
+        kept = lax.dynamic_slice(array, (core * shards, 0, 0, 0), size)
+        received = swap(lax.dynamic_slice(array, ((1 - core) * shards, 0, 0, 0), size))
+        _, count, dim = homes[axis]
+
+        def chunk(k):
+            place = place_of(axis, k)
+            return lax.dynamic_index_in_dim(kept, place, dim, keepdims=False).astype(
+                F32
+            ) + lax.dynamic_index_in_dim(received, place, dim, keepdims=False).astype(F32)
+
+        total = chunk(0)
+        for k in range(1, count):
+            total = total + crossed_back(chunk(k).astype(BF16), axis, k).astype(F32)
+        return total
+
+    def sum_rest(axis, total, *held):
+        result = lax.dynamic_index_in_dim(total, place_of(axis, 0), 0, keepdims=False)
         if held:
-            received = after(received, *held)
-
-        def chunk(owner, start, stop):
-            place = (start, owner, 0, 0)
-            part = (stop - start, 1, part_rows, width)
-            summed = lax.dynamic_slice(kept, place, part).astype(F32) + lax.dynamic_slice(
-                received, place, part
-            ).astype(F32)
-            return summed[:, 0].astype(BF16)
-
-        if shards == 4:
-            middle = planes // 2
-            chunks = [
-                chunk(shard, 0, planes),
-                chunk(shard ^ 1, 0, planes),
-                chunk(shard ^ 2, 0, planes),
-                chunk(shard ^ 3, 0, middle),
-                chunk(shard ^ 3, middle, planes),
-            ]
-        else:
-            chunks = [
-                chunk(lax.rem(shard - k + shards, shards), 0, planes) for k in range(shards)
-            ]
-        first_step = scatter_first(chunks, 0)
-        second_step = scatter_second(chunks, first_step, 0)
-        lined = scatter_end(chunks, first_step, second_step, 0)
-        return {"first": first_step, "second": second_step, "lined": lined}
-
-    def plane_scatter(lined):
-        total = lax.dynamic_index_in_dim(lined, plane, 0, keepdims=False)
-        for k in range(1, planes):
-            sent = lax.dynamic_index_in_dim(
-                lined, lax.rem(plane - k + planes, planes), 0, keepdims=False
-            )
-            total = total + shifted(sent.astype(BF16), "expert", -k).astype(F32)
-        return total
-
-    def regrouped(halves):
+            result = after(result, *held)
+        for k in range(1, homes[axis][1]):
+            part = lax.dynamic_index_in_dim(total, place_of(axis, k), 0, keepdims=False)
+            result = result + crossed_back(part.astype(BF16), axis, k).astype(F32)
+        return result.astype(BF16)
+
+    def exchanged(halves):
         kept = jnp.where(first, halves[0], halves[1])
         sent = jnp.where(first, halves[1], halves[0])
-        received = swap(sent.astype(BF16)).astype(F32)
-        return by_layer(kept, received)
+        return kept, swap(sent)
 
     start = mine_of(inputs)[0]
     side = jnp.where(
@@ -1158,7 +1256,9 @@
     attended, kept_one = attend(
         start.astype(F32), [(half[None], 0) for half in first_qkv], side, True
     )
-    first_output, _ = dense_weights(after(lined_output, *ring_end), kept_one["query_rot"])
+    first_output, _, _ = dense_weights(
+        after(lined_output, *ring_end), held=(kept_one["query_rot"],)
+    )
     rows = gathered_rows_of(kept_one, attended, first_output)
     result_one = combine(kept_one, mix(0, kept_one, rows, first_experts))
 
@@ -1170,22 +1270,27 @@
         False,
     )
     attended = after(attended, last_rows)
-    rows = gathered_rows_of(kept_two, attended, [half[:, qkv_columns:] for half in second_pack])
-    mix(1, kept_two, rows, second_experts)
-
-    grad_mid, scattered_two, packed_two, _, result_two = backward(1, kept_two, last_rows, None)
-    pack_two = lax.psum_scatter(
-        packed_two.reshape(2 * model, packed_two.shape[2]),
-        ("section", "expert", "shard"),
-        scatter_dimension=0,
-        tiled=True,
+    rows = gathered_rows_of(
+        kept_two, attended, [second_pack[half, :, qkv_columns:] for half in range(2)]
+    )
+    partial = mix(1, kept_two, rows, second_experts)
+    grad_mid, scattered_two, packed_two, _, _, result_two = backward(
+        1, kept_two, last_rows, None
     )
     mid_rows = jnp.concatenate(slots_of(grad_mid, "expert"), axis=0)
-    mid_rows = after(mid_rows, scattered_two)
-    grad_start, scattered_one, packed_one, output_one, _ = backward(
+    packed_two, scattered_two, _ = lax.optimization_barrier((packed_two, scattered_two, mid_rows))
+    pack_two = lax.psum_scatter(packed_two, ("section", "shard"), scatter_dimension=0)
+    grad_start, scattered_one, packed_one, output_one, pack_two, _ = backward(
         0, kept_one, mid_rows, pack_two
     )
-    qkv_one = [packed_one[0], packed_one[1]]
+    qkv_one = sum_over("shard", packed_one)
+    qkv_one, output_one = lax.optimization_barrier((qkv_one, output_one))
+    pack_two, scattered_one, _ = lax.optimization_barrier((pack_two, scattered_one, qkv_one))
+    pack_two = lax.psum_scatter(pack_two, "expert", scatter_dimension=0)
+    expert_mine_half, expert_other_half = exchanged([scattered_one, scattered_two])
+    grad_gate, grad_up, grad_down = expert_outputs(expert_mine_half, expert_other_half, core)
+    qkv_one = sum_rest("expert", qkv_one, grad_gate)
+    output_one = sum_rest("shard", output_one)
 
     def placed(by_layers):
         own = jnp.where(first, by_layers[0], by_layers[1])
@@ -1194,13 +1299,9 @@
 
     layer_local = placed([result_one, result_two])
     input_local = placed([grad_start, grad_mid])
-    expert_low, expert_high = regrouped([scattered_one, scattered_two])
-    output_scatter = dense_scatter(output_one, swap(output_one[1]))
-    qkv_scatter = dense_scatter(qkv_one, swap(qkv_one[1]))
-    dense_one = jnp.concatenate(
-        [plane_scatter(qkv_scatter["lined"]), plane_scatter(output_scatter["lined"])], axis=1
-    )
-    dense_low, dense_high = regrouped([dense_one, pack_two.astype(F32)])
+    dense_one = jnp.concatenate([qkv_one, output_one], axis=1)
+    dense_low, dense_high = by_layer(*exchanged([dense_one, pack_two]))
+    dense_low, dense_high = dense_low.astype(F32), dense_high.astype(F32)
 
     def both(start, stop):
         return jnp.concatenate([dense_low[:, start:stop], dense_high[:, start:stop]], axis=1)
@@ -1216,11 +1317,6 @@
         )
 
     side = dense_low[:, half_qkv:qkv_columns]
-
-    def third(index):
-        start = index * half_hidden
-        stop = start + half_hidden
-        return jnp.concatenate([expert_low[:, :, start:stop], expert_high[:, :, start:stop]], axis=2)
 
     out_shape = (1, 2, 1, span_rows, model)
     return (
@@ -1233,9 +1329,9 @@
         both(qkv_columns, qkv_columns + output_half)[None],
         side[:, 1][None],
         side[:, 2 : 2 + all_experts][None],
-        third(0)[None],
-        third(1)[None],
-        jnp.swapaxes(third(2), 1, 2)[None],
+        grad_gate[None],
+        grad_up[None],
+        grad_down[None],
     )
 
 

time: 1520 us -> 1330 us (0.88)
  waiting for transfers between devices: 811 us -> 662 us
  matrix products: 33.9 us -> 10.4 us
  starting transfers between devices: 103 us -> 86.6 us
    ppermute x20 -> x8, waiting for transfers between devices: 133 us -> 51.6 us  [flipped(): lax.ppermute(array, 'shard', [(i, i ^ mask) for i in range(lax.axis_size(...]
    ppermute x60, waiting for transfers between devices: 620 us -> 584 us  [crossed(): return lax.ppermute(array, axis, [(i, i ^ by) for i in range(length)])]
    pallas_call x2 -> x5, Pallas kernels: 30.1 us -> 56 us  [the longest x2 30.5 us: qkv_backward(): pl.pallas_call(body, grid_spec=pltpu.PrefetchScalarGridSpec(num_scalar_pr...]
    all_gather x1 -> x2, waiting for transfers between devices: 33.6 us -> 10.1 us  [the longest x1 10.1 us: on_device(): lax.all_gather(jnp.concatenate([qkv_mine[1], output_mine[1]], axis=1), 'e...]
  transfers between devices with their start and end apart: 98 -> 88, of which waited for: 57 -> 54; matrix products, arithmetic and copies ran while one was open for 10% -> 10% of each run, Pallas kernels for 17% -> 23%
where the time goes in v3:
time: 1330 us; the launch traced here: 1320 us
  waiting for transfers between devices  662 us (50%)
  Pallas kernels  386 us (29%)
  starting transfers between devices  86.6 us (7%)
  local copies, waits for them, and re-layouts  82.6 us (6%)
  other arithmetic  76.5 us (6%)
  between operations  15.8 us (1%)
    ppermute x60, waiting for transfers between devices, crossed(): return lax.ppermute(array, axis, [(i, i ^ by) for i in range(length)])  584 us
    pallas_call x2, Pallas kernels, moe_backward_rows(): pl.pallas_call(body, grid_spec=pltpu.PrefetchScalarGridSpec(num_scalar_pr...  81.4 us
    pallas_call x2, Pallas kernels, moe_forward(): pl.pallas_call(body, grid_spec=pltpu.PrefetchScalarGridSpec(num_scalar_pr...  69 us
    pallas_call x2, Pallas kernels, moe_backward_weights(): pl.pallas_call(body, grid_spec=pltpu.PrefetchScalarGridSpec(num_scalar_pr...  67 us
    ppermute x60, starting transfers between devices, crossed(): return lax.ppermute(array, axis, [(i, i ^ by) for i in range(length)])  55.6 us
    pallas_call x2, Pallas kernels, attention_backward(): pl.pallas_call(body, grid_spec=pltpu.PrefetchScalarGridSpec(num_scalar_pr...  53.7 us
    ppermute x8, waiting for transfers between devices, flipped(): lax.ppermute(array, 'shard', [(i, i ^ mask) for i in range(lax.axis_size(...  51.6 us
    pallas_call x2, Pallas kernels, attention_forward(): pl.pallas_call(body, grid_spec=pltpu.PrefetchScalarGridSpec(num_scalar_pr...  34.7 us
  transfers between devices with their start and end apart: 88, of which 54 were waited for; matrix products, arithmetic and copies ran while one was open for 10% of the time, Pallas kernels for 23%

profile of v3, /device:TPU:9, one launch (start us, length us, event | category | flops | bytes accessed | tf_op | source)
XLA Modules:
  0.0 1320.0 jit_solution(451673927493049564)
XLA Ops:
  19.3 8.4 collective-permute-done.4
  31.2 11.5 collective-permute-done.6
  49.0 19.0 %collective-permute-done.7.refs_1_ = bf16[4,96,1408]{2,1,0:T(8,128)(2,1)} collective-permute-done((bf16[4,96,1408]{2,1,0:T(8,128)(2,1)}, bf16[4,96,1408]{2,1,0:T(8,128)(2,1)}, u32[]{:S(2)}, u32[]{:S(2)}) %collective-permute-start.7) | collective-permute-done | bytes 1081376 | tf_op jit(solution)/shard_map/ppermute | solution.py:43
  94.5 9.1 collective-permute-done.10.refs_4_
  104.4 4.9 broadcast_select_fusion.2
  110.3 10.1 all-gather.11.cloned.1.call-done
  122.3 5.3 line_up.2
  137.2 4.1 collective-permute-done.21
  141.4 4.4 collective-permute-done.22
  151.9 7.4 qkv_forward.2
  159.3 14.2 %collective-permute-done.23.refs_1_ = bf16[4,96,768]{2,1,0:T(8,128)(2,1)S(1)} collective-permute-done((bf16[4,96,768]{2,1,0:T(8,128)(2,1)S(1)}, bf16[4,96,768]{2,1,0:T(8,128)(2,1)S(1)}, u32[]{:S(2)}, u32[]{:S(2)}) %collective-permute-start.23) | collective-permute-done | bytes 589856 | tf_op jit(solution)/shard_map/ppermute | solution.py:43
  179.0 7.2 collective-permute-done.25.refs_3_
  187.7 4.1 line_up.3.refs_9_
  199.6 22.2 %collective-permute-done.18.refs_3_ = bf16[256,1024]{1,0:T(8,128)(2,1)} collective-permute-done((bf16[256,1024]{1,0:T(8,128)(2,1)}, bf16[256,1024]{1,0:T(8,128)(2,1)}, u32[]{:S(2)}, u32[]{:S(2)}) %collective-permute-start.18) | collective-permute-done | bytes 524320 | tf_op jit(solution)/shard_map/ppermute | solution.py:50
  223.4 17.4 %attention_forward.2 = (bf16[256,1536]{1,0:T(8,128)(2,1)}, f32[4,8,256]{2,1,0:T(8,128)}) custom-call(s32[4]{0:T(128)} %pad_add_fusion.1.owner_ref, s32[1024,128]{1,0:T(8,128)} %broadcast_in_dim.37.seg_all_ref, s32[8,256]{1,0:T(8,128)} %broadcast_in_dim.38.seg_ref, bf16[256,1536]{1,0:T(8,128)(2,1)} %get-tuple-element.90.q_ref, ...), custom_call_target="tpu_custom_call" | custom-call | flops 18699999232 | bytes 1000000 | tf_op jit(solution)/shard_map/attention_forward/pallas_call | solution.py:801
  251.0 26.8 %collective-permute-done.28 = bf16[256,1536]{1,0:T(8,128)(2,1)} collective-permute-done((bf16[256,1536]{1,0:T(8,128)(2,1)}, bf16[256,1536]{1,0:T(8,128)(2,1)}, u32[]{:S(2)}, u32[]{:S(2)}) %collective-permute-start.28) | collective-permute-done | bytes 786464 | tf_op jit(solution)/shard_map/ppermute | solution.py:50
  281.9 33.7 %collective-permute-done.30 = bf16[256,1536]{1,0:T(8,128)(2,1)} collective-permute-done((bf16[256,1536]{1,0:T(8,128)(2,1)}, bf16[256,1536]{1,0:T(8,128)(2,1)}, u32[]{:S(2)}, u32[]{:S(2)}) %collective-permute-start.30) | collective-permute-done | bytes 786464 | tf_op jit(solution)/shard_map/ppermute | solution.py:50
  321.8 34.7 %moe_forward.2 = (bf16[1024,1536]{1,0:T(8,128)(2,1)}, bf16[5,1024,1024]{2,1,0:T(8,128)(2,1)}) custom-call(bf16[1024,1536]{1,0:T(8,128)(2,1)} %copy-done.30, f32[1024,128]{1,0:T(8,128)} %pad.14.gates_ref, bf16[8,5,384,768]{3,2,1,0:T(8,128)(2,1)} %bitcast.240), custom_call_target="tpu_custom_call" | custom-call | flops 44000002048 | bytes 1000000 | tf_op jit(solution)/shard_map/moe_forward/pallas_call | solution.py:198
  362.8 7.9 copy.100
  370.7 4.7 copy-done.2
  376.4 12.8 collective-permute-done.32
  392.5 33.7 %collective-permute-done.34 = bf16[256,1536]{1,0:T(8,128)(2,1)} collective-permute-done((bf16[256,1536]{1,0:T(8,128)(2,1)}, bf16[256,1536]{1,0:T(8,128)(2,1)}, u32[]{:S(2)}, u32[]{:S(2)}) %collective-permute-start.34) | collective-permute-done | bytes 786464 | tf_op jit(solution)/shard_map/ppermute | solution.py:50
  429.5 7.8 qkv_forward.3
  443.4 17.2 %collective-permute-done.35.refs_1_ = bf16[256,1024]{1,0:T(8,128)(2,1)} collective-permute-done((bf16[256,1024]{1,0:T(8,128)(2,1)}, bf16[256,1024]{1,0:T(8,128)(2,1)}, u32[]{:S(2)}, u32[]{:S(2)}) %collective-permute-start.35) | collective-permute-done | bytes 524320 | tf_op jit(solution)/shard_map/ppermute | solution.py:50
  461.8 20.5 %collective-permute-done.37.refs_3_ = bf16[256,1024]{1,0:T(8,128)(2,1)} collective-permute-done((bf16[256,1024]{1,0:T(8,128)(2,1)}, bf16[256,1024]{1,0:T(8,128)(2,1)}, u32[]{:S(2)}, u32[]{:S(2)}) %collective-permute-start.37) | collective-permute-done | bytes 524320 | tf_op jit(solution)/shard_map/ppermute | solution.py:50
  482.3 17.2 %attention_forward.3 = (bf16[256,1536]{1,0:T(8,128)(2,1)}, f32[4,8,256]{2,1,0:T(8,128)}) custom-call(s32[4]{0:T(128)} %pad_add_fusion.1.owner_ref, s32[1024,128]{1,0:T(8,128)} %broadcast_in_dim.37.seg_all_ref, s32[8,256]{1,0:T(8,128)} %broadcast_in_dim.38.seg_ref, bf16[256,1536]{1,0:T(8,128)(2,1)} %get-tuple-element.102.q_ref, ...), custom_call_target="tpu_custom_call" | custom-call | flops 18699999232 | bytes 1000000 | tf_op jit(solution)/shard_map/attention_forward/pallas_call | solution.py:801
  501.5 7.4 collective-permute-done.40
  518.6 4.8 slice_bitcast_fusion
  523.5 21.5 %collective-permute-done.41 = bf16[256,1536]{1,0:T(8,128)(2,1)S(1)} collective-permute-done((bf16[256,1536]{1,0:T(8,128)(2,1)S(1)}, bf16[256,1536]{1,0:T(8,128)(2,1)S(1)}, u32[]{:S(2)}, u32[]{:S(2)}) %collective-permute-start.41) | collective-permute-done | bytes 786464 | tf_op jit(solution)/shard_map/ppermute | solution.py:50
  548.4 34.7 %collective-permute-done.43 = bf16[256,1536]{1,0:T(8,128)(2,1)S(1)} collective-permute-done((bf16[256,1536]{1,0:T(8,128)(2,1)S(1)}, bf16[256,1536]{1,0:T(8,128)(2,1)S(1)}, u32[]{:S(2)}, u32[]{:S(2)}) %collective-permute-start.43) | collective-permute-done | bytes 786464 | tf_op jit(solution)/shard_map/ppermute | solution.py:50
  587.0 34.2 %moe_forward.3 = (bf16[1024,1536]{1,0:T(8,128)(2,1)}, bf16[5,1024,1024]{2,1,0:T(8,128)(2,1)}) custom-call(bf16[1024,1536]{1,0:T(8,128)(2,1)} %copy-done.31, f32[1024,128]{1,0:T(8,128)} %pad.15.gates_ref, bf16[8,5,384,768]{3,2,1,0:T(8,128)(2,1)} %bitcast.242), custom_call_target="tpu_custom_call" | custom-call | flops 44000002048 | bytes 1000000 | tf_op jit(solution)/shard_map/moe_forward/pallas_call | solution.py:198
  621.3 40.6 %moe_backward_rows.2 = (bf16[1024,1664]{1,0:T(8,128)(2,1)}, bf16[5,1024,1024]{2,1,0:T(8,128)(2,1)}, bf16[5,1024,512]{2,1,0:T(8,128)(2,1)}) custom-call(bf16[1024,1536]{1,0:T(8,128)(2,1)} %constant_dynamic-update-slice_fusion.9.grads_ref, f32[1024,128]{1,0:T(8,128)} %pad.15.gates_ref, bf16[5,1024,1024]{2,1,0:T(8,128)(2,1)} %get-tuple-element.107.raw_ref, ...), custom_call_target="tpu_custom_call" | custom-call | flops 52800000000 | bytes 1000000 | tf_op jit(solution)/shard_map/moe_backward_rows/pallas_call | solution.py:293
  667.6 33.3 %moe_backward_weights.2 = bf16[8,5,384,768]{3,2,1,0:T(8,128)(2,1)} custom-call(bf16[1024,1536]{1,0:T(8,128)(2,1)} %copy-done.31, bf16[1024,1536]{1,0:T(8,128)(2,1)} %constant_dynamic-update-slice_fusion.9.grads_ref, bf16[5,1024,1024]{2,1,0:T(8,128)(2,1)} %get-tuple-element.109.d_raw_ref, bf16[5,1024,512]{2,1,0:T(8,128)(2,1)} %get-tuple-element.110.act_ref), custom_call_target="tpu_custom_call" | custom-call | flops 37399998464 | bytes 1000000 | tf_op jit(solution)/shard_map/moe_backward_weights/pallas_call | solution.py:355
  701.7 35.5 %collective-permute-done.46.refs_3_ = bf16[256,1664]{1,0:T(8,128)(2,1)} collective-permute-done((bf16[256,1664]{1,0:T(8,128)(2,1)S(1)}, bf16[256,1664]{1,0:T(8,128)(2,1)}, u32[]{:S(2)}, u32[]{:S(2)}) %collective-permute-start.46) | collective-permute-done | bytes 852000 | tf_op jit(solution)/shard_map/ppermute | solution.py:50
  737.3 8.8 branch_backward.2
  751.7 27.0 %attention_backward.2 = (bf16[256,1536]{1,0:T(8,128)(2,1)}, bf16[256,1024]{1,0:T(8,128)(2,1)}, bf16[256,1024]{1,0:T(8,128)(2,1)}, bf16[256,1024]{1,0:T(8,128)(2,1)}, bf16[256,1024]{1,0:T(8,128)(2,1)}) custom-call(s32[4]{0:T(128)} %pad_add_fusion.1.owner_ref, s32[1024,128]{1,0:T(8,128)} %broadcast_in_dim.37.seg_all_ref, s32[8,256]{1,0:T(8,128)} %broadcast_in_dim.38.seg_ref, ...), custom_call_target="tpu_custom_call" | custom-call | flops 29699999744 | bytes 1000000 | tf_op jit(solution)/shard_map/attention_backward/pallas_call | solution.py:879
  783.7 30.9 %collective-permute-done.49 = bf16[256,1536]{1,0:T(8,128)(2,1)} collective-permute-done((bf16[256,1536]{1,0:T(8,128)(2,1)S(1)}, bf16[256,1536]{1,0:T(8,128)(2,1)}, u32[]{:S(2)}, u32[]{:S(2)}) %collective-permute-start.49) | collective-permute-done | bytes 786464 | tf_op jit(solution)/shard_map/ppermute | solution.py:50
  818.8 16.9 %qkv_backward.2 = (f32[256,1536]{1,0:T(8,128)}, bf16[8,4,96,2176]{3,2,1,0:T(8,128)(2,1)}) custom-call(s32[1]{0:T(128)} %constant.282.clone.1.flip_ref, bf16[256,1536]{1,0:T(8,128)(2,1)} %get-tuple-element.122.n_ref, bf16[256,1536]{1,0:T(8,128)(2,1)} %get-tuple-element.123.dq_ref, bf16[256,1024]{1,0:T(8,128)(2,1)} %get-tuple-element.118.refs_0_, ...), custom_call_target="tpu_custom_call" | custom-call | flops 15399999488 | bytes 1000000 | tf_op jit(solution)/shard_map/qkv_backward/pallas_call | solution.py:682
  840.9 24.5 %collective-permute-done.54 = bf16[256,1536]{1,0:T(8,128)(2,1)S(1)} collective-permute-done((bf16[256,1536]{1,0:T(8,128)(2,1)S(1)}, bf16[256,1536]{1,0:T(8,128)(2,1)S(1)}, u32[]{:S(2)}, u32[]{:S(2)}) %collective-permute-start.54) | collective-permute-done | bytes 786464 | tf_op jit(solution)/shard_map/ppermute | solution.py:50
  866.7 35.6 %collective-permute-done.56 = bf16[256,1536]{1,0:T(8,128)(2,1)S(1)} collective-permute-done((bf16[256,1536]{1,0:T(8,128)(2,1)S(1)}, bf16[256,1536]{1,0:T(8,128)(2,1)S(1)}, u32[]{:S(2)}, u32[]{:S(2)}) %collective-permute-start.56) | collective-permute-done | bytes 786464 | tf_op jit(solution)/shard_map/ppermute | solution.py:50
  904.1 5.3 reduce-scatter.5.cloned.1.call-done
  911.5 40.8 %moe_backward_rows.3 = (bf16[1024,1664]{1,0:T(8,128)(2,1)}, bf16[5,1024,1024]{2,1,0:T(8,128)(2,1)}, bf16[5,1024,512]{2,1,0:T(8,128)(2,1)}) custom-call(bf16[1024,1536]{1,0:T(8,128)(2,1)} %pad_maximum_fusion.3.grads_ref, f32[1024,128]{1,0:T(8,128)} %pad.14.gates_ref, bf16[5,1024,1024]{2,1,0:T(8,128)(2,1)} %get-tuple-element.131.raw_ref, ...), custom_call_target="tpu_custom_call" | custom-call | flops 52800000000 | bytes 1000000 | tf_op jit(solution)/shard_map/moe_backward_rows/pallas_call | solution.py:293
  958.0 33.6 %moe_backward_weights.3 = bf16[8,5,384,768]{3,2,1,0:T(8,128)(2,1)} custom-call(bf16[1024,1536]{1,0:T(8,128)(2,1)} %copy-done.30, bf16[1024,1536]{1,0:T(8,128)(2,1)} %pad_maximum_fusion.3.grads_ref, bf16[5,1024,1024]{2,1,0:T(8,128)(2,1)} %get-tuple-element.133.d_raw_ref, bf16[5,1024,512]{2,1,0:T(8,128)(2,1)} %get-tuple-element.134.act_ref), custom_call_target="tpu_custom_call" | custom-call | flops 37399998464 | bytes 1000000 | tf_op jit(solution)/shard_map/moe_backward_weights/pallas_call | solution.py:355
  994.5 35.4 %collective-permute-done.59.refs_3_ = bf16[256,1664]{1,0:T(8,128)(2,1)} collective-permute-done((bf16[256,1664]{1,0:T(8,128)(2,1)S(1)}, bf16[256,1664]{1,0:T(8,128)(2,1)}, u32[]{:S(2)}, u32[]{:S(2)}) %collective-permute-start.59) | collective-permute-done | bytes 852000 | tf_op jit(solution)/shard_map/ppermute | solution.py:50
  1029.9 8.8 branch_backward.3
  1038.8 26.8 %attention_backward.3 = (bf16[256,1536]{1,0:T(8,128)(2,1)}, bf16[256,1024]{1,0:T(8,128)(2,1)}, bf16[256,1024]{1,0:T(8,128)(2,1)}, bf16[256,1024]{1,0:T(8,128)(2,1)}, bf16[256,1024]{1,0:T(8,128)(2,1)}) custom-call(s32[4]{0:T(128)} %pad_add_fusion.1.owner_ref, s32[1024,128]{1,0:T(8,128)} %broadcast_in_dim.37.seg_all_ref, s32[8,256]{1,0:T(8,128)} %broadcast_in_dim.38.seg_ref, ...), custom_call_target="tpu_custom_call" | custom-call | flops 29699999744 | bytes 1000000 | tf_op jit(solution)/shard_map/attention_backward/pallas_call | solution.py:879
  1068.5 7.8 collective-permute-done.60.refs_1_
  1079.4 15.4 %collective-permute-done.62.refs_3_ = bf16[256,1024]{1,0:T(8,128)(2,1)S(1)} collective-permute-done((bf16[256,1024]{1,0:T(8,128)(2,1)}, bf16[256,1024]{1,0:T(8,128)(2,1)S(1)}, u32[]{:S(2)}, u32[]{:S(2)}) %collective-permute-start.62) | collective-permute-done | bytes 524320 | tf_op jit(solution)/shard_map/ppermute | solution.py:50
  1095.5 13.6 %qkv_backward.3 = (f32[256,1536]{1,0:T(8,128)}, bf16[8,4,96,1408]{3,2,1,0:T(8,128)(2,1)}) custom-call(s32[1]{0:T(128)} %bitcast.58.flip_ref.core_ref, bf16[256,1536]{1,0:T(8,128)(2,1)} %get-tuple-element.137.n_ref, bf16[256,1536]{1,0:T(8,128)(2,1)} %get-tuple-element.140.dq_ref, bf16[256,1024]{1,0:T(8,128)(2,1)} %get-tuple-element.141.refs_0_, ...), custom_call_target="tpu_custom_call" | custom-call | flops 15399999488 | bytes 1000000 | tf_op jit(solution)/shard_map/qkv_backward/pallas_call | solution.py:682
  1109.2 4.9 constant_dynamic-slice_fusion.1
  1114.1 8.9 collective-permute-start.64
  1128.0 5.7 collective-permute-done.68
  1137.1 5.1 fusion.10
  1147.8 7.3 collective-permute-done.69
  1156.0 28.6 %collective-permute-done.70 = bf16[4,96,768]{2,1,0:T(8,128)(2,1)} collective-permute-done((bf16[4,96,768]{2,1,0:T(8,128)(2,1)}, bf16[4,96,768]{2,1,0:T(8,128)(2,1)}, u32[]{:S(2)}, u32[]{:S(2)}) %collective-permute-start.70) | collective-permute-done | bytes 589856 | tf_op jit(solution)/shard_map/ppermute | solution.py:50
  1184.7 4.3 collective-permute-start.50
  1189.0 8.9 collective-permute-done.71
  1200.8 27.4 %collective-permute-done.67 = bf16[4,96,1408]{2,1,0:T(8,128)(2,1)} collective-permute-done((bf16[4,96,1408]{2,1,0:T(8,128)(2,1)}, bf16[4,96,1408]{2,1,0:T(8,128)(2,1)}, u32[]{:S(2)}, u32[]{:S(2)}) %collective-permute-start.67) | collective-permute-done | bytes 1081376 | tf_op jit(solution)/shard_map/ppermute | solution.py:50
  1228.2 4.2 fusion.1
  1234.9 5.7 broadcast_select_fusion
  1259.9 7.9 expert_outputs.1
  1267.8 8.6 collective-permute-done.73
  1276.3 4.5 collective-permute-done.74
  1280.8 19.6 %collective-permute-done.75 = bf16[96,1408]{1,0:T(8,128)(2,1)} collective-permute-done((bf16[96,1408]{1,0:T(8,128)(2,1)S(1)}, bf16[96,1408]{1,0:T(8,128)(2,1)}, u32[]{:S(2)}, u32[]{:S(2)}) %collective-permute-start.75) | collective-permute-done | bytes 270368 | tf_op jit(solution)/shard_map/ppermute | solution.py:50
  (439 shorter events, 242.8 us)
Async XLA Ops:
  7.2 113.2 %all-gather.11.cloned.1.call-start = ((), (), s32[]{:S(2)}) async-start(), calls=%async_computation.9 | async-start | bytes 2088960 | tf_op jit(solution)/shard_map/all_gather | solution.py:1034
  19.2 23.5 %collective-permute-start.6 = (bf16[96,1408]{1,0:T(8,128)(2,1)S(1)}, bf16[96,1408]{1,0:T(8,128)(2,1)S(1)}, u32[]{:S(2)}, u32[]{:S(2)}) collective-permute-start(bf16[96,1408]{1,0:T(8,128)(2,1)S(1)} %get-tuple-element.305), channel_id=1, source_target_pairs={{0,12},{4,8},{8,4},{12,0},{1,13},{5,9},{9,5},{13,1},{2,14},{6,10},... | collective-permute-start | bytes 811016 | tf_op jit(solution)/shard_map/ppermute | solution.py:50
  43.9 24.2 %collective-permute-start.7 = (bf16[4,96,1408]{2,1,0:T(8,128)(2,1)}, bf16[4,96,1408]{2,1,0:T(8,128)(2,1)}, u32[]{:S(2)}, u32[]{:S(2)}) collective-permute-start(bf16[4,96,1408]{2,1,0:T(8,128)(2,1)} %pad_maximum_fusion.6.refs_0_), channel_id=1, source_target_pairs={{0,1},{1,0},{2,3},{3,2},{4,5},{5,4},{6,7},{7,6},{8,9},{9,8},{10,11... | collective-permute-start | bytes 3244040 | tf_op jit(solution)/shard_map/ppermute | solution.py:43
  45.1 23.9 %collective-permute-start.8 = (bf16[4,96,1408]{2,1,0:T(8,128)(2,1)}, bf16[4,96,1408]{2,1,0:T(8,128)(2,1)}, u32[]{:S(2)}, u32[]{:S(2)}) collective-permute-start(bf16[4,96,1408]{2,1,0:T(8,128)(2,1)} %pad_maximum_fusion.6.refs_0_), channel_id=1, source_target_pairs={{0,2},{1,3},{2,0},{3,1},{4,6},{5,7},{6,4},{7,5},{8,10},{9,11},{10,... | collective-permute-start | bytes 3244040 | tf_op jit(solution)/shard_map/ppermute | solution.py:43
  72.1 32.3 %collective-permute-start.31 = (bf16[5,384,768]{2,1,0:T(8,128)(2,1)}, bf16[5,384,768]{2,1,0:T(8,128)(2,1)}, u32[]{:S(2)}, u32[]{:S(2)}) collective-permute-start(bf16[5,384,768]{2,1,0:T(8,128)(2,1)} %broadcast_select_fusion.4), channel_id=1, source_target_pairs={{0,16},{16,0},{1,17},{17,1},{2,18},{18,2},{3,19},{19,3},{4,20},{20... | collective-permute-start | bytes 8847368 | tf_op jit(solution)/shard_map/ppermute | solution.py:34
  83.9 237.9 %all-gather.9.cloned.1.call-start = ((), (), s32[]{:S(2)}) async-start(), calls=%async_computation.8 | async-start | bytes 26542080 | tf_op jit(solution)/shard_map/all_gather | solution.py:1031
  93.2 16.2 %collective-permute-start.9 = (bf16[2,96,1408]{2,1,0:T(8,128)(2,1)S(1)}, bf16[2,96,1408]{2,1,0:T(8,128)(2,1)S(1)}, u32[]{:S(2)}, u32[]{:S(2)}) collective-permute-start(bf16[2,96,1408]{2,1,0:T(8,128)(2,1)S(1)} %slice.315), channel_id=1, source_target_pairs={{0,2},{1,3},{2,0},{3,1},{4,6},{5,7},{6,4},{7,5},{8,10},{9,11},{10,... | collective-permute-start | bytes 1622024 | tf_op jit(solution)/shard_map/ppermute | solution.py:43
  110.2 252.5 %all-gather.13.cloned.1.call-start = ((), (), s32[]{:S(2)}) async-start(), calls=%async_computation.10 | async-start | bytes 15040512 | tf_op jit(solution)/shard_map/all_gather | solution.py:1037
  120.4 466.6 %all-gather.15.cloned.1.call-start = ((), (), s32[]{:S(2)}) async-start(), calls=%async_computation.11 | async-start | bytes 26542080 | tf_op jit(solution)/shard_map/all_gather | solution.py:1043
  121.0 788.5 %reduce-scatter.5.cloned.1.call-start = ((), (), s32[]{:S(2)}) async-start(), calls=%async_computation.4 | async-start | bytes 26542080 | tf_op jit(solution)/shard_map/reduce_scatter | solution.py:1163
  127.5 20.8 %collective-permute-start.15 = (bf16[1536,1408]{1,0:T(8,128)(2,1)}, bf16[1536,1408]{1,0:T(8,128)(2,1)}, u32[]{:S(2)}, u32[]{:S(2)}) collective-permute-start(bf16[1536,1408]{1,0:T(8,128)(2,1)} %line_up.2), channel_id=1, source_target_pairs={{0,16},{16,0},{1,17},{17,1},{2,18},{18,2},{3,19},{19,3},{4,20},{20... | collective-permute-start | bytes 12976136 | tf_op jit(solution)/shard_map/ppermute | solution.py:34
  145.9 27.6 %collective-permute-start.23 = (bf16[4,96,768]{2,1,0:T(8,128)(2,1)S(1)}, bf16[4,96,768]{2,1,0:T(8,128)(2,1)S(1)}, u32[]{:S(2)}, u32[]{:S(2)}) collective-permute-start(bf16[4,96,768]{2,1,0:T(8,128)(2,1)S(1)} %pad_maximum_fusion.8.refs_0_), channel_id=1, source_target_pairs={{0,1},{1,0},{2,3},{3,2},{4,5},{5,4},{6,7},{7,6},{8,9},{9,8},{10,11... | collective-permute-start | bytes 1769480 | tf_op jit(solution)/shard_map/ppermute | solution.py:43
  147.2 27.5 %collective-permute-start.24 = (bf16[4,96,768]{2,1,0:T(8,128)(2,1)S(1)}, bf16[4,96,768]{2,1,0:T(8,128)(2,1)S(1)}, u32[]{:S(2)}, u32[]{:S(2)}) collective-permute-start(bf16[4,96,768]{2,1,0:T(8,128)(2,1)S(1)} %pad_maximum_fusion.8.refs_0_), channel_id=1, source_target_pairs={{0,2},{1,3},{2,0},{3,1},{4,6},{5,7},{6,4},{7,5},{8,10},{9,11},{10,... | collective-permute-start | bytes 1769480 | tf_op jit(solution)/shard_map/ppermute | solution.py:43
  176.4 21.3 %collective-permute-start.16 = (bf16[256,1024]{1,0:T(8,128)(2,1)}, bf16[256,1024]{1,0:T(8,128)(2,1)}, u32[]{:S(2)}, u32[]{:S(2)}) collective-permute-start(bf16[256,1024]{1,0:T(8,128)(2,1)} %get-tuple-element.91.refs_0_), channel_id=1, source_target_pairs={{0,1},{1,0},{2,3},{3,2},{4,5},{5,4},{6,7},{7,6},{8,9},{9,8},{10,11... | collective-permute-start | bytes 1572872 | tf_op jit(solution)/shard_map/ppermute | solution.py:50
  177.5 22.2 %collective-permute-start.17 = (bf16[256,1024]{1,0:T(8,128)(2,1)}, bf16[256,1024]{1,0:T(8,128)(2,1)}, u32[]{:S(2)}, u32[]{:S(2)}) collective-permute-start(bf16[256,1024]{1,0:T(8,128)(2,1)} %get-tuple-element.91.refs_0_), channel_id=1, source_target_pairs={{0,2},{1,3},{2,0},{3,1},{4,6},{5,7},{6,4},{7,5},{8,10},{9,11},{10,... | collective-permute-start | bytes 1572872 | tf_op jit(solution)/shard_map/ppermute | solution.py:50
  177.7 44.1 %collective-permute-start.18 = (bf16[256,1024]{1,0:T(8,128)(2,1)}, bf16[256,1024]{1,0:T(8,128)(2,1)}, u32[]{:S(2)}, u32[]{:S(2)}) collective-permute-start(bf16[256,1024]{1,0:T(8,128)(2,1)} %get-tuple-element.91.refs_0_), channel_id=1, source_target_pairs={{0,3},{1,2},{2,1},{3,0},{4,7},{5,6},{6,5},{7,4},{8,11},{9,10},{10,... | collective-permute-start | bytes 1572872 | tf_op jit(solution)/shard_map/ppermute | solution.py:50
  191.7 50.3 %collective-permute-start.27 = (bf16[1536,768]{1,0:T(8,128)(2,1)}, bf16[1536,768]{1,0:T(8,128)(2,1)S(1)}, u32[]{:S(2)}, u32[]{:S(2)}) collective-permute-start(bf16[1536,768]{1,0:T(8,128)(2,1)} %line_up.3.refs_9_), channel_id=1, source_target_pairs={{0,16},{16,0},{1,17},{17,1},{2,18},{18,2},{3,19},{19,3},{4,20},{20... | collective-permute-start | bytes 7077896 | tf_op jit(solution)/shard_map/ppermute | solution.py:34
  247.9 29.9 %collective-permute-start.28 = (bf16[256,1536]{1,0:T(8,128)(2,1)}, bf16[256,1536]{1,0:T(8,128)(2,1)}, u32[]{:S(2)}, u32[]{:S(2)}) collective-permute-start(bf16[256,1536]{1,0:T(8,128)(2,1)} %multiply_convert_fusion.1.refs_9_), channel_id=1, source_target_pairs={{0,4},{4,0},{8,12},{12,8},{1,5},{5,1},{9,13},{13,9},{2,6},{6,2},{1... | collective-permute-start | bytes 2359304 | tf_op jit(solution)/shard_map/ppermute | solution.py:50
  247.9 34.0 %collective-permute-start.29 = (bf16[256,1536]{1,0:T(8,128)(2,1)}, bf16[256,1536]{1,0:T(8,128)(2,1)}, u32[]{:S(2)}, u32[]{:S(2)}) collective-permute-start(bf16[256,1536]{1,0:T(8,128)(2,1)} %multiply_convert_fusion.1.refs_9_), channel_id=1, source_target_pairs={{0,8},{4,12},{8,0},{12,4},{1,9},{5,13},{9,1},{13,5},{2,10},{6,14},... | collective-permute-start | bytes 2359304 | tf_op jit(solution)/shard_map/ppermute | solution.py:50
  250.3 65.3 %collective-permute-start.30 = (bf16[256,1536]{1,0:T(8,128)(2,1)}, bf16[256,1536]{1,0:T(8,128)(2,1)}, u32[]{:S(2)}, u32[]{:S(2)}) collective-permute-start(bf16[256,1536]{1,0:T(8,128)(2,1)} %multiply_convert_fusion.1.refs_9_), channel_id=1, source_target_pairs={{0,12},{4,8},{8,4},{12,0},{1,13},{5,9},{9,5},{13,1},{2,14},{6,10},... | collective-permute-start | bytes 2359304 | tf_op jit(solution)/shard_map/ppermute | solution.py:50
  360.1 29.1 %collective-permute-start.32 = (bf16[256,1536]{1,0:T(8,128)(2,1)}, bf16[256,1536]{1,0:T(8,128)(2,1)}, u32[]{:S(2)}, u32[]{:S(2)}) collective-permute-start(bf16[256,1536]{1,0:T(8,128)(2,1)} %get-tuple-element.271), channel_id=1, source_target_pairs={{0,4},{4,0},{8,12},{12,8},{1,5},{5,1},{9,13},{13,9},{2,6},{6,2},{1... | collective-permute-start | bytes 2359304 | tf_op jit(solution)/shard_map/ppermute | solution.py:50
  360.1 32.4 %collective-permute-start.33 = (bf16[256,1536]{1,0:T(8,128)(2,1)}, bf16[256,1536]{1,0:T(8,128)(2,1)}, u32[]{:S(2)}, u32[]{:S(2)}) collective-permute-start(bf16[256,1536]{1,0:T(8,128)(2,1)} %get-tuple-element.270), channel_id=1, source_target_pairs={{0,8},{4,12},{8,0},{12,4},{1,9},{5,13},{9,1},{13,5},{2,10},{6,14},... | collective-permute-start | bytes 2359304 | tf_op jit(solution)/shard_map/ppermute | solution.py:50
  362.5 63.8 %collective-permute-start.34 = (bf16[256,1536]{1,0:T(8,128)(2,1)}, bf16[256,1536]{1,0:T(8,128)(2,1)}, u32[]{:S(2)}, u32[]{:S(2)}) collective-permute-start(bf16[256,1536]{1,0:T(8,128)(2,1)} %get-tuple-element.269), channel_id=1, source_target_pairs={{0,12},{4,8},{8,4},{12,0},{1,13},{5,9},{9,5},{13,1},{2,14},{6,10},... | collective-permute-start | bytes 2359304 | tf_op jit(solution)/shard_map/ppermute | solution.py:50
  437.3 23.3 %collective-permute-start.35 = (bf16[256,1024]{1,0:T(8,128)(2,1)}, bf16[256,1024]{1,0:T(8,128)(2,1)}, u32[]{:S(2)}, u32[]{:S(2)}) collective-permute-start(bf16[256,1024]{1,0:T(8,128)(2,1)} %get-tuple-element.103.refs_0_), channel_id=1, source_target_pairs={{0,1},{1,0},{2,3},{3,2},{4,5},{5,4},{6,7},{7,6},{8,9},{9,8},{10,11... | collective-permute-start | bytes 1572872 | tf_op jit(solution)/shard_map/ppermute | solution.py:50
  437.8 24.0 %collective-permute-start.36 = (bf16[256,1024]{1,0:T(8,128)(2,1)}, bf16[256,1024]{1,0:T(8,128)(2,1)}, u32[]{:S(2)}, u32[]{:S(2)}) collective-permute-start(bf16[256,1024]{1,0:T(8,128)(2,1)} %get-tuple-element.103.refs_0_), channel_id=1, source_target_pairs={{0,2},{1,3},{2,0},{3,1},{4,6},{5,7},{6,4},{7,5},{8,10},{9,11},{10,... | collective-permute-start | bytes 1572872 | tf_op jit(solution)/shard_map/ppermute | solution.py:50
  437.8 44.5 %collective-permute-start.37 = (bf16[256,1024]{1,0:T(8,128)(2,1)}, bf16[256,1024]{1,0:T(8,128)(2,1)}, u32[]{:S(2)}, u32[]{:S(2)}) collective-permute-start(bf16[256,1024]{1,0:T(8,128)(2,1)} %get-tuple-element.103.refs_0_), channel_id=1, source_target_pairs={{0,3},{1,2},{2,1},{3,0},{4,7},{5,6},{6,5},{7,4},{8,11},{9,10},{10,... | collective-permute-start | bytes 1572872 | tf_op jit(solution)/shard_map/ppermute | solution.py:50
  440.0 59.6 %collective-permute-start.38 = (bf16[256,1536]{1,0:T(8,128)(2,1)S(1)}, bf16[256,1536]{1,0:T(8,128)(2,1)S(1)}, u32[]{:S(2)}, u32[]{:S(2)}) collective-permute-start(bf16[256,1536]{1,0:T(8,128)(2,1)S(1)} %dynamic-slice_bitcast_fusion.refs_8_), channel_id=1, source_target_pairs={{0,4},{4,0},{8,12},{12,8},{1,5},{5,1},{9,13},{13,9},{2,6},{6,2},{1... | collective-permute-start | bytes 2359304 | tf_op jit(solution)/shard_map/ppermute | solution.py:50
  440.1 60.5 %collective-permute-start.39 = (bf16[256,1536]{1,0:T(8,128)(2,1)S(1)}, bf16[256,1536]{1,0:T(8,128)(2,1)S(1)}, u32[]{:S(2)}, u32[]{:S(2)}) collective-permute-start(bf16[256,1536]{1,0:T(8,128)(2,1)S(1)} %dynamic-slice_bitcast_fusion.refs_8_), channel_id=1, source_target_pairs={{0,8},{4,12},{8,0},{12,4},{1,9},{5,13},{9,1},{13,5},{2,10},{6,14},... | collective-permute-start | bytes 2359304 | tf_op jit(solution)/shard_map/ppermute | solution.py:50
  460.6 48.3 %collective-permute-start.40 = (bf16[256,1536]{1,0:T(8,128)(2,1)S(1)}, bf16[256,1536]{1,0:T(8,128)(2,1)S(1)}, u32[]{:S(2)}, u32[]{:S(2)}) collective-permute-start(bf16[256,1536]{1,0:T(8,128)(2,1)S(1)} %dynamic-slice_bitcast_fusion.refs_8_), channel_id=1, source_target_pairs={{0,12},{4,8},{8,4},{12,0},{1,13},{5,9},{9,5},{13,1},{2,14},{6,10},... | collective-permute-start | bytes 2359304 | tf_op jit(solution)/shard_map/ppermute | solution.py:50
  515.3 29.6 %collective-permute-start.41 = (bf16[256,1536]{1,0:T(8,128)(2,1)S(1)}, bf16[256,1536]{1,0:T(8,128)(2,1)S(1)}, u32[]{:S(2)}, u32[]{:S(2)}) collective-permute-start(bf16[256,1536]{1,0:T(8,128)(2,1)S(1)} %multiply_convert_fusion.refs_9_), channel_id=1, source_target_pairs={{0,4},{4,0},{8,12},{12,8},{1,5},{5,1},{9,13},{13,9},{2,6},{6,2},{1... | collective-permute-start | bytes 2359304 | tf_op jit(solution)/shard_map/ppermute | solution.py:50
  515.4 33.0 %collective-permute-start.42 = (bf16[256,1536]{1,0:T(8,128)(2,1)S(1)}, bf16[256,1536]{1,0:T(8,128)(2,1)S(1)}, u32[]{:S(2)}, u32[]{:S(2)}) collective-permute-start(bf16[256,1536]{1,0:T(8,128)(2,1)S(1)} %multiply_convert_fusion.refs_9_), channel_id=1, source_target_pairs={{0,8},{4,12},{8,0},{12,4},{1,9},{5,13},{9,1},{13,5},{2,10},{6,14},... | collective-permute-start | bytes 2359304 | tf_op jit(solution)/shard_map/ppermute | solution.py:50
  517.3 65.8 %collective-permute-start.43 = (bf16[256,1536]{1,0:T(8,128)(2,1)S(1)}, bf16[256,1536]{1,0:T(8,128)(2,1)S(1)}, u32[]{:S(2)}, u32[]{:S(2)}) collective-permute-start(bf16[256,1536]{1,0:T(8,128)(2,1)S(1)} %multiply_convert_fusion.refs_9_), channel_id=1, source_target_pairs={{0,12},{4,8},{8,4},{12,0},{1,13},{5,9},{9,5},{13,1},{2,14},{6,10},... | collective-permute-start | bytes 2359304 | tf_op jit(solution)/shard_map/ppermute | solution.py:50
  665.0 36.7 %collective-permute-start.44 = (bf16[256,1664]{1,0:T(8,128)(2,1)S(1)}, bf16[256,1664]{1,0:T(8,128)(2,1)}, u32[]{:S(2)}, u32[]{:S(2)}) collective-permute-start(bf16[256,1664]{1,0:T(8,128)(2,1)S(1)} %get-tuple-element.262), channel_id=1, source_target_pairs={{0,4},{4,0},{8,12},{12,8},{1,5},{5,1},{9,13},{13,9},{2,6},{6,2},{1... | collective-permute-start | bytes 2555912 | tf_op jit(solution)/shard_map/ppermute | solution.py:50
  665.0 36.7 %collective-permute-start.45 = (bf16[256,1664]{1,0:T(8,128)(2,1)S(1)}, bf16[256,1664]{1,0:T(8,128)(2,1)}, u32[]{:S(2)}, u32[]{:S(2)}) collective-permute-start(bf16[256,1664]{1,0:T(8,128)(2,1)S(1)} %get-tuple-element.261), channel_id=1, source_target_pairs={{0,8},{4,12},{8,0},{12,4},{1,9},{5,13},{9,1},{13,5},{2,10},{6,14},... | collective-permute-start | bytes 2555912 | tf_op jit(solution)/shard_map/ppermute | solution.py:50
  666.4 70.8 %collective-permute-start.46 = (bf16[256,1664]{1,0:T(8,128)(2,1)S(1)}, bf16[256,1664]{1,0:T(8,128)(2,1)}, u32[]{:S(2)}, u32[]{:S(2)}) collective-permute-start(bf16[256,1664]{1,0:T(8,128)(2,1)S(1)} %get-tuple-element.260), channel_id=1, source_target_pairs={{0,12},{4,8},{8,4},{12,0},{1,13},{5,9},{9,5},{13,1},{2,14},{6,10},... | collective-permute-start | bytes 2555912 | tf_op jit(solution)/shard_map/ppermute | solution.py:50
  746.1 292.6 %reduce-scatter.7.cloned.1.call-start = ((), (), s32[]{:S(2)}) async-start(), calls=%async_computation.5 | async-start | bytes 15040512 | tf_op jit(solution)/shard_map/reduce_scatter | solution.py:1282
  749.1 33.3 %collective-permute-start.47 = (bf16[256,1536]{1,0:T(8,128)(2,1)}, bf16[256,1536]{1,0:T(8,128)(2,1)}, u32[]{:S(2)}, u32[]{:S(2)}) collective-permute-start(bf16[256,1536]{1,0:T(8,128)(2,1)} %get-tuple-element.267), channel_id=1, source_target_pairs={{0,4},{4,0},{8,12},{12,8},{1,5},{5,1},{9,13},{13,9},{2,6},{6,2},{1... | collective-permute-start | bytes 2359304 | tf_op jit(solution)/shard_map/ppermute | solution.py:50
  749.1 34.6 %collective-permute-start.48 = (bf16[256,1536]{1,0:T(8,128)(2,1)S(1)}, bf16[256,1536]{1,0:T(8,128)(2,1)}, u32[]{:S(2)}, u32[]{:S(2)}) collective-permute-start(bf16[256,1536]{1,0:T(8,128)(2,1)S(1)} %get-tuple-element.266), channel_id=1, source_target_pairs={{0,8},{4,12},{8,0},{12,4},{1,9},{5,13},{9,1},{13,5},{2,10},{6,14},... | collective-permute-start | bytes 2359304 | tf_op jit(solution)/shard_map/ppermute | solution.py:50
  750.1 64.6 %collective-permute-start.49 = (bf16[256,1536]{1,0:T(8,128)(2,1)S(1)}, bf16[256,1536]{1,0:T(8,128)(2,1)}, u32[]{:S(2)}, u32[]{:S(2)}) collective-permute-start(bf16[256,1536]{1,0:T(8,128)(2,1)S(1)} %get-tuple-element.265), channel_id=1, source_target_pairs={{0,12},{4,8},{8,4},{12,0},{1,13},{5,9},{9,5},{13,1},{2,14},{6,10},... | collective-permute-start | bytes 2359304 | tf_op jit(solution)/shard_map/ppermute | solution.py:50
  778.7 38.9 %collective-permute-start.51 = (bf16[256,1024]{1,0:T(8,128)(2,1)}, bf16[256,1024]{1,0:T(8,128)(2,1)S(1)}, u32[]{:S(2)}, u32[]{:S(2)}) collective-permute-start(bf16[256,1024]{1,0:T(8,128)(2,1)} %get-tuple-element.124), channel_id=1, source_target_pairs={{0,1},{1,0},{2,3},{3,2},{4,5},{5,4},{6,7},{7,6},{8,9},{9,8},{10,11... | collective-permute-start | bytes 1572872 | tf_op jit(solution)/shard_map/ppermute | solution.py:50
  780.3 37.4 %collective-permute-start.52 = (bf16[256,1024]{1,0:T(8,128)(2,1)}, bf16[256,1024]{1,0:T(8,128)(2,1)S(1)}, u32[]{:S(2)}, u32[]{:S(2)}) collective-permute-start(bf16[256,1024]{1,0:T(8,128)(2,1)} %get-tuple-element.125), channel_id=1, source_target_pairs={{0,2},{1,3},{2,0},{3,1},{4,6},{5,7},{6,4},{7,5},{8,10},{9,11},{10,... | collective-permute-start | bytes 1572872 | tf_op jit(solution)/shard_map/ppermute | solution.py:50
  782.4 35.3 %collective-permute-start.53 = (bf16[256,1024]{1,0:T(8,128)(2,1)}, bf16[256,1024]{1,0:T(8,128)(2,1)S(1)}, u32[]{:S(2)}, u32[]{:S(2)}) collective-permute-start(bf16[256,1024]{1,0:T(8,128)(2,1)} %get-tuple-element.126), channel_id=1, source_target_pairs={{0,3},{1,2},{2,1},{3,0},{4,7},{5,6},{6,5},{7,4},{8,11},{9,10},{10,... | collective-permute-start | bytes 1572872 | tf_op jit(solution)/shard_map/ppermute | solution.py:50
  838.1 27.2 %collective-permute-start.54 = (bf16[256,1536]{1,0:T(8,128)(2,1)S(1)}, bf16[256,1536]{1,0:T(8,128)(2,1)S(1)}, u32[]{:S(2)}, u32[]{:S(2)}) collective-permute-start(bf16[256,1536]{1,0:T(8,128)(2,1)S(1)} %add_convert_fusion.3.refs_8_), channel_id=1, source_target_pairs={{0,4},{4,0},{8,12},{12,8},{1,5},{5,1},{9,13},{13,9},{2,6},{6,2},{1... | collective-permute-start | bytes 2359304 | tf_op jit(solution)/shard_map/ppermute | solution.py:50
  838.2 28.5 %collective-permute-start.55 = (bf16[256,1536]{1,0:T(8,128)(2,1)S(1)}, bf16[256,1536]{1,0:T(8,128)(2,1)S(1)}, u32[]{:S(2)}, u32[]{:S(2)}) collective-permute-start(bf16[256,1536]{1,0:T(8,128)(2,1)S(1)} %add_convert_fusion.3.refs_8_), channel_id=1, source_target_pairs={{0,8},{4,12},{8,0},{12,4},{1,9},{5,13},{9,1},{13,5},{2,10},{6,14},... | collective-permute-start | bytes 2359304 | tf_op jit(solution)/shard_map/ppermute | solution.py:50
  838.9 63.4 %collective-permute-start.56 = (bf16[256,1536]{1,0:T(8,128)(2,1)S(1)}, bf16[256,1536]{1,0:T(8,128)(2,1)S(1)}, u32[]{:S(2)}, u32[]{:S(2)}) collective-permute-start(bf16[256,1536]{1,0:T(8,128)(2,1)S(1)} %add_convert_fusion.3.refs_8_), channel_id=1, source_target_pairs={{0,12},{4,8},{8,4},{12,0},{1,13},{5,9},{9,5},{13,1},{2,14},{6,10},... | collective-permute-start | bytes 2359304 | tf_op jit(solution)/shard_map/ppermute | solution.py:50
  909.5 325.4 %reduce-scatter.9.cloned.1.call-start = ((), (), s32[]{:S(2)}) async-start(), calls=%async_computation.6 | async-start | bytes 26542080 | tf_op jit(solution)/shard_map/reduce_scatter | solution.py:1163
  955.4 36.3 %collective-permute-start.57 = (bf16[256,1664]{1,0:T(8,128)(2,1)S(1)}, bf16[256,1664]{1,0:T(8,128)(2,1)}, u32[]{:S(2)}, u32[]{:S(2)}) collective-permute-start(bf16[256,1664]{1,0:T(8,128)(2,1)S(1)} %get-tuple-element.258), channel_id=1, source_target_pairs={{0,4},{4,0},{8,12},{12,8},{1,5},{5,1},{9,13},{13,9},{2,6},{6,2},{1... | collective-permute-start | bytes 2555912 | tf_op jit(solution)/shard_map/ppermute | solution.py:50
  955.6 38.9 %collective-permute-start.58 = (bf16[256,1664]{1,0:T(8,128)(2,1)S(1)}, bf16[256,1664]{1,0:T(8,128)(2,1)}, u32[]{:S(2)}, u32[]{:S(2)}) collective-permute-start(bf16[256,1664]{1,0:T(8,128)(2,1)S(1)} %get-tuple-element.257), channel_id=1, source_target_pairs={{0,8},{4,12},{8,0},{12,4},{1,9},{5,13},{9,1},{13,5},{2,10},{6,14},... | collective-permute-start | bytes 2555912 | tf_op jit(solution)/shard_map/ppermute | solution.py:50
  957.8 72.1 %collective-permute-start.59 = (bf16[256,1664]{1,0:T(8,128)(2,1)S(1)}, bf16[256,1664]{1,0:T(8,128)(2,1)}, u32[]{:S(2)}, u32[]{:S(2)}) collective-permute-start(bf16[256,1664]{1,0:T(8,128)(2,1)S(1)} %get-tuple-element.256), channel_id=1, source_target_pairs={{0,12},{4,8},{8,4},{12,0},{1,13},{5,9},{9,5},{13,1},{2,14},{6,10},... | collective-permute-start | bytes 2555912 | tf_op jit(solution)/shard_map/ppermute | solution.py:50
  1038.7 262.8 %reduce-scatter.11.cloned.1.call-start = ((), (), s32[]{:S(2)}) async-start(), calls=%async_computation.7 | async-start | bytes 2088960 | tf_op jit(solution)/shard_map/reduce_scatter | solution.py:1289
  1068.2 26.5 %collective-permute-start.62 = (bf16[256,1024]{1,0:T(8,128)(2,1)}, bf16[256,1024]{1,0:T(8,128)(2,1)S(1)}, u32[]{:S(2)}, u32[]{:S(2)}) collective-permute-start(bf16[256,1024]{1,0:T(8,128)(2,1)} %get-tuple-element.144), channel_id=1, source_target_pairs={{0,3},{1,2},{2,1},{3,0},{4,7},{5,6},{6,5},{7,4},{8,11},{9,10},{10,... | collective-permute-start | bytes 1572872 | tf_op jit(solution)/shard_map/ppermute | solution.py:50
  1114.1 23.0 %collective-permute-start.64 = (bf16[4,4,96,1408]{3,2,1,0:T(8,128)(2,1)}, bf16[4,4,96,1408]{3,2,1,0:T(8,128)(2,1)}, u32[]{:S(2)}, u32[]{:S(2)}) collective-permute-start(bf16[4,4,96,1408]{3,2,1,0:T(8,128)(2,1)} %constant_dynamic-slice_fusion.1), channel_id=1, source_target_pairs={{0,16},{16,0},{1,17},{17,1},{2,18},{18,2},{3,19},{19,3},{4,20},{20... | collective-permute-start | bytes 12976136 | tf_op jit(solution)/shard_map/ppermute | solution.py:34
  1137.1 18.0 %collective-permute-start.69 = (bf16[4,96,768]{2,1,0:T(8,128)(2,1)}, bf16[4,96,768]{2,1,0:T(8,128)(2,1)S(1)}, u32[]{:S(2)}, u32[]{:S(2)}) collective-permute-start(bf16[4,96,768]{2,1,0:T(8,128)(2,1)} %get-tuple-element.251), channel_id=1, source_target_pairs={{0,4},{4,0},{8,12},{12,8},{1,5},{5,1},{9,13},{13,9},{2,6},{6,2},{1... | collective-permute-start | bytes 1769480 | tf_op jit(solution)/shard_map/ppermute | solution.py:50
  1142.2 58.5 %collective-permute-start.65 = (bf16[4,96,1408]{2,1,0:T(8,128)(2,1)}, bf16[4,96,1408]{2,1,0:T(8,128)(2,1)S(1)}, u32[]{:S(2)}, u32[]{:S(2)}) collective-permute-start(bf16[4,96,1408]{2,1,0:T(8,128)(2,1)} %get-tuple-element.246), channel_id=1, source_target_pairs={{0,1},{1,0},{2,3},{3,2},{4,5},{5,4},{6,7},{7,6},{8,9},{9,8},{10,11... | collective-permute-start | bytes 3244040 | tf_op jit(solution)/shard_map/ppermute | solution.py:50
  1143.3 57.5 %collective-permute-start.66 = (bf16[4,96,1408]{2,1,0:T(8,128)(2,1)}, bf16[4,96,1408]{2,1,0:T(8,128)(2,1)}, u32[]{:S(2)}, u32[]{:S(2)}) collective-permute-start(bf16[4,96,1408]{2,1,0:T(8,128)(2,1)} %get-tuple-element.248), channel_id=1, source_target_pairs={{0,2},{1,3},{2,0},{3,1},{4,6},{5,7},{6,4},{7,5},{8,10},{9,11},{10,... | collective-permute-start | bytes 3244040 | tf_op jit(solution)/shard_map/ppermute | solution.py:50
  1143.8 84.5 %collective-permute-start.67 = (bf16[4,96,1408]{2,1,0:T(8,128)(2,1)}, bf16[4,96,1408]{2,1,0:T(8,128)(2,1)}, u32[]{:S(2)}, u32[]{:S(2)}) collective-permute-start(bf16[4,96,1408]{2,1,0:T(8,128)(2,1)} %get-tuple-element.247), channel_id=1, source_target_pairs={{0,3},{1,2},{2,1},{3,0},{4,7},{5,6},{6,5},{7,4},{8,11},{9,10},{10,... | collective-permute-start | bytes 3244040 | tf_op jit(solution)/shard_map/ppermute | solution.py:50
  1144.9 39.8 %collective-permute-start.70 = (bf16[4,96,768]{2,1,0:T(8,128)(2,1)}, bf16[4,96,768]{2,1,0:T(8,128)(2,1)}, u32[]{:S(2)}, u32[]{:S(2)}) collective-permute-start(bf16[4,96,768]{2,1,0:T(8,128)(2,1)} %get-tuple-element.253), channel_id=1, source_target_pairs={{0,8},{4,12},{8,0},{12,4},{1,9},{5,13},{9,1},{13,5},{2,10},{6,14},... | collective-permute-start | bytes 1769480 | tf_op jit(solution)/shard_map/ppermute | solution.py:50
  1155.1 42.7 %collective-permute-start.71 = (bf16[4,96,768]{2,1,0:T(8,128)(2,1)}, bf16[4,96,768]{2,1,0:T(8,128)(2,1)}, u32[]{:S(2)}, u32[]{:S(2)}) collective-permute-start(bf16[4,96,768]{2,1,0:T(8,128)(2,1)} %get-tuple-element.252), channel_id=1, source_target_pairs={{0,12},{4,8},{8,4},{12,0},{1,13},{5,9},{9,5},{13,1},{2,14},{6,10},... | collective-permute-start | bytes 1769480 | tf_op jit(solution)/shard_map/ppermute | solution.py:50
  1184.7 56.4 %collective-permute-start.50 = (bf16[256,1536]{1,0:T(8,128)(2,1)S(1)}, bf16[256,1536]{1,0:T(8,128)(2,1)}, u32[]{:S(2)}, u32[]{:S(2)}) collective-permute-start(bf16[256,1536]{1,0:T(8,128)(2,1)S(1)} %broadcast_select_fusion.8), channel_id=1, source_target_pairs={{0,16},{16,0},{1,17},{17,1},{2,18},{18,2},{3,19},{19,3},{4,20},{20... | collective-permute-start | bytes 2359304 | tf_op jit(solution)/shard_map/ppermute | solution.py:34
  1240.6 19.2 %collective-permute-start.72 = (bf16[5,384,768]{2,1,0:T(8,128)(2,1)}, bf16[5,384,768]{2,1,0:T(8,128)(2,1)}, u32[]{:S(2)}, u32[]{:S(2)}) collective-permute-start(bf16[5,384,768]{2,1,0:T(8,128)(2,1)} %get-tuple-element.254), channel_id=1, source_target_pairs={{0,16},{16,0},{1,17},{17,1},{2,18},{18,2},{3,19},{19,3},{4,20},{20... | collective-permute-start | bytes 8847368 | tf_op jit(solution)/shard_map/ppermute | solution.py:34
  1249.0 55.3 %collective-permute-start.63 = (bf16[256,1536]{1,0:T(8,128)(2,1)}, bf16[256,1536]{1,0:T(8,128)(2,1)S(1)}, u32[]{:S(2)}, u32[]{:S(2)}) collective-permute-start(bf16[256,1536]{1,0:T(8,128)(2,1)} %get-tuple-element.236), channel_id=1, source_target_pairs={{0,16},{16,0},{1,17},{17,1},{2,18},{18,2},{3,19},{19,3},{4,20},{20... | collective-permute-start | bytes 2359304 | tf_op jit(solution)/shard_map/ppermute | solution.py:34
  1254.3 22.0 %collective-permute-start.73 = (bf16[96,1408]{1,0:T(8,128)(2,1)}, bf16[96,1408]{1,0:T(8,128)(2,1)S(1)}, u32[]{:S(2)}, u32[]{:S(2)}) collective-permute-start(bf16[96,1408]{1,0:T(8,128)(2,1)} %get-tuple-element.276), channel_id=1, source_target_pairs={{0,4},{4,0},{8,12},{12,8},{1,5},{5,1},{9,13},{13,9},{2,6},{6,2},{1... | collective-permute-start | bytes 811016 | tf_op jit(solution)/shard_map/ppermute | solution.py:50
  1255.1 25.7 %collective-permute-start.74 = (bf16[96,1408]{1,0:T(8,128)(2,1)}, bf16[96,1408]{1,0:T(8,128)(2,1)S(1)}, u32[]{:S(2)}, u32[]{:S(2)}) collective-permute-start(bf16[96,1408]{1,0:T(8,128)(2,1)} %get-tuple-element.278), channel_id=1, source_target_pairs={{0,8},{4,12},{8,0},{12,4},{1,9},{5,13},{9,1},{13,5},{2,10},{6,14},... | collective-permute-start | bytes 811016 | tf_op jit(solution)/shard_map/ppermute | solution.py:50
  1258.5 41.9 %collective-permute-start.75 = (bf16[96,1408]{1,0:T(8,128)(2,1)S(1)}, bf16[96,1408]{1,0:T(8,128)(2,1)}, u32[]{:S(2)}, u32[]{:S(2)}) collective-permute-start(bf16[96,1408]{1,0:T(8,128)(2,1)S(1)} %get-tuple-element.277), channel_id=1, source_target_pairs={{0,12},{4,8},{8,4},{12,0},{1,13},{5,9},{9,5},{13,1},{2,14},{6,10},... | collective-permute-start | bytes 811016 | tf_op jit(solution)/shard_map/ppermute | solution.py:50
  (104 other events, 2058.6 us)
Sparse Core Ops, SparseCore 0:
  84.0 36.2 all-gather.10
  122.8 153.0 all-gather.8
  277.8 75.4 all-gather.12
  355.0 141.1 all-gather.14
  746.2 163.1 reduce-scatter.4
  913.4 96.5 reduce-scatter.6
  1038.9 195.9 reduce-scatter.8
  1243.6 55.6 reduce-scatter.10

commit v4 on v3

--- a/solution.py
+++ b/solution.py
@@ -1189,7 +1189,8 @@
             result = combine(kept, partial, d_slots[0])
             d_query_raw, result = lax.optimization_barrier((d_query_raw, result))
         else:
-            grad_output = sum_over("expert", grad_output)
+            earlier = sum_rest("expert", after(earlier, d_branch), d_slots[0])
+            d_query_raw, earlier = lax.optimization_barrier((d_query_raw, earlier))
         d_kv_slots = [d_slots[0]] + [
             crossed_back(d_slots[k], "shard", k) for k in range(1, shards)
         ]
@@ -1218,7 +1219,7 @@
     def place_of(axis, k):
         return partner(axis, k, True) if k else homes[axis][0]
 
-    def sum_over(axis, array):
+    def sum_over(axis, array, *held):
         size = (shards, *array.shape[1:])
         kept = lax.dynamic_slice(array, (core * shards, 0, 0, 0), size)
         received = swap(lax.dynamic_slice(array, ((1 - core) * shards, 0, 0, 0), size))
@@ -1231,18 +1232,23 @@
             ) + lax.dynamic_index_in_dim(received, place, dim, keepdims=False).astype(F32)
 
         total = chunk(0)
+        chunks = [chunk(k).astype(BF16) for k in range(1, count)]
+        if held:
+            *chunks, later = lax.optimization_barrier((*chunks, *held))
         for k in range(1, count):
-            total = total + crossed_back(chunk(k).astype(BF16), axis, k).astype(F32)
-        return total
-
-    def sum_rest(axis, total, *held):
+            total = total + crossed_back(chunks[k - 1], axis, k).astype(F32)
+        return (total, later) if held else total
+
+    def sum_rest(axis, total, *held, meanwhile=None):
         result = lax.dynamic_index_in_dim(total, place_of(axis, 0), 0, keepdims=False)
-        if held:
-            result = after(result, *held)
+        backs = []
         for k in range(1, homes[axis][1]):
             part = lax.dynamic_index_in_dim(total, place_of(axis, k), 0, keepdims=False)
-            result = result + crossed_back(part.astype(BF16), axis, k).astype(F32)
-        return result.astype(BF16)
+            backs.append(crossed_back(part.astype(BF16), axis, k))
+        if meanwhile is not None:
+            held = (meanwhile(backs[0]),)
+        result = after(result, *held) if held else result
+        return sum((back.astype(F32) for back in backs), result.astype(F32)).astype(BF16)
 
     def exchanged(halves):
         kept = jnp.where(first, halves[0], halves[1])
@@ -1283,13 +1289,18 @@
     grad_start, scattered_one, packed_one, output_one, pack_two, _ = backward(
         0, kept_one, mid_rows, pack_two
     )
-    qkv_one = sum_over("shard", packed_one)
+    qkv_one, output_one = sum_over("shard", packed_one, output_one)
+    output_one = sum_over("expert", output_one)
     qkv_one, output_one = lax.optimization_barrier((qkv_one, output_one))
-    pack_two, scattered_one, _ = lax.optimization_barrier((pack_two, scattered_one, qkv_one))
-    pack_two = lax.psum_scatter(pack_two, "expert", scatter_dimension=0)
-    expert_mine_half, expert_other_half = exchanged([scattered_one, scattered_two])
-    grad_gate, grad_up, grad_down = expert_outputs(expert_mine_half, expert_other_half, core)
-    qkv_one = sum_rest("expert", qkv_one, grad_gate)
+    expert_grads = []
+
+    def unpack(returned):
+        halves = exchanged([after(scattered_one, qkv_one, returned), scattered_two])
+        expert_grads.extend(expert_outputs(*halves, core))
+        return expert_grads[0]
+
+    qkv_one = sum_rest("expert", qkv_one, meanwhile=unpack)
+    grad_gate, grad_up, grad_down = expert_grads
     output_one = sum_rest("shard", output_one)
 
     def placed(by_layers):

time: 1330 us -> 1320 us (level)
    ppermute x60 -> x63, waiting for transfers between devices: 584 us -> 573 us  [crossed(): return lax.ppermute(array, axis, [(i, i ^ by) for i in range(length)])]
    ppermute x60 -> x63, starting transfers between devices: 55.6 us -> 61.8 us  [crossed(): return lax.ppermute(array, axis, [(i, i ^ by) for i in range(length)])]
    unnamed x169 -> x161, local copies, waits for them, and re-layouts: 27.8 us -> 29.3 us
  transfers between devices with their start and end apart: 88 -> 90, of which waited for: 54 -> 52; matrix products, arithmetic and copies ran while one was open for 10% -> 10% of each run, Pallas kernels for 23% -> 23%
where the time goes in v4:
time: 1320 us; the launch traced here: 1310 us
  waiting for transfers between devices  650 us (49%)
  Pallas kernels  387 us (29%)
  starting transfers between devices  91.6 us (7%)
  local copies, waits for them, and re-layouts  85.9 us (7%)
  other arithmetic  69.8 us (5%)
  between operations  15.9 us (1%)
    ppermute x63, waiting for transfers between devices, crossed(): return lax.ppermute(array, axis, [(i, i ^ by) for i in range(length)])  573 us
    pallas_call x2, Pallas kernels, moe_backward_rows(): pl.pallas_call(body, grid_spec=pltpu.PrefetchScalarGridSpec(num_scalar_pr...  81.4 us
    pallas_call x2, Pallas kernels, moe_forward(): pl.pallas_call(body, grid_spec=pltpu.PrefetchScalarGridSpec(num_scalar_pr...  69 us
    pallas_call x2, Pallas kernels, moe_backward_weights(): pl.pallas_call(body, grid_spec=pltpu.PrefetchScalarGridSpec(num_scalar_pr...  67 us
    ppermute x63, starting transfers between devices, crossed(): return lax.ppermute(array, axis, [(i, i ^ by) for i in range(length)])  61.8 us
    pallas_call x2, Pallas kernels, attention_backward(): pl.pallas_call(body, grid_spec=pltpu.PrefetchScalarGridSpec(num_scalar_pr...  54.4 us
    ppermute x8, waiting for transfers between devices, flipped(): lax.ppermute(array, 'shard', [(i, i ^ mask) for i in range(lax.axis_size(...  51.6 us
    pallas_call x2, Pallas kernels, attention_forward(): pl.pallas_call(body, grid_spec=pltpu.PrefetchScalarGridSpec(num_scalar_pr...  34.7 us
  transfers between devices with their start and end apart: 90, of which 52 were waited for; matrix products, arithmetic and copies ran while one was open for 10% of the time, Pallas kernels for 23%

profile of v4, /device:TPU:9, one launch (start us, length us, event | category | flops | bytes accessed | tf_op | source)
XLA Modules:
  0.0 1310.4 jit_solution(5478503859393391197)
XLA Ops:
  19.3 8.4 collective-permute-done.4
  27.7 3.5 collective-permute-done.5
  31.2 11.5 collective-permute-done.6
  49.0 19.0 %collective-permute-done.7.refs_1_ = bf16[4,96,1408]{2,1,0:T(8,128)(2,1)} collective-permute-done((bf16[4,96,1408]{2,1,0:T(8,128)(2,1)}, bf16[4,96,1408]{2,1,0:T(8,128)(2,1)}, u32[]{:S(2)}, u32[]{:S(2)}) %collective-permute-start.7) | collective-permute-done | bytes 1081376 | tf_op jit(solution)/shard_map/ppermute | solution.py:43
  94.5 9.1 collective-permute-done.10.refs_4_
  104.4 4.9 broadcast_select_fusion.2
  110.3 10.1 all-gather.11.cloned.1.call-done
  122.3 5.3 line_up.2
  137.2 4.1 collective-permute-done.21
  141.4 4.4 collective-permute-done.22
  151.9 7.4 qkv_forward.2
  159.3 14.2 %collective-permute-done.23.refs_1_ = bf16[4,96,768]{2,1,0:T(8,128)(2,1)S(1)} collective-permute-done((bf16[4,96,768]{2,1,0:T(8,128)(2,1)S(1)}, bf16[4,96,768]{2,1,0:T(8,128)(2,1)S(1)}, u32[]{:S(2)}, u32[]{:S(2)}) %collective-permute-start.23) | collective-permute-done | bytes 589856 | tf_op jit(solution)/shard_map/ppermute | solution.py:43
  179.0 7.2 collective-permute-done.25.refs_3_
  187.7 4.1 line_up.3.refs_9_
  199.6 22.2 %collective-permute-done.18.refs_3_ = bf16[256,1024]{1,0:T(8,128)(2,1)} collective-permute-done((bf16[256,1024]{1,0:T(8,128)(2,1)}, bf16[256,1024]{1,0:T(8,128)(2,1)}, u32[]{:S(2)}, u32[]{:S(2)}) %collective-permute-start.18) | collective-permute-done | bytes 524320 | tf_op jit(solution)/shard_map/ppermute | solution.py:50
  223.4 17.4 %attention_forward.2 = (bf16[256,1536]{1,0:T(8,128)(2,1)}, f32[4,8,256]{2,1,0:T(8,128)}) custom-call(s32[4]{0:T(128)} %pad_add_fusion.1.owner_ref, s32[1024,128]{1,0:T(8,128)} %broadcast_in_dim.37.seg_all_ref, s32[8,256]{1,0:T(8,128)} %broadcast_in_dim.38.seg_ref, bf16[256,1536]{1,0:T(8,128)(2,1)} %get-tuple-element.97.q_ref, ...), custom_call_target="tpu_custom_call" | custom-call | flops 18699999232 | bytes 1000000 | tf_op jit(solution)/shard_map/attention_forward/pallas_call | solution.py:801
  251.0 26.8 %collective-permute-done.28 = bf16[256,1536]{1,0:T(8,128)(2,1)} collective-permute-done((bf16[256,1536]{1,0:T(8,128)(2,1)}, bf16[256,1536]{1,0:T(8,128)(2,1)}, u32[]{:S(2)}, u32[]{:S(2)}) %collective-permute-start.28) | collective-permute-done | bytes 786464 | tf_op jit(solution)/shard_map/ppermute | solution.py:50
  277.8 4.1 collective-permute-done.29
  281.9 33.7 %collective-permute-done.30 = bf16[256,1536]{1,0:T(8,128)(2,1)} collective-permute-done((bf16[256,1536]{1,0:T(8,128)(2,1)}, bf16[256,1536]{1,0:T(8,128)(2,1)}, u32[]{:S(2)}, u32[]{:S(2)}) %collective-permute-start.30) | collective-permute-done | bytes 786464 | tf_op jit(solution)/shard_map/ppermute | solution.py:50
  321.8 34.7 %moe_forward.2 = (bf16[1024,1536]{1,0:T(8,128)(2,1)}, bf16[5,1024,1024]{2,1,0:T(8,128)(2,1)}) custom-call(bf16[1024,1536]{1,0:T(8,128)(2,1)} %copy-done.30, f32[1024,128]{1,0:T(8,128)} %pad.14.gates_ref, bf16[8,5,384,768]{3,2,1,0:T(8,128)(2,1)} %bitcast.241), custom_call_target="tpu_custom_call" | custom-call | flops 44000002048 | bytes 1000000 | tf_op jit(solution)/shard_map/moe_forward/pallas_call | solution.py:198
  356.6 3.6 fusion.48
  362.8 7.9 copy.100
  370.7 4.7 copy-done.2
  376.4 12.8 collective-permute-done.32
  392.5 33.7 %collective-permute-done.34 = bf16[256,1536]{1,0:T(8,128)(2,1)} collective-permute-done((bf16[256,1536]{1,0:T(8,128)(2,1)}, bf16[256,1536]{1,0:T(8,128)(2,1)}, u32[]{:S(2)}, u32[]{:S(2)}) %collective-permute-start.34) | collective-permute-done | bytes 786464 | tf_op jit(solution)/shard_map/ppermute | solution.py:50
  429.5 7.8 qkv_forward.3
  443.4 17.2 %collective-permute-done.35.refs_1_ = bf16[256,1024]{1,0:T(8,128)(2,1)} collective-permute-done((bf16[256,1024]{1,0:T(8,128)(2,1)}, bf16[256,1024]{1,0:T(8,128)(2,1)}, u32[]{:S(2)}, u32[]{:S(2)}) %collective-permute-start.35) | collective-permute-done | bytes 524320 | tf_op jit(solution)/shard_map/ppermute | solution.py:50
  461.8 20.5 %collective-permute-done.37.refs_3_ = bf16[256,1024]{1,0:T(8,128)(2,1)} collective-permute-done((bf16[256,1024]{1,0:T(8,128)(2,1)}, bf16[256,1024]{1,0:T(8,128)(2,1)}, u32[]{:S(2)}, u32[]{:S(2)}) %collective-permute-start.37) | collective-permute-done | bytes 524320 | tf_op jit(solution)/shard_map/ppermute | solution.py:50
  482.3 17.2 %attention_forward.3 = (bf16[256,1536]{1,0:T(8,128)(2,1)}, f32[4,8,256]{2,1,0:T(8,128)}) custom-call(s32[4]{0:T(128)} %pad_add_fusion.1.owner_ref, s32[1024,128]{1,0:T(8,128)} %broadcast_in_dim.37.seg_all_ref, s32[8,256]{1,0:T(8,128)} %broadcast_in_dim.38.seg_ref, bf16[256,1536]{1,0:T(8,128)(2,1)} %get-tuple-element.109.q_ref, ...), custom_call_target="tpu_custom_call" | custom-call | flops 18699999232 | bytes 1000000 | tf_op jit(solution)/shard_map/attention_forward/pallas_call | solution.py:801
  501.5 7.4 collective-permute-done.40
  518.6 4.8 slice_bitcast_fusion
  523.5 21.5 %collective-permute-done.41 = bf16[256,1536]{1,0:T(8,128)(2,1)S(1)} collective-permute-done((bf16[256,1536]{1,0:T(8,128)(2,1)S(1)}, bf16[256,1536]{1,0:T(8,128)(2,1)S(1)}, u32[]{:S(2)}, u32[]{:S(2)}) %collective-permute-start.41) | collective-permute-done | bytes 786464 | tf_op jit(solution)/shard_map/ppermute | solution.py:50
  548.4 34.7 %collective-permute-done.43 = bf16[256,1536]{1,0:T(8,128)(2,1)S(1)} collective-permute-done((bf16[256,1536]{1,0:T(8,128)(2,1)S(1)}, bf16[256,1536]{1,0:T(8,128)(2,1)S(1)}, u32[]{:S(2)}, u32[]{:S(2)}) %collective-permute-start.43) | collective-permute-done | bytes 786464 | tf_op jit(solution)/shard_map/ppermute | solution.py:50
  587.0 34.2 %moe_forward.3 = (bf16[1024,1536]{1,0:T(8,128)(2,1)}, bf16[5,1024,1024]{2,1,0:T(8,128)(2,1)}) custom-call(bf16[1024,1536]{1,0:T(8,128)(2,1)} %copy-done.31, f32[1024,128]{1,0:T(8,128)} %pad.15.gates_ref, bf16[8,5,384,768]{3,2,1,0:T(8,128)(2,1)} %bitcast.243), custom_call_target="tpu_custom_call" | custom-call | flops 44000002048 | bytes 1000000 | tf_op jit(solution)/shard_map/moe_forward/pallas_call | solution.py:198
  621.3 40.6 %moe_backward_rows.2 = (bf16[1024,1664]{1,0:T(8,128)(2,1)}, bf16[5,1024,1024]{2,1,0:T(8,128)(2,1)}, bf16[5,1024,512]{2,1,0:T(8,128)(2,1)}) custom-call(bf16[1024,1536]{1,0:T(8,128)(2,1)} %constant_dynamic-update-slice_fusion.9.grads_ref, f32[1024,128]{1,0:T(8,128)} %pad.15.gates_ref, bf16[5,1024,1024]{2,1,0:T(8,128)(2,1)} %get-tuple-element.114.raw_ref, ...), custom_call_target="tpu_custom_call" | custom-call | flops 52800000000 | bytes 1000000 | tf_op jit(solution)/shard_map/moe_backward_rows/pallas_call | solution.py:293
  667.6 33.3 %moe_backward_weights.2 = bf16[8,5,384,768]{3,2,1,0:T(8,128)(2,1)} custom-call(bf16[1024,1536]{1,0:T(8,128)(2,1)} %copy-done.31, bf16[1024,1536]{1,0:T(8,128)(2,1)} %constant_dynamic-update-slice_fusion.9.grads_ref, bf16[5,1024,1024]{2,1,0:T(8,128)(2,1)} %get-tuple-element.116.d_raw_ref, bf16[5,1024,512]{2,1,0:T(8,128)(2,1)} %get-tuple-element.117.act_ref), custom_call_target="tpu_custom_call" | custom-call | flops 37399998464 | bytes 1000000 | tf_op jit(solution)/shard_map/moe_backward_weights/pallas_call | solution.py:355
  701.7 35.5 %collective-permute-done.46.refs_3_ = bf16[256,1664]{1,0:T(8,128)(2,1)} collective-permute-done((bf16[256,1664]{1,0:T(8,128)(2,1)S(1)}, bf16[256,1664]{1,0:T(8,128)(2,1)}, u32[]{:S(2)}, u32[]{:S(2)}) %collective-permute-start.46) | collective-permute-done | bytes 852000 | tf_op jit(solution)/shard_map/ppermute | solution.py:50
  737.3 8.8 branch_backward.2
  751.7 27.0 %attention_backward.2 = (bf16[256,1536]{1,0:T(8,128)(2,1)}, bf16[256,1024]{1,0:T(8,128)(2,1)}, bf16[256,1024]{1,0:T(8,128)(2,1)}, bf16[256,1024]{1,0:T(8,128)(2,1)}, bf16[256,1024]{1,0:T(8,128)(2,1)}) custom-call(s32[4]{0:T(128)} %pad_add_fusion.1.owner_ref, s32[1024,128]{1,0:T(8,128)} %broadcast_in_dim.37.seg_all_ref, s32[8,256]{1,0:T(8,128)} %broadcast_in_dim.38.seg_ref, ...), custom_call_target="tpu_custom_call" | custom-call | flops 29699999744 | bytes 1000000 | tf_op jit(solution)/shard_map/attention_backward/pallas_call | solution.py:879
  783.7 30.9 %collective-permute-done.49 = bf16[256,1536]{1,0:T(8,128)(2,1)} collective-permute-done((bf16[256,1536]{1,0:T(8,128)(2,1)S(1)}, bf16[256,1536]{1,0:T(8,128)(2,1)}, u32[]{:S(2)}, u32[]{:S(2)}) %collective-permute-start.49) | collective-permute-done | bytes 786464 | tf_op jit(solution)/shard_map/ppermute | solution.py:50
  818.8 16.9 %qkv_backward.2 = (f32[256,1536]{1,0:T(8,128)}, bf16[8,4,96,2176]{3,2,1,0:T(8,128)(2,1)}) custom-call(s32[1]{0:T(128)} %constant.292.clone.1.flip_ref, bf16[256,1536]{1,0:T(8,128)(2,1)} %get-tuple-element.129.n_ref, bf16[256,1536]{1,0:T(8,128)(2,1)} %get-tuple-element.130.dq_ref, bf16[256,1024]{1,0:T(8,128)(2,1)} %get-tuple-element.125.refs_0_, ...), custom_call_target="tpu_custom_call" | custom-call | flops 15399999488 | bytes 1000000 | tf_op jit(solution)/shard_map/qkv_backward/pallas_call | solution.py:682
  840.9 24.5 %collective-permute-done.54 = bf16[256,1536]{1,0:T(8,128)(2,1)S(1)} collective-permute-done((bf16[256,1536]{1,0:T(8,128)(2,1)S(1)}, bf16[256,1536]{1,0:T(8,128)(2,1)S(1)}, u32[]{:S(2)}, u32[]{:S(2)}) %collective-permute-start.54) | collective-permute-done | bytes 786464 | tf_op jit(solution)/shard_map/ppermute | solution.py:50
  866.7 35.6 %collective-permute-done.56 = bf16[256,1536]{1,0:T(8,128)(2,1)S(1)} collective-permute-done((bf16[256,1536]{1,0:T(8,128)(2,1)S(1)}, bf16[256,1536]{1,0:T(8,128)(2,1)S(1)}, u32[]{:S(2)}, u32[]{:S(2)}) %collective-permute-start.56) | collective-permute-done | bytes 786464 | tf_op jit(solution)/shard_map/ppermute | solution.py:50
  904.1 5.3 reduce-scatter.4.cloned.1.call-done
  911.5 40.8 %moe_backward_rows.3 = (bf16[1024,1664]{1,0:T(8,128)(2,1)}, bf16[5,1024,1024]{2,1,0:T(8,128)(2,1)}, bf16[5,1024,512]{2,1,0:T(8,128)(2,1)}) custom-call(bf16[1024,1536]{1,0:T(8,128)(2,1)} %pad_maximum_fusion.3.grads_ref, f32[1024,128]{1,0:T(8,128)} %pad.14.gates_ref, bf16[5,1024,1024]{2,1,0:T(8,128)(2,1)} %get-tuple-element.138.raw_ref, ...), custom_call_target="tpu_custom_call" | custom-call | flops 52800000000 | bytes 1000000 | tf_op jit(solution)/shard_map/moe_backward_rows/pallas_call | solution.py:293
  958.0 33.6 %moe_backward_weights.3 = bf16[8,5,384,768]{3,2,1,0:T(8,128)(2,1)} custom-call(bf16[1024,1536]{1,0:T(8,128)(2,1)} %copy-done.30, bf16[1024,1536]{1,0:T(8,128)(2,1)} %pad_maximum_fusion.3.grads_ref, bf16[5,1024,1024]{2,1,0:T(8,128)(2,1)} %get-tuple-element.140.d_raw_ref, bf16[5,1024,512]{2,1,0:T(8,128)(2,1)} %get-tuple-element.141.act_ref), custom_call_target="tpu_custom_call" | custom-call | flops 37399998464 | bytes 1000000 | tf_op jit(solution)/shard_map/moe_backward_weights/pallas_call | solution.py:355
  994.5 35.4 %collective-permute-done.59.refs_3_ = bf16[256,1664]{1,0:T(8,128)(2,1)} collective-permute-done((bf16[256,1664]{1,0:T(8,128)(2,1)S(1)}, bf16[256,1664]{1,0:T(8,128)(2,1)}, u32[]{:S(2)}, u32[]{:S(2)}) %collective-permute-start.59) | collective-permute-done | bytes 852000 | tf_op jit(solution)/shard_map/ppermute | solution.py:50
  1029.9 8.8 branch_backward.3
  1044.5 27.4 %attention_backward.3 = (bf16[256,1536]{1,0:T(8,128)(2,1)}, bf16[256,1024]{1,0:T(8,128)(2,1)}, bf16[256,1024]{1,0:T(8,128)(2,1)}, bf16[256,1024]{1,0:T(8,128)(2,1)}, bf16[256,1024]{1,0:T(8,128)(2,1)}) custom-call(s32[4]{0:T(128)} %pad_add_fusion.1.owner_ref, s32[1024,128]{1,0:T(8,128)} %broadcast_in_dim.37.seg_all_ref, s32[8,256]{1,0:T(8,128)} %broadcast_in_dim.38.seg_ref, ...), custom_call_target="tpu_custom_call" | custom-call | flops 29699999744 | bytes 1000000 | tf_op jit(solution)/shard_map/attention_backward/pallas_call | solution.py:879
  1074.7 3.6 collective-permute-done.62
  1078.5 4.5 collective-permute-done.63.refs_1_
  1083.0 22.0 %collective-permute-done.65.refs_3_ = bf16[256,1024]{1,0:T(8,128)(2,1)} collective-permute-done((bf16[256,1024]{1,0:T(8,128)(2,1)}, bf16[256,1024]{1,0:T(8,128)(2,1)}, u32[]{:S(2)}, u32[]{:S(2)}) %collective-permute-start.65) | collective-permute-done | bytes 524320 | tf_op jit(solution)/shard_map/ppermute | solution.py:50
  1105.0 13.7 %qkv_backward.3 = (f32[256,1536]{1,0:T(8,128)}, bf16[8,4,96,1408]{3,2,1,0:T(8,128)(2,1)}) custom-call(s32[1]{0:T(128)} %bitcast.58.flip_ref.core_ref, bf16[256,1536]{1,0:T(8,128)(2,1)} %get-tuple-element.144.n_ref, bf16[256,1536]{1,0:T(8,128)(2,1)} %get-tuple-element.157.dq_ref, bf16[256,1024]{1,0:T(8,128)(2,1)} %get-tuple-element.155.refs_0_, ...), custom_call_target="tpu_custom_call" | custom-call | flops 15399999488 | bytes 1000000 | tf_op jit(solution)/shard_map/qkv_backward/pallas_call | solution.py:682
  1118.7 4.9 constant_dynamic-slice_fusion.1
  1123.6 10.9 collective-permute-start.67
  1136.6 5.2 collective-permute-done.67
  1141.8 5.3 fusion.12
  1159.0 27.9 %collective-permute-done.68 = bf16[4,96,1408]{2,1,0:T(8,128)(2,1)S(1)} collective-permute-done((bf16[4,96,1408]{2,1,0:T(8,128)(2,1)}, bf16[4,96,1408]{2,1,0:T(8,128)(2,1)S(1)}, u32[]{:S(2)}, u32[]{:S(2)}) %collective-permute-start.68) | collective-permute-done | bytes 1081376 | tf_op jit(solution)/shard_map/ppermute | solution.py:50
  1189.0 44.7 %collective-permute-done.70 = bf16[4,96,1408]{2,1,0:T(8,128)(2,1)} collective-permute-done((bf16[4,96,1408]{2,1,0:T(8,128)(2,1)}, bf16[4,96,1408]{2,1,0:T(8,128)(2,1)}, u32[]{:S(2)}, u32[]{:S(2)}) %collective-permute-start.70) | collective-permute-done | bytes 1081376 | tf_op jit(solution)/shard_map/ppermute | solution.py:50
  1243.8 4.9 collective-permute-done.75
  1248.7 4.7 broadcast_select_fusion
  1270.8 7.8 expert_outputs.1
  1278.7 5.6 collective-permute-done.77
  1284.3 8.7 collective-permute-done.78
  (436 shorter events, 235.4 us)
Async XLA Ops:
  7.2 113.2 %all-gather.11.cloned.1.call-start = ((), (), s32[]{:S(2)}) async-start(), calls=%async_computation.7 | async-start | bytes 2088960 | tf_op jit(solution)/shard_map/all_gather | solution.py:1034
  19.2 23.5 %collective-permute-start.6 = (bf16[96,1408]{1,0:T(8,128)(2,1)S(1)}, bf16[96,1408]{1,0:T(8,128)(2,1)S(1)}, u32[]{:S(2)}, u32[]{:S(2)}) collective-permute-start(bf16[96,1408]{1,0:T(8,128)(2,1)S(1)} %get-tuple-element.323), channel_id=1, source_target_pairs={{0,12},{4,8},{8,4},{12,0},{1,13},{5,9},{9,5},{13,1},{2,14},{6,10},... | collective-permute-start | bytes 811016 | tf_op jit(solution)/shard_map/ppermute | solution.py:50
  43.9 24.2 %collective-permute-start.7 = (bf16[4,96,1408]{2,1,0:T(8,128)(2,1)}, bf16[4,96,1408]{2,1,0:T(8,128)(2,1)}, u32[]{:S(2)}, u32[]{:S(2)}) collective-permute-start(bf16[4,96,1408]{2,1,0:T(8,128)(2,1)} %pad_maximum_fusion.6.refs_0_), channel_id=1, source_target_pairs={{0,1},{1,0},{2,3},{3,2},{4,5},{5,4},{6,7},{7,6},{8,9},{9,8},{10,11... | collective-permute-start | bytes 3244040 | tf_op jit(solution)/shard_map/ppermute | solution.py:43
  45.1 23.9 %collective-permute-start.8 = (bf16[4,96,1408]{2,1,0:T(8,128)(2,1)}, bf16[4,96,1408]{2,1,0:T(8,128)(2,1)}, u32[]{:S(2)}, u32[]{:S(2)}) collective-permute-start(bf16[4,96,1408]{2,1,0:T(8,128)(2,1)} %pad_maximum_fusion.6.refs_0_), channel_id=1, source_target_pairs={{0,2},{1,3},{2,0},{3,1},{4,6},{5,7},{6,4},{7,5},{8,10},{9,11},{10,... | collective-permute-start | bytes 3244040 | tf_op jit(solution)/shard_map/ppermute | solution.py:43
  72.1 32.3 %collective-permute-start.31 = (bf16[5,384,768]{2,1,0:T(8,128)(2,1)}, bf16[5,384,768]{2,1,0:T(8,128)(2,1)}, u32[]{:S(2)}, u32[]{:S(2)}) collective-permute-start(bf16[5,384,768]{2,1,0:T(8,128)(2,1)} %broadcast_select_fusion.4), channel_id=1, source_target_pairs={{0,16},{16,0},{1,17},{17,1},{2,18},{18,2},{3,19},{19,3},{4,20},{20... | collective-permute-start | bytes 8847368 | tf_op jit(solution)/shard_map/ppermute | solution.py:34
  83.9 237.9 %all-gather.9.cloned.1.call-start = ((), (), s32[]{:S(2)}) async-start(), calls=%async_computation.6 | async-start | bytes 26542080 | tf_op jit(solution)/shard_map/all_gather | solution.py:1031
  93.2 16.2 %collective-permute-start.9 = (bf16[2,96,1408]{2,1,0:T(8,128)(2,1)S(1)}, bf16[2,96,1408]{2,1,0:T(8,128)(2,1)S(1)}, u32[]{:S(2)}, u32[]{:S(2)}) collective-permute-start(bf16[2,96,1408]{2,1,0:T(8,128)(2,1)S(1)} %slice.315), channel_id=1, source_target_pairs={{0,2},{1,3},{2,0},{3,1},{4,6},{5,7},{6,4},{7,5},{8,10},{9,11},{10,... | collective-permute-start | bytes 1622024 | tf_op jit(solution)/shard_map/ppermute | solution.py:43
  110.2 252.5 %all-gather.13.cloned.1.call-start = ((), (), s32[]{:S(2)}) async-start(), calls=%async_computation.8 | async-start | bytes 15040512 | tf_op jit(solution)/shard_map/all_gather | solution.py:1037
  120.4 466.6 %all-gather.15.cloned.1.call-start = ((), (), s32[]{:S(2)}) async-start(), calls=%async_computation.9 | async-start | bytes 26542080 | tf_op jit(solution)/shard_map/all_gather | solution.py:1043
  121.0 788.5 %reduce-scatter.4.cloned.1.call-start = ((), (), s32[]{:S(2)}) async-start(), calls=%async_computation.3 | async-start | bytes 26542080 | tf_op jit(solution)/shard_map/reduce_scatter | solution.py:1163
  127.5 20.8 %collective-permute-start.15 = (bf16[1536,1408]{1,0:T(8,128)(2,1)}, bf16[1536,1408]{1,0:T(8,128)(2,1)}, u32[]{:S(2)}, u32[]{:S(2)}) collective-permute-start(bf16[1536,1408]{1,0:T(8,128)(2,1)} %line_up.2), channel_id=1, source_target_pairs={{0,16},{16,0},{1,17},{17,1},{2,18},{18,2},{3,19},{19,3},{4,20},{20... | collective-permute-start | bytes 12976136 | tf_op jit(solution)/shard_map/ppermute | solution.py:34
  145.9 27.6 %collective-permute-start.23 = (bf16[4,96,768]{2,1,0:T(8,128)(2,1)S(1)}, bf16[4,96,768]{2,1,0:T(8,128)(2,1)S(1)}, u32[]{:S(2)}, u32[]{:S(2)}) collective-permute-start(bf16[4,96,768]{2,1,0:T(8,128)(2,1)S(1)} %pad_maximum_fusion.8.refs_0_), channel_id=1, source_target_pairs={{0,1},{1,0},{2,3},{3,2},{4,5},{5,4},{6,7},{7,6},{8,9},{9,8},{10,11... | collective-permute-start | bytes 1769480 | tf_op jit(solution)/shard_map/ppermute | solution.py:43
  147.2 27.5 %collective-permute-start.24 = (bf16[4,96,768]{2,1,0:T(8,128)(2,1)S(1)}, bf16[4,96,768]{2,1,0:T(8,128)(2,1)S(1)}, u32[]{:S(2)}, u32[]{:S(2)}) collective-permute-start(bf16[4,96,768]{2,1,0:T(8,128)(2,1)S(1)} %pad_maximum_fusion.8.refs_0_), channel_id=1, source_target_pairs={{0,2},{1,3},{2,0},{3,1},{4,6},{5,7},{6,4},{7,5},{8,10},{9,11},{10,... | collective-permute-start | bytes 1769480 | tf_op jit(solution)/shard_map/ppermute | solution.py:43
  176.4 21.3 %collective-permute-start.16 = (bf16[256,1024]{1,0:T(8,128)(2,1)}, bf16[256,1024]{1,0:T(8,128)(2,1)}, u32[]{:S(2)}, u32[]{:S(2)}) collective-permute-start(bf16[256,1024]{1,0:T(8,128)(2,1)} %get-tuple-element.98.refs_0_), channel_id=1, source_target_pairs={{0,1},{1,0},{2,3},{3,2},{4,5},{5,4},{6,7},{7,6},{8,9},{9,8},{10,11... | collective-permute-start | bytes 1572872 | tf_op jit(solution)/shard_map/ppermute | solution.py:50
  177.5 22.2 %collective-permute-start.17 = (bf16[256,1024]{1,0:T(8,128)(2,1)}, bf16[256,1024]{1,0:T(8,128)(2,1)}, u32[]{:S(2)}, u32[]{:S(2)}) collective-permute-start(bf16[256,1024]{1,0:T(8,128)(2,1)} %get-tuple-element.98.refs_0_), channel_id=1, source_target_pairs={{0,2},{1,3},{2,0},{3,1},{4,6},{5,7},{6,4},{7,5},{8,10},{9,11},{10,... | collective-permute-start | bytes 1572872 | tf_op jit(solution)/shard_map/ppermute | solution.py:50
  177.7 44.1 %collective-permute-start.18 = (bf16[256,1024]{1,0:T(8,128)(2,1)}, bf16[256,1024]{1,0:T(8,128)(2,1)}, u32[]{:S(2)}, u32[]{:S(2)}) collective-permute-start(bf16[256,1024]{1,0:T(8,128)(2,1)} %get-tuple-element.98.refs_0_), channel_id=1, source_target_pairs={{0,3},{1,2},{2,1},{3,0},{4,7},{5,6},{6,5},{7,4},{8,11},{9,10},{10,... | collective-permute-start | bytes 1572872 | tf_op jit(solution)/shard_map/ppermute | solution.py:50
  191.7 50.3 %collective-permute-start.27 = (bf16[1536,768]{1,0:T(8,128)(2,1)}, bf16[1536,768]{1,0:T(8,128)(2,1)S(1)}, u32[]{:S(2)}, u32[]{:S(2)}) collective-permute-start(bf16[1536,768]{1,0:T(8,128)(2,1)} %line_up.3.refs_9_), channel_id=1, source_target_pairs={{0,16},{16,0},{1,17},{17,1},{2,18},{18,2},{3,19},{19,3},{4,20},{20... | collective-permute-start | bytes 7077896 | tf_op jit(solution)/shard_map/ppermute | solution.py:34
  247.9 29.9 %collective-permute-start.28 = (bf16[256,1536]{1,0:T(8,128)(2,1)}, bf16[256,1536]{1,0:T(8,128)(2,1)}, u32[]{:S(2)}, u32[]{:S(2)}) collective-permute-start(bf16[256,1536]{1,0:T(8,128)(2,1)} %multiply_convert_fusion.1.refs_9_), channel_id=1, source_target_pairs={{0,4},{4,0},{8,12},{12,8},{1,5},{5,1},{9,13},{13,9},{2,6},{6,2},{1... | collective-permute-start | bytes 2359304 | tf_op jit(solution)/shard_map/ppermute | solution.py:50
  247.9 34.0 %collective-permute-start.29 = (bf16[256,1536]{1,0:T(8,128)(2,1)}, bf16[256,1536]{1,0:T(8,128)(2,1)}, u32[]{:S(2)}, u32[]{:S(2)}) collective-permute-start(bf16[256,1536]{1,0:T(8,128)(2,1)} %multiply_convert_fusion.1.refs_9_), channel_id=1, source_target_pairs={{0,8},{4,12},{8,0},{12,4},{1,9},{5,13},{9,1},{13,5},{2,10},{6,14},... | collective-permute-start | bytes 2359304 | tf_op jit(solution)/shard_map/ppermute | solution.py:50
  250.3 65.3 %collective-permute-start.30 = (bf16[256,1536]{1,0:T(8,128)(2,1)}, bf16[256,1536]{1,0:T(8,128)(2,1)}, u32[]{:S(2)}, u32[]{:S(2)}) collective-permute-start(bf16[256,1536]{1,0:T(8,128)(2,1)} %multiply_convert_fusion.1.refs_9_), channel_id=1, source_target_pairs={{0,12},{4,8},{8,4},{12,0},{1,13},{5,9},{9,5},{13,1},{2,14},{6,10},... | collective-permute-start | bytes 2359304 | tf_op jit(solution)/shard_map/ppermute | solution.py:50
  360.1 29.1 %collective-permute-start.32 = (bf16[256,1536]{1,0:T(8,128)(2,1)}, bf16[256,1536]{1,0:T(8,128)(2,1)}, u32[]{:S(2)}, u32[]{:S(2)}) collective-permute-start(bf16[256,1536]{1,0:T(8,128)(2,1)} %get-tuple-element.285), channel_id=1, source_target_pairs={{0,4},{4,0},{8,12},{12,8},{1,5},{5,1},{9,13},{13,9},{2,6},{6,2},{1... | collective-permute-start | bytes 2359304 | tf_op jit(solution)/shard_map/ppermute | solution.py:50
  360.1 32.4 %collective-permute-start.33 = (bf16[256,1536]{1,0:T(8,128)(2,1)}, bf16[256,1536]{1,0:T(8,128)(2,1)}, u32[]{:S(2)}, u32[]{:S(2)}) collective-permute-start(bf16[256,1536]{1,0:T(8,128)(2,1)} %get-tuple-element.284), channel_id=1, source_target_pairs={{0,8},{4,12},{8,0},{12,4},{1,9},{5,13},{9,1},{13,5},{2,10},{6,14},... | collective-permute-start | bytes 2359304 | tf_op jit(solution)/shard_map/ppermute | solution.py:50
  362.5 63.8 %collective-permute-start.34 = (bf16[256,1536]{1,0:T(8,128)(2,1)}, bf16[256,1536]{1,0:T(8,128)(2,1)}, u32[]{:S(2)}, u32[]{:S(2)}) collective-permute-start(bf16[256,1536]{1,0:T(8,128)(2,1)} %get-tuple-element.283), channel_id=1, source_target_pairs={{0,12},{4,8},{8,4},{12,0},{1,13},{5,9},{9,5},{13,1},{2,14},{6,10},... | collective-permute-start | bytes 2359304 | tf_op jit(solution)/shard_map/ppermute | solution.py:50
  437.3 23.3 %collective-permute-start.35 = (bf16[256,1024]{1,0:T(8,128)(2,1)}, bf16[256,1024]{1,0:T(8,128)(2,1)}, u32[]{:S(2)}, u32[]{:S(2)}) collective-permute-start(bf16[256,1024]{1,0:T(8,128)(2,1)} %get-tuple-element.110.refs_0_), channel_id=1, source_target_pairs={{0,1},{1,0},{2,3},{3,2},{4,5},{5,4},{6,7},{7,6},{8,9},{9,8},{10,11... | collective-permute-start | bytes 1572872 | tf_op jit(solution)/shard_map/ppermute | solution.py:50
  437.8 24.0 %collective-permute-start.36 = (bf16[256,1024]{1,0:T(8,128)(2,1)}, bf16[256,1024]{1,0:T(8,128)(2,1)}, u32[]{:S(2)}, u32[]{:S(2)}) collective-permute-start(bf16[256,1024]{1,0:T(8,128)(2,1)} %get-tuple-element.110.refs_0_), channel_id=1, source_target_pairs={{0,2},{1,3},{2,0},{3,1},{4,6},{5,7},{6,4},{7,5},{8,10},{9,11},{10,... | collective-permute-start | bytes 1572872 | tf_op jit(solution)/shard_map/ppermute | solution.py:50
  437.8 44.5 %collective-permute-start.37 = (bf16[256,1024]{1,0:T(8,128)(2,1)}, bf16[256,1024]{1,0:T(8,128)(2,1)}, u32[]{:S(2)}, u32[]{:S(2)}) collective-permute-start(bf16[256,1024]{1,0:T(8,128)(2,1)} %get-tuple-element.110.refs_0_), channel_id=1, source_target_pairs={{0,3},{1,2},{2,1},{3,0},{4,7},{5,6},{6,5},{7,4},{8,11},{9,10},{10,... | collective-permute-start | bytes 1572872 | tf_op jit(solution)/shard_map/ppermute | solution.py:50
  440.0 59.6 %collective-permute-start.38 = (bf16[256,1536]{1,0:T(8,128)(2,1)S(1)}, bf16[256,1536]{1,0:T(8,128)(2,1)S(1)}, u32[]{:S(2)}, u32[]{:S(2)}) collective-permute-start(bf16[256,1536]{1,0:T(8,128)(2,1)S(1)} %dynamic-slice_bitcast_fusion.refs_8_), channel_id=1, source_target_pairs={{0,4},{4,0},{8,12},{12,8},{1,5},{5,1},{9,13},{13,9},{2,6},{6,2},{1... | collective-permute-start | bytes 2359304 | tf_op jit(solution)/shard_map/ppermute | solution.py:50
  440.1 60.5 %collective-permute-start.39 = (bf16[256,1536]{1,0:T(8,128)(2,1)S(1)}, bf16[256,1536]{1,0:T(8,128)(2,1)S(1)}, u32[]{:S(2)}, u32[]{:S(2)}) collective-permute-start(bf16[256,1536]{1,0:T(8,128)(2,1)S(1)} %dynamic-slice_bitcast_fusion.refs_8_), channel_id=1, source_target_pairs={{0,8},{4,12},{8,0},{12,4},{1,9},{5,13},{9,1},{13,5},{2,10},{6,14},... | collective-permute-start | bytes 2359304 | tf_op jit(solution)/shard_map/ppermute | solution.py:50
  460.6 48.3 %collective-permute-start.40 = (bf16[256,1536]{1,0:T(8,128)(2,1)S(1)}, bf16[256,1536]{1,0:T(8,128)(2,1)S(1)}, u32[]{:S(2)}, u32[]{:S(2)}) collective-permute-start(bf16[256,1536]{1,0:T(8,128)(2,1)S(1)} %dynamic-slice_bitcast_fusion.refs_8_), channel_id=1, source_target_pairs={{0,12},{4,8},{8,4},{12,0},{1,13},{5,9},{9,5},{13,1},{2,14},{6,10},... | collective-permute-start | bytes 2359304 | tf_op jit(solution)/shard_map/ppermute | solution.py:50
  515.3 29.6 %collective-permute-start.41 = (bf16[256,1536]{1,0:T(8,128)(2,1)S(1)}, bf16[256,1536]{1,0:T(8,128)(2,1)S(1)}, u32[]{:S(2)}, u32[]{:S(2)}) collective-permute-start(bf16[256,1536]{1,0:T(8,128)(2,1)S(1)} %multiply_convert_fusion.refs_9_), channel_id=1, source_target_pairs={{0,4},{4,0},{8,12},{12,8},{1,5},{5,1},{9,13},{13,9},{2,6},{6,2},{1... | collective-permute-start | bytes 2359304 | tf_op jit(solution)/shard_map/ppermute | solution.py:50
  515.4 33.0 %collective-permute-start.42 = (bf16[256,1536]{1,0:T(8,128)(2,1)S(1)}, bf16[256,1536]{1,0:T(8,128)(2,1)S(1)}, u32[]{:S(2)}, u32[]{:S(2)}) collective-permute-start(bf16[256,1536]{1,0:T(8,128)(2,1)S(1)} %multiply_convert_fusion.refs_9_), channel_id=1, source_target_pairs={{0,8},{4,12},{8,0},{12,4},{1,9},{5,13},{9,1},{13,5},{2,10},{6,14},... | collective-permute-start | bytes 2359304 | tf_op jit(solution)/shard_map/ppermute | solution.py:50
  517.3 65.8 %collective-permute-start.43 = (bf16[256,1536]{1,0:T(8,128)(2,1)S(1)}, bf16[256,1536]{1,0:T(8,128)(2,1)S(1)}, u32[]{:S(2)}, u32[]{:S(2)}) collective-permute-start(bf16[256,1536]{1,0:T(8,128)(2,1)S(1)} %multiply_convert_fusion.refs_9_), channel_id=1, source_target_pairs={{0,12},{4,8},{8,4},{12,0},{1,13},{5,9},{9,5},{13,1},{2,14},{6,10},... | collective-permute-start | bytes 2359304 | tf_op jit(solution)/shard_map/ppermute | solution.py:50
  665.0 36.7 %collective-permute-start.44 = (bf16[256,1664]{1,0:T(8,128)(2,1)S(1)}, bf16[256,1664]{1,0:T(8,128)(2,1)}, u32[]{:S(2)}, u32[]{:S(2)}) collective-permute-start(bf16[256,1664]{1,0:T(8,128)(2,1)S(1)} %get-tuple-element.276), channel_id=1, source_target_pairs={{0,4},{4,0},{8,12},{12,8},{1,5},{5,1},{9,13},{13,9},{2,6},{6,2},{1... | collective-permute-start | bytes 2555912 | tf_op jit(solution)/shard_map/ppermute | solution.py:50
  665.0 36.7 %collective-permute-start.45 = (bf16[256,1664]{1,0:T(8,128)(2,1)S(1)}, bf16[256,1664]{1,0:T(8,128)(2,1)}, u32[]{:S(2)}, u32[]{:S(2)}) collective-permute-start(bf16[256,1664]{1,0:T(8,128)(2,1)S(1)} %get-tuple-element.275), channel_id=1, source_target_pairs={{0,8},{4,12},{8,0},{12,4},{1,9},{5,13},{9,1},{13,5},{2,10},{6,14},... | collective-permute-start | bytes 2555912 | tf_op jit(solution)/shard_map/ppermute | solution.py:50
  666.4 70.8 %collective-permute-start.46 = (bf16[256,1664]{1,0:T(8,128)(2,1)S(1)}, bf16[256,1664]{1,0:T(8,128)(2,1)}, u32[]{:S(2)}, u32[]{:S(2)}) collective-permute-start(bf16[256,1664]{1,0:T(8,128)(2,1)S(1)} %get-tuple-element.274), channel_id=1, source_target_pairs={{0,12},{4,8},{8,4},{12,0},{1,13},{5,9},{9,5},{13,1},{2,14},{6,10},... | collective-permute-start | bytes 2555912 | tf_op jit(solution)/shard_map/ppermute | solution.py:50
  746.1 292.6 %reduce-scatter.6.cloned.1.call-start = ((), (), s32[]{:S(2)}) async-start(), calls=%async_computation.4 | async-start | bytes 15040512 | tf_op jit(solution)/shard_map/reduce_scatter | solution.py:1288
  749.1 33.3 %collective-permute-start.47 = (bf16[256,1536]{1,0:T(8,128)(2,1)}, bf16[256,1536]{1,0:T(8,128)(2,1)}, u32[]{:S(2)}, u32[]{:S(2)}) collective-permute-start(bf16[256,1536]{1,0:T(8,128)(2,1)} %get-tuple-element.281), channel_id=1, source_target_pairs={{0,4},{4,0},{8,12},{12,8},{1,5},{5,1},{9,13},{13,9},{2,6},{6,2},{1... | collective-permute-start | bytes 2359304 | tf_op jit(solution)/shard_map/ppermute | solution.py:50
  749.1 34.6 %collective-permute-start.48 = (bf16[256,1536]{1,0:T(8,128)(2,1)S(1)}, bf16[256,1536]{1,0:T(8,128)(2,1)}, u32[]{:S(2)}, u32[]{:S(2)}) collective-permute-start(bf16[256,1536]{1,0:T(8,128)(2,1)S(1)} %get-tuple-element.280), channel_id=1, source_target_pairs={{0,8},{4,12},{8,0},{12,4},{1,9},{5,13},{9,1},{13,5},{2,10},{6,14},... | collective-permute-start | bytes 2359304 | tf_op jit(solution)/shard_map/ppermute | solution.py:50
  750.1 64.6 %collective-permute-start.49 = (bf16[256,1536]{1,0:T(8,128)(2,1)S(1)}, bf16[256,1536]{1,0:T(8,128)(2,1)}, u32[]{:S(2)}, u32[]{:S(2)}) collective-permute-start(bf16[256,1536]{1,0:T(8,128)(2,1)S(1)} %get-tuple-element.279), channel_id=1, source_target_pairs={{0,12},{4,8},{8,4},{12,0},{1,13},{5,9},{9,5},{13,1},{2,14},{6,10},... | collective-permute-start | bytes 2359304 | tf_op jit(solution)/shard_map/ppermute | solution.py:50
  778.7 38.9 %collective-permute-start.51 = (bf16[256,1024]{1,0:T(8,128)(2,1)}, bf16[256,1024]{1,0:T(8,128)(2,1)S(1)}, u32[]{:S(2)}, u32[]{:S(2)}) collective-permute-start(bf16[256,1024]{1,0:T(8,128)(2,1)} %get-tuple-element.131), channel_id=1, source_target_pairs={{0,1},{1,0},{2,3},{3,2},{4,5},{5,4},{6,7},{7,6},{8,9},{9,8},{10,11... | collective-permute-start | bytes 1572872 | tf_op jit(solution)/shard_map/ppermute | solution.py:50
  780.3 37.4 %collective-permute-start.52 = (bf16[256,1024]{1,0:T(8,128)(2,1)}, bf16[256,1024]{1,0:T(8,128)(2,1)S(1)}, u32[]{:S(2)}, u32[]{:S(2)}) collective-permute-start(bf16[256,1024]{1,0:T(8,128)(2,1)} %get-tuple-element.132), channel_id=1, source_target_pairs={{0,2},{1,3},{2,0},{3,1},{4,6},{5,7},{6,4},{7,5},{8,10},{9,11},{10,... | collective-permute-start | bytes 1572872 | tf_op jit(solution)/shard_map/ppermute | solution.py:50
  782.4 35.3 %collective-permute-start.53 = (bf16[256,1024]{1,0:T(8,128)(2,1)}, bf16[256,1024]{1,0:T(8,128)(2,1)S(1)}, u32[]{:S(2)}, u32[]{:S(2)}) collective-permute-start(bf16[256,1024]{1,0:T(8,128)(2,1)} %get-tuple-element.133), channel_id=1, source_target_pairs={{0,3},{1,2},{2,1},{3,0},{4,7},{5,6},{6,5},{7,4},{8,11},{9,10},{10,... | collective-permute-start | bytes 1572872 | tf_op jit(solution)/shard_map/ppermute | solution.py:50
  838.1 27.2 %collective-permute-start.54 = (bf16[256,1536]{1,0:T(8,128)(2,1)S(1)}, bf16[256,1536]{1,0:T(8,128)(2,1)S(1)}, u32[]{:S(2)}, u32[]{:S(2)}) collective-permute-start(bf16[256,1536]{1,0:T(8,128)(2,1)S(1)} %add_convert_fusion.3.refs_8_), channel_id=1, source_target_pairs={{0,4},{4,0},{8,12},{12,8},{1,5},{5,1},{9,13},{13,9},{2,6},{6,2},{1... | collective-permute-start | bytes 2359304 | tf_op jit(solution)/shard_map/ppermute | solution.py:50
  838.2 28.5 %collective-permute-start.55 = (bf16[256,1536]{1,0:T(8,128)(2,1)S(1)}, bf16[256,1536]{1,0:T(8,128)(2,1)S(1)}, u32[]{:S(2)}, u32[]{:S(2)}) collective-permute-start(bf16[256,1536]{1,0:T(8,128)(2,1)S(1)} %add_convert_fusion.3.refs_8_), channel_id=1, source_target_pairs={{0,8},{4,12},{8,0},{12,4},{1,9},{5,13},{9,1},{13,5},{2,10},{6,14},... | collective-permute-start | bytes 2359304 | tf_op jit(solution)/shard_map/ppermute | solution.py:50
  838.9 63.4 %collective-permute-start.56 = (bf16[256,1536]{1,0:T(8,128)(2,1)S(1)}, bf16[256,1536]{1,0:T(8,128)(2,1)S(1)}, u32[]{:S(2)}, u32[]{:S(2)}) collective-permute-start(bf16[256,1536]{1,0:T(8,128)(2,1)S(1)} %add_convert_fusion.3.refs_8_), channel_id=1, source_target_pairs={{0,12},{4,8},{8,4},{12,0},{1,13},{5,9},{9,5},{13,1},{2,14},{6,10},... | collective-permute-start | bytes 2359304 | tf_op jit(solution)/shard_map/ppermute | solution.py:50
  909.5 339.2 %reduce-scatter.8.cloned.1.call-start = ((), (), s32[]{:S(2)}) async-start(), calls=%async_computation.5 | async-start | bytes 26542080 | tf_op jit(solution)/shard_map/reduce_scatter | solution.py:1163
  955.4 36.3 %collective-permute-start.57 = (bf16[256,1664]{1,0:T(8,128)(2,1)S(1)}, bf16[256,1664]{1,0:T(8,128)(2,1)}, u32[]{:S(2)}, u32[]{:S(2)}) collective-permute-start(bf16[256,1664]{1,0:T(8,128)(2,1)S(1)} %get-tuple-element.272), channel_id=1, source_target_pairs={{0,4},{4,0},{8,12},{12,8},{1,5},{5,1},{9,13},{13,9},{2,6},{6,2},{1... | collective-permute-start | bytes 2555912 | tf_op jit(solution)/shard_map/ppermute | solution.py:50
  955.6 38.9 %collective-permute-start.58 = (bf16[256,1664]{1,0:T(8,128)(2,1)S(1)}, bf16[256,1664]{1,0:T(8,128)(2,1)}, u32[]{:S(2)}, u32[]{:S(2)}) collective-permute-start(bf16[256,1664]{1,0:T(8,128)(2,1)S(1)} %get-tuple-element.271), channel_id=1, source_target_pairs={{0,8},{4,12},{8,0},{12,4},{1,9},{5,13},{9,1},{13,5},{2,10},{6,14},... | collective-permute-start | bytes 2555912 | tf_op jit(solution)/shard_map/ppermute | solution.py:50
  957.8 72.1 %collective-permute-start.59 = (bf16[256,1664]{1,0:T(8,128)(2,1)S(1)}, bf16[256,1664]{1,0:T(8,128)(2,1)}, u32[]{:S(2)}, u32[]{:S(2)}) collective-permute-start(bf16[256,1664]{1,0:T(8,128)(2,1)S(1)} %get-tuple-element.270), channel_id=1, source_target_pairs={{0,12},{4,8},{8,4},{12,0},{1,13},{5,9},{9,5},{13,1},{2,14},{6,10},... | collective-permute-start | bytes 2555912 | tf_op jit(solution)/shard_map/ppermute | solution.py:50
  1041.0 32.1 %collective-permute-start.60 = (bf16[96,2176]{1,0:T(8,128)(2,1)}, bf16[96,2176]{1,0:T(8,128)(2,1)S(1)}, u32[]{:S(2)}, u32[]{:S(2)}) collective-permute-start(bf16[96,2176]{1,0:T(8,128)(2,1)} %get-tuple-element.302), channel_id=1, source_target_pairs={{0,4},{4,0},{8,12},{12,8},{1,5},{5,1},{9,13},{13,9},{2,6},{6,2},{1... | collective-permute-start | bytes 1253384 | tf_op jit(solution)/shard_map/ppermute | solution.py:50
  1041.0 33.6 %collective-permute-start.61 = (bf16[96,2176]{1,0:T(8,128)(2,1)S(1)}, bf16[96,2176]{1,0:T(8,128)(2,1)S(1)}, u32[]{:S(2)}, u32[]{:S(2)}) collective-permute-start(bf16[96,2176]{1,0:T(8,128)(2,1)S(1)} %get-tuple-element.301), channel_id=1, source_target_pairs={{0,8},{4,12},{8,0},{12,4},{1,9},{5,13},{9,1},{13,5},{2,10},{6,14},... | collective-permute-start | bytes 1253384 | tf_op jit(solution)/shard_map/ppermute | solution.py:50
  1044.5 33.8 %collective-permute-start.62 = (bf16[96,2176]{1,0:T(8,128)(2,1)S(1)}, bf16[96,2176]{1,0:T(8,128)(2,1)S(1)}, u32[]{:S(2)}, u32[]{:S(2)}) collective-permute-start(bf16[96,2176]{1,0:T(8,128)(2,1)S(1)} %get-tuple-element.300), channel_id=1, source_target_pairs={{0,12},{4,8},{8,4},{12,0},{1,13},{5,9},{9,5},{13,1},{2,14},{6,10},... | collective-permute-start | bytes 1253384 | tf_op jit(solution)/shard_map/ppermute | solution.py:50
  1073.1 31.9 %collective-permute-start.65 = (bf16[256,1024]{1,0:T(8,128)(2,1)}, bf16[256,1024]{1,0:T(8,128)(2,1)}, u32[]{:S(2)}, u32[]{:S(2)}) collective-permute-start(bf16[256,1024]{1,0:T(8,128)(2,1)} %get-tuple-element.160), channel_id=1, source_target_pairs={{0,3},{1,2},{2,1},{3,0},{4,7},{5,6},{6,5},{7,4},{8,11},{9,10},{10,... | collective-permute-start | bytes 1572872 | tf_op jit(solution)/shard_map/ppermute | solution.py:50
  1123.6 18.3 %collective-permute-start.67 = (bf16[4,4,96,1408]{3,2,1,0:T(8,128)(2,1)}, bf16[4,4,96,1408]{3,2,1,0:T(8,128)(2,1)}, u32[]{:S(2)}, u32[]{:S(2)}) collective-permute-start(bf16[4,4,96,1408]{3,2,1,0:T(8,128)(2,1)} %constant_dynamic-slice_fusion.1), channel_id=1, source_target_pairs={{0,16},{16,0},{1,17},{17,1},{2,18},{18,2},{3,19},{19,3},{4,20},{20... | collective-permute-start | bytes 12976136 | tf_op jit(solution)/shard_map/ppermute | solution.py:34
  1149.1 37.9 %collective-permute-start.68 = (bf16[4,96,1408]{2,1,0:T(8,128)(2,1)}, bf16[4,96,1408]{2,1,0:T(8,128)(2,1)S(1)}, u32[]{:S(2)}, u32[]{:S(2)}) collective-permute-start(bf16[4,96,1408]{2,1,0:T(8,128)(2,1)} %get-tuple-element.166), channel_id=1, source_target_pairs={{0,1},{1,0},{2,3},{3,2},{4,5},{5,4},{6,7},{7,6},{8,9},{9,8},{10,11... | collective-permute-start | bytes 3244040 | tf_op jit(solution)/shard_map/ppermute | solution.py:50
  1149.1 39.9 %collective-permute-start.69 = (bf16[4,96,1408]{2,1,0:T(8,128)(2,1)}, bf16[4,96,1408]{2,1,0:T(8,128)(2,1)S(1)}, u32[]{:S(2)}, u32[]{:S(2)}) collective-permute-start(bf16[4,96,1408]{2,1,0:T(8,128)(2,1)} %get-tuple-element.167), channel_id=1, source_target_pairs={{0,2},{1,3},{2,0},{3,1},{4,6},{5,7},{6,4},{7,5},{8,10},{9,11},{10,... | collective-permute-start | bytes 3244040 | tf_op jit(solution)/shard_map/ppermute | solution.py:50
  1150.2 83.5 %collective-permute-start.70 = (bf16[4,96,1408]{2,1,0:T(8,128)(2,1)}, bf16[4,96,1408]{2,1,0:T(8,128)(2,1)}, u32[]{:S(2)}, u32[]{:S(2)}) collective-permute-start(bf16[4,96,1408]{2,1,0:T(8,128)(2,1)} %get-tuple-element.168), channel_id=1, source_target_pairs={{0,3},{1,2},{2,1},{3,0},{4,7},{5,6},{6,5},{7,4},{8,11},{9,10},{10,... | collective-permute-start | bytes 3244040 | tf_op jit(solution)/shard_map/ppermute | solution.py:50
  1156.1 80.1 %collective-permute-start.72 = (bf16[4,96,768]{2,1,0:T(8,128)(2,1)S(1)}, bf16[4,96,768]{2,1,0:T(8,128)(2,1)S(1)}, u32[]{:S(2)}, u32[]{:S(2)}) collective-permute-start(bf16[4,96,768]{2,1,0:T(8,128)(2,1)S(1)} %get-tuple-element.265), channel_id=1, source_target_pairs={{0,4},{4,0},{8,12},{12,8},{1,5},{5,1},{9,13},{13,9},{2,6},{6,2},{1... | collective-permute-start | bytes 1769480 | tf_op jit(solution)/shard_map/ppermute | solution.py:50
  1157.6 78.7 %collective-permute-start.73 = (bf16[4,96,768]{2,1,0:T(8,128)(2,1)S(1)}, bf16[4,96,768]{2,1,0:T(8,128)(2,1)S(1)}, u32[]{:S(2)}, u32[]{:S(2)}) collective-permute-start(bf16[4,96,768]{2,1,0:T(8,128)(2,1)S(1)} %get-tuple-element.267), channel_id=1, source_target_pairs={{0,8},{4,12},{8,0},{12,4},{1,9},{5,13},{9,1},{13,5},{2,10},{6,14},... | collective-permute-start | bytes 1769480 | tf_op jit(solution)/shard_map/ppermute | solution.py:50
  1186.9 49.3 %collective-permute-start.74 = (bf16[4,96,768]{2,1,0:T(8,128)(2,1)S(1)}, bf16[4,96,768]{2,1,0:T(8,128)(2,1)S(1)}, u32[]{:S(2)}, u32[]{:S(2)}) collective-permute-start(bf16[4,96,768]{2,1,0:T(8,128)(2,1)S(1)} %get-tuple-element.266), channel_id=1, source_target_pairs={{0,12},{4,8},{8,4},{12,0},{1,13},{5,9},{9,5},{13,1},{2,14},{6,10},... | collective-permute-start | bytes 1769480 | tf_op jit(solution)/shard_map/ppermute | solution.py:50
  1253.5 15.7 %collective-permute-start.76 = (bf16[5,384,768]{2,1,0:T(8,128)(2,1)S(1)}, bf16[5,384,768]{2,1,0:T(8,128)(2,1)S(1)}, u32[]{:S(2)}, u32[]{:S(2)}) collective-permute-start(bf16[5,384,768]{2,1,0:T(8,128)(2,1)S(1)} %get-tuple-element.268), channel_id=1, source_target_pairs={{0,16},{16,0},{1,17},{17,1},{2,18},{18,2},{3,19},{19,3},{4,20},{20... | collective-permute-start | bytes 8847368 | tf_op jit(solution)/shard_map/ppermute | solution.py:34
  1260.9 33.8 %collective-permute-start.66 = (bf16[256,1536]{1,0:T(8,128)(2,1)}, bf16[256,1536]{1,0:T(8,128)(2,1)S(1)}, u32[]{:S(2)}, u32[]{:S(2)}) collective-permute-start(bf16[256,1536]{1,0:T(8,128)(2,1)} %get-tuple-element.250), channel_id=1, source_target_pairs={{0,16},{16,0},{1,17},{17,1},{2,18},{18,2},{3,19},{19,3},{4,20},{20... | collective-permute-start | bytes 2359304 | tf_op jit(solution)/shard_map/ppermute | solution.py:34
  1265.9 18.3 %collective-permute-start.77 = (bf16[96,1408]{1,0:T(8,128)(2,1)}, bf16[96,1408]{1,0:T(8,128)(2,1)S(1)}, u32[]{:S(2)}, u32[]{:S(2)}) collective-permute-start(bf16[96,1408]{1,0:T(8,128)(2,1)} %get-tuple-element.292), channel_id=1, source_target_pairs={{0,8},{4,12},{8,0},{12,4},{1,9},{5,13},{9,1},{13,5},{2,10},{6,14},... | collective-permute-start | bytes 811016 | tf_op jit(solution)/shard_map/ppermute | solution.py:50
  1267.9 25.1 %collective-permute-start.78 = (bf16[96,1408]{1,0:T(8,128)(2,1)}, bf16[96,1408]{1,0:T(8,128)(2,1)}, u32[]{:S(2)}, u32[]{:S(2)}) collective-permute-start(bf16[96,1408]{1,0:T(8,128)(2,1)} %get-tuple-element.291), channel_id=1, source_target_pairs={{0,12},{4,8},{8,4},{12,0},{1,13},{5,9},{9,5},{13,1},{2,14},{6,10},... | collective-permute-start | bytes 811016 | tf_op jit(solution)/shard_map/ppermute | solution.py:50
  (102 other events, 1969.2 us)
Sparse Core Ops, SparseCore 0:
  84.0 36.2 all-gather.10
  122.8 153.0 all-gather.8
  277.8 75.4 all-gather.12
  355.0 141.1 all-gather.14
  746.2 163.1 reduce-scatter.3
  913.4 96.5 reduce-scatter.5
  1038.9 201.4 reduce-scatter.7
